TPU v7x, 32 devices: a whole 2x2x4 slice. The times are simulated.
32 devices in a mesh: groups: 2 (over y), date: 8 (over z, x), strip: 2 (over core).
Axes of the slice: x: 2, y: 2, z: 4, core: 2. Of those that a mesh axis runs over, the one named last changes fastest.
Arguments:
- slc: bfloat16 [2, 48, 128, 1024], P(None, 'date', 'groups', 'strip'), parts along dimension 2, may hold values from -60 to 60
- pair_list: int32 [192, 2], replicated, may hold values from 0 to 47, as said below
- az_half: int32 [192], replicated, may hold values from 4 to 8
- rng_half: int32 [192], replicated, may hold values from 12 to 16
Outputs:
- coherence: float32 [2, 192, 128, 1024], P(None, 'date', 'groups', 'strip'), parts along dimension 2
There are 2 independent parts, one for each index of `groups`. A program takes and returns all parts, laid end to end along the dimension named above; an argument that names none is the same for every part. Nothing has to cross between parts.
Inputs may be any that keep to these rules, and one draw needn't show every extreme that they name: `pair_list`: row (4) d + j has reference date d. For j < 3 its secondary is d + (j + 1) c_d with a sign c_d of +1 or -1 shared by the 3 rows of date d; row (4) d + 3 has secondary d + e_d g_d with e_d of +1 or -1 and g_d between 22 and 24.
All inputs are finite; a program needn't handle non-finite values.
Results may differ from a plain program's by a relative error of at most 0.0003.
Values may be sent and summed in bfloat16 or wider, within the bound.
No kernel may reach another device: no remote copies, remote signals or barrier semaphores. Data moves between devices by JAX's collectives and lax.ppermute only.
A program may use at most 128 MiB of HBM per device.

v0:
```python
from functools import reduce

import jax
import jax.numpy as jnp
from jax import lax
from jax.sharding import PartitionSpec as P

HALO = 16
NEAR = 3
YEAR = 29


EPSILON = 1e-06


def padded(cells, sides, width):
    for axis, dim in sides:
        count = lax.axis_size(axis)
        ends = count - 1
        head = lax.slice_in_dim(cells, 0, width, axis=dim)
        tail = lax.slice_in_dim(cells, cells.shape[dim] - width, cells.shape[dim], axis=dim)
        cells = jnp.concatenate(
            [
                lax.ppermute(tail, axis, [(i, (i + 1) % count) for i in range(ends)]),
                cells,
                lax.ppermute(head, axis, [((i + 1) % count, i) for i in range(ends)]),
            ],
            axis=dim,
        )
    return cells


def passed_along(block, axis, distance):
    devices = range(lax.axis_size(axis))
    route = [(i - distance, i) for i in devices if i - distance in devices]
    return lax.ppermute(block, axis, route)


def pair_products(first_strip, second_strip):
    a_real = first_strip[0].astype(jnp.float32)
    a_imag = first_strip[1].astype(jnp.float32)
    b_real = second_strip[0].astype(jnp.float32)
    b_imag = second_strip[1].astype(jnp.float32)
    return jnp.stack(
        [
            a_real * b_real + a_imag * b_imag,
            a_imag * b_real - a_real * b_imag,
            a_real * a_real + a_imag * a_imag,
            b_real * b_real + b_imag * b_imag,
        ]
    )


def range_looks(cross_terms, reaches, out_width):
    in_width = cross_terms.shape[3]
    margin = (in_width - out_width) // 2
    tile_width = 128
    tile_count = out_width // tile_width
    windows = jnp.stack(
        [
            cross_terms[:, :, :, tile * tile_width : tile * tile_width + tile_width + 2 * margin]
            for tile in range(tile_count)
        ],
        axis=3,
    )
    in_index = jnp.arange(tile_width + 2 * margin, dtype=jnp.int32)[None, :, None]
    out_index = jnp.arange(tile_width, dtype=jnp.int32)[None, None, :]
    band_cols = (jnp.abs(in_index - margin - out_index) <= reaches[:, None, None]).astype(
        jnp.float32
    )
    summed = jnp.einsum("qprtc,pcw->qprtw", windows, band_cols, precision=lax.Precision.HIGHEST)
    return summed.reshape(summed.shape[0], summed.shape[1], summed.shape[2], out_width)


def azimuth_looks(ranged, heights):
    row_count = ranged.shape[2]
    row_index = jnp.arange(row_count, dtype=jnp.int32)
    band_rows = (
        jnp.abs(row_index[None, :, None] - row_index[None, None, :]) <= heights[:, None, None]
    ).astype(jnp.float32)
    looked = jnp.einsum("pab,qpbc->qpac", band_rows, ranged, precision=lax.Precision.HIGHEST)
    inverse = lax.rsqrt(looked[2] * looked[3] + EPSILON)
    return jnp.stack([looked[0] * inverse, looked[1] * inverse])


def body(slc, pair_list, az_half, rng_half):
    date_count = slc.shape[1]
    out_width = slc.shape[3]
    devices = lax.axis_size("date")
    per_date = pair_list.shape[0] // (date_count * devices)
    pair_count = per_date * date_count
    pair_start = lax.axis_index("date") * pair_count
    total_dates = date_count * devices
    year_low = min(YEAR, total_dates // 2 - 2)
    widened = padded(slc, (("strip", 3),), HALO)
    my_pairs = lax.dynamic_slice_in_dim(pair_list, pair_start, pair_count, 0)
    my_reach = lax.dynamic_slice_in_dim(rng_half, pair_start, pair_count, 0)
    first_date = lax.axis_index("date") * date_count
    nearby = padded(widened, (("date", 1),), NEAR)
    annual_of = pair_list[:, 1].reshape(total_dates, per_date)[:, per_date - 1]
    arrivals = [[] for own_slot in range(date_count)]
    for direction in (1, -1):
        by_distance = {}
        for own_slot in range(date_count):
            for gap_size in range(year_low, year_low + 3):
                distance = direction * ((own_slot + direction * gap_size) // date_count)
                if distance in by_distance:
                    by_distance[distance] = by_distance[distance] + [own_slot]
                else:
                    by_distance[distance] = [own_slot]
        for distance in sorted(by_distance):
            slot_list = sorted(set(by_distance[distance]))
            receiver = lax.axis_index("date") - direction * distance
            rec_dates = receiver * date_count + jnp.array(slot_list, dtype=jnp.int32)
            inside = (rec_dates >= 0) & (rec_dates < total_dates)
            wanted = jnp.take(annual_of, jnp.clip(rec_dates, 0, total_dates - 1))
            local_index = wanted - first_date
            usable = inside & (local_index >= 0) & (local_index < date_count)
            packed = jnp.take(widened, jnp.clip(local_index, 0, date_count - 1), axis=1)
            packed = jnp.where(usable[None, :, None, None], packed, jnp.zeros_like(packed))
            if direction == 1:
                arrived = passed_along(packed, "date", -distance)
            else:
                arrived = passed_along(packed, "date", distance)
            for slot_pos, own_slot in enumerate(slot_list):
                arrivals[own_slot].append(arrived[:, slot_pos])
    annual_strips = jnp.stack(
        [reduce(jnp.add, slot_arrivals) for slot_arrivals in arrivals], axis=1
    )
    near_index = jnp.clip(my_pairs[:, 1] - first_date + NEAR, 0, date_count + 2 * NEAR - 1)
    near_strips = jnp.take(nearby, near_index, axis=1)
    shaped = near_strips.reshape(
        2, date_count, per_date, near_strips.shape[2], near_strips.shape[3]
    )
    sec_strips = jnp.concatenate([shaped[:, :, :NEAR], annual_strips[:, :, None]], axis=2).reshape(
        near_strips.shape
    )
    ref_strips = jnp.take(widened, my_pairs[:, 0] - first_date, axis=1)
    ranged = range_looks(pair_products(ref_strips, sec_strips), my_reach, out_width)
    my_heights = lax.dynamic_slice_in_dim(az_half, pair_start, pair_count, 0)
    return azimuth_looks(ranged, my_heights)


def solution(mesh):
    placed = (P(None, "date", "groups", "strip"), P(), P(), P())
    return jax.shard_map(
        body,
        mesh=mesh,
        in_specs=placed,
        out_specs=P(None, "date", "groups", "strip"),
        check_vma=False,
    )
```

profile of v0, /device:TPU:15, one launch (start us, length us, event | category | flops | bytes accessed | tf_op | source)
XLA Modules:
  0.0 172.1 jit_solution(13481519174907657230)
XLA Ops:
  0.0 1.1 fusion.50
  1.2 1.3 collective-permute-start
  2.5 3.0 %collective-permute-start.1 = (bf16[2,6,64,16]{3,2,1,0:T(8,128)(2,1)S(1)}, bf16[2,6,64,16]{3,2,1,0:T(8,128)(2,1)S(1)}, u32[]{:S(2)}, u32[]{:S(2)}) collective-permute-start(bf16[2,6,64,16]{3,2,1,0:T(8,128)(2,1)S(1)} %get-tuple-element.44), channel_id=1, source_target_pairs={{1,0},{3,2},{5,4},{7,6},{9,8},{11,10},{13,12},{15,14},{17,16},{19,... | collective-permute-start | bytes 73736 | tf_op jit(solution)/shard_map/ppermute | solution.py:26
  5.6 0.7 slice_reduce_fusion.1
  6.3 0.1 reshape_squeeze.3
  6.4 0.2 slice_reduce_fusion
  6.6 0.6 gather_fusion.4
  7.2 0.6 gather_fusion.6
  8.0 0.6 gather_fusion.2
  8.7 0.7 compare_select_fusion.1
  9.3 0.6 gather_fusion.8
  10.0 0.7 compare_and_fusion.4
  10.7 0.8 constant_dynamic-slice_fusion
  11.5 0.7 subtract_abs_fusion
  12.2 0.1 broadcast_in_dim.87
  12.3 0.8 dynamic_slice.9
  13.1 0.8 dynamic_slice.11
  13.8 0.0 collective-permute-done
  13.8 0.0 collective-permute-done.1
  13.8 1.7 pad_maximum_fusion.4
  15.5 1.1 fusion.49
  16.6 0.7 gather_fusion.5
  17.4 1.1 bitcast_select_fusion.1
  18.5 1.3 collective-permute-start.5
  19.8 0.7 gather_fusion.7
  20.5 1.2 bitcast_select_fusion
  21.7 6.8 %collective-permute-start.6 = (bf16[2,6,64,544]{3,2,0,1:T(8,128)(2,1)}, bf16[2,6,64,544]{3,2,0,1:T(8,128)(2,1)}, u32[]{:S(2)}, u32[]{:S(2)}) collective-permute-start(bf16[2,6,64,544]{3,2,0,1:T(8,128)(2,1)} %bitcast_select_fusion), channel_id=1, source_target_pairs={{0,8},{2,10},{4,12},{6,14},{1,9},{3,11},{5,13},{7,15},{16,24},{18,... | collective-permute-start | bytes 2506760 | tf_op jit(solution)/shard_map/ppermute | solution.py:36
  28.5 0.6 gather_fusion.3
  29.1 0.8 bitcast_select_fusion.3
  29.9 2.0 %collective-permute-start.4 = (bf16[2,2,64,544]{3,2,0,1:T(8,128)(2,1)}, bf16[2,2,64,544]{3,2,0,1:T(8,128)(2,1)S(1)}, u32[]{:S(2)}, u32[]{:S(2)}) collective-permute-start(bf16[2,2,64,544]{3,2,0,1:T(8,128)(2,1)} %bitcast_select_fusion.3), channel_id=1, source_target_pairs={{6,0},{8,2},{10,4},{12,6},{14,8},{7,1},{9,3},{11,5},{13,7},{15,9},... | collective-permute-start | bytes 835592 | tf_op jit(solution)/shard_map/ppermute | solution.py:36
  32.0 4.0 %collective-permute-start.2 = (bf16[2,3,64,544]{3,2,1,0:T(8,128)(2,1)}, bf16[2,3,64,544]{3,2,1,0:T(8,128)(2,1)S(1)}, u32[]{:S(2)}, u32[]{:S(2)}) collective-permute-start(bf16[2,3,64,544]{3,2,1,0:T(8,128)(2,1)} %get-tuple-element.41), channel_id=1, source_target_pairs={{0,2},{2,4},{4,6},{6,8},{8,10},{10,12},{12,14},{1,3},{3,5},{5,7},{... | collective-permute-start | bytes 1253384 | tf_op jit(solution)/shard_map/ppermute | solution.py:24
  36.0 1.9 %collective-permute-start.3 = (bf16[2,3,64,544]{3,2,1,0:T(8,128)(2,1)}, bf16[2,3,64,544]{3,2,1,0:T(8,128)(2,1)}, u32[]{:S(2)}, u32[]{:S(2)}) collective-permute-start(bf16[2,3,64,544]{3,2,1,0:T(8,128)(2,1)} %get-tuple-element.42), channel_id=1, source_target_pairs={{2,0},{4,2},{6,4},{8,6},{10,8},{12,10},{14,12},{3,1},{5,3},{7,5},{... | collective-permute-start | bytes 1253384 | tf_op jit(solution)/shard_map/ppermute | solution.py:26
  37.9 3.2 %gather_fusion = bf16[24,2,64,544]{3,2,1,0:T(8,128)(2,1)} fusion(bf16[2,6,64,544]{3,2,1,0:T(8,128)(2,1)S(1)} %pad_maximum_fusion.4, s32[1024]{0:T(1024)S(1)} %pad_clamp_fusion.9), kind=kCustom, calls=%fused_computation.8 | custom fusion | bytes 6684768 | tf_op jit(solution)/shard_map/jit(_take)/gather | solution.py:138
  41.1 4.5 %select_bitcast_fusion = bf16[2,24,64,544]{3,2,0,1:T(8,128)(2,1)} fusion(bf16[24,2,64,544]{3,2,1,0:T(8,128)(2,1)} %gather_fusion, pred[24]{0:T(512)(128)(4,1)S(1)} %get-tuple-element.6), kind=kLoop, calls=%fused_computation.43 | loop fusion | flops 1671168 | bytes 6684696 | tf_op jit(solution)/shard_map/jit(_take)/select_n | solution.py:138
  45.6 0.6 gather_fusion.9
  46.3 0.9 bitcast_select_fusion.2
  47.1 33.7 %collective-permute-done.2 = bf16[2,3,64,544]{3,2,1,0:T(8,128)(2,1)S(1)} collective-permute-done((bf16[2,3,64,544]{3,2,1,0:T(8,128)(2,1)}, bf16[2,3,64,544]{3,2,1,0:T(8,128)(2,1)S(1)}, u32[]{:S(2)}, u32[]{:S(2)}) %collective-permute-start.2) | collective-permute-done | bytes 417824 | tf_op jit(solution)/shard_map/ppermute | solution.py:24
  80.9 1.9 %collective-permute-start.7 = (bf16[2,2,64,544]{3,2,0,1:T(8,128)(2,1)}, bf16[2,2,64,544]{3,2,0,1:T(8,128)(2,1)}, u32[]{:S(2)}, u32[]{:S(2)}) collective-permute-start(bf16[2,2,64,544]{3,2,0,1:T(8,128)(2,1)} %bitcast_select_fusion.2), channel_id=1, source_target_pairs={{0,6},{2,8},{4,10},{6,12},{8,14},{1,7},{3,9},{5,11},{7,13},{9,15},... | collective-permute-start | bytes 835592 | tf_op jit(solution)/shard_map/ppermute | solution.py:36
  82.8 0.0 copy-done.2
  82.8 9.9 %collective-permute-done.3 = bf16[2,3,64,544]{3,2,1,0:T(8,128)(2,1)} collective-permute-done((bf16[2,3,64,544]{3,2,1,0:T(8,128)(2,1)}, bf16[2,3,64,544]{3,2,1,0:T(8,128)(2,1)}, u32[]{:S(2)}, u32[]{:S(2)}) %collective-permute-start.3) | collective-permute-done | bytes 417824 | tf_op jit(solution)/shard_map/ppermute | solution.py:26
  92.7 1.8 %pad_maximum_fusion.3 = bf16[2,12,64,544]{3,2,1,0:T(8,128)(2,1)S(1)} fusion(bf16[2,3,64,544]{3,2,1,0:T(8,128)(2,1)} %collective-permute-done.3, bf16[2,6,64,16]{3,2,1,0:T(8,128)(2,1)S(1)} %collective-permute-done.1, bf16[2,6,64,512]{3,2,1,0:T(8,128)(2,1)S(1)} %copy-done.1, bf16[2,6,64,16]{3,2,1,0:T(8,128)(2,1)S(1)} %collective-permute-done, ...), kind=kLoop, calls=%fused_computation.52 | loop fusion | flops 8355840 | bytes 3342336 | tf_op jit(solution)/shard_map/concatenate | solution.py:22
  94.5 3.2 %gather_fusion.1 = bf16[24,2,64,544]{3,2,1,0:T(8,128)(2,1)} fusion(bf16[2,12,64,544]{3,2,1,0:T(8,128)(2,1)S(1)} %pad_maximum_fusion.3, s32[1024]{0:T(1024)S(1)} %pad_clamp_fusion.8), kind=kCustom, calls=%fused_computation.9 | custom fusion | bytes 6684768 | tf_op jit(solution)/shard_map/jit(_take)/gather | solution.py:131
  97.6 2.7 %copy_select_fusion = bf16[2,6,3,64,544]{4,3,2,1,0:T(8,128)(2,1)S(1)} fusion(pred[6,3]{1,0:T(8,128)(4,1)S(1)} %bitcast.65, bf16[2,6,4,64,544]{4,3,0,2,1:T(8,128)(2,1)} %bitcast.60), kind=kLoop, calls=%fused_computation.49 | loop fusion | flops 1253376 | bytes 5455890 | tf_op jit(solution)/shard_map/jit(_take)/select_n | solution.py:131
  100.4 0.0 collective-permute-done.4
  100.4 0.0 collective-permute-done.5
  100.4 0.0 collective-permute-done.6
  100.4 1.1 fusion.37
  101.5 1.1 fusion.36
  102.6 1.0 fusion.35
  103.6 1.0 fusion.34
  104.6 0.0 collective-permute-done.7
  104.7 1.2 fusion.33
  105.8 1.2 fusion.32
  107.0 0.8 pad_maximum_fusion.2
  107.8 1.3 copy-done
  109.1 2.6 %fusion.18 = (f32[1,24,64,544]{3,2,0,1:T(8,128)S(1)}, f32[1,24,64,544]{3,2,0,1:T(8,128)S(1)}, f32[1,24,64,544]{3,2,0,1:T(8,128)S(1)}, f32[1,24,64,544]{3,2,0,1:T(8,128)S(1)}) fusion(bf16[1,24,64,544]{3,2,0,1:T(8,128)(2,1)S(1)} %bitcast.62, bf16[1,24,64,544]{3,2,0,1:T(8,128)(2,1)S(1)} %bitcast.61, bf16[2,24,64,544]{3,2,0,1:T(8,128)(2,1)S(1)} %copy-done), kind=kLoop, calls=%fused_computation.38 | loop fusion | flops 13369344 | bytes 20054016 | tf_op jit(solution)/shard_map/add | solution.py:46
  111.7 5.8 %pad_maximum_fusion = f32[4,24,64,544]{3,2,0,1:T(8,128)} fusion(f32[1,24,64,544]{3,2,0,1:T(8,128)S(1)} %get-tuple-element.38, f32[1,24,64,544]{3,2,0,1:T(8,128)S(1)} %get-tuple-element.37, f32[1,24,64,544]{3,2,0,1:T(8,128)S(1)} %get-tuple-element.36, f32[1,24,64,544]{3,2,0,1:T(8,128)S(1)} %get-tuple-element.35), kind=kLoop, calls=%fused_computation.18 | loop fusion | flops 10027008 | bytes 26738688 | tf_op jit(solution)/shard_map/stack | solution.py:44
  117.5 18.1 %slice_bitcast_fusion.3 = (f32[4,24,64,1,160]{4,2,3,0,1:T(8,128)}, f32[4,24,64,1,160]{4,2,3,0,1:T(8,128)}, f32[4,24,64,1,160]{4,2,3,0,1:T(8,128)}, f32[4,24,64,1,160]{4,2,3,0,1:T(8,128)}) fusion(f32[4,24,64,544]{3,2,0,1:T(8,128)} %pad_maximum_fusion), kind=kLoop, calls=%fused_computation.25 | loop fusion | bytes 31457280 | tf_op jit(solution)/shard_map/stack | solution.py:59
  135.5 0.0 copy-done.3
  135.5 18.9 %fusion.14 = f32[24,4,4,8,8,128]{5,4,3,2,1,0:T(8,128)} fusion(f32[4,24,64,1,160]{4,2,3,0,1:T(8,128)} %get-tuple-element.30, f32[4,24,64,1,160]{4,2,3,0,1:T(8,128)} %get-tuple-element.31, f32[4,24,64,1,160]{4,2,3,0,1:T(8,128)} %get-tuple-element.32, f32[4,24,64,1,160]{4,2,3,0,1:T(8,128)} %get-tuple-element.29, s32[160,128]{1,0:T(8,128)S(1)} %copy-done.3, ...), kind=kOutput, calls=%fused_computation.36 | convolution fusion | flops 6052085760 | bytes 28393568 | tf_op jit(solution)/shard_map/qprtc,pcw->qprtw/dot_general | solution.py:71
  154.5 11.4 %fusion.11 = f32[4,24,64,512]{3,2,0,1:T(8,128)S(1)} fusion(f32[24,4,4,8,8,128]{5,4,3,2,1,0:T(8,128)} %fusion.14, s32[64,64]{1,0:T(8,128)S(1)} %subtract_abs_fusion.1, s32[24]{0:T(128)S(1)} %dynamic_slice.11), kind=kOutput, calls=%fused_computation.35 | convolution fusion | flops 2416017408 | bytes 25182304 | tf_op jit(solution)/shard_map/pab,qpbc->qpac/dot_general | solution.py:81
  165.9 1.9 %slice_multiply_fusion.2 = (f32[1,24,64,512]{3,2,0,1:T(8,128)S(1)}, f32[1,24,64,512]{3,2,0,1:T(8,128)S(1)}) fusion(f32[4,24,64,512]{3,2,0,1:T(8,128)S(1)} %fusion.11), kind=kLoop, calls=%fused_computation.48 | loop fusion | flops 3145728 | bytes 18874368 | tf_op jit(solution)/shard_map/mul | solution.py:83
  167.8 0.9 pad_maximum_fusion.1
  168.6 3.4 %copy.31 = f32[2,24,64,512]{3,2,1,0:T(8,128)} copy(f32[2,24,64,512]{3,2,0,1:T(8,128)S(1)} %pad_maximum_fusion.1) | data formatting | bytes 12582912 | tf_op jit(solution)/shard_map/stack | solution.py:83
  (26 shorter events, 0.2 us)
Async XLA Ops:
  1.2 12.7 %collective-permute-start = (bf16[2,6,64,16]{3,2,1,0:T(8,128)(2,1)S(1)}, bf16[2,6,64,16]{3,2,1,0:T(8,128)(2,1)S(1)}, u32[]{:S(2)}, u32[]{:S(2)}) collective-permute-start(bf16[2,6,64,16]{3,2,1,0:T(8,128)(2,1)S(1)} %get-tuple-element.43), channel_id=1, source_target_pairs={{0,1},{2,3},{4,5},{6,7},{8,9},{10,11},{12,13},{14,15},{16,17},{18,... | collective-permute-start | bytes 73736 | tf_op jit(solution)/shard_map/ppermute | solution.py:24
  2.5 11.4 %collective-permute-start.1 = (bf16[2,6,64,16]{3,2,1,0:T(8,128)(2,1)S(1)}, bf16[2,6,64,16]{3,2,1,0:T(8,128)(2,1)S(1)}, u32[]{:S(2)}, u32[]{:S(2)}) collective-permute-start(bf16[2,6,64,16]{3,2,1,0:T(8,128)(2,1)S(1)} %get-tuple-element.44), channel_id=1, source_target_pairs={{1,0},{3,2},{5,4},{7,6},{9,8},{11,10},{13,12},{15,14},{17,16},{19,... | collective-permute-start | bytes 73736 | tf_op jit(solution)/shard_map/ppermute | solution.py:26
  18.5 81.9 %collective-permute-start.5 = (bf16[2,6,64,544]{3,2,0,1:T(8,128)(2,1)}, bf16[2,6,64,544]{3,2,0,1:T(8,128)(2,1)}, u32[]{:S(2)}, u32[]{:S(2)}) collective-permute-start(bf16[2,6,64,544]{3,2,0,1:T(8,128)(2,1)} %bitcast_select_fusion.1), channel_id=1, source_target_pairs={{8,0},{10,2},{12,4},{14,6},{9,1},{11,3},{13,5},{15,7},{24,16},{26,... | collective-permute-start | bytes 2506760 | tf_op jit(solution)/shard_map/ppermute | solution.py:36
  21.7 78.7 %collective-permute-start.6 = (bf16[2,6,64,544]{3,2,0,1:T(8,128)(2,1)}, bf16[2,6,64,544]{3,2,0,1:T(8,128)(2,1)}, u32[]{:S(2)}, u32[]{:S(2)}) collective-permute-start(bf16[2,6,64,544]{3,2,0,1:T(8,128)(2,1)} %bitcast_select_fusion), channel_id=1, source_target_pairs={{0,8},{2,10},{4,12},{6,14},{1,9},{3,11},{5,13},{7,15},{16,24},{18,... | collective-permute-start | bytes 2506760 | tf_op jit(solution)/shard_map/ppermute | solution.py:36
  29.9 70.5 %collective-permute-start.4 = (bf16[2,2,64,544]{3,2,0,1:T(8,128)(2,1)}, bf16[2,2,64,544]{3,2,0,1:T(8,128)(2,1)S(1)}, u32[]{:S(2)}, u32[]{:S(2)}) collective-permute-start(bf16[2,2,64,544]{3,2,0,1:T(8,128)(2,1)} %bitcast_select_fusion.3), channel_id=1, source_target_pairs={{6,0},{8,2},{10,4},{12,6},{14,8},{7,1},{9,3},{11,5},{13,7},{15,9},... | collective-permute-start | bytes 835592 | tf_op jit(solution)/shard_map/ppermute | solution.py:36
  32.0 48.9 %collective-permute-start.2 = (bf16[2,3,64,544]{3,2,1,0:T(8,128)(2,1)}, bf16[2,3,64,544]{3,2,1,0:T(8,128)(2,1)S(1)}, u32[]{:S(2)}, u32[]{:S(2)}) collective-permute-start(bf16[2,3,64,544]{3,2,1,0:T(8,128)(2,1)} %get-tuple-element.41), channel_id=1, source_target_pairs={{0,2},{2,4},{4,6},{6,8},{8,10},{10,12},{12,14},{1,3},{3,5},{5,7},{... | collective-permute-start | bytes 1253384 | tf_op jit(solution)/shard_map/ppermute | solution.py:24
  36.0 56.6 %collective-permute-start.3 = (bf16[2,3,64,544]{3,2,1,0:T(8,128)(2,1)}, bf16[2,3,64,544]{3,2,1,0:T(8,128)(2,1)}, u32[]{:S(2)}, u32[]{:S(2)}) collective-permute-start(bf16[2,3,64,544]{3,2,1,0:T(8,128)(2,1)} %get-tuple-element.42), channel_id=1, source_target_pairs={{2,0},{4,2},{6,4},{8,6},{10,8},{12,10},{14,12},{3,1},{5,3},{7,5},{... | collective-permute-start | bytes 1253384 | tf_op jit(solution)/shard_map/ppermute | solution.py:26
  41.1 51.5 %copy-start.1 = (bf16[2,6,64,512]{3,2,1,0:T(8,128)(2,1)S(1)}, bf16[2,6,64,512]{3,2,1,0:T(8,128)(2,1)}, u32[]{:S(2)}) copy-start(bf16[2,6,64,512]{3,2,1,0:T(8,128)(2,1)} %param.16) | copy-start | bytes 2359300
  80.9 1.9 %copy-start.2 = (bf16[2,3,64,544]{3,2,1,0:T(8,128)(2,1)}, bf16[2,3,64,544]{3,2,1,0:T(8,128)(2,1)S(1)}, u32[]{:S(2)}) copy-start(bf16[2,3,64,544]{3,2,1,0:T(8,128)(2,1)S(1)} %collective-permute-done.2) | copy-start | bytes 1253380
  80.9 23.8 %collective-permute-start.7 = (bf16[2,2,64,544]{3,2,0,1:T(8,128)(2,1)}, bf16[2,2,64,544]{3,2,0,1:T(8,128)(2,1)}, u32[]{:S(2)}, u32[]{:S(2)}) collective-permute-start(bf16[2,2,64,544]{3,2,0,1:T(8,128)(2,1)} %bitcast_select_fusion.2), channel_id=1, source_target_pairs={{0,6},{2,8},{4,10},{6,12},{8,14},{1,7},{3,9},{5,11},{7,13},{9,15},... | collective-permute-start | bytes 835592 | tf_op jit(solution)/shard_map/ppermute | solution.py:36
  107.0 2.1 %copy-start = (bf16[2,24,64,544]{3,2,0,1:T(8,128)(2,1)S(1)}, bf16[2,24,64,544]{3,2,0,1:T(8,128)(2,1)}, u32[]{:S(2)}) copy-start(bf16[2,24,64,544]{3,2,0,1:T(8,128)(2,1)} %select_bitcast_fusion) | copy-start | bytes 10027012
  117.5 18.1 %copy-start.3 = (s32[160,128]{1,0:T(8,128)S(1)}, s32[160,128]{1,0:T(8,128)}, u32[]{:S(2)}) copy-start(s32[160,128]{1,0:T(8,128)} %subtract_abs_fusion) | copy-start | bytes 245764
where the time goes:
time: 173 us; the launch traced here: 172 us
  waiting for transfers between devices  43.6 us (25%)
  local copies, waits for them, and re-layouts  40 us (23%)
  other arithmetic  35.4 us (20%)
  matrix products  30.3 us (18%)
  starting transfers between devices  22.3 us (13%)
    ppermute x2, waiting for transfers between devices, padded(): lax.ppermute(tail, axis, [(i, (i + 1) % count) for i in range(ends)])  33.7 us
    dot_general x1, matrix products, range_looks(): jnp.einsum('qprtc,pcw->qprtw', windows, band_cols, precision=lax.Precisio...  18.9 us
    another operation x1, local copies, waits for them, and re-layouts, range_looks(): jnp.stack([cross_terms[:, :, :, tile * tile_width:tile * tile_width + til...  18.1 us
    ppermute x4, starting transfers between devices, passed_along(): return lax.ppermute(block, axis, route)  12 us
    dot_general x1, matrix products, azimuth_looks(): jnp.einsum('pab,qpbc->qpac', band_rows, ranged, precision=lax.Precision.H...  11.4 us
    ppermute x2, waiting for transfers between devices, padded(): lax.ppermute(head, axis, [((i + 1) % count, i) for i in range(ends)])  9.88 us
    another operation x1, other arithmetic, pair_products(): jnp.stack([a_real * b_real + a_imag * b_imag, a_imag * b_real - a_real *...  5.79 us
    unnamed x5, other arithmetic  5.38 us
  transfers between devices with their start and end apart: 8, of which 2 were waited for; matrix products, arithmetic and copies ran while one was open for 19% of the time, Pallas kernels for 0%

commit v1 on v0

v1 whole, which is shorter than its diff:
```python
import functools

import jax
import jax.numpy as jnp
from jax import lax
from jax.experimental import pallas as pl
from jax.experimental.pallas import tpu as pltpu
from jax.sharding import PartitionSpec as P

HALO = 16
REACH_LO = 12
NEAR = 3
YEAR = 29
EPSILON = 1e-06
TILE = 128
VMEM_BYTES = 40 * 1024 * 1024
ANY = pl.BlockSpec(memory_space=pl.ANY)
SMEM = pl.BlockSpec(memory_space=pltpu.SMEM)


def run_copies(copies):
    for copy in copies:
        copy.start()
    for copy in copies:
        copy.wait()


def outer_kernel(plan, slc_ref, pairs_ref, early_ref, x_ref, z_ref, far_ref, sems):
    me = lax.axis_index("date")
    dates, late = plan["dates"], plan["late"]
    ends, half, per_date = plan["devices"] - 1, plan["devices"] // 2, plan["per_date"]
    first = me * dates
    last_dates = dates - NEAR
    odd = lax.rem(me, 2)
    mate = lax.rem(me + half, 2 * half)
    mate_slot = jnp.where(mate < half, late, 0)
    copies = []
    for k in range(dates - late):
        wanted = pairs_ref[1, (mate * dates + mate_slot + k) * per_date + NEAR] - first
        wanted = jnp.clip(wanted, 0, dates - 1)
        copies.append((slc_ref.at[:, wanted], early_ref.at[:, k]))
    copies.append((slc_ref.at[:, pl.ds(jnp.where(odd == 1, 0, last_dates), NEAR)], x_ref))
    copies.append((slc_ref.at[:, pl.ds(jnp.where(odd == 1, last_dates, 0), NEAR)], z_ref))
    far = jnp.where(me < half, half - 1, half)
    far_slot = jnp.where(me < half, dates - late, 0)
    for k in range(late):
        wanted = pairs_ref[1, (far * dates + far_slot + k) * per_date + NEAR] - first
        wanted = jnp.clip(wanted, 0, dates - 1)
        copies.append((slc_ref.at[:, wanted], far_ref.at[:, k]))
    run_copies([pltpu.make_async_copy(a, b, sems.at[n]) for n, (a, b) in enumerate(copies)])


def rim_kernel(count, *refs):
    sources, out_ref, sems = refs[:count], refs[count], refs[count + 1]
    cols = sources[0].shape[3]
    start = pl.multiple_of(jnp.where(lax.axis_index("strip") == 0, cols - TILE, 0), TILE)
    copies = []
    place = 0
    for n, source in enumerate(sources):
        here = out_ref.at[:, pl.ds(place, source.shape[1])]
        copies.append(
            pltpu.make_async_copy(source.at[:, :, :, pl.ds(start, TILE)], here, sems.at[n])
        )
        place += source.shape[1]
    run_copies(copies)


def rims(*sources):
    planes, _, rows, _ = sources[0].shape
    total = sum(source.shape[1] for source in sources)
    tiles = pl.pallas_call(
        functools.partial(rim_kernel, len(sources)),
        out_shape=jax.ShapeDtypeStruct((planes, total, rows, TILE), sources[0].dtype),
        in_specs=[ANY] * len(sources),
        out_specs=ANY,
        scratch_shapes=[pltpu.SemaphoreType.DMA((len(sources),))],
        name="rim_blocks",
    )(*sources)
    return lax.ppermute(tiles, "strip", [(0, 1), (1, 0)])


def late_kernel(plan, slc_ref, x_ref, z_ref, rim_ref, pairs_ref, out_ref, rim_buf, sems, rim_sems):
    me = lax.axis_index("date")
    strip = lax.axis_index("strip")
    dates, late = plan["dates"], plan["late"]
    half, per_date = plan["devices"] // 2, plan["per_date"]
    rows = plan["rows"]
    odd = lax.rem(me, 2)
    mate = lax.rem(me + half, 2 * half)
    mate_slot = jnp.where(mate < half, 0, dates - late)
    for k in range(late):
        wanted = pairs_ref[1, (mate * dates + mate_slot + k) * per_date + NEAR] - me * dates
        wanted = jnp.clip(wanted, -NEAR, dates + NEAR - 1)
        own = (wanted >= 0) & (wanted < dates)
        below = wanted < 0
        spot = jnp.where(below, wanted + NEAR, wanted - dates)
        from_x = below == (odd == 1)
        place = jnp.where(own, wanted, spot + jnp.where(from_x, dates, dates + NEAR))
        here = [out_ref.at[pl.ds((2 * k + c) * rows, rows)] for c in range(2)]

        def send(source, index):
            for c in range(2):
                pltpu.make_async_copy(source.at[c, index], here[c], sems.at[2 * k + c]).start()

        pl.when(own)(functools.partial(send, slc_ref, jnp.clip(wanted, 0, dates - 1)))
        spot = jnp.clip(spot, 0, NEAR - 1)
        pl.when(jnp.logical_not(own) & from_x)(functools.partial(send, x_ref, spot))
        pl.when(jnp.logical_not(own) & jnp.logical_not(from_x))(
            functools.partial(send, z_ref, spot)
        )
        pltpu.make_async_copy(rim_ref.at[:, place], rim_buf.at[:, k], rim_sems.at[k]).start()
    lane = lax.broadcasted_iota(jnp.int32, (rows, TILE), 1)
    packed = jnp.zeros((rows, TILE), jnp.float32)
    for k in range(late):
        pltpu.make_async_copy(rim_ref.at[:, 0], rim_buf.at[:, k], rim_sems.at[k]).wait()
        for c in range(2):
            spot = (2 * k + c) * HALO
            moved = pltpu.roll(rim_buf[c, k].astype(jnp.float32), spot + strip * HALO, 1)
            packed = jnp.where((lane >= spot) & (lane < spot + HALO), moved, packed)
    packed = packed.astype(jnp.bfloat16)
    base = 2 * late * rows
    rim_rows = plan["rim_rows"]
    for n in range(rows // rim_rows):
        out_ref[base : base + rim_rows, n * TILE : (n + 1) * TILE] = packed[
            n * rim_rows : (n + 1) * rim_rows
        ]
    for n in range(2 * late):
        pltpu.make_async_copy(
            slc_ref.at[0, 0], out_ref.at[pl.ds(n * rows, rows)], sems.at[n]
        ).wait()


def bands_kernel(cols, out_ref):
    strip = lax.axis_index("strip")
    wide = out_ref.shape[2]
    reach = pl.program_id(0) + REACH_LO

    def band(places, targets):
        return (jnp.abs(places - targets) <= reach).astype(jnp.float32).astype(jnp.bfloat16)

    shape = (wide, wide)
    row = lax.broadcasted_iota(jnp.int32, shape, 0)
    col = lax.broadcasted_iota(jnp.int32, shape, 1)
    out_ref[0, 0:wide] = band(row, col)
    shape = (TILE, wide)
    row = lax.broadcasted_iota(jnp.int32, shape, 0)
    col = lax.broadcasted_iota(jnp.int32, shape, 1)
    beyond = jnp.where(strip == 0, cols + row, row - TILE)
    middle = TILE // 2
    first = band(jnp.where(row < middle, wide + row, beyond), col)
    second = band(jnp.where(row < middle, beyond, wide - TILE + row), col + wide)
    for n, part in enumerate((first, first, second, second)):
        out_ref[0, wide + n * TILE : wide + (n + 1) * TILE] = part


def split(values):
    high = values.astype(jnp.bfloat16)
    low = (values - high.astype(jnp.float32)).astype(jnp.bfloat16)
    return high, low


def cross_terms(a_real, a_imag, b_real, b_imag):
    a_real, a_imag, b_real, b_imag = [
        part.astype(jnp.float32) for part in (a_real, a_imag, b_real, b_imag)
    ]
    return (
        a_real * b_real + a_imag * b_imag,
        a_imag * b_real - a_real * b_imag,
        a_real * a_real + a_imag * a_imag,
        b_real * b_real + b_imag * b_imag,
    )


def coherence(a_main, a_rim, b_main, b_rim, bands, height, store, scratch):
    high_ref, low_ref, side_ref, stack_ref = scratch
    rows, cols = a_main(0).shape
    wide = cols // 2
    lane = lax.broadcasted_iota(jnp.int32, (rows, TILE), 1)
    inner = lane < TILE // 2
    mains = cross_terms(a_main(0), a_main(1), b_main(0), b_main(1))
    edges = cross_terms(a_rim(0), a_rim(1), b_rim(0), b_rim(1))
    for f in range(4):
        here = slice(f * rows, (f + 1) * rows)
        high, low = split(mains[f])
        high_ref[here] = high
        low_ref[here] = low
        first = jnp.where(inner, mains[f][:, wide : wide + TILE], edges[f])
        second = jnp.where(inner, edges[f], mains[f][:, wide - TILE : wide])
        for n, part in enumerate((first, second)):
            high, low = split(part)
            side_ref[n, here, 0:TILE] = high
            side_ref[n, here, TILE : 2 * TILE] = low
    for n in range(2):
        there = slice(n * wide, (n + 1) * wide)
        inside = bands(0, wide)
        ranged = jnp.dot(high_ref[:, there], inside, preferred_element_type=jnp.float32)
        ranged += jnp.dot(low_ref[:, there], inside, preferred_element_type=jnp.float32)
        ranged += jnp.dot(
            side_ref[n],
            bands(wide + 2 * n * TILE, wide + 2 * (n + 1) * TILE),
            preferred_element_type=jnp.float32,
        )
        high, low = split(ranged)
        for f in range(4):
            stack_ref[f, 0:rows, there] = high[f * rows : (f + 1) * rows]
            stack_ref[f, rows : 2 * rows, there] = low[f * rows : (f + 1) * rows]
    row = lax.broadcasted_iota(jnp.int32, (rows, 2 * rows), 0)
    col = lax.broadcasted_iota(jnp.int32, (rows, 2 * rows), 1)
    col = jnp.where(col < rows, col, col - rows)
    band = (jnp.abs(row - col) <= height).astype(jnp.float32).astype(jnp.bfloat16)
    looked = [
        jnp.dot(band, stack_ref[f], preferred_element_type=jnp.float32) for f in range(4)
    ]
    inverse = lax.rsqrt(looked[2] * looked[3] + EPSILON)
    store(0, looked[0] * inverse)
    store(1, looked[1] * inverse)


def work_scratch(rows, cols):
    return [
        pltpu.VMEM((4 * rows, cols), jnp.bfloat16),
        pltpu.VMEM((4 * rows, cols), jnp.bfloat16),
        pltpu.VMEM((2, 4 * rows, 2 * TILE), jnp.bfloat16),
        pltpu.VMEM((4, 2 * rows, cols), jnp.bfloat16),
    ]


def near_kernel(plan, who_ref, pairs_ref, az_ref, rng_ref, slc_hbm, x_hbm, z_hbm, rim_hbm,
                bands_ref, out_ref, ext, rim, sems, *scratch):
    step = pl.program_id(0)
    dates, per_date = plan["dates"], plan["per_date"]
    me, flip = who_ref[0], who_ref[2]

    @pl.when(step == 0)
    def _():
        x_at = jnp.where(flip == 1, 0, dates + NEAR)
        z_at = jnp.where(flip == 1, dates + NEAR, 0)
        run_copies(
            [
                pltpu.make_async_copy(slc_hbm, ext.at[:, pl.ds(NEAR, dates)], sems.at[0]),
                pltpu.make_async_copy(x_hbm, ext.at[:, pl.ds(x_at, NEAR)], sems.at[1]),
                pltpu.make_async_copy(z_hbm, ext.at[:, pl.ds(z_at, NEAR)], sems.at[2]),
                pltpu.make_async_copy(
                    rim_hbm.at[:, pl.ds(0, dates)], rim.at[:, pl.ds(NEAR, dates)], sems.at[3]
                ),
                pltpu.make_async_copy(
                    rim_hbm.at[:, pl.ds(dates, NEAR)], rim.at[:, pl.ds(x_at, NEAR)], sems.at[4]
                ),
                pltpu.make_async_copy(
                    rim_hbm.at[:, pl.ds(dates + NEAR, NEAR)],
                    rim.at[:, pl.ds(z_at, NEAR)],
                    sems.at[5],
                ),
            ]
        )

    slot = step // NEAR
    pair = (me * dates + slot) * per_date + lax.rem(step, NEAR)
    other = jnp.clip(pairs_ref[1, pair] - me * dates + NEAR, 0, dates + 2 * NEAR - 1)
    own = slot + NEAR
    width = jnp.clip(rng_ref[pair] - REACH_LO, 0, HALO - REACH_LO)

    def store(c, values):
        out_ref[c, 0, 0] = values

    coherence(
        lambda c: ext[c, own],
        lambda c: rim[c, own],
        lambda c: ext[c, other],
        lambda c: rim[c, other],
        lambda a, b: bands_ref[width, a:b],
        az_ref[pair],
        store,
        scratch,
    )


def annual_kernel(plan, who_ref, pairs_ref, az_ref, rng_ref, slc_ref, own_rim_ref, early_ref,
                  far_ref, rim_ref, far_rim_ref, bands_ref, _, out_ref, *scratch):
    step = pl.program_id(0)
    dates, per_date = plan["dates"], plan["per_date"]
    me, base, lower = who_ref[0], who_ref[3], who_ref[4]
    date = me * dates + base + step
    pair = date * per_date + NEAR
    partner = pairs_ref[1, pair]
    from_far = jnp.where(lower == 1, partner < date, partner > date) & (who_ref[5] == 1)

    def store(c, values):
        out_ref[c, 0, 0] = values

    coherence(
        lambda c: slc_ref[c, 0],
        lambda c: own_rim_ref[c, 0],
        lambda c: jnp.where(from_far, far_ref[c, 0], early_ref[c, 0]),
        lambda c: jnp.where(from_far, far_rim_ref[c, 0], rim_ref[c, 0]),
        lambda a, b: bands_ref[0, a:b],
        az_ref[pair],
        store,
        scratch,
    )


def last_kernel(plan, who_ref, pairs_ref, az_ref, rng_ref, slc_ref, own_rim_ref, late_ref,
                late_rim_ref, bands_ref, _, out_ref, *scratch):
    step = pl.program_id(0)
    dates, per_date, rows = plan["dates"], plan["per_date"], plan["rows"]
    pair = (who_ref[0] * dates + who_ref[6] + step) * per_date + NEAR
    tiles = late_rim_ref.shape[1] // TILE

    def store(c, values):
        out_ref[c, 0, 0] = values

    def late_rim(c):
        packed = jnp.concatenate(
            [late_rim_ref[:, n * TILE : (n + 1) * TILE] for n in range(tiles)], axis=0
        )
        shift = 2 * TILE - (2 * step + c + who_ref[1]) * HALO
        return pltpu.roll(packed.astype(jnp.float32), lax.rem(shift, TILE), 1)

    coherence(
        lambda c: slc_ref[c, 0],
        lambda c: own_rim_ref[c, 0],
        lambda c: late_ref[c * rows : (c + 1) * rows],
        late_rim,
        lambda a, b: bands_ref[0, a:b],
        az_ref[pair],
        store,
        scratch,
    )


def arrivals_by_distance(slc, pair_list, plan):
    dates, per_date, devices = plan["dates"], plan["per_date"], plan["devices"]
    total = dates * devices
    me = lax.axis_index("date")
    annual_of = pair_list[:, 1].reshape(total, per_date)[:, per_date - 1]
    sums = [None] * dates
    for direction in (1, -1):
        by_distance = {}
        for slot in range(dates):
            for gap in range(plan["year"], plan["year"] + 3):
                distance = (slot + direction * gap) // dates
                by_distance.setdefault(distance, set()).add(slot)
        for distance in sorted(by_distance):
            slots = sorted(by_distance[distance])
            wanted_by = (me - distance) * dates + jnp.array(slots, dtype=jnp.int32)
            inside = (wanted_by >= 0) & (wanted_by < total)
            local = jnp.take(annual_of, jnp.clip(wanted_by, 0, total - 1)) - me * dates
            usable = inside & (local >= 0) & (local < dates)
            packed = jnp.take(slc, jnp.clip(local, 0, dates - 1), axis=1)
            packed = jnp.where(usable[None, :, None, None], packed, jnp.zeros_like(packed))
            route = [(i + distance, i) for i in range(devices) if 0 <= i + distance < devices]
            arrived = lax.ppermute(packed, "date", route)
            for n, slot in enumerate(slots):
                part = arrived[:, n]
                sums[slot] = part if sums[slot] is None else sums[slot] + part
    return jnp.stack(sums, axis=1)


def body(slc, pair_list, az_half, rng_half):
    planes, dates, rows, cols = slc.shape
    devices = lax.axis_size("date")
    total = dates * devices
    per_date = pair_list.shape[0] // total
    year = min(YEAR, total // 2 - 2)
    half = devices // 2
    late = half * dates - year
    plan = {
        "dates": dates,
        "devices": devices,
        "per_date": per_date,
        "year": year,
        "late": late,
        "rows": rows,
        "rim_rows": rows * TILE // cols,
    }
    me, strip = lax.axis_index("date"), lax.axis_index("strip")
    odd = lax.rem(me, 2)
    lower = (me < half).astype(jnp.int32)
    opposite = devices % 2 == 0 and 0 < late <= NEAR and 2 * late <= dates
    pairs = pair_list.T
    dtype = slc.dtype
    params = pltpu.CompilerParams(vmem_limit_bytes=VMEM_BYTES)

    def images(count):
        return jax.ShapeDtypeStruct((planes, count, rows, cols), dtype)

    if opposite:
        early, beside_x, beside_z, far = pl.pallas_call(
            functools.partial(outer_kernel, plan),
            out_shape=(images(dates - late), images(NEAR), images(NEAR), images(late)),
            in_specs=[ANY, SMEM],
            out_specs=(ANY,) * 4,
            scratch_shapes=[pltpu.SemaphoreType.DMA((dates + 2,))],
            name="outgoing_images",
        )(slc, pairs)
        early = lax.ppermute(
            early, "date", [(i, (i + half) % devices) for i in range(devices)]
        )
        beside_x = lax.ppermute(beside_x, "date", [(i, i ^ 1) for i in range(devices)])
        steps = [(i, i + 1) for i in range(1, devices - 1, 2)]
        beside_z = lax.ppermute(beside_z, "date", steps + [(b, a) for a, b in steps])
        far = lax.ppermute(far, "date", [(0, half - 1), (devices - 1, half)])
        flip = odd
        base = jnp.where(lower == 1, late, 0)
        last_base = jnp.where(lower == 1, 0, dates - late)
        any_far = 1
    else:
        early = arrivals_by_distance(slc, pair_list, plan)
        ups = [(i, i + 1) for i in range(devices - 1)]
        beside_x = lax.ppermute(slc[:, :NEAR], "date", [(b, a) for a, b in ups])
        beside_z = lax.ppermute(slc[:, dates - NEAR :], "date", ups)
        far = early[:, :1]
        flip, base, last_base, any_far = 0, 0, 0, 0
    who = jnp.stack(
        [jnp.asarray(v, jnp.int32) for v in (me, strip, flip, base, lower, any_far, last_base)]
    )
    rim = rims(slc, beside_x, beside_z)
    if opposite:
        late_rows = 2 * late * rows + plan["rim_rows"]
        payload = pl.pallas_call(
            functools.partial(late_kernel, plan),
            out_shape=jax.ShapeDtypeStruct((late_rows, cols), dtype),
            in_specs=[ANY] * 4 + [SMEM],
            out_specs=pl.BlockSpec(memory_space=pltpu.VMEM),
            scratch_shapes=[
                pltpu.VMEM((2, late, rows, TILE), dtype),
                pltpu.SemaphoreType.DMA((2 * late,)),
                pltpu.SemaphoreType.DMA((late,)),
            ],
            compiler_params=params,
            name="late_images",
        )(slc, beside_x, beside_z, rim, pairs)
        payload = lax.ppermute(
            payload, "date", [(i, (i + half) % devices) for i in range(devices)]
        )
    wide = cols // 2
    widths = HALO - REACH_LO + 1
    band_rows = wide + 4 * TILE
    bands = pl.pallas_call(
        functools.partial(bands_kernel, cols),
        grid=(widths,),
        out_shape=jax.ShapeDtypeStruct((widths, band_rows, wide), jnp.bfloat16),
        out_specs=pl.BlockSpec((1, band_rows, wide), lambda n: (n, 0, 0)),
        name="range_bands",
    )()
    out_shape = jax.ShapeDtypeStruct((planes, dates, per_date, rows, cols), jnp.float32)
    block = (planes, 1, 1, rows, cols)
    scalars = (who, pairs, az_half, rng_half)
    dims = ext = dates + 2 * NEAR

    def cost(count):
        return pl.CostEstimate(
            flops=count * 4 * rows * cols * 2000,
            bytes_accessed=count * planes * rows * cols * 4,
            transcendentals=0,
        )

    out = pl.pallas_call(
        functools.partial(near_kernel, plan),
        grid_spec=pltpu.PrefetchScalarGridSpec(
            num_scalar_prefetch=4,
            grid=(dates * NEAR,),
            in_specs=[ANY] * 4
            + [pl.BlockSpec((widths, band_rows, wide), lambda n, *_: (0, 0, 0))],
            out_specs=pl.BlockSpec(block, lambda n, *_: (0, n // NEAR, lax.rem(n, NEAR), 0, 0)),
            scratch_shapes=[
                pltpu.VMEM((planes, ext, rows, cols), dtype),
                pltpu.VMEM((planes, ext, rows, TILE), dtype),
                pltpu.SemaphoreType.DMA((6,)),
            ]
            + work_scratch(rows, cols),
        ),
        out_shape=out_shape,
        compiler_params=params,
        cost_estimate=cost(dates * NEAR),
        name="near_pairs",
    )(*scalars, slc, beside_x, beside_z, rim, bands)

    early_count = early.shape[1]
    far_count = far.shape[1]
    early_rim = rims(early, far)

    def own_slot(n, who_ref, *_):
        return (0, who_ref[3] + n, 0, 0)

    def far_slot(n, who_ref):
        skip = jnp.where(who_ref[4] == 1, early_count - far_count, 0)
        return jnp.clip(n - skip, 0, far_count - 1)

    def band_block(start):
        def of(n, who_ref, pairs_ref, az_ref, rng_ref):
            pair = (who_ref[0] * dates + who_ref[start] + n) * per_date + NEAR
            return (jnp.clip(rng_ref[pair] - REACH_LO, 0, widths - 1), 0, 0)

        return pl.BlockSpec((1, band_rows, wide), of)

    image, strip_rim = (planes, 1, rows, cols), (planes, 1, rows, TILE)
    out = pl.pallas_call(
        functools.partial(annual_kernel, plan),
        grid_spec=pltpu.PrefetchScalarGridSpec(
            num_scalar_prefetch=4,
            grid=(early_count,),
            in_specs=[
                pl.BlockSpec(image, own_slot),
                pl.BlockSpec(strip_rim, own_slot),
                pl.BlockSpec(image, lambda n, *_: (0, n, 0, 0)),
                pl.BlockSpec(image, lambda n, who_ref, *_: (0, far_slot(n, who_ref), 0, 0)),
                pl.BlockSpec(strip_rim, lambda n, *_: (0, n, 0, 0)),
                pl.BlockSpec(
                    strip_rim,
                    lambda n, who_ref, *_: (0, early_count + far_slot(n, who_ref), 0, 0),
                ),
                band_block(3),
                ANY,
            ],
            out_specs=pl.BlockSpec(
                block, lambda n, who_ref, *_: (0, who_ref[3] + n, NEAR, 0, 0)
            ),
            scratch_shapes=work_scratch(rows, cols),
        ),
        out_shape=out_shape,
        input_output_aliases={11: 0},
        compiler_params=params,
        cost_estimate=cost(early_count),
        name="annual_pairs",
    )(*scalars, slc, rim, early, far, early_rim, early_rim, bands, out)

    if opposite:
        rim_rows = plan["rim_rows"]

        def last_slot(n, who_ref, *_):
            return (0, who_ref[6] + n, 0, 0)

        out = pl.pallas_call(
            functools.partial(last_kernel, plan),
            grid_spec=pltpu.PrefetchScalarGridSpec(
                num_scalar_prefetch=4,
                grid=(late,),
                in_specs=[
                    pl.BlockSpec(image, last_slot),
                    pl.BlockSpec(strip_rim, last_slot),
                    pl.BlockSpec((2 * rows, cols), lambda n, *_: (n, 0)),
                    pl.BlockSpec(
                        (rim_rows, cols), lambda n, *_: (2 * late * rows // rim_rows, 0)
                    ),
                    band_block(6),
                    ANY,
                ],
                out_specs=pl.BlockSpec(
                    block, lambda n, who_ref, *_: (0, who_ref[6] + n, NEAR, 0, 0)
                ),
                scratch_shapes=work_scratch(rows, cols),
            ),
            out_shape=out_shape,
            input_output_aliases={9: 0},
            compiler_params=params,
            cost_estimate=cost(late),
            name="last_pairs",
        )(*scalars, slc, rim, payload, payload, bands, out)
    return out.reshape(planes, dates * per_date, rows, cols)


def solution(mesh):
    placed = (P(None, "date", "groups", "strip"), P(), P(), P())
    return jax.shard_map(
        body,
        mesh=mesh,
        in_specs=placed,
        out_specs=P(None, "date", "groups", "strip"),
        check_vma=False,
    )
```

time: 173 us -> 144 us (0.83)
  the two profiles are of different devices: /device:TPU:15 before, /device:TPU:0 now
where the time goes in v1:
time: 144 us
  Pallas kernels  95.1 us (66%)
  starting transfers between devices  24.4 us (17%)
  waiting for transfers between devices  16 us (11%)
  local copies, waits for them, and re-layouts  8.3 us (6%)
    pallas_call x1, Pallas kernels, body(): pl.pallas_call(functools.partial(outer_kernel, plan), out_shape=(images(d...  49.7 us
    pallas_call x2, Pallas kernels, rims(): pl.pallas_call(functools.partial(rim_kernel, len(sources)), out_shape=jax...  20.1 us
    pallas_call x1, Pallas kernels, body(): pl.pallas_call(functools.partial(near_kernel, plan), grid_spec=pltpu.Pref...  14.5 us
    ppermute x1, waiting for transfers between devices, body(): lax.ppermute(beside_x, 'date', [(i, i ^ 1) for i in range(devices)])  12.1 us
    ppermute x1, starting transfers between devices, body(): far = lax.ppermute(far, 'date', [(0, half - 1), (devices - 1, half)])  11.9 us
    unnamed x32, local copies, waits for them, and re-layouts  8.21 us
    pallas_call x1, Pallas kernels, body(): pl.pallas_call(functools.partial(annual_kernel, plan), grid_spec=pltpu.Pr...  4.4 us
    ppermute x1, starting transfers between devices, body(): lax.ppermute(payload, 'date', [(i, (i + half) % devices) for i in range(d...  4.38 us
  transfers between devices with their start and end apart: 7, of which 2 were waited for; matrix products, arithmetic and copies ran while one was open for 0% of the time, Pallas kernels for 30%

profile of v1, /device:TPU:0, one launch (start us, length us, event | category | flops | bytes accessed | tf_op | source)
XLA Modules:
  0.0 143.9 jit_solution(11733079143212274785)
XLA Ops:
  0.0 0.0 copy-start
  0.0 0.0 copy-start.13
  0.0 0.0 copy-start.15
  0.0 0.0 copy-start.14
  0.0 49.7 %outgoing_images.1 = (bf16[2,4,64,512]{3,2,1,0:T(8,128)(2,1)}, bf16[2,3,64,512]{3,2,1,0:T(8,128)(2,1)}, bf16[2,3,64,512]{3,2,1,0:T(8,128)(2,1)}, bf16[2,2,64,512]{3,2,1,0:T(8,128)(2,1)}) custom-call(bf16[2,6,64,512]{3,2,1,0:T(8,128)(2,1)} %slc_ref.7, s32[2,192]{1,0:T(2,128)} %bitcast.8), custom_call_target="tpu_custom_call" | custom-call | tf_op jit(solution)/shard_map/outgoing_images/pallas_call | solution.py:389
  49.7 3.0 %collective-permute-start = (bf16[2,3,64,512]{3,2,1,0:T(8,128)(2,1)}, bf16[2,3,64,512]{3,2,1,0:T(8,128)(2,1)S(1)}, u32[]{:S(2)}, u32[]{:S(2)}) collective-permute-start(bf16[2,3,64,512]{3,2,1,0:T(8,128)(2,1)} %get-tuple-element.9), channel_id=1, source_target_pairs={{0,2},{2,0},{4,6},{6,4},{8,10},{10,8},{12,14},{14,12},{1,3},{3,1},... | collective-permute-start | bytes 1179656 | tf_op jit(solution)/shard_map/ppermute | solution.py:400
  52.7 0.7 collective-permute-start.1
  53.4 4.3 %collective-permute-start.4 = (bf16[2,4,64,512]{3,2,1,0:T(8,128)(2,1)}, bf16[2,4,64,512]{3,2,1,0:T(8,128)(2,1)S(1)}, u32[]{:S(2)}, u32[]{:S(2)}) collective-permute-start(bf16[2,4,64,512]{3,2,1,0:T(8,128)(2,1)} %get-tuple-element.11), channel_id=1, source_target_pairs={{0,8},{2,10},{4,12},{6,14},{8,0},{10,2},{12,4},{14,6},{1,9},{3,11}... | collective-permute-start | bytes 1572872 | tf_op jit(solution)/shard_map/ppermute | solution.py:397
  57.7 12.1 %collective-permute-done.refs_1_.x_ref.x_hbm = bf16[2,3,64,512]{3,2,1,0:T(8,128)(2,1)S(1)} collective-permute-done((bf16[2,3,64,512]{3,2,1,0:T(8,128)(2,1)}, bf16[2,3,64,512]{3,2,1,0:T(8,128)(2,1)S(1)}, u32[]{:S(2)}, u32[]{:S(2)}) %collective-permute-start) | collective-permute-done | bytes 393248 | tf_op jit(solution)/shard_map/ppermute | solution.py:400
  69.8 0.0 copy-start.5
  69.8 0.0 collective-permute-done.1.refs_2_.z_ref.z_hbm
  69.8 0.7 copy-done.5
  70.6 0.0 copy-start.7
  70.6 0.7 copy-done.7
  71.3 13.0 %rim_blocks.2 = bf16[2,12,64,128]{3,2,1,0:T(8,128)(2,1)} custom-call(bf16[2,6,64,512]{3,2,1,0:T(8,128)(2,1)} %slc_ref.7, bf16[2,3,64,512]{3,2,1,0:T(8,128)(2,1)} %copy-done.5, bf16[2,3,64,512]{3,2,1,0:T(8,128)(2,1)} %copy-done.7), custom_call_target="tpu_custom_call" | custom-call | tf_op jit(solution)/shard_map/rim_blocks/pallas_call | solution.py:71
  84.4 0.1 collective-permute-start.2
  84.4 11.9 %collective-permute-start.5 = (bf16[2,2,64,512]{3,2,1,0:T(8,128)(2,1)}, bf16[2,2,64,512]{3,2,1,0:T(8,128)(2,1)S(1)}, u32[]{:S(2)}, u32[]{:S(2)}) collective-permute-start(bf16[2,2,64,512]{3,2,1,0:T(8,128)(2,1)} %get-tuple-element.12), channel_id=1, source_target_pairs={{0,6},{14,8},{1,7},{15,9},{16,22},{30,24},{17,23},{31,25}} | collective-permute-start | bytes 786440 | tf_op jit(solution)/shard_map/ppermute | solution.py:403
  96.3 2.6 %range_bands.1.bands_ref = bf16[5,768,256]{2,1,0:T(8,128)(2,1)} custom-call(), custom_call_target="tpu_custom_call" | custom-call | tf_op jit(solution)/shard_map/range_bands/pallas_call | solution.py:440
  98.9 0.1 stack.27.who_ref
  99.0 3.8 %collective-permute-done.5.refs_1_.far_ref = bf16[2,2,64,512]{3,2,1,0:T(8,128)(2,1)S(1)} collective-permute-done((bf16[2,2,64,512]{3,2,1,0:T(8,128)(2,1)}, bf16[2,2,64,512]{3,2,1,0:T(8,128)(2,1)S(1)}, u32[]{:S(2)}, u32[]{:S(2)}) %collective-permute-start.5) | collective-permute-done | bytes 262176 | tf_op jit(solution)/shard_map/ppermute | solution.py:403
  102.8 0.0 copy-start.10
  102.8 0.0 collective-permute-done.4.refs_0_.early_ref
  102.8 0.7 copy-done.10
  103.5 0.0 copy-start.3
  103.5 0.8 copy-done.3
  104.3 7.1 %rim_blocks.3 = bf16[2,6,64,128]{3,2,1,0:T(8,128)(2,1)} custom-call(bf16[2,4,64,512]{3,2,1,0:T(8,128)(2,1)} %copy-done.3, bf16[2,2,64,512]{3,2,1,0:T(8,128)(2,1)} %copy-done.10), custom_call_target="tpu_custom_call" | custom-call | tf_op jit(solution)/shard_map/rim_blocks/pallas_call | solution.py:71
  111.4 0.1 collective-permute-start.6
  111.5 0.0 collective-permute-done.2.rim_ref.rim_hbm.own_rim_ref
  111.5 0.0 copy-done
  111.5 0.0 copy-start.6
  111.5 1.0 copy-done.6
  112.5 0.0 copy-start.8
  112.5 1.0 copy-done.8
  113.5 0.0 copy-start.12
  113.5 0.7 copy-done.12
  114.2 1.2 late_images.1
  115.4 4.4 %collective-permute-start.3 = (bf16[272,512]{1,0:T(8,128)(2,1)S(1)}, bf16[272,512]{1,0:T(8,128)(2,1)S(1)}, u32[]{:S(2)}, u32[]{:S(2)}) collective-permute-start(bf16[272,512]{1,0:T(8,128)(2,1)S(1)} %late_images.1), channel_id=1, source_target_pairs={{0,8},{2,10},{4,12},{6,14},{8,0},{10,2},{12,4},{14,6},{1,9},{3,11}... | collective-permute-start | bytes 835592 | tf_op jit(solution)/shard_map/ppermute | solution.py:434
  119.8 0.0 copy-done.13
  119.8 0.0 copy-done.15
  119.8 0.0 copy-done.14
  119.8 0.0 copy-start.1
  119.8 1.5 %copy-done.1 = bf16[5,768,256]{2,1,0:T(8,128)(2,1)S(1)} copy-done((bf16[5,768,256]{2,1,0:T(8,128)(2,1)S(1)}, bf16[5,768,256]{2,1,0:T(8,128)(2,1)}, u32[]{:S(2)}) %copy-start.1) | copy-done | bytes 1966104
  121.3 0.0 copy-start.9
  121.3 1.0 copy-done.9
  122.3 0.0 copy-start.2
  122.3 0.0 copy-start.4
  122.3 0.0 copy-start.11
  122.3 14.5 %near_pairs.1._ = f32[2,6,4,64,512]{4,3,2,1,0:T(8,128)} custom-call(s32[7]{0:T(128)S(1)} %stack.27.who_ref, s32[2,192]{1,0:T(2,128)S(1)} %bitcast.10, s32[192]{0:T(256)S(1)} %copy-done.14, s32[192]{0:T(256)S(1)} %copy-done.15, bf16[2,6,64,512]{3,2,1,0:T(8,128)(2,1)S(1)} %copy-done, bf16[2,3,64,512]{3,2,1,0:T(8,128)(2,1)S(1)} %copy-done.6, ...), custom_call_target="tpu_custom_call" | custom-call | flops 4718592000 | bytes 4718592 | tf_op jit(solution)/shard_map/near_pairs/pallas_call | solution.py:459
  136.8 0.0 collective-permute-done.6.rim_ref.far_rim_ref
  136.8 0.0 copy-done.2
  136.8 0.0 copy-done.4
  136.9 0.0 copy-done.11
  136.9 4.4 %annual_pairs.1._ = f32[2,6,4,64,512]{4,3,2,1,0:T(8,128)} custom-call(s32[7]{0:T(128)S(1)} %stack.27.who_ref, s32[2,192]{1,0:T(2,128)S(1)} %bitcast.11, s32[192]{0:T(256)S(1)} %copy-done.14, s32[192]{0:T(256)S(1)} %copy-done.15, bf16[2,6,64,512]{3,2,1,0:T(8,128)(2,1)S(1)} %copy-done, ...), custom_call_target="tpu_custom_call", output_to_operand_aliasing={{}: (11, {})} | custom-call | flops 1048576000 | bytes 1048576 | tf_op jit(solution)/shard_map/annual_pairs/pallas_call | solution.py:499
  141.3 0.0 collective-permute-done.3.late_ref.late_rim_ref
  141.3 2.6 %last_pairs.1 = f32[2,6,4,64,512]{4,3,2,1,0:T(8,128)} custom-call(s32[7]{0:T(128)S(1)} %stack.27.who_ref, s32[2,192]{1,0:T(2,128)S(1)} %bitcast.12, s32[192]{0:T(256)S(1)} %copy-done.14, s32[192]{0:T(256)S(1)} %copy-done.15, bf16[2,6,64,512]{3,2,1,0:T(8,128)(2,1)S(1)} %copy-done, ...), custom_call_target="tpu_custom_call", output_to_operand_aliasing={{}: (9, {})} | custom-call | flops 524288000 | bytes 524288 | tf_op jit(solution)/shard_map/last_pairs/pallas_call | solution.py:535
Async XLA Ops:
  0.0 111.5 %copy-start = (bf16[2,6,64,512]{3,2,1,0:T(8,128)(2,1)S(1)}, bf16[2,6,64,512]{3,2,1,0:T(8,128)(2,1)}, u32[]{:S(2)}) copy-start(bf16[2,6,64,512]{3,2,1,0:T(8,128)(2,1)} %slc_ref.7) | copy-start | bytes 2359300
  0.0 119.8 %copy-start.13 = (s32[192,2]{0,1:T(2,128)S(1)}, s32[192,2]{0,1:T(2,128)}, u32[]{:S(2)}) copy-start(s32[192,2]{0,1:T(2,128)} %param.5) | copy-start | bytes 4612
  0.0 119.8 %copy-start.15 = (s32[192]{0:T(256)S(1)}, s32[192]{0:T(256)}, u32[]{:S(2)}) copy-start(s32[192]{0:T(256)} %rng_ref.5) | copy-start | bytes 2308
  0.0 119.8 %copy-start.14 = (s32[192]{0:T(256)S(1)}, s32[192]{0:T(256)}, u32[]{:S(2)}) copy-start(s32[192]{0:T(256)} %az_ref.5) | copy-start | bytes 2308
  49.7 20.1 %collective-permute-start = (bf16[2,3,64,512]{3,2,1,0:T(8,128)(2,1)}, bf16[2,3,64,512]{3,2,1,0:T(8,128)(2,1)S(1)}, u32[]{:S(2)}, u32[]{:S(2)}) collective-permute-start(bf16[2,3,64,512]{3,2,1,0:T(8,128)(2,1)} %get-tuple-element.9), channel_id=1, source_target_pairs={{0,2},{2,0},{4,6},{6,4},{8,10},{10,8},{12,14},{14,12},{1,3},{3,1},... | collective-permute-start | bytes 1179656 | tf_op jit(solution)/shard_map/ppermute | solution.py:400
  52.7 17.1 %collective-permute-start.1 = (bf16[2,3,64,512]{3,2,1,0:T(8,128)(2,1)}, bf16[2,3,64,512]{3,2,1,0:T(8,128)(2,1)S(1)}, u32[]{:S(2)}, u32[]{:S(2)}) collective-permute-start(bf16[2,3,64,512]{3,2,1,0:T(8,128)(2,1)} %get-tuple-element.10), channel_id=1, source_target_pairs={{2,4},{6,8},{10,12},{4,2},{8,6},{12,10},{3,5},{7,9},{11,13},{5,3},... | collective-permute-start | bytes 1179656 | tf_op jit(solution)/shard_map/ppermute | solution.py:402
  53.4 49.4 %collective-permute-start.4 = (bf16[2,4,64,512]{3,2,1,0:T(8,128)(2,1)}, bf16[2,4,64,512]{3,2,1,0:T(8,128)(2,1)S(1)}, u32[]{:S(2)}, u32[]{:S(2)}) collective-permute-start(bf16[2,4,64,512]{3,2,1,0:T(8,128)(2,1)} %get-tuple-element.11), channel_id=1, source_target_pairs={{0,8},{2,10},{4,12},{6,14},{8,0},{10,2},{12,4},{14,6},{1,9},{3,11}... | collective-permute-start | bytes 1572872 | tf_op jit(solution)/shard_map/ppermute | solution.py:397
  69.8 0.8 copy-start.5
  70.6 0.7 copy-start.7
  84.4 27.1 %collective-permute-start.2 = (bf16[2,12,64,128]{3,2,1,0:T(8,128)(2,1)}, bf16[2,12,64,128]{3,2,1,0:T(8,128)(2,1)S(1)}, u32[]{:S(2)}, u32[]{:S(2)}) collective-permute-start(bf16[2,12,64,128]{3,2,1,0:T(8,128)(2,1)} %rim_blocks.2), channel_id=1, source_target_pairs={{0,1},{1,0},{2,3},{3,2},{4,5},{5,4},{6,7},{7,6},{8,9},{9,8},{10,11... | collective-permute-start | bytes 1179656 | tf_op jit(solution)/shard_map/ppermute | solution.py:79
  84.4 18.4 %collective-permute-start.5 = (bf16[2,2,64,512]{3,2,1,0:T(8,128)(2,1)}, bf16[2,2,64,512]{3,2,1,0:T(8,128)(2,1)S(1)}, u32[]{:S(2)}, u32[]{:S(2)}) collective-permute-start(bf16[2,2,64,512]{3,2,1,0:T(8,128)(2,1)} %get-tuple-element.12), channel_id=1, source_target_pairs={{0,6},{14,8},{1,7},{15,9},{16,22},{30,24},{17,23},{31,25}} | collective-permute-start | bytes 786440 | tf_op jit(solution)/shard_map/ppermute | solution.py:403
  102.8 0.7 copy-start.10
  103.5 0.8 copy-start.3
  111.4 25.4 %collective-permute-start.6 = (bf16[2,6,64,128]{3,2,1,0:T(8,128)(2,1)}, bf16[2,6,64,128]{3,2,1,0:T(8,128)(2,1)S(1)}, u32[]{:S(2)}, u32[]{:S(2)}) collective-permute-start(bf16[2,6,64,128]{3,2,1,0:T(8,128)(2,1)} %rim_blocks.3), channel_id=1, source_target_pairs={{0,1},{1,0},{2,3},{3,2},{4,5},{5,4},{6,7},{7,6},{8,9},{9,8},{10,11... | collective-permute-start | bytes 589832 | tf_op jit(solution)/shard_map/ppermute | solution.py:79
  111.5 1.0 copy-start.6
  112.5 1.0 copy-start.8
  113.5 0.7 copy-start.12
  115.4 25.9 %collective-permute-start.3 = (bf16[272,512]{1,0:T(8,128)(2,1)S(1)}, bf16[272,512]{1,0:T(8,128)(2,1)S(1)}, u32[]{:S(2)}, u32[]{:S(2)}) collective-permute-start(bf16[272,512]{1,0:T(8,128)(2,1)S(1)} %late_images.1), channel_id=1, source_target_pairs={{0,8},{2,10},{4,12},{6,14},{8,0},{10,2},{12,4},{14,6},{1,9},{3,11}... | collective-permute-start | bytes 835592 | tf_op jit(solution)/shard_map/ppermute | solution.py:434
  119.8 1.5 %copy-start.1 = (bf16[5,768,256]{2,1,0:T(8,128)(2,1)S(1)}, bf16[5,768,256]{2,1,0:T(8,128)(2,1)}, u32[]{:S(2)}) copy-start(bf16[5,768,256]{2,1,0:T(8,128)(2,1)} %range_bands.1.bands_ref) | copy-start | bytes 5898244
  121.3 1.0 copy-start.9
  122.3 14.5 %copy-start.2 = (bf16[5,768,256]{2,1,0:T(8,128)(2,1)S(1)}, bf16[5,768,256]{2,1,0:T(8,128)(2,1)}, u32[]{:S(2)}) copy-start(bf16[5,768,256]{2,1,0:T(8,128)(2,1)} %range_bands.1.bands_ref) | copy-start | bytes 5898244
  122.3 14.5 %copy-start.4 = (bf16[2,4,64,512]{3,2,1,0:T(8,128)(2,1)S(1)}, bf16[2,4,64,512]{3,2,1,0:T(8,128)(2,1)}, u32[]{:S(2)}) copy-start(bf16[2,4,64,512]{3,2,1,0:T(8,128)(2,1)} %copy-done.3) | copy-start | bytes 1572868
  122.3 14.5 %copy-start.11 = (bf16[2,2,64,512]{3,2,1,0:T(8,128)(2,1)S(1)}, bf16[2,2,64,512]{3,2,1,0:T(8,128)(2,1)}, u32[]{:S(2)}) copy-start(bf16[2,2,64,512]{3,2,1,0:T(8,128)(2,1)} %copy-done.10) | copy-start | bytes 786436

commit v2 on v1

v2 whole, which is shorter than its diff:
```python
import functools

import jax
import jax.numpy as jnp
from jax import lax
from jax.experimental import pallas as pl
from jax.experimental.pallas import tpu as pltpu
from jax.sharding import PartitionSpec as P

HALO = 16
REACH_LO = 12
NEAR = 3
YEAR = 29
EPSILON = 1e-06
TILE = 128
VMEM_BYTES = 20 * 1024 * 1024
SMALL_BYTES = 4 * 1024 * 1024
ANY = pl.BlockSpec(memory_space=pl.ANY)
SMEM = pl.BlockSpec(memory_space=pltpu.SMEM)
VMEM = pl.BlockSpec(memory_space=pltpu.VMEM)
HBM = pl.BlockSpec(memory_space=pltpu.HBM)


def small_params():
    return pltpu.CompilerParams(vmem_limit_bytes=SMALL_BYTES)


def run_copies(copies):
    for copy in copies:
        copy.start()
    for copy in copies:
        copy.wait()


def wanted_image(plan, pairs_ref, device, slot):
    dates = plan["dates"]
    date = device * dates + slot
    return pairs_ref[1, date * plan["per_date"] + NEAR] - lax.axis_index("date") * dates


def gather_strips(tiles, strip):
    lane = lax.broadcasted_iota(jnp.int32, tiles[0].shape, 1)
    packed = jnp.zeros(tiles[0].shape, jnp.float32)
    for n, tile in enumerate(tiles):
        spot = n * HALO
        moved = pltpu.roll(tile.astype(jnp.float32), spot + strip * HALO, 1)
        packed = jnp.where((lane >= spot) & (lane < spot + HALO), moved, packed)
    return packed.astype(jnp.bfloat16)


def place_strip(packed, n, strip):
    shift = 2 * TILE - (n + strip) * HALO
    return pltpu.roll(packed.astype(jnp.float32), lax.rem(shift, TILE), 1).astype(jnp.bfloat16)


def early_kernel(plan, slc_ref, pairs_ref, early_ref, strips_ref, sems):
    me, strip = lax.axis_index("date"), lax.axis_index("strip")
    dates, late, cols = plan["dates"], plan["late"], plan["cols"]
    half = plan["devices"] // 2
    mate = lax.rem(me + half, 2 * half)
    mate_slot = jnp.where(mate < half, late, 0)
    copies = []
    for k in range(dates - late):
        wanted = jnp.clip(wanted_image(plan, pairs_ref, mate, mate_slot + k), 0, dates - 1)
        copies.append(
            pltpu.make_async_copy(slc_ref.at[:, wanted], early_ref.at[:, k], sems.at[k])
        )
    run_copies(copies)
    tiles = []
    for k in range(dates - late):
        for c in range(2):
            left, right = early_ref[c, k, :, :TILE], early_ref[c, k, :, cols - TILE :]
            tiles.append(jnp.where(strip == 1, left, right))
    strips_ref[...] = gather_strips(tiles, 1 - strip)


def beside_kernel(plan, slc_ref, x_ref, z_ref, sems):
    odd = lax.rem(lax.axis_index("date"), 2)
    last = plan["dates"] - NEAR
    run_copies(
        [
            pltpu.make_async_copy(
                slc_ref.at[:, pl.ds(jnp.where(odd == 1, 0, last), NEAR)], x_ref, sems.at[0]
            ),
            pltpu.make_async_copy(
                slc_ref.at[:, pl.ds(jnp.where(odd == 1, last, 0), NEAR)], z_ref, sems.at[1]
            ),
        ]
    )


def rim_kernel(count, *refs):
    sources, out_ref, sems = refs[:count], refs[count], refs[count + 1]
    cols = sources[0].shape[3]
    start = pl.multiple_of(jnp.where(lax.axis_index("strip") == 0, cols - TILE, 0), TILE)
    copies = []
    place = 0
    for n, source in enumerate(sources):
        here = out_ref.at[:, pl.ds(place, source.shape[1])]
        copies.append(
            pltpu.make_async_copy(source.at[:, :, :, pl.ds(start, TILE)], here, sems.at[n])
        )
        place += source.shape[1]
    run_copies(copies)


def rims(*sources):
    planes, _, rows, _ = sources[0].shape
    total = sum(source.shape[1] for source in sources)
    tiles = pl.pallas_call(
        functools.partial(rim_kernel, len(sources)),
        out_shape=jax.ShapeDtypeStruct((planes, total, rows, TILE), sources[0].dtype),
        in_specs=[HBM] + [ANY] * (len(sources) - 1),
        out_specs=VMEM,
        scratch_shapes=[pltpu.SemaphoreType.DMA((len(sources),))],
        compiler_params=small_params(),
        name="rim_blocks",
    )(*sources)
    return lax.ppermute(tiles, "strip", [(0, 1), (1, 0)])


def late_kernel(plan, slc_ref, x_ref, z_ref, rim_ref, pairs_ref, late_ref, far_ref, rim_buf, sems,
                rim_sems):
    me, strip = lax.axis_index("date"), lax.axis_index("strip")
    dates, late, rows, cols = plan["dates"], plan["late"], plan["rows"], plan["cols"]
    half = plan["devices"] // 2
    odd = lax.rem(me, 2)
    mate = lax.rem(me + half, 2 * half)
    far = jnp.where(me < half, half - 1, half)
    routes = (
        (late_ref, mate, jnp.where(mate < half, 0, dates - late)),
        (far_ref, far, jnp.where(me < half, dates - late, 0)),
    )
    for r, (out_ref, device, slot) in enumerate(routes):
        for k in range(late):
            wanted = wanted_image(plan, pairs_ref, device, slot + k)
            wanted = jnp.clip(wanted, -NEAR, dates + NEAR - 1)
            own = (wanted >= 0) & (wanted < dates)
            below = wanted < 0
            spot = jnp.where(below, wanted + NEAR, wanted - dates)
            from_x = below == (odd == 1)
            place = jnp.where(own, wanted, spot + jnp.where(from_x, dates, dates + NEAR))

            def send(source, index):
                for c in range(2):
                    here = out_ref.at[pl.ds((2 * k + c) * rows, rows)]
                    pltpu.make_async_copy(source.at[c, index], here, sems.at[r, k, c]).start()

            pl.when(own)(functools.partial(send, slc_ref, jnp.clip(wanted, 0, dates - 1)))
            spot = jnp.clip(spot, 0, NEAR - 1)
            pl.when(jnp.logical_not(own) & from_x)(functools.partial(send, x_ref, spot))
            pl.when(jnp.logical_not(own) & jnp.logical_not(from_x))(
                functools.partial(send, z_ref, spot)
            )
            pltpu.make_async_copy(
                rim_ref.at[:, place], rim_buf.at[r, :, k], rim_sems.at[r, k]
            ).start()
    base, rim_rows = 2 * late * rows, plan["rim_rows"]
    for r, (out_ref, _, _) in enumerate(routes):
        for k in range(late):
            pltpu.make_async_copy(
                rim_ref.at[:, 0], rim_buf.at[r, :, k], rim_sems.at[r, k]
            ).wait()
        tiles = [rim_buf[r, c, k] for k in range(late) for c in range(2)]
        packed = gather_strips(tiles, strip)
        for n in range(rows // rim_rows):
            out_ref[base : base + rim_rows, n * TILE : (n + 1) * TILE] = packed[
                n * rim_rows : (n + 1) * rim_rows
            ]
        for k in range(late):
            for c in range(2):
                here = out_ref.at[pl.ds((2 * k + c) * rows, rows)]
                pltpu.make_async_copy(slc_ref.at[0, 0], here, sems.at[r, k, c]).wait()


def unpack_late(ref, n, strip, rows):
    packed = jnp.concatenate(
        [ref[:, t * TILE : (t + 1) * TILE] for t in range(ref.shape[1] // TILE)], axis=0
    )
    return place_strip(packed, n, strip)


def bands_kernel(cols, out_ref):
    strip = lax.axis_index("strip")
    wide = out_ref.shape[2]
    reach = pl.program_id(0) + REACH_LO

    def band(places, targets):
        return (jnp.abs(places - targets) <= reach).astype(jnp.float32).astype(jnp.bfloat16)

    shape = (wide, wide)
    row = lax.broadcasted_iota(jnp.int32, shape, 0)
    col = lax.broadcasted_iota(jnp.int32, shape, 1)
    out_ref[0, 0:wide] = band(row, col)
    shape = (TILE, wide)
    row = lax.broadcasted_iota(jnp.int32, shape, 0)
    col = lax.broadcasted_iota(jnp.int32, shape, 1)
    beyond = jnp.where(strip == 0, cols + row, row - TILE)
    middle = TILE // 2
    first = band(jnp.where(row < middle, wide + row, beyond), col)
    second = band(jnp.where(row < middle, beyond, wide - TILE + row), col + wide)
    for n, part in enumerate((first, first, second, second)):
        out_ref[0, wide + n * TILE : wide + (n + 1) * TILE] = part


def split(values):
    high = values.astype(jnp.bfloat16)
    low = (values - high.astype(jnp.float32)).astype(jnp.bfloat16)
    return high, low


def cross_terms(a_real, a_imag, b_real, b_imag):
    a_real, a_imag, b_real, b_imag = [
        part.astype(jnp.float32) for part in (a_real, a_imag, b_real, b_imag)
    ]
    return (
        a_real * b_real + a_imag * b_imag,
        a_imag * b_real - a_real * b_imag,
        a_real * a_real + a_imag * a_imag,
        b_real * b_real + b_imag * b_imag,
    )


def coherence(a_main, a_rim, b_main, b_rim, bands, height, store, scratch):
    high_ref, low_ref, side_ref, stack_ref = scratch
    rows, cols = a_main(0).shape
    wide = cols // 2
    lane = lax.broadcasted_iota(jnp.int32, (rows, TILE), 1)
    inner = lane < TILE // 2
    mains = cross_terms(a_main(0), a_main(1), b_main(0), b_main(1))
    edges = cross_terms(a_rim(0), a_rim(1), b_rim(0), b_rim(1))
    for f in range(4):
        here = slice(f * rows, (f + 1) * rows)
        high, low = split(mains[f])
        high_ref[here] = high
        low_ref[here] = low
        first = jnp.where(inner, mains[f][:, wide : wide + TILE], edges[f])
        second = jnp.where(inner, edges[f], mains[f][:, wide - TILE : wide])
        for n, part in enumerate((first, second)):
            high, low = split(part)
            side_ref[n, here, 0:TILE] = high
            side_ref[n, here, TILE : 2 * TILE] = low
    for n in range(2):
        there = slice(n * wide, (n + 1) * wide)
        inside = bands(0, wide)
        ranged = jnp.dot(high_ref[:, there], inside, preferred_element_type=jnp.float32)
        ranged += jnp.dot(low_ref[:, there], inside, preferred_element_type=jnp.float32)
        ranged += jnp.dot(
            side_ref[n],
            bands(wide + 2 * n * TILE, wide + 2 * (n + 1) * TILE),
            preferred_element_type=jnp.float32,
        )
        high, low = split(ranged)
        for f in range(4):
            stack_ref[f, 0:rows, there] = high[f * rows : (f + 1) * rows]
            stack_ref[f, rows : 2 * rows, there] = low[f * rows : (f + 1) * rows]
    row = lax.broadcasted_iota(jnp.int32, (rows, 2 * rows), 0)
    col = lax.broadcasted_iota(jnp.int32, (rows, 2 * rows), 1)
    col = jnp.where(col < rows, col, col - rows)
    band = (jnp.abs(row - col) <= height).astype(jnp.float32).astype(jnp.bfloat16)
    looked = [
        jnp.dot(band, stack_ref[f], preferred_element_type=jnp.float32) for f in range(4)
    ]
    inverse = lax.rsqrt(looked[2] * looked[3] + EPSILON)
    store(0, looked[0] * inverse)
    store(1, looked[1] * inverse)


def work_scratch(rows, cols):
    return [
        pltpu.VMEM((4 * rows, cols), jnp.bfloat16),
        pltpu.VMEM((4 * rows, cols), jnp.bfloat16),
        pltpu.VMEM((2, 4 * rows, 2 * TILE), jnp.bfloat16),
        pltpu.VMEM((4, 2 * rows, cols), jnp.bfloat16),
    ]


def near_kernel(plan, who_ref, pairs_ref, az_ref, rng_ref, slc_hbm, x_hbm, z_hbm, rim_hbm,
                bands_ref, out_ref, ext, rim, sems, *scratch):
    step = pl.program_id(0)
    dates, per_date = plan["dates"], plan["per_date"]
    me, flip = who_ref[0], who_ref[2]

    @pl.when(step == 0)
    def _():
        x_at = jnp.where(flip == 1, 0, dates + NEAR)
        z_at = jnp.where(flip == 1, dates + NEAR, 0)
        run_copies(
            [
                pltpu.make_async_copy(slc_hbm, ext.at[:, pl.ds(NEAR, dates)], sems.at[0]),
                pltpu.make_async_copy(x_hbm, ext.at[:, pl.ds(x_at, NEAR)], sems.at[1]),
                pltpu.make_async_copy(z_hbm, ext.at[:, pl.ds(z_at, NEAR)], sems.at[2]),
                pltpu.make_async_copy(
                    rim_hbm.at[:, pl.ds(0, dates)], rim.at[:, pl.ds(NEAR, dates)], sems.at[3]
                ),
                pltpu.make_async_copy(
                    rim_hbm.at[:, pl.ds(dates, NEAR)], rim.at[:, pl.ds(x_at, NEAR)], sems.at[4]
                ),
                pltpu.make_async_copy(
                    rim_hbm.at[:, pl.ds(dates + NEAR, NEAR)],
                    rim.at[:, pl.ds(z_at, NEAR)],
                    sems.at[5],
                ),
            ]
        )

    slot = step // NEAR
    pair = (me * dates + slot) * per_date + lax.rem(step, NEAR)
    other = jnp.clip(pairs_ref[1, pair] - me * dates + NEAR, 0, dates + 2 * NEAR - 1)
    own = slot + NEAR
    width = jnp.clip(rng_ref[pair] - REACH_LO, 0, HALO - REACH_LO)

    def store(c, values):
        out_ref[c, 0, 0] = values

    coherence(
        lambda c: ext[c, own],
        lambda c: rim[c, own],
        lambda c: ext[c, other],
        lambda c: rim[c, other],
        lambda a, b: bands_ref[width, a:b],
        az_ref[pair],
        store,
        scratch,
    )


def annual_kernel(plan, who_ref, pairs_ref, az_ref, rng_ref, slc_ref, own_rim_ref, early_ref,
                  strips_ref, far_ref, far_rim_ref, bands_ref, _, out_ref, *scratch):
    step = pl.program_id(0)
    dates, per_date, rows = plan["dates"], plan["per_date"], plan["rows"]
    strip = who_ref[1]
    date = who_ref[0] * dates + who_ref[3] + step
    pair = date * per_date + NEAR
    partner = pairs_ref[1, pair]
    from_far = jnp.where(who_ref[4] == 1, partner < date, partner > date)
    far = far_step(plan, step, who_ref[4])

    def store(c, values):
        out_ref[c, 0, 0] = values

    def main(c):
        return jnp.where(from_far, far_ref[c * rows : (c + 1) * rows], early_ref[c, 0])

    def rim(c):
        return jnp.where(
            from_far,
            unpack_late(far_rim_ref, 2 * far + c, strip, rows),
            place_strip(strips_ref[...], 2 * step + c, strip),
        )

    coherence(
        lambda c: slc_ref[c, 0],
        lambda c: own_rim_ref[c, 0],
        main,
        rim,
        lambda a, b: bands_ref[0, a:b],
        az_ref[pair],
        store,
        scratch,
    )


def far_step(plan, step, lower):
    skip = jnp.where(lower == 1, plan["dates"] - 2 * plan["late"], 0)
    return jnp.clip(step - skip, 0, plan["late"] - 1)


def last_kernel(plan, who_ref, pairs_ref, az_ref, rng_ref, slc_ref, own_rim_ref, late_ref,
                late_rim_ref, bands_ref, _, out_ref, *scratch):
    step = pl.program_id(0)
    dates, per_date, rows = plan["dates"], plan["per_date"], plan["rows"]
    pair = (who_ref[0] * dates + who_ref[5] + step) * per_date + NEAR

    def store(c, values):
        out_ref[c, 0, 0] = values

    coherence(
        lambda c: slc_ref[c, 0],
        lambda c: own_rim_ref[c, 0],
        lambda c: late_ref[c * rows : (c + 1) * rows],
        lambda c: unpack_late(late_rim_ref, 2 * step + c, who_ref[1], rows),
        lambda a, b: bands_ref[0, a:b],
        az_ref[pair],
        store,
        scratch,
    )


def plain_kernel(plan, who_ref, pairs_ref, az_ref, rng_ref, slc_ref, own_rim_ref, other_ref,
                 other_rim_ref, bands_ref, _, out_ref, *scratch):
    date = who_ref[0] * plan["dates"] + pl.program_id(0)

    def store(c, values):
        out_ref[c, 0, 0] = values

    coherence(
        lambda c: slc_ref[c, 0],
        lambda c: own_rim_ref[c, 0],
        lambda c: other_ref[c, 0],
        lambda c: other_rim_ref[c, 0],
        lambda a, b: bands_ref[0, a:b],
        az_ref[date * plan["per_date"] + NEAR],
        store,
        scratch,
    )


def arrivals_by_distance(slc, pair_list, plan):
    dates, per_date, devices = plan["dates"], plan["per_date"], plan["devices"]
    total = dates * devices
    me = lax.axis_index("date")
    annual_of = pair_list[:, 1].reshape(total, per_date)[:, per_date - 1]
    sums = [None] * dates
    for direction in (1, -1):
        by_distance = {}
        for slot in range(dates):
            for gap in range(plan["year"], plan["year"] + 3):
                distance = (slot + direction * gap) // dates
                by_distance.setdefault(distance, set()).add(slot)
        for distance in sorted(by_distance):
            slots = sorted(by_distance[distance])
            wanted_by = (me - distance) * dates + jnp.array(slots, dtype=jnp.int32)
            inside = (wanted_by >= 0) & (wanted_by < total)
            local = jnp.take(annual_of, jnp.clip(wanted_by, 0, total - 1)) - me * dates
            usable = inside & (local >= 0) & (local < dates)
            packed = jnp.take(slc, jnp.clip(local, 0, dates - 1), axis=1)
            packed = jnp.where(usable[None, :, None, None], packed, jnp.zeros_like(packed))
            route = [(i + distance, i) for i in range(devices) if 0 <= i + distance < devices]
            arrived = lax.ppermute(packed, "date", route)
            for n, slot in enumerate(slots):
                part = arrived[:, n]
                sums[slot] = part if sums[slot] is None else sums[slot] + part
    return jnp.stack(sums, axis=1)


def body(slc, pair_list, az_half, rng_half):
    planes, dates, rows, cols = slc.shape
    devices = lax.axis_size("date")
    total = dates * devices
    per_date = pair_list.shape[0] // total
    year = min(YEAR, total // 2 - 2)
    half = devices // 2
    late = half * dates - year
    rim_rows = rows * TILE // cols
    plan = {
        "dates": dates,
        "devices": devices,
        "per_date": per_date,
        "year": year,
        "late": late,
        "rows": rows,
        "cols": cols,
        "rim_rows": rim_rows,
    }
    me, strip = lax.axis_index("date"), lax.axis_index("strip")
    lower = (me < half).astype(jnp.int32)
    opposite = devices % 2 == 0 and 0 < late <= NEAR and 2 * late <= dates
    opposite = opposite and 2 * (dates - late) * HALO <= TILE
    pairs = pair_list.T
    dtype = slc.dtype
    params = pltpu.CompilerParams(vmem_limit_bytes=VMEM_BYTES)

    def images(count):
        return jax.ShapeDtypeStruct((planes, count, rows, cols), dtype)

    if opposite:
        swap = [(i, (i + half) % devices) for i in range(devices)]
        early, strips = pl.pallas_call(
            functools.partial(early_kernel, plan),
            out_shape=(images(dates - late), jax.ShapeDtypeStruct((rows, TILE), dtype)),
            in_specs=[HBM, SMEM],
            out_specs=(VMEM, VMEM),
            scratch_shapes=[pltpu.SemaphoreType.DMA((dates - late,))],
            compiler_params=small_params(),
            name="early_images",
        )(slc, pairs)
        slc, early, strips = lax.optimization_barrier((slc, early, strips))
        beside_x, beside_z = pl.pallas_call(
            functools.partial(beside_kernel, plan),
            out_shape=(images(NEAR), images(NEAR)),
            in_specs=[HBM],
            out_specs=(VMEM, VMEM),
            scratch_shapes=[pltpu.SemaphoreType.DMA((2,))],
            compiler_params=small_params(),
            name="beside_images",
        )(slc)
        early = lax.ppermute(early, "date", swap)
        strips = lax.ppermute(
            strips, ("date", "strip"), [(2 * a + s, 2 * b + 1 - s) for a, b in swap for s in (0, 1)]
        )
        beside_x = lax.ppermute(beside_x, "date", [(i, i ^ 1) for i in range(devices)])
        steps = [(i, i + 1) for i in range(1, devices - 1, 2)]
        beside_z = lax.ppermute(beside_z, "date", steps + [(b, a) for a, b in steps])
        flip = lax.rem(me, 2)
        base = jnp.where(lower == 1, late, 0)
        last_base = jnp.where(lower == 1, 0, dates - late)
    else:
        annual = arrivals_by_distance(slc, pair_list, plan)
        ups = [(i, i + 1) for i in range(devices - 1)]
        beside_x = lax.ppermute(slc[:, :NEAR], "date", [(b, a) for a, b in ups])
        beside_z = lax.ppermute(slc[:, dates - NEAR :], "date", ups)
        flip, base, last_base = 0, 0, 0
    who = jnp.stack(
        [jnp.asarray(v, jnp.int32) for v in (me, strip, flip, base, lower, last_base)]
    )
    rim = rims(slc, beside_x, beside_z)
    if opposite:
        late_shape = jax.ShapeDtypeStruct((2 * late * rows + rim_rows, cols), dtype)
        payload, far = pl.pallas_call(
            functools.partial(late_kernel, plan),
            out_shape=(late_shape, late_shape),
            in_specs=[HBM] + [ANY] * 3 + [SMEM],
            out_specs=(VMEM, VMEM),
            scratch_shapes=[
                pltpu.VMEM((2, 2, late, rows, TILE), dtype),
                pltpu.SemaphoreType.DMA((2, late, 2)),
                pltpu.SemaphoreType.DMA((2, late)),
            ],
            compiler_params=small_params(),
            name="late_images",
        )(slc, beside_x, beside_z, rim, pairs)
        payload = lax.ppermute(payload, "date", swap)
        far = lax.ppermute(far, "date", [(0, half - 1), (devices - 1, half)])
    wide = cols // 2
    widths = HALO - REACH_LO + 1
    band_rows = wide + 4 * TILE
    bands = pl.pallas_call(
        functools.partial(bands_kernel, cols),
        grid=(widths,),
        out_shape=jax.ShapeDtypeStruct((widths, band_rows, wide), jnp.bfloat16),
        out_specs=pl.BlockSpec((1, band_rows, wide), lambda n: (n, 0, 0)),
        compiler_params=small_params(),
        name="range_bands",
    )()
    out_shape = jax.ShapeDtypeStruct((planes, dates, per_date, rows, cols), jnp.float32)
    block = (planes, 1, 1, rows, cols)
    scalars = (who, pairs, az_half, rng_half)
    ext = dates + 2 * NEAR

    def cost(count):
        return pl.CostEstimate(
            flops=count,
            bytes_accessed=count,
            transcendentals=0,
        )

    out = pl.pallas_call(
        functools.partial(near_kernel, plan),
        grid_spec=pltpu.PrefetchScalarGridSpec(
            num_scalar_prefetch=4,
            grid=(dates * NEAR,),
            in_specs=[HBM]
            + [ANY] * 3
            + [pl.BlockSpec((widths, band_rows, wide), lambda n, *_: (0, 0, 0))],
            out_specs=pl.BlockSpec(block, lambda n, *_: (0, n // NEAR, lax.rem(n, NEAR), 0, 0)),
            scratch_shapes=[
                pltpu.VMEM((planes, ext, rows, cols), dtype),
                pltpu.VMEM((planes, ext, rows, TILE), dtype),
                pltpu.SemaphoreType.DMA((6,)),
            ]
            + work_scratch(rows, cols),
        ),
        out_shape=out_shape,
        compiler_params=params,
        cost_estimate=cost(dates * NEAR),
        name="near_pairs",
    )(*scalars, slc, beside_x, beside_z, rim, bands)

    image, strip_rim = (planes, 1, rows, cols), (planes, 1, rows, TILE)

    def own_slot(start):
        return lambda n, who_ref, *_: (0, who_ref[start] + n, 0, 0)

    def band_block(start):
        def of(n, who_ref, pairs_ref, az_ref, rng_ref):
            pair = (who_ref[0] * dates + who_ref[start] + n) * per_date + NEAR
            return (jnp.clip(rng_ref[pair] - REACH_LO, 0, widths - 1), 0, 0)

        return pl.BlockSpec((1, band_rows, wide), of)

    def annual_pairs(kernel, start, count, others, specs, name):
        return pl.pallas_call(
            functools.partial(kernel, plan),
            grid_spec=pltpu.PrefetchScalarGridSpec(
                num_scalar_prefetch=4,
                grid=(count,),
                in_specs=[
                    pl.BlockSpec(image, own_slot(start)),
                    pl.BlockSpec(strip_rim, own_slot(start)),
                    *specs,
                    band_block(start),
                    ANY,
                ],
                out_specs=pl.BlockSpec(
                    block, lambda n, who_ref, *_: (0, who_ref[start] + n, NEAR, 0, 0)
                ),
                scratch_shapes=work_scratch(rows, cols),
            ),
            out_shape=out_shape,
            input_output_aliases={len(specs) + 7: 0},
            compiler_params=params,
            cost_estimate=cost(count),
            name=name,
        )(*scalars, slc, rim, *others, bands, out)

    rim_place = pl.BlockSpec((rim_rows, cols), lambda n, *_: (2 * late * rows // rim_rows, 0))
    if opposite:
        specs = [
            pl.BlockSpec(image, lambda n, *_: (0, n, 0, 0)),
            pl.BlockSpec((rows, TILE), lambda n, *_: (0, 0)),
            pl.BlockSpec(
                (2 * rows, cols), lambda n, who_ref, *_: (far_step(plan, n, who_ref[4]), 0)
            ),
            rim_place,
        ]
        out = annual_pairs(
            annual_kernel, 3, dates - late, (early, strips, far, far), specs, "annual_pairs"
        )
        specs = [pl.BlockSpec((2 * rows, cols), lambda n, *_: (n, 0)), rim_place]
        out = annual_pairs(last_kernel, 5, late, (payload, payload), specs, "last_pairs")
    else:
        specs = [pl.BlockSpec(image, own_slot(3)), pl.BlockSpec(strip_rim, own_slot(3))]
        out = annual_pairs(
            plain_kernel, 3, dates, (annual, rims(annual)), specs, "annual_pairs"
        )
    return out.reshape(planes, dates * per_date, rows, cols)


def solution(mesh):
    placed = (P(None, "date", "groups", "strip"), P(), P(), P())
    return jax.shard_map(
        body,
        mesh=mesh,
        in_specs=placed,
        out_specs=P(None, "date", "groups", "strip"),
        check_vma=False,
    )
```

time: 144 us -> 73.3 us (0.51)
  Pallas kernels: 95.1 us -> 28.5 us
  waiting for transfers between devices: 16 us -> 27 us
  starting transfers between devices: 24.4 us -> 13.7 us
  local copies, waits for them, and re-layouts: 8.3 us -> 3.6 us
    pallas_call x4 -> x5, Pallas kernels: 57.9 us -> 13.6 us  [the longest x2 8.93 us: annual_pairs(): pl.pallas_call(functools.partial(kernel, plan), grid_spec=pltpu.PrefetchS...]
    pallas_call x2 -> x1, Pallas kernels: 20.1 us -> 0.1 us  [rims(): pl.pallas_call(functools.partial(rim_kernel, len(sources)), out_shape=jax...]
    ppermute x2 -> x3, waiting for transfers between devices: 0.01 us -> 10.9 us  [the longest x1 10.9 us: body(): lax.ppermute(strips, ('date', 'strip'), [(2 * a + s, 2 * b + 1 - s) for a...]
    ppermute x1, starting transfers between devices: 11.9 us -> 4.17 us  [body(): far = lax.ppermute(far, 'date', [(0, half - 1), (devices - 1, half)])]
    unnamed x32 -> x18, local copies, waits for them, and re-layouts: 8.21 us -> 3.52 us
    ppermute x1, waiting for transfers between devices: 12.1 us -> 16.1 us  [body(): lax.ppermute(beside_x, 'date', [(i, i ^ 1) for i in range(devices)])]
    ppermute x1, waiting for transfers between devices: 3.82 us -> 0.01 us  [body(): far = lax.ppermute(far, 'date', [(0, half - 1), (devices - 1, half)])]
    ppermute x2 -> x3, starting transfers between devices: 8.68 us -> 5.75 us  [the longest x1 3.64 us: body(): early = lax.ppermute(early, 'date', swap)]
  transfers between devices with their start and end apart: 7 -> 7, of which waited for: 2 -> 2; matrix products, arithmetic and copies ran while one was open for 0% -> 0% of each run, Pallas kernels for 30% -> 31%
where the time goes in v2:
time: 73.3 us; the launch traced here: 72.9 us
  Pallas kernels  28.5 us (39%)
  waiting for transfers between devices  27 us (37%)
  starting transfers between devices  13.7 us (19%)
  local copies, waits for them, and re-layouts  3.6 us (5%)
    ppermute x1, waiting for transfers between devices, body(): lax.ppermute(beside_x, 'date', [(i, i ^ 1) for i in range(devices)])  16.1 us
    pallas_call x1, Pallas kernels, body(): pl.pallas_call(functools.partial(near_kernel, plan), grid_spec=pltpu.Pref...  14.3 us
    ppermute x1, waiting for transfers between devices, body(): lax.ppermute(strips, ('date', 'strip'), [(2 * a + s, 2 * b + 1 - s) for a...  10.9 us
    pallas_call x2, Pallas kernels, annual_pairs(): pl.pallas_call(functools.partial(kernel, plan), grid_spec=pltpu.PrefetchS...  8.93 us
    ppermute x1, starting transfers between devices, body(): far = lax.ppermute(far, 'date', [(0, half - 1), (devices - 1, half)])  4.17 us
    ppermute x1, starting transfers between devices, body(): early = lax.ppermute(early, 'date', swap)  3.64 us
    unnamed x18, local copies, waits for them, and re-layouts  3.52 us
    ppermute x1, starting transfers between devices, body(): lax.ppermute(beside_x, 'date', [(i, i ^ 1) for i in range(devices)])  3 us
  transfers between devices with their start and end apart: 7, of which 2 were waited for; matrix products, arithmetic and copies ran while one was open for 0% of the time, Pallas kernels for 31%

profile of v2, /device:TPU:0, one launch (start us, length us, event | category | flops | bytes accessed | tf_op | source)
XLA Modules:
  0.0 72.9 jit_solution(7561512869375817604)
XLA Ops:
  0.0 0.0 copy-start.7
  0.0 0.0 copy-start
  0.0 1.1 %copy-done = bf16[2,6,64,512]{3,2,1,0:T(8,128)(2,1)S(1)} copy-done((bf16[2,6,64,512]{3,2,1,0:T(8,128)(2,1)S(1)}, bf16[2,6,64,512]{3,2,1,0:T(8,128)(2,1)}, u32[]{:S(2)}) %copy-start) | copy-done | bytes 786456
  1.1 0.0 copy-start.4
  1.2 0.7 copy-done.4
  1.8 0.0 copy-start.1
  1.8 0.0 copy-start.6
  1.8 0.0 copy-start.8
  1.8 1.8 %early_images.1 = (bf16[2,4,64,512]{3,2,1,0:T(8,128)(2,1)}, bf16[64,128]{1,0:T(8,128)(2,1)}) custom-call(bf16[2,6,64,512]{3,2,1,0:T(8,128)(2,1)S(1)} %copy-done, s32[2,192]{1,0:T(2,128)S(1)} %bitcast.8), custom_call_target="tpu_custom_call" | custom-call | tf_op jit(solution)/shard_map/early_images/pallas_call | solution.py:469
  3.7 0.2 beside_images.1
  3.9 3.0 %collective-permute-start = (bf16[2,3,64,512]{3,2,1,0:T(8,128)(2,1)S(1)}, bf16[2,3,64,512]{3,2,1,0:T(8,128)(2,1)S(1)}, u32[]{:S(2)}, u32[]{:S(2)}) collective-permute-start(bf16[2,3,64,512]{3,2,1,0:T(8,128)(2,1)S(1)} %get-tuple-element.17), channel_id=1, source_target_pairs={{0,2},{2,0},{4,6},{6,4},{8,10},{10,8},{12,14},{14,12},{1,3},{3,1},... | collective-permute-start | bytes 1179656 | tf_op jit(solution)/shard_map/ppermute | solution.py:492
  6.9 0.7 collective-permute-start.1
  7.6 16.1 %collective-permute-done.refs_1_.x_ref.x_hbm = bf16[2,3,64,512]{3,2,1,0:T(8,128)(2,1)S(1)} collective-permute-done((bf16[2,3,64,512]{3,2,1,0:T(8,128)(2,1)S(1)}, bf16[2,3,64,512]{3,2,1,0:T(8,128)(2,1)S(1)}, u32[]{:S(2)}, u32[]{:S(2)}) %collective-permute-start) | collective-permute-done | bytes 393248 | tf_op jit(solution)/shard_map/ppermute | solution.py:492
  23.7 0.0 collective-permute-done.1.refs_2_.z_ref.z_hbm
  23.7 0.0 copy-start.2
  23.7 0.1 rim_blocks.1
  23.8 0.1 collective-permute-start.2
  23.9 3.6 %collective-permute-start.4 = (bf16[2,4,64,512]{3,2,1,0:T(8,128)(2,1)}, bf16[2,4,64,512]{3,2,1,0:T(8,128)(2,1)}, u32[]{:S(2)}, u32[]{:S(2)}) collective-permute-start(bf16[2,4,64,512]{3,2,1,0:T(8,128)(2,1)} %get-tuple-element.20), channel_id=1, source_target_pairs={{0,8},{2,10},{4,12},{6,14},{8,0},{10,2},{12,4},{14,6},{1,9},{3,11}... | collective-permute-start | bytes 1572872 | tf_op jit(solution)/shard_map/ppermute | solution.py:488
  27.6 0.0 collective-permute-done.2.rim_ref.rim_hbm.own_rim_ref
  27.6 0.0 copy-start.5
  27.6 0.7 copy-done.5
  28.2 2.6 %late_images.1 = (bf16[272,512]{1,0:T(8,128)(2,1)}, bf16[272,512]{1,0:T(8,128)(2,1)}) custom-call(bf16[2,6,64,512]{3,2,1,0:T(8,128)(2,1)S(1)} %copy-done, bf16[2,3,64,512]{3,2,1,0:T(8,128)(2,1)S(1)} %collective-permute-done.refs_1_.x_ref.x_hbm, bf16[2,3,64,512]{3,2,1,0:T(8,128)(2,1)S(1)} %collective-permute-done.1.refs_2_.z_ref.z_hbm, ...), custom_call_target="tpu_custom_call" | custom-call | tf_op jit(solution)/shard_map/late_images/pallas_call | solution.py:510
  30.8 0.0 copy-done.2
  30.8 4.2 %collective-permute-start.6 = (bf16[272,512]{1,0:T(8,128)(2,1)}, bf16[272,512]{1,0:T(8,128)(2,1)}, u32[]{:S(2)}, u32[]{:S(2)}) collective-permute-start(bf16[272,512]{1,0:T(8,128)(2,1)} %get-tuple-element.22), channel_id=1, source_target_pairs={{0,6},{14,8},{1,7},{15,9},{16,22},{30,24},{17,23},{31,25}} | collective-permute-start | bytes 835592 | tf_op jit(solution)/shard_map/ppermute | solution.py:524
  35.0 0.0 collective-permute-start.3
  35.0 2.1 %collective-permute-start.5 = (bf16[64,128]{1,0:T(8,128)(2,1)}, bf16[64,128]{1,0:T(8,128)(2,1)}, u32[]{:S(2)}, u32[]{:S(2)}) collective-permute-start(bf16[64,128]{1,0:T(8,128)(2,1)} %get-tuple-element.21), channel_id=1, source_target_pairs={{0,9},{1,8},{2,11},{3,10},{4,13},{5,12},{6,15},{7,14},{8,1},{9,0},... | collective-permute-start | bytes 49160 | tf_op jit(solution)/shard_map/ppermute | solution.py:489
  37.1 0.5 range_bands.1.bands_ref
  37.7 0.1 stack.27.who_ref
  37.7 0.0 copy-done.7
  37.7 0.0 copy-done.1
  37.7 0.0 copy-done.6
  37.8 0.0 copy-done.8
  37.8 0.0 copy-start.3
  37.8 1.0 %copy-done.3 = bf16[2,3,64,512]{3,2,1,0:T(8,128)(2,1)S(1)} copy-done((bf16[2,3,64,512]{3,2,1,0:T(8,128)(2,1)S(1)}, bf16[2,3,64,512]{3,2,1,0:T(8,128)(2,1)}, u32[]{:S(2)}) %copy-start.3) | copy-done | bytes 393240
  38.8 14.3 %near_pairs.1._ = f32[2,6,4,64,512]{4,3,2,1,0:T(8,128)} custom-call(s32[6]{0:T(128)S(1)} %stack.27.who_ref, s32[2,192]{1,0:T(2,128)S(1)} %bitcast.10, s32[192]{0:T(256)S(1)} %copy-done.7, s32[192]{0:T(256)S(1)} %copy-done.8, bf16[2,6,64,512]{3,2,1,0:T(8,128)(2,1)S(1)} %copy-done.1, bf16[2,3,64,512]{3,2,1,0:T(8,128)(2,1)S(1)} %collective-permute-done.refs_1_.x_ref.x_hbm, ...), custom_call_target="tpu_custom_call" | custom-call | flops 18 | bytes 18 | tf_op jit(solution)/shard_map/near_pairs/pallas_call | solution.py:548
  53.1 10.9 %collective-permute-done.5.strips_ref = bf16[64,128]{1,0:T(8,128)(2,1)} collective-permute-done((bf16[64,128]{1,0:T(8,128)(2,1)}, bf16[64,128]{1,0:T(8,128)(2,1)}, u32[]{:S(2)}, u32[]{:S(2)}) %collective-permute-start.5) | collective-permute-done | bytes 16416 | tf_op jit(solution)/shard_map/ppermute | solution.py:489
  64.0 0.0 collective-permute-done.4.early_ref
  64.0 0.0 collective-permute-done.6.far_ref.far_rim_ref
  64.0 5.4 %annual_pairs.1._ = f32[2,6,4,64,512]{4,3,2,1,0:T(8,128)} custom-call(s32[6]{0:T(128)S(1)} %stack.27.who_ref, s32[2,192]{1,0:T(2,128)S(1)} %bitcast.11, s32[192]{0:T(256)S(1)} %copy-done.7, s32[192]{0:T(256)S(1)} %copy-done.8, bf16[2,6,64,512]{3,2,1,0:T(8,128)(2,1)S(1)} %copy-done.1, ...), custom_call_target="tpu_custom_call", output_to_operand_aliasing={{}: (11, {})} | custom-call | flops 4 | bytes 4 | tf_op jit(solution)/shard_map/annual_pairs/pallas_call | solution.py:583
  69.4 0.0 collective-permute-done.3.late_ref.late_rim_ref
  69.4 3.5 %last_pairs.1 = f32[2,6,4,64,512]{4,3,2,1,0:T(8,128)} custom-call(s32[6]{0:T(128)S(1)} %stack.27.who_ref, s32[2,192]{1,0:T(2,128)S(1)} %bitcast.12, s32[192]{0:T(256)S(1)} %copy-done.7, s32[192]{0:T(256)S(1)} %copy-done.8, bf16[2,6,64,512]{3,2,1,0:T(8,128)(2,1)S(1)} %copy-done.1, ...), custom_call_target="tpu_custom_call", output_to_operand_aliasing={{}: (9, {})} | custom-call | flops 2 | bytes 2 | tf_op jit(solution)/shard_map/last_pairs/pallas_call | solution.py:583
Async XLA Ops:
  0.0 37.7 %copy-start.7 = (s32[192]{0:T(256)S(1)}, s32[192]{0:T(256)}, u32[]{:S(2)}) copy-start(s32[192]{0:T(256)} %az_ref.5) | copy-start | bytes 2308
  0.0 1.1 %copy-start = (bf16[2,6,64,512]{3,2,1,0:T(8,128)(2,1)S(1)}, bf16[2,6,64,512]{3,2,1,0:T(8,128)(2,1)}, u32[]{:S(2)}) copy-start(bf16[2,6,64,512]{3,2,1,0:T(8,128)(2,1)} %slc_ref.5) | copy-start | bytes 2359300
  1.1 0.7 copy-start.4
  1.8 35.9 %copy-start.1 = (bf16[2,6,64,512]{3,2,1,0:T(8,128)(2,1)S(1)}, bf16[2,6,64,512]{3,2,1,0:T(8,128)(2,1)}, u32[]{:S(2)}) copy-start(bf16[2,6,64,512]{3,2,1,0:T(8,128)(2,1)} %slc_ref.5) | copy-start | bytes 2359300
  1.8 35.9 %copy-start.6 = (s32[192,2]{0,1:T(2,128)S(1)}, s32[192,2]{0,1:T(2,128)}, u32[]{:S(2)}) copy-start(s32[192,2]{0,1:T(2,128)} %param.5) | copy-start | bytes 4612
  1.8 35.9 %copy-start.8 = (s32[192]{0:T(256)S(1)}, s32[192]{0:T(256)}, u32[]{:S(2)}) copy-start(s32[192]{0:T(256)} %rng_ref.5) | copy-start | bytes 2308
  3.9 19.8 %collective-permute-start = (bf16[2,3,64,512]{3,2,1,0:T(8,128)(2,1)S(1)}, bf16[2,3,64,512]{3,2,1,0:T(8,128)(2,1)S(1)}, u32[]{:S(2)}, u32[]{:S(2)}) collective-permute-start(bf16[2,3,64,512]{3,2,1,0:T(8,128)(2,1)S(1)} %get-tuple-element.17), channel_id=1, source_target_pairs={{0,2},{2,0},{4,6},{6,4},{8,10},{10,8},{12,14},{14,12},{1,3},{3,1},... | collective-permute-start | bytes 1179656 | tf_op jit(solution)/shard_map/ppermute | solution.py:492
  6.9 16.8 %collective-permute-start.1 = (bf16[2,3,64,512]{3,2,1,0:T(8,128)(2,1)S(1)}, bf16[2,3,64,512]{3,2,1,0:T(8,128)(2,1)S(1)}, u32[]{:S(2)}, u32[]{:S(2)}) collective-permute-start(bf16[2,3,64,512]{3,2,1,0:T(8,128)(2,1)S(1)} %get-tuple-element.18), channel_id=1, source_target_pairs={{2,4},{6,8},{10,12},{4,2},{8,6},{12,10},{3,5},{7,9},{11,13},{5,3},... | collective-permute-start | bytes 1179656 | tf_op jit(solution)/shard_map/ppermute | solution.py:494
  23.7 7.1 %copy-start.2 = (bf16[2,3,64,512]{3,2,1,0:T(8,128)(2,1)}, bf16[2,3,64,512]{3,2,1,0:T(8,128)(2,1)S(1)}, u32[]{:S(2)}) copy-start(bf16[2,3,64,512]{3,2,1,0:T(8,128)(2,1)S(1)} %collective-permute-done.1.refs_2_.z_ref.z_hbm) | copy-start | bytes 1179652
  23.8 3.7 %collective-permute-start.2 = (bf16[2,12,64,128]{3,2,1,0:T(8,128)(2,1)S(1)}, bf16[2,12,64,128]{3,2,1,0:T(8,128)(2,1)S(1)}, u32[]{:S(2)}, u32[]{:S(2)}) collective-permute-start(bf16[2,12,64,128]{3,2,1,0:T(8,128)(2,1)S(1)} %rim_blocks.1), channel_id=1, source_target_pairs={{0,1},{1,0},{2,3},{3,2},{4,5},{5,4},{6,7},{7,6},{8,9},{9,8},{10,11... | collective-permute-start | bytes 1179656 | tf_op jit(solution)/shard_map/ppermute | solution.py:119
  23.9 40.1 %collective-permute-start.4 = (bf16[2,4,64,512]{3,2,1,0:T(8,128)(2,1)}, bf16[2,4,64,512]{3,2,1,0:T(8,128)(2,1)}, u32[]{:S(2)}, u32[]{:S(2)}) collective-permute-start(bf16[2,4,64,512]{3,2,1,0:T(8,128)(2,1)} %get-tuple-element.20), channel_id=1, source_target_pairs={{0,8},{2,10},{4,12},{6,14},{8,0},{10,2},{12,4},{14,6},{1,9},{3,11}... | collective-permute-start | bytes 1572872 | tf_op jit(solution)/shard_map/ppermute | solution.py:488
  27.6 0.7 copy-start.5
  30.8 33.2 %collective-permute-start.6 = (bf16[272,512]{1,0:T(8,128)(2,1)}, bf16[272,512]{1,0:T(8,128)(2,1)}, u32[]{:S(2)}, u32[]{:S(2)}) collective-permute-start(bf16[272,512]{1,0:T(8,128)(2,1)} %get-tuple-element.22), channel_id=1, source_target_pairs={{0,6},{14,8},{1,7},{15,9},{16,22},{30,24},{17,23},{31,25}} | collective-permute-start | bytes 835592 | tf_op jit(solution)/shard_map/ppermute | solution.py:524
  35.0 34.4 %collective-permute-start.3 = (bf16[272,512]{1,0:T(8,128)(2,1)}, bf16[272,512]{1,0:T(8,128)(2,1)}, u32[]{:S(2)}, u32[]{:S(2)}) collective-permute-start(bf16[272,512]{1,0:T(8,128)(2,1)} %get-tuple-element.19), channel_id=1, source_target_pairs={{0,8},{2,10},{4,12},{6,14},{8,0},{10,2},{12,4},{14,6},{1,9},{3,11}... | collective-permute-start | bytes 835592 | tf_op jit(solution)/shard_map/ppermute | solution.py:523
  35.0 29.0 %collective-permute-start.5 = (bf16[64,128]{1,0:T(8,128)(2,1)}, bf16[64,128]{1,0:T(8,128)(2,1)}, u32[]{:S(2)}, u32[]{:S(2)}) collective-permute-start(bf16[64,128]{1,0:T(8,128)(2,1)} %get-tuple-element.21), channel_id=1, source_target_pairs={{0,9},{1,8},{2,11},{3,10},{4,13},{5,12},{6,15},{7,14},{8,1},{9,0},... | collective-permute-start | bytes 49160 | tf_op jit(solution)/shard_map/ppermute | solution.py:489
  37.8 1.0 %copy-start.3 = (bf16[2,3,64,512]{3,2,1,0:T(8,128)(2,1)S(1)}, bf16[2,3,64,512]{3,2,1,0:T(8,128)(2,1)}, u32[]{:S(2)}) copy-start(bf16[2,3,64,512]{3,2,1,0:T(8,128)(2,1)} %copy-done.2) | copy-start | bytes 1179652

commit v3 on v0

v3 whole, which is shorter than its diff:
```python
import functools

import jax
import jax.numpy as jnp
from jax import lax
from jax.experimental import pallas as pl
from jax.experimental.pallas import tpu as pltpu
from jax.sharding import PartitionSpec as P

HALO = 16
REACH_LO = 12
NEAR = 3
YEAR = 29
EPSILON = 1e-06
TILE = 128
INNER = TILE // 2
ANY = pl.BlockSpec(memory_space=pl.ANY)
SMEM = pl.BlockSpec(memory_space=pltpu.SMEM)
VMEM = pl.BlockSpec(memory_space=pltpu.VMEM)


def limit(mebibytes):
    return pltpu.CompilerParams(vmem_limit_bytes=mebibytes * 1024 * 1024)


def run_copies(copies):
    for copy in copies:
        copy.start()
    for copy in copies:
        copy.wait()


def gather_strips(tiles, side):
    lane = lax.broadcasted_iota(jnp.int32, tiles[0].shape, 1)
    packed = jnp.zeros(tiles[0].shape, jnp.float32)
    for n, tile in enumerate(tiles):
        spot = n * HALO
        moved = pltpu.roll(tile.astype(jnp.float32), spot + side * HALO, 1)
        packed = jnp.where((lane >= spot) & (lane < spot + HALO), moved, packed)
    return packed.astype(jnp.bfloat16)


def place_strip(packed, n, side):
    shift = 2 * TILE - (n + side) * HALO
    return pltpu.roll(packed.astype(jnp.float32), lax.rem(shift, TILE), 1).astype(jnp.bfloat16)


def write_strips(out_ref, packed):
    rows, cols = packed.shape[0], out_ref.shape[1]
    part = rows * TILE // cols
    base = out_ref.shape[0] - part
    for n in range(rows // part):
        out_ref[base:, n * TILE : (n + 1) * TILE] = packed[n * part : (n + 1) * part]


def read_strips(ref, rows):
    cols = ref.shape[1]
    base = ref.shape[0] - rows * TILE // cols
    return jnp.concatenate(
        [ref[base:, n * TILE : (n + 1) * TILE] for n in range(cols // TILE)], axis=0
    )


def early_kernel(plan, slc_ref, pairs_ref, early_ref, strips_ref, rim_ref, sems):
    me, strip = lax.axis_index("date"), lax.axis_index("strip")
    dates, late, cols = plan["dates"], plan["late"], plan["cols"]
    half = plan["devices"] // 2
    mate = lax.rem(me + half, 2 * half)
    mate_slot = jnp.where(mate < half, late, 0)
    start = pl.multiple_of(jnp.where(strip == 0, cols - TILE, 0), TILE)
    copies = [
        pltpu.make_async_copy(
            slc_ref.at[:, :, :, pl.ds(start, TILE)], rim_ref, sems.at[dates - late]
        )
    ]
    for k in range(dates - late):
        date = mate * dates + mate_slot + k
        wanted = pairs_ref[1, date * plan["per_date"] + NEAR] - me * dates
        wanted = jnp.clip(wanted, 0, dates - 1)
        copies.append(
            pltpu.make_async_copy(slc_ref.at[:, wanted], early_ref.at[:, k], sems.at[k])
        )
    run_copies(copies)
    tiles = []
    for k in range(dates - late):
        for c in range(2):
            left, right = early_ref[c, k, :, :TILE], early_ref[c, k, :, cols - TILE :]
            tiles.append(jnp.where(strip == 1, left, right))
    strips_ref[...] = gather_strips(tiles, 1 - strip)


def rim_kernel(slc_ref, rim_ref, sem):
    cols = slc_ref.shape[3]
    start = pl.multiple_of(jnp.where(lax.axis_index("strip") == 0, cols - TILE, 0), TILE)
    run_copies([pltpu.make_async_copy(slc_ref.at[:, :, :, pl.ds(start, TILE)], rim_ref, sem)])


def beside_kernel(plan, slc_ref, rim_ref, inner_ref, outer_ref, sems):
    me, strip = lax.axis_index("date"), lax.axis_index("strip")
    dates, rows = plan["dates"], plan["rows"]
    upper = me >= plan["devices"] // 2
    last = dates - NEAR
    copies = []
    firsts = (jnp.where(upper, last, 0), jnp.where(upper, 0, last))
    for r, (out_ref, first) in enumerate(zip((inner_ref, outer_ref), firsts)):
        for k in range(NEAR):
            for c in range(2):
                here = out_ref.at[pl.ds((2 * k + c) * rows, rows)]
                copies.append(
                    pltpu.make_async_copy(slc_ref.at[c, first + k], here, sems.at[r, k, c])
                )
    for copy in copies:
        copy.start()
    for out_ref, first in zip((inner_ref, outer_ref), firsts):
        tiles = [rim_ref[c, first + k] for k in range(NEAR) for c in range(2)]
        write_strips(out_ref, gather_strips(tiles, strip))
    for copy in copies:
        copy.wait()


def late_kernel(plan, slc_ref, rim_ref, inner_ref, meta_ref, _, late_ref, tiles_ref):
    me, strip = lax.axis_index("date"), lax.axis_index("strip")
    dates, late, rows = plan["dates"], plan["late"], plan["rows"]
    half = plan["devices"] // 2
    mate = lax.rem(me + half, 2 * half)
    mate_slot = jnp.where(mate < half, 0, dates - late)
    packed = read_strips(inner_ref, rows)
    for k in range(late):
        date = mate * dates + mate_slot + k
        wanted = meta_ref[date * plan["per_date"] + NEAR] - me * dates
        own = (wanted >= 0) & (wanted < dates)
        own_at = jnp.clip(wanted, 0, dates - 1)
        other_at = jnp.clip(jnp.where(me < half, wanted - dates, wanted + NEAR), 0, NEAR - 1)
        for c in range(2):
            here = pl.ds((2 * k + c) * rows, rows)

            @pl.when(own)
            def _():
                late_ref[here] = slc_ref[c, own_at]
                tiles_ref[k, c] = rim_ref[c, own_at]

            @pl.when(jnp.logical_not(own))
            def _():
                there = pl.multiple_of((2 * other_at + c) * rows, rows)
                late_ref[here] = inner_ref[pl.ds(there, rows)]
                tiles_ref[k, c] = place_strip(packed, 2 * other_at + c, strip)

    tiles = [tiles_ref[k, c] for k in range(late) for c in range(2)]
    write_strips(late_ref, gather_strips(tiles, strip))


def bands_kernel(cols, out_ref):
    strip = lax.axis_index("strip")
    wide = out_ref.shape[3]
    reach = pl.program_id(0) + REACH_LO

    def band(places, targets):
        return (jnp.abs(places - targets) <= reach).astype(jnp.float32).astype(jnp.bfloat16)

    def indices(shape):
        return lax.broadcasted_iota(jnp.int32, shape, 0), lax.broadcasted_iota(jnp.int32, shape, 1)

    inside = band(*indices((wide, wide)))
    row, col = indices((TILE, wide))
    beyond = jnp.where(strip == 0, cols + row, row - TILE)
    first = band(jnp.where(row < INNER, wide + row, beyond), col)
    second = band(jnp.where(row < INNER, beyond, wide - TILE + row), col + wide)
    for n, part in enumerate((first, second)):
        out_ref[0, n, 0:wide] = inside
        out_ref[0, n, wide : 2 * wide] = inside
        out_ref[0, n, 2 * wide : 2 * wide + TILE] = part
        out_ref[0, n, 2 * wide + TILE : 2 * wide + 2 * TILE] = part


def split(values):
    high = values.astype(jnp.bfloat16)
    low = (values - high.astype(jnp.float32)).astype(jnp.bfloat16)
    return high, low


def put(ref, here, t, values):
    wide = 2 * TILE
    depth = 2 * wide + 2 * TILE
    for low, part in enumerate(split(values)):
        side = [n * depth + 2 * wide + low * TILE for n in range(2)]
        if t < 4:
            at = (t // 2) * depth + low * wide + (t % 2) * TILE
            ref[*here, at : at + TILE] = part
        if t == 2:
            ref[*here, side[0] : side[0] + INNER] = part[:, :INNER]
        if t == 1:
            ref[*here, side[1] + INNER : side[1] + TILE] = part[:, INNER:]
        if t == 4:
            ref[*here, side[0] + INNER : side[0] + TILE] = part[:, INNER:]
            ref[*here, side[1] : side[1] + INNER] = part[:, :INNER]


def tile_of(main, rim, t):
    return [
        (rim(c) if t == 4 else main(c, slice(t * TILE, (t + 1) * TILE))).astype(jnp.float32)
        for c in range(2)
    ]


class Pairs:
    def __init__(self, plan, meta_ref, slc_ref, rim_ref, bands_ref, powers_ref, out_ref, scratch):
        self.plan, self.meta_ref = plan, meta_ref
        self.slc_ref, self.rim_ref = slc_ref, rim_ref
        self.bands_ref, self.powers_ref, self.out_ref = bands_ref, powers_ref, out_ref
        (self.left_ref, self.stack_ref, self.other_ref, self.other_rim_ref, self.stage_ref,
         self.count_ref, self.sems) = scratch
        self.me, self.strip = lax.axis_index("date"), lax.axis_index("strip")
        self.count_ref[0] = 0

    def partner(self, pair):
        return self.meta_ref[pair]

    def own_other(self, index):
        return (
            lambda c, cols: self.slc_ref[c, index, :, cols],
            lambda c: self.rim_ref[c, index],
        )

    def fetched_other(self):
        return (
            lambda c, cols: self.other_ref[c, :, cols],
            lambda c: self.other_rim_ref[c],
        )

    def fetch_payload(self, ref, index):
        rows = self.plan["rows"]
        packed = read_strips(ref, rows)
        for c in range(2):
            at = pl.multiple_of((2 * index + c) * rows, rows)
            self.other_ref[c] = ref[pl.ds(at, rows)]
            self.other_rim_ref[c] = place_strip(packed, 2 * index + c, self.strip)

    def out_copy(self, slot, pair):
        return pltpu.make_async_copy(
            self.stage_ref.at[slot], self.out_ref.at[:, pair], self.sems.at[slot]
        )

    def finish(self):
        count = self.count_ref[0]

        @pl.when(count >= 1)
        def _():
            self.out_copy(lax.rem(count + 1, 2), 0).wait()

        @pl.when(count >= 2)
        def _():
            self.out_copy(lax.rem(count, 2), 0).wait()

    def run(self, slot, kind, other, other_power=None):
        plan, left_ref, stack_ref = self.plan, self.left_ref, self.stack_ref
        rows, dates, per_date = plan["rows"], plan["dates"], plan["per_date"]
        count = self.count_ref[0]
        stage = lax.rem(count, 2)

        @pl.when(count >= 2)
        def _():
            self.out_copy(stage, 0).wait()

        pair = (self.me * dates + slot) * per_date + kind
        height = self.meta_ref[plan["pairs"] + pair]
        width = self.meta_ref[2 * plan["pairs"] + pair] - REACH_LO
        width = jnp.clip(width, 0, HALO - REACH_LO)
        part = [(pl.ds(f * rows, rows),) for f in range(4)]
        left_ref[*part[2]] = self.powers_ref[slot]
        if other_power is not None:
            left_ref[*part[3]] = self.powers_ref[other_power]
        first = self.own_other(slot)
        for t in range(5):
            a_real, a_imag = tile_of(*first, t)
            b_real, b_imag = tile_of(*other, t)
            put(left_ref, part[0], t, a_real * b_real + a_imag * b_imag)
            put(left_ref, part[1], t, a_imag * b_real - a_real * b_imag)
            if other_power is None:
                put(left_ref, part[3], t, b_real * b_real + b_imag * b_imag)
        depth = self.bands_ref.shape[2]
        wide = self.bands_ref.shape[3]
        for n in range(2):
            ranged = jnp.dot(
                left_ref[:, n * depth : (n + 1) * depth],
                self.bands_ref[width, n],
                preferred_element_type=jnp.float32,
            )
            for low, values in enumerate(split(ranged)):
                for f in range(4):
                    stack_ref[f, low * rows : (low + 1) * rows, n * wide : (n + 1) * wide] = values[
                        f * rows : (f + 1) * rows
                    ]
        row = lax.broadcasted_iota(jnp.int32, (rows, 2 * rows), 0)
        col = lax.broadcasted_iota(jnp.int32, (rows, 2 * rows), 1)
        col = jnp.where(col < rows, col, col - rows)
        band = (jnp.abs(row - col) <= height).astype(jnp.float32).astype(jnp.bfloat16)
        looked = [
            jnp.dot(band, stack_ref[f], preferred_element_type=jnp.float32) for f in range(4)
        ]
        inverse = lax.rsqrt(looked[2] * looked[3] + EPSILON)
        for c in range(2):
            self.stage_ref[stage, c] = looked[c] * inverse
        self.out_copy(stage, slot * per_date + kind).start()
        self.count_ref[0] = count + 1


def own_kernel(plan, meta_ref, slc_ref, rim_ref, bands_ref, out_ref, powers_ref, *scratch):
    pairs = Pairs(plan, meta_ref, slc_ref, rim_ref, bands_ref, powers_ref, out_ref, scratch)
    dates = plan["dates"]

    def power(slot, carry):
        for t in range(5):
            real, imag = tile_of(*pairs.own_other(slot), t)
            put(powers_ref, (slot, slice(None)), t, real * real + imag * imag)
        return carry

    lax.fori_loop(0, dates, power, 0)

    def step(n, carry):
        slot, kind = n // NEAR, lax.rem(n, NEAR)
        pair = (pairs.me * dates + slot) * plan["per_date"] + kind
        local = pairs.partner(pair) - pairs.me * dates

        @pl.when((local >= 0) & (local < dates))
        def _():
            pairs.run(slot, kind, pairs.own_other(local), local)

        return carry

    lax.fori_loop(0, dates * NEAR, step, 0)
    pairs.finish()


def rest_kernel(plan, meta_ref, slc_ref, rim_ref, bands_ref, powers_ref, inner_ref, outer_ref,
                middle_ref, _, out_ref, *scratch):
    pairs = Pairs(plan, meta_ref, slc_ref, rim_ref, bands_ref, powers_ref, out_ref, scratch)
    dates, half = plan["dates"], plan["devices"] // 2
    upper = pairs.me >= half
    if plan["halves"]:
        in_middle = jnp.where(upper, pairs.me == half, pairs.me == half - 1)
    else:
        upper, in_middle = True, False

    def step(n, carry):
        slot, kind = n // NEAR, lax.rem(n, NEAR)
        pair = (pairs.me * dates + slot) * plan["per_date"] + kind
        local = pairs.partner(pair) - pairs.me * dates
        below = local < 0
        index = jnp.clip(jnp.where(below, local + NEAR, local - dates), 0, NEAR - 1)
        inner = below == upper

        @pl.when(below | (local >= dates))
        def _():
            middle = inner & in_middle
            pl.when(middle)(lambda: pairs.fetch_payload(middle_ref, index))
            pl.when(inner & jnp.logical_not(middle))(
                lambda: pairs.fetch_payload(inner_ref, index)
            )
            pl.when(jnp.logical_not(inner))(lambda: pairs.fetch_payload(outer_ref, index))
            pairs.run(slot, kind, pairs.fetched_other())

        return carry

    lax.fori_loop(0, dates * NEAR, step, 0)
    pairs.finish()


def annual_kernel(plan, is_late, meta_ref, slc_ref, rim_ref, bands_ref, powers_ref, inner_ref,
                  outer_ref, images_ref, strips_ref, _, out_ref, *scratch):
    pairs = Pairs(plan, meta_ref, slc_ref, rim_ref, bands_ref, powers_ref, out_ref, scratch)
    dates, late, rows = plan["dates"], plan["late"], plan["rows"]
    half = plan["devices"] // 2
    me, split_date = pairs.me, half * dates
    lower = me < half
    if is_late:
        base, count = jnp.where(lower, 0, dates - late), late
    else:
        base, count = jnp.where(lower, late, 0), dates - late

    def fetch_early(k):
        packed = strips_ref[...]
        for c in range(2):
            pairs.other_ref[c] = images_ref[c, k]
            pairs.other_rim_ref[c] = place_strip(packed, 2 * k + c, pairs.strip)

    def step(k, carry):
        slot = base + k
        date = me * dates + slot
        other = pairs.partner(date * plan["per_date"] + NEAR)
        far = (other < split_date) == lower
        from_inner = jnp.where(lower, me != 0, me == half)
        inner_at = jnp.where(lower, other, other - (2 * split_date - NEAR))
        outer_at = jnp.where(lower, other - (split_date - NEAR), other - split_date)

        @pl.when(far & from_inner)
        def _():
            pairs.fetch_payload(inner_ref, jnp.clip(inner_at, 0, NEAR - 1))

        @pl.when(far & jnp.logical_not(from_inner))
        def _():
            pairs.fetch_payload(outer_ref, jnp.clip(outer_at, 0, NEAR - 1))

        @pl.when(jnp.logical_not(far))
        def _():
            if is_late:
                pairs.fetch_payload(images_ref, k)
            else:
                fetch_early(k)

        pairs.run(slot, NEAR, pairs.fetched_other())
        return carry

    lax.fori_loop(0, count, step, 0)
    pairs.finish()


def plain_kernel(plan, meta_ref, slc_ref, rim_ref, bands_ref, powers_ref, images_ref,
                 image_rim_ref, _, out_ref, *scratch):
    pairs = Pairs(plan, meta_ref, slc_ref, rim_ref, bands_ref, powers_ref, out_ref, scratch)

    def step(slot, carry):
        other = (
            lambda c, cols: images_ref[c, slot, :, cols],
            lambda c: image_rim_ref[c, slot],
        )
        pairs.run(slot, NEAR, other)
        return carry

    lax.fori_loop(0, plan["dates"], step, 0)
    pairs.finish()


def arrivals_by_distance(slc, pair_list, plan):
    dates, per_date, devices = plan["dates"], plan["per_date"], plan["devices"]
    total = dates * devices
    me = lax.axis_index("date")
    annual_of = pair_list[:, 1].reshape(total, per_date)[:, per_date - 1]
    sums = [None] * dates
    for direction in (1, -1):
        by_distance = {}
        for slot in range(dates):
            for gap in range(plan["year"], plan["year"] + 3):
                distance = (slot + direction * gap) // dates
                by_distance.setdefault(distance, set()).add(slot)
        for distance in sorted(by_distance):
            slots = sorted(by_distance[distance])
            wanted_by = (me - distance) * dates + jnp.array(slots, dtype=jnp.int32)
            inside = (wanted_by >= 0) & (wanted_by < total)
            local = jnp.take(annual_of, jnp.clip(wanted_by, 0, total - 1)) - me * dates
            usable = inside & (local >= 0) & (local < dates)
            packed = jnp.take(slc, jnp.clip(local, 0, dates - 1), axis=1)
            packed = jnp.where(usable[None, :, None, None], packed, jnp.zeros_like(packed))
            route = [(i + distance, i) for i in range(devices) if 0 <= i + distance < devices]
            arrived = lax.ppermute(packed, "date", route)
            for n, slot in enumerate(slots):
                part = arrived[:, n]
                sums[slot] = part if sums[slot] is None else sums[slot] + part
    return jnp.stack(sums, axis=1)


def payload_of(images, rim, strip):
    planes, count, rows, cols = images.shape
    edges = jnp.where(strip == 0, rim[..., :HALO], rim[..., TILE - HALO :])
    edges = jnp.transpose(edges, (2, 1, 0, 3)).reshape(rows, count * planes * HALO)
    edges = jnp.pad(edges, ((0, 0), (0, TILE - edges.shape[1])))
    part = rows * TILE // cols
    edges = jnp.transpose(edges.reshape(rows // part, part, TILE), (1, 0, 2)).reshape(part, cols)
    stacked = jnp.transpose(images, (1, 0, 2, 3)).reshape(count * planes * rows, cols)
    return jnp.concatenate([stacked, edges], axis=0)


def body(slc, pair_list, az_half, rng_half):
    planes, dates, rows, cols = slc.shape
    devices = lax.axis_size("date")
    total = dates * devices
    per_date = pair_list.shape[0] // total
    year = min(YEAR, total // 2 - 2)
    half = devices // 2
    late = half * dates - year
    halves = devices % 2 == 0 and 0 < late <= NEAR and 2 * late <= dates
    halves = halves and 2 * (dates - late) * HALO <= TILE
    plan = {
        "dates": dates,
        "devices": devices,
        "per_date": per_date,
        "year": year,
        "late": late,
        "rows": rows,
        "cols": cols,
        "pairs": total * per_date,
        "halves": halves,
    }
    dtype = slc.dtype
    rim_rows = rows * TILE // cols
    meta = jnp.concatenate([pair_list[:, 1], az_half, rng_half])
    swap_strips = [(0, 1), (1, 0)]

    def images(count):
        return jax.ShapeDtypeStruct((planes, count, rows, cols), dtype)

    def rim_shape(count):
        return jax.ShapeDtypeStruct((planes, count, rows, TILE), dtype)

    def payload_shape(count):
        return jax.ShapeDtypeStruct((planes * count * rows + rim_rows, cols), dtype)

    def swapped_rims(values):
        out = pl.pallas_call(
            rim_kernel,
            out_shape=rim_shape(values.shape[1]),
            in_specs=[ANY],
            out_specs=VMEM,
            scratch_shapes=[pltpu.SemaphoreType.DMA],
            compiler_params=limit(4),
            name="rim_blocks",
        )(values)
        return lax.ppermute(out, "strip", swap_strips)

    wide = cols // 2
    widths = HALO - REACH_LO + 1
    band_shape = (2, 2 * wide + 2 * TILE, wide)
    bands = pl.pallas_call(
        functools.partial(bands_kernel, cols),
        grid=(widths,),
        out_shape=jax.ShapeDtypeStruct((widths, *band_shape), jnp.bfloat16),
        out_specs=pl.BlockSpec((1, *band_shape), lambda n: (n, 0, 0, 0)),
        compiler_params=limit(4),
        name="range_bands",
    )()
    if halves:
        swap = [(i, (i + half) % devices) for i in range(devices)]
        early, strips, rim = pl.pallas_call(
            functools.partial(early_kernel, plan),
            out_shape=(
                images(dates - late),
                jax.ShapeDtypeStruct((rows, TILE), dtype),
                rim_shape(dates),
            ),
            in_specs=[ANY, SMEM],
            out_specs=(VMEM, VMEM, VMEM),
            scratch_shapes=[pltpu.SemaphoreType.DMA((dates - late + 1,))],
            compiler_params=limit(56),
            name="early_images",
        )(slc, pair_list.T)
        early = lax.ppermute(early, "date", swap)
        rim = lax.ppermute(rim, "strip", swap_strips)
        strips = lax.ppermute(
            strips, ("date", "strip"), [(2 * a + s, 2 * b + 1 - s) for a, b in swap for s in (0, 1)]
        )
        inner, outer = pl.pallas_call(
            functools.partial(beside_kernel, plan),
            out_shape=(payload_shape(NEAR), payload_shape(NEAR)),
            in_specs=[ANY, VMEM],
            out_specs=(VMEM, VMEM),
            scratch_shapes=[pltpu.SemaphoreType.DMA((2, NEAR, 2))],
            compiler_params=limit(4),
            name="beside_images",
        )(slc, rim)
        down = [(i, (i - 1) % half) for i in range(half)]
        down += [(half + i, half + (i + 1) % half) for i in range(half)]
        middle = lax.ppermute(outer, "date", [(half - 1, half), (half, half - 1)])
        inner = lax.ppermute(inner, "date", down)
        outer = lax.ppermute(outer, "date", [(b, a) for a, b in down])
    else:
        rim = swapped_rims(slc)
        annual = arrivals_by_distance(slc, pair_list, plan)
        strip = lax.axis_index("strip")
        ups = [(i, i + 1) for i in range(devices - 1)]
        inner = payload_of(slc[:, dates - NEAR :], rim[:, dates - NEAR :], strip)
        outer = payload_of(slc[:, :NEAR], rim[:, :NEAR], strip)
        inner = lax.ppermute(inner, "date", ups)
        outer = lax.ppermute(outer, "date", [(b, a) for a, b in ups])
        middle = inner

    out_shape = jax.ShapeDtypeStruct((planes, dates * per_date, rows, cols), jnp.float32)
    depth = 2 * band_shape[1]
    scratch = [
        pltpu.VMEM((4 * rows, depth), jnp.bfloat16),
        pltpu.VMEM((4, 2 * rows, cols), jnp.bfloat16),
        pltpu.VMEM((planes, rows, cols), dtype),
        pltpu.VMEM((planes, rows, TILE), dtype),
        pltpu.VMEM((2, planes, rows, cols), jnp.float32),
        pltpu.SMEM((1,), jnp.int32),
        pltpu.SemaphoreType.DMA((2,)),
    ]

    def cost(flops):
        return pl.CostEstimate(flops=flops, bytes_accessed=1, transcendentals=0)

    out, powers = pl.pallas_call(
        functools.partial(own_kernel, plan),
        out_shape=(out_shape, jax.ShapeDtypeStruct((dates, rows, depth), jnp.bfloat16)),
        in_specs=[SMEM, VMEM, VMEM, VMEM],
        out_specs=(ANY, VMEM),
        scratch_shapes=scratch,
        compiler_params=limit(24),
        cost_estimate=cost(20_000_000_000),
        name="own_pairs",
    )(meta, slc, rim, bands)

    def more_pairs(kernel, out, others, name):
        return pl.pallas_call(
            functools.partial(kernel, plan),
            out_shape=out_shape,
            in_specs=[SMEM] + [VMEM] * (4 + len(others)) + [ANY],
            out_specs=ANY,
            scratch_shapes=scratch,
            input_output_aliases={5 + len(others): 0},
            compiler_params=limit(24),
            cost_estimate=cost(1),
            name=name,
        )(meta, slc, rim, bands, powers, *others, out)

    if halves:
        payload = pl.pallas_call(
            functools.partial(late_kernel, plan),
            out_shape=payload_shape(late),
            in_specs=[VMEM, VMEM, VMEM, SMEM, ANY],
            out_specs=VMEM,
            scratch_shapes=[pltpu.VMEM((late, planes, rows, TILE), dtype)],
            compiler_params=limit(4),
            name="late_images",
        )(slc, rim, inner, meta, powers)
        payload = lax.ppermute(payload, "date", swap)
    out = more_pairs(rest_kernel, out, (inner, outer, middle), "near_pairs")
    if halves:
        kernel = lambda plan, *refs: annual_kernel(plan, False, *refs)
        out = more_pairs(kernel, out, (inner, outer, early, strips), "annual_pairs")
        kernel = lambda plan, *refs: annual_kernel(plan, True, *refs)
        out = more_pairs(kernel, out, (inner, outer, payload, strips), "last_pairs")
    else:
        out = more_pairs(plain_kernel, out, (annual, swapped_rims(annual)), "annual_pairs")
    return out


def solution(mesh):
    placed = (P(None, "date", "groups", "strip"), P(), P(), P())
    return jax.shard_map(
        body,
        mesh=mesh,
        in_specs=placed,
        out_specs=P(None, "date", "groups", "strip"),
        check_vma=False,
    )
```

time: 173 us -> 59.7 us (0.35)
  the two profiles are of different devices: /device:TPU:15 before, /device:TPU:0 now
where the time goes in v3:
time: 59.7 us; the launch traced here: 59.1 us
  Pallas kernels  27.3 us (46%)
  starting transfers between devices  15.6 us (26%)
  waiting for transfers between devices  12.3 us (21%)
  local copies, waits for them, and re-layouts  2.96 us (5%)
  other arithmetic  0.77 us (1%)
    pallas_call x1, Pallas kernels, body(): pl.pallas_call(functools.partial(own_kernel, plan), out_shape=(out_shape,...  11.2 us
    pallas_call x3, Pallas kernels, more_pairs(): pl.pallas_call(functools.partial(kernel, plan), out_shape=out_shape, in_s...  10.7 us
    ppermute x1, waiting for transfers between devices, body(): lax.ppermute(strips, ('date', 'strip'), [(2 * a + s, 2 * b + 1 - s) for a...  10.7 us
    ppermute x1, starting transfers between devices, body(): payload = lax.ppermute(payload, 'date', swap)  6.92 us
    ppermute x1, starting transfers between devices, body(): early = lax.ppermute(early, 'date', swap)  3.66 us
    pallas_call x1, Pallas kernels, body(): pl.pallas_call(functools.partial(early_kernel, plan), out_shape=(images(d...  2.83 us
    ppermute x1, starting transfers between devices, body(): inner = lax.ppermute(inner, 'date', down)  2.31 us
    unnamed x8, local copies, waits for them, and re-layouts  2.27 us
  transfers between devices with their start and end apart: 7, of which 2 were waited for; matrix products, arithmetic and copies ran while one was open for 2% of the time, Pallas kernels for 37%

profile of v3, /device:TPU:0, one launch (start us, length us, event | category | flops | bytes accessed | tf_op | source)
XLA Modules:
  0.0 59.1 jit_solution(14529516394469788128)
XLA Ops:
  0.0 2.8 %early_images.1 = (bf16[2,4,64,512]{3,2,1,0:T(8,128)(2,1)}, bf16[64,128]{1,0:T(8,128)(2,1)}, bf16[2,6,64,128]{3,2,1,0:T(8,128)(2,1)}) custom-call(bf16[2,6,64,512]{3,2,1,0:T(8,128)(2,1)} %refs_1_.3, s32[2,192]{1,0:T(2,128)} %bitcast.2), custom_call_target="tpu_custom_call" | custom-call | tf_op jit(solution)/shard_map/early_images/pallas_call | solution.py:532
  2.8 0.5 collective-permute-start
  3.4 3.7 %collective-permute-start.5 = (bf16[2,4,64,512]{3,2,1,0:T(8,128)(2,1)}, bf16[2,4,64,512]{3,2,1,0:T(8,128)(2,1)S(1)}, u32[]{:S(2)}, u32[]{:S(2)}) collective-permute-start(bf16[2,4,64,512]{3,2,1,0:T(8,128)(2,1)} %get-tuple-element.17), channel_id=1, source_target_pairs={{0,8},{2,10},{4,12},{6,14},{8,0},{10,2},{12,4},{14,6},{1,9},{3,11}... | collective-permute-start | bytes 1572872 | tf_op jit(solution)/shard_map/ppermute | solution.py:545
  7.0 0.7 %slice.3 = s32[192,1]{0,1:T(1,128)S(1)} slice(s32[192,2]{0,1:T(2,128)} %param.5), slice={[0:192], [1:2]} | slice | bytes 1536 | tf_op jit(solution)/shard_map/slice | solution.py:495
  7.7 0.5 range_bands.1.bands_ref.refs_3_
  8.2 0.8 %pad_add_fusion.meta_ref.refs_0_ = s32[576]{0:T(1024)S(1)} fusion(s32[192]{0:T(256)} %param.7, s32[192]{0:T(256)} %param.6, s32[192]{0:T(256)S(1)} %bitcast.3), kind=kLoop, calls=%fused_computation | loop fusion | flops 1152 | bytes 4608 | tf_op jit(solution)/shard_map/concatenate | solution.py:495
  9.0 0.0 collective-permute-done.rim_ref.refs_2_
  9.0 0.0 copy-start
  9.0 1.1 %copy-done = bf16[2,6,64,512]{3,2,1,0:T(8,128)(2,1)S(1)} copy-done((bf16[2,6,64,512]{3,2,1,0:T(8,128)(2,1)S(1)}, bf16[2,6,64,512]{3,2,1,0:T(8,128)(2,1)}, u32[]{:S(2)}) %copy-start) | copy-done | bytes 786456
  10.2 1.2 %beside_images.1 = (bf16[400,512]{1,0:T(8,128)(2,1)S(1)}, bf16[400,512]{1,0:T(8,128)(2,1)S(1)}) custom-call(bf16[2,6,64,512]{3,2,1,0:T(8,128)(2,1)S(1)} %copy-done, bf16[2,6,64,128]{3,2,1,0:T(8,128)(2,1)S(1)} %collective-permute-done.rim_ref.refs_2_), custom_call_target="tpu_custom_call" | custom-call | tf_op jit(solution)/shard_map/beside_images/pallas_call | solution.py:550
  11.4 0.7 %collective-permute-start.6 = (bf16[400,512]{1,0:T(8,128)(2,1)S(1)}, bf16[400,512]{1,0:T(8,128)(2,1)S(1)}, u32[]{:S(2)}, u32[]{:S(2)}) collective-permute-start(bf16[400,512]{1,0:T(8,128)(2,1)S(1)} %get-tuple-element.15), channel_id=1, source_target_pairs={{6,8},{8,6},{7,9},{9,7},{22,24},{24,22},{23,25},{25,23}} | collective-permute-start | bytes 1228808 | tf_op jit(solution)/shard_map/ppermute | solution.py:561
  12.1 1.5 %collective-permute-start.2 = (bf16[400,512]{1,0:T(8,128)(2,1)S(1)}, bf16[400,512]{1,0:T(8,128)(2,1)S(1)}, u32[]{:S(2)}, u32[]{:S(2)}) collective-permute-start(bf16[400,512]{1,0:T(8,128)(2,1)S(1)} %get-tuple-element.15), channel_id=1, source_target_pairs={{6,0},{0,2},{2,4},{4,6},{10,8},{12,10},{14,12},{8,14},{7,1},{1,3},... | collective-permute-start | bytes 1228808 | tf_op jit(solution)/shard_map/ppermute | solution.py:563
  13.6 2.3 %collective-permute-start.1 = (bf16[400,512]{1,0:T(8,128)(2,1)S(1)}, bf16[400,512]{1,0:T(8,128)(2,1)S(1)}, u32[]{:S(2)}, u32[]{:S(2)}) collective-permute-start(bf16[400,512]{1,0:T(8,128)(2,1)S(1)} %get-tuple-element.14), channel_id=1, source_target_pairs={{0,6},{2,0},{4,2},{6,4},{8,10},{10,12},{12,14},{14,8},{1,7},{3,1},... | collective-permute-start | bytes 1228808 | tf_op jit(solution)/shard_map/ppermute | solution.py:562
  15.9 0.0 copy-start.1
  15.9 1.1 %copy-done.1 = bf16[2,6,64,512]{3,2,1,0:T(8,128)(2,1)S(1)} copy-done((bf16[2,6,64,512]{3,2,1,0:T(8,128)(2,1)S(1)}, bf16[2,6,64,512]{3,2,1,0:T(8,128)(2,1)}, u32[]{:S(2)}) %copy-start.1) | copy-done | bytes 786456
  17.1 0.0 copy-start.3
  17.1 0.0 copy-start.2
  17.1 11.2 %own_pairs.1 = (f32[2,24,64,512]{3,2,1,0:T(8,128)}, bf16[6,64,1536]{2,1,0:T(8,128)(2,1)S(1)}) custom-call(s32[576]{0:T(1024)S(1)} %pad_add_fusion.meta_ref.refs_0_, bf16[2,6,64,512]{3,2,1,0:T(8,128)(2,1)S(1)} %copy-done.1, bf16[2,6,64,128]{3,2,1,0:T(8,128)(2,1)S(1)} %collective-permute-done.rim_ref.refs_2_, ...), custom_call_target="tpu_custom_call" | custom-call | flops 20000000000 | bytes 1 | tf_op jit(solution)/shard_map/own_pairs/pallas_call | solution.py:590
  28.3 1.6 %collective-permute-done.1.inner_ref.refs_5_ = bf16[400,512]{1,0:T(8,128)(2,1)S(1)} collective-permute-done((bf16[400,512]{1,0:T(8,128)(2,1)S(1)}, bf16[400,512]{1,0:T(8,128)(2,1)S(1)}, u32[]{:S(2)}, u32[]{:S(2)}) %collective-permute-start.1) | collective-permute-done | bytes 409632 | tf_op jit(solution)/shard_map/ppermute | solution.py:562
  29.9 0.7 %late_images.1 = bf16[272,512]{1,0:T(8,128)(2,1)S(1)} custom-call(bf16[2,6,64,512]{3,2,1,0:T(8,128)(2,1)S(1)} %copy-done.1, bf16[2,6,64,128]{3,2,1,0:T(8,128)(2,1)S(1)} %collective-permute-done.rim_ref.refs_2_, bf16[400,512]{1,0:T(8,128)(2,1)S(1)} %collective-permute-done.1.inner_ref.refs_5_, s32[576]{0:T(1024)S(1)} %pad_add_fusion.meta_ref.refs_0_, ...), custom_call_target="tpu_custom_call" | custom-call | tf_op jit(solution)/shard_map/late_images/pallas_call | solution.py:615
  30.6 6.9 %collective-permute-start.3 = (bf16[272,512]{1,0:T(8,128)(2,1)S(1)}, bf16[272,512]{1,0:T(8,128)(2,1)S(1)}, u32[]{:S(2)}, u32[]{:S(2)}) collective-permute-start(bf16[272,512]{1,0:T(8,128)(2,1)S(1)} %late_images.1), channel_id=1, source_target_pairs={{0,8},{2,10},{4,12},{6,14},{8,0},{10,2},{12,4},{14,6},{1,9},{3,11}... | collective-permute-start | bytes 835592 | tf_op jit(solution)/shard_map/ppermute | solution.py:624
  37.6 0.0 copy-done.3
  37.6 0.0 collective-permute-start.4
  37.6 0.0 collective-permute-done.6.middle_ref
  37.6 0.0 collective-permute-done.2.outer_ref.refs_6_
  37.6 0.0 copy-done.2
  37.6 3.9 %near_pairs.1.refs_9_ = f32[2,24,64,512]{3,2,1,0:T(8,128)} custom-call(s32[576]{0:T(1024)S(1)} %pad_add_fusion.meta_ref.refs_0_, bf16[2,6,64,512]{3,2,1,0:T(8,128)(2,1)S(1)} %copy-done.2, bf16[2,6,64,128]{3,2,1,0:T(8,128)(2,1)S(1)} %collective-permute-done.rim_ref.refs_2_, ...), custom_call_target="tpu_custom_call", output_to_operand_aliasing={{}: (8, {})} | custom-call | flops 1 | bytes 1 | tf_op jit(solution)/shard_map/near_pairs/pallas_call | solution.py:602
  41.5 10.7 %collective-permute-done.4.refs_8_ = bf16[64,128]{1,0:T(8,128)(2,1)S(1)} collective-permute-done((bf16[64,128]{1,0:T(8,128)(2,1)S(1)}, bf16[64,128]{1,0:T(8,128)(2,1)S(1)}, u32[]{:S(2)}, u32[]{:S(2)}) %collective-permute-start.4) | collective-permute-done | bytes 16416 | tf_op jit(solution)/shard_map/ppermute | solution.py:547
  52.2 0.0 collective-permute-done.5.refs_7_
  52.2 4.1 %annual_pairs.1.refs_9_ = f32[2,24,64,512]{3,2,1,0:T(8,128)} custom-call(s32[576]{0:T(1024)S(1)} %pad_add_fusion.meta_ref.refs_0_, bf16[2,6,64,512]{3,2,1,0:T(8,128)(2,1)S(1)} %copy-done.2, bf16[2,6,64,128]{3,2,1,0:T(8,128)(2,1)S(1)} %collective-permute-done.rim_ref.refs_2_, ...), custom_call_target="tpu_custom_call", output_to_operand_aliasing={{}: (9, {})} | custom-call | flops 1 | bytes 1 | tf_op jit(solution)/shard_map/annual_pairs/pallas_call | solution.py:602
  56.4 0.0 collective-permute-done.3.refs_7_
  56.4 2.7 %last_pairs.1 = f32[2,24,64,512]{3,2,1,0:T(8,128)} custom-call(s32[576]{0:T(1024)S(1)} %pad_add_fusion.meta_ref.refs_0_, bf16[2,6,64,512]{3,2,1,0:T(8,128)(2,1)S(1)} %copy-done.2, bf16[2,6,64,128]{3,2,1,0:T(8,128)(2,1)S(1)} %collective-permute-done.rim_ref.refs_2_, ...), custom_call_target="tpu_custom_call", output_to_operand_aliasing={{}: (9, {})} | custom-call | flops 1 | bytes 1 | tf_op jit(solution)/shard_map/last_pairs/pallas_call | solution.py:602
Async XLA Ops:
  2.8 6.2 %collective-permute-start = (bf16[2,6,64,128]{3,2,1,0:T(8,128)(2,1)}, bf16[2,6,64,128]{3,2,1,0:T(8,128)(2,1)S(1)}, u32[]{:S(2)}, u32[]{:S(2)}) collective-permute-start(bf16[2,6,64,128]{3,2,1,0:T(8,128)(2,1)} %get-tuple-element.12), channel_id=1, source_target_pairs={{0,1},{1,0},{2,3},{3,2},{4,5},{5,4},{6,7},{7,6},{8,9},{9,8},{10,11... | collective-permute-start | bytes 589832 | tf_op jit(solution)/shard_map/ppermute | solution.py:546
  3.4 48.9 %collective-permute-start.5 = (bf16[2,4,64,512]{3,2,1,0:T(8,128)(2,1)}, bf16[2,4,64,512]{3,2,1,0:T(8,128)(2,1)S(1)}, u32[]{:S(2)}, u32[]{:S(2)}) collective-permute-start(bf16[2,4,64,512]{3,2,1,0:T(8,128)(2,1)} %get-tuple-element.17), channel_id=1, source_target_pairs={{0,8},{2,10},{4,12},{6,14},{8,0},{10,2},{12,4},{14,6},{1,9},{3,11}... | collective-permute-start | bytes 1572872 | tf_op jit(solution)/shard_map/ppermute | solution.py:545
  9.0 1.1 %copy-start = (bf16[2,6,64,512]{3,2,1,0:T(8,128)(2,1)S(1)}, bf16[2,6,64,512]{3,2,1,0:T(8,128)(2,1)}, u32[]{:S(2)}) copy-start(bf16[2,6,64,512]{3,2,1,0:T(8,128)(2,1)} %refs_1_.3) | copy-start | bytes 2359300
  11.4 26.2 %collective-permute-start.6 = (bf16[400,512]{1,0:T(8,128)(2,1)S(1)}, bf16[400,512]{1,0:T(8,128)(2,1)S(1)}, u32[]{:S(2)}, u32[]{:S(2)}) collective-permute-start(bf16[400,512]{1,0:T(8,128)(2,1)S(1)} %get-tuple-element.15), channel_id=1, source_target_pairs={{6,8},{8,6},{7,9},{9,7},{22,24},{24,22},{23,25},{25,23}} | collective-permute-start | bytes 1228808 | tf_op jit(solution)/shard_map/ppermute | solution.py:561
  12.1 25.5 %collective-permute-start.2 = (bf16[400,512]{1,0:T(8,128)(2,1)S(1)}, bf16[400,512]{1,0:T(8,128)(2,1)S(1)}, u32[]{:S(2)}, u32[]{:S(2)}) collective-permute-start(bf16[400,512]{1,0:T(8,128)(2,1)S(1)} %get-tuple-element.15), channel_id=1, source_target_pairs={{6,0},{0,2},{2,4},{4,6},{10,8},{12,10},{14,12},{8,14},{7,1},{1,3},... | collective-permute-start | bytes 1228808 | tf_op jit(solution)/shard_map/ppermute | solution.py:563
  13.6 16.3 %collective-permute-start.1 = (bf16[400,512]{1,0:T(8,128)(2,1)S(1)}, bf16[400,512]{1,0:T(8,128)(2,1)S(1)}, u32[]{:S(2)}, u32[]{:S(2)}) collective-permute-start(bf16[400,512]{1,0:T(8,128)(2,1)S(1)} %get-tuple-element.14), channel_id=1, source_target_pairs={{0,6},{2,0},{4,2},{6,4},{8,10},{10,12},{12,14},{14,8},{1,7},{3,1},... | collective-permute-start | bytes 1228808 | tf_op jit(solution)/shard_map/ppermute | solution.py:562
  15.9 1.1 %copy-start.1 = (bf16[2,6,64,512]{3,2,1,0:T(8,128)(2,1)S(1)}, bf16[2,6,64,512]{3,2,1,0:T(8,128)(2,1)}, u32[]{:S(2)}) copy-start(bf16[2,6,64,512]{3,2,1,0:T(8,128)(2,1)} %refs_1_.3) | copy-start | bytes 2359300
  17.1 20.5 %copy-start.3 = (bf16[64,128]{1,0:T(8,128)(2,1)S(1)}, bf16[64,128]{1,0:T(8,128)(2,1)}, u32[]{:S(2)}) copy-start(bf16[64,128]{1,0:T(8,128)(2,1)} %get-tuple-element.16) | copy-start | bytes 49156
  17.1 20.5 %copy-start.2 = (bf16[2,6,64,512]{3,2,1,0:T(8,128)(2,1)S(1)}, bf16[2,6,64,512]{3,2,1,0:T(8,128)(2,1)}, u32[]{:S(2)}) copy-start(bf16[2,6,64,512]{3,2,1,0:T(8,128)(2,1)} %refs_1_.3) | copy-start | bytes 2359300
  30.6 25.7 %collective-permute-start.3 = (bf16[272,512]{1,0:T(8,128)(2,1)S(1)}, bf16[272,512]{1,0:T(8,128)(2,1)S(1)}, u32[]{:S(2)}, u32[]{:S(2)}) collective-permute-start(bf16[272,512]{1,0:T(8,128)(2,1)S(1)} %late_images.1), channel_id=1, source_target_pairs={{0,8},{2,10},{4,12},{6,14},{8,0},{10,2},{12,4},{14,6},{1,9},{3,11}... | collective-permute-start | bytes 835592 | tf_op jit(solution)/shard_map/ppermute | solution.py:624
  37.6 14.7 %collective-permute-start.4 = (bf16[64,128]{1,0:T(8,128)(2,1)S(1)}, bf16[64,128]{1,0:T(8,128)(2,1)S(1)}, u32[]{:S(2)}, u32[]{:S(2)}) collective-permute-start(bf16[64,128]{1,0:T(8,128)(2,1)S(1)} %copy-done.3), channel_id=1, source_target_pairs={{0,9},{1,8},{2,11},{3,10},{4,13},{5,12},{6,15},{7,14},{8,1},{9,0},... | collective-permute-start | bytes 49160 | tf_op jit(solution)/shard_map/ppermute | solution.py:547

commit v4 on v3

--- a/solution.py
+++ b/solution.py
@@ -118,7 +118,8 @@
         copy.wait()
 
 
-def late_kernel(plan, slc_ref, rim_ref, inner_ref, meta_ref, _, late_ref, tiles_ref):
+def late_kernel(plan, slc_ref, rim_ref, inner_ref, pairs_ref, *refs):
+    late_ref, tiles_ref = refs[-2:]
     me, strip = lax.axis_index("date"), lax.axis_index("strip")
     dates, late, rows = plan["dates"], plan["late"], plan["rows"]
     half = plan["devices"] // 2
@@ -127,7 +128,7 @@
     packed = read_strips(inner_ref, rows)
     for k in range(late):
         date = mate * dates + mate_slot + k
-        wanted = meta_ref[date * plan["per_date"] + NEAR] - me * dates
+        wanted = pairs_ref[1, date * plan["per_date"] + NEAR] - me * dates
         own = (wanted >= 0) & (wanted < dates)
         own_at = jnp.clip(wanted, 0, dates - 1)
         other_at = jnp.clip(jnp.where(me < half, wanted - dates, wanted + NEAR), 0, NEAR - 1)
@@ -203,8 +204,9 @@
 
 
 class Pairs:
-    def __init__(self, plan, meta_ref, slc_ref, rim_ref, bands_ref, powers_ref, out_ref, scratch):
-        self.plan, self.meta_ref = plan, meta_ref
+    def __init__(self, plan, lists, slc_ref, rim_ref, bands_ref, powers_ref, out_ref, scratch):
+        self.plan = plan
+        self.pairs_ref, self.az_ref, self.rng_ref = lists
         self.slc_ref, self.rim_ref = slc_ref, rim_ref
         self.bands_ref, self.powers_ref, self.out_ref = bands_ref, powers_ref, out_ref
         (self.left_ref, self.stack_ref, self.other_ref, self.other_rim_ref, self.stage_ref,
@@ -213,7 +215,7 @@
         self.count_ref[0] = 0
 
     def partner(self, pair):
-        return self.meta_ref[pair]
+        return self.pairs_ref[1, pair]
 
     def own_other(self, index):
         return (
@@ -262,9 +264,8 @@
             self.out_copy(stage, 0).wait()
 
         pair = (self.me * dates + slot) * per_date + kind
-        height = self.meta_ref[plan["pairs"] + pair]
-        width = self.meta_ref[2 * plan["pairs"] + pair] - REACH_LO
-        width = jnp.clip(width, 0, HALO - REACH_LO)
+        height = self.az_ref[pair]
+        width = jnp.clip(self.rng_ref[pair] - REACH_LO, 0, HALO - REACH_LO)
         part = [(pl.ds(f * rows, rows),) for f in range(4)]
         left_ref[*part[2]] = self.powers_ref[slot]
         if other_power is not None:
@@ -304,8 +305,8 @@
         self.count_ref[0] = count + 1
 
 
-def own_kernel(plan, meta_ref, slc_ref, rim_ref, bands_ref, out_ref, powers_ref, *scratch):
-    pairs = Pairs(plan, meta_ref, slc_ref, rim_ref, bands_ref, powers_ref, out_ref, scratch)
+def own_kernel(plan, lists, slc_ref, rim_ref, bands_ref, out_ref, powers_ref, *scratch):
+    pairs = Pairs(plan, lists, slc_ref, rim_ref, bands_ref, powers_ref, out_ref, scratch)
     dates = plan["dates"]
 
     def power(slot, carry):
@@ -331,9 +332,9 @@
     pairs.finish()
 
 
-def rest_kernel(plan, meta_ref, slc_ref, rim_ref, bands_ref, powers_ref, inner_ref, outer_ref,
+def rest_kernel(plan, lists, slc_ref, rim_ref, bands_ref, powers_ref, inner_ref, outer_ref,
                 middle_ref, _, out_ref, *scratch):
-    pairs = Pairs(plan, meta_ref, slc_ref, rim_ref, bands_ref, powers_ref, out_ref, scratch)
+    pairs = Pairs(plan, lists, slc_ref, rim_ref, bands_ref, powers_ref, out_ref, scratch)
     dates, half = plan["dates"], plan["devices"] // 2
     upper = pairs.me >= half
     if plan["halves"]:
@@ -365,13 +366,14 @@
     pairs.finish()
 
 
-def annual_kernel(plan, is_late, meta_ref, slc_ref, rim_ref, bands_ref, powers_ref, inner_ref,
+def annual_kernel(plan, is_late, lists, slc_ref, rim_ref, bands_ref, powers_ref, inner_ref,
                   outer_ref, images_ref, strips_ref, _, out_ref, *scratch):
-    pairs = Pairs(plan, meta_ref, slc_ref, rim_ref, bands_ref, powers_ref, out_ref, scratch)
+    pairs = Pairs(plan, lists, slc_ref, rim_ref, bands_ref, powers_ref, out_ref, scratch)
     dates, late, rows = plan["dates"], plan["late"], plan["rows"]
     half = plan["devices"] // 2
     me, split_date = pairs.me, half * dates
     lower = me < half
+    mate = jnp.where(lower, 1, 0)
     if is_late:
         base, count = jnp.where(lower, 0, dates - late), late
     else:
@@ -380,7 +382,7 @@
     def fetch_early(k):
         packed = strips_ref[...]
         for c in range(2):
-            pairs.other_ref[c] = images_ref[c, k]
+            pairs.other_ref[c] = images_ref[mate, c, k]
             pairs.other_rim_ref[c] = place_strip(packed, 2 * k + c, pairs.strip)
 
     def step(k, carry):
@@ -403,7 +405,7 @@
         @pl.when(jnp.logical_not(far))
         def _():
             if is_late:
-                pairs.fetch_payload(images_ref, k)
+                pairs.fetch_payload(images_ref.at[mate], k)
             else:
                 fetch_early(k)
 
@@ -414,9 +416,9 @@
     pairs.finish()
 
 
-def plain_kernel(plan, meta_ref, slc_ref, rim_ref, bands_ref, powers_ref, images_ref,
+def plain_kernel(plan, lists, slc_ref, rim_ref, bands_ref, powers_ref, images_ref,
                  image_rim_ref, _, out_ref, *scratch):
-    pairs = Pairs(plan, meta_ref, slc_ref, rim_ref, bands_ref, powers_ref, out_ref, scratch)
+    pairs = Pairs(plan, lists, slc_ref, rim_ref, bands_ref, powers_ref, out_ref, scratch)
 
     def step(slot, carry):
         other = (
@@ -492,7 +494,7 @@
     }
     dtype = slc.dtype
     rim_rows = rows * TILE // cols
-    meta = jnp.concatenate([pair_list[:, 1], az_half, rng_half])
+    lists = (pair_list.T, az_half, rng_half)
     swap_strips = [(0, 1), (1, 0)]
 
     def images(count):
@@ -529,6 +531,7 @@
     )()
     if halves:
         swap = [(i, (i + half) % devices) for i in range(devices)]
+        mates = [[i, i + half] for i in range(half)]
         early, strips, rim = pl.pallas_call(
             functools.partial(early_kernel, plan),
             out_shape=(
@@ -541,8 +544,8 @@
             scratch_shapes=[pltpu.SemaphoreType.DMA((dates - late + 1,))],
             compiler_params=limit(56),
             name="early_images",
-        )(slc, pair_list.T)
-        early = lax.ppermute(early, "date", swap)
+        )(slc, lists[0])
+        early = lax.all_gather(early, "date", axis_index_groups=mates)
         rim = lax.ppermute(rim, "strip", swap_strips)
         strips = lax.ppermute(
             strips, ("date", "strip"), [(2 * a + s, 2 * b + 1 - s) for a, b in swap for s in (0, 1)]
@@ -553,7 +556,7 @@
             in_specs=[ANY, VMEM],
             out_specs=(VMEM, VMEM),
             scratch_shapes=[pltpu.SemaphoreType.DMA((2, NEAR, 2))],
-            compiler_params=limit(4),
+            compiler_params=limit(56),
             name="beside_images",
         )(slc, rim)
         down = [(i, (i - 1) % half) for i in range(half)]
@@ -588,40 +591,40 @@
         return pl.CostEstimate(flops=flops, bytes_accessed=1, transcendentals=0)
 
     out, powers = pl.pallas_call(
-        functools.partial(own_kernel, plan),
+        lambda *refs: own_kernel(plan, refs[:3], *refs[3:]),
         out_shape=(out_shape, jax.ShapeDtypeStruct((dates, rows, depth), jnp.bfloat16)),
-        in_specs=[SMEM, VMEM, VMEM, VMEM],
+        in_specs=[SMEM] * 3 + [VMEM] * 3,
         out_specs=(ANY, VMEM),
         scratch_shapes=scratch,
         compiler_params=limit(24),
         cost_estimate=cost(20_000_000_000),
         name="own_pairs",
-    )(meta, slc, rim, bands)
+    )(*lists, slc, rim, bands)
 
     def more_pairs(kernel, out, others, name):
         return pl.pallas_call(
-            functools.partial(kernel, plan),
+            lambda *refs: kernel(plan, refs[:3], *refs[3:]),
             out_shape=out_shape,
-            in_specs=[SMEM] + [VMEM] * (4 + len(others)) + [ANY],
+            in_specs=[SMEM] * 3 + [VMEM] * (4 + len(others)) + [ANY],
             out_specs=ANY,
             scratch_shapes=scratch,
-            input_output_aliases={5 + len(others): 0},
+            input_output_aliases={7 + len(others): 0},
             compiler_params=limit(24),
             cost_estimate=cost(1),
             name=name,
-        )(meta, slc, rim, bands, powers, *others, out)
+        )(*lists, slc, rim, bands, powers, *others, out)
 
     if halves:
         payload = pl.pallas_call(
             functools.partial(late_kernel, plan),
             out_shape=payload_shape(late),
-            in_specs=[VMEM, VMEM, VMEM, SMEM, ANY],
+            in_specs=[VMEM, VMEM, VMEM, SMEM, ANY, ANY],
             out_specs=VMEM,
             scratch_shapes=[pltpu.VMEM((late, planes, rows, TILE), dtype)],
             compiler_params=limit(4),
             name="late_images",
-        )(slc, rim, inner, meta, powers)
-        payload = lax.ppermute(payload, "date", swap)
+        )(slc, rim, inner, lists[0], powers, strips)
+        payload = lax.all_gather(payload, "date", axis_index_groups=mates)
     out = more_pairs(rest_kernel, out, (inner, outer, middle), "near_pairs")
     if halves:
         kernel = lambda plan, *refs: annual_kernel(plan, False, *refs)

time: 59.7 us -> 94.5 us (1.58); the launches traced: 59.1 us -> 92.9 us
  blocking collectives: 0 us -> 27.9 us
  between operations: 0.1 us -> 13.6 us
  waiting for transfers between devices: 12.3 us -> 0.2 us
  local copies, waits for them, and re-layouts: 2.96 us -> 10.2 us
  starting transfers between devices: 15.6 us -> 11.3 us
  Pallas kernels: 27.3 us -> 29.7 us
    all_gather x0 -> x1, blocking collectives: none -> 27.9 us  [body(): payload = lax.all_gather(payload, 'date', axis_index_groups=mates)]
    ppermute x1, waiting for transfers between devices: 10.7 us -> 0.01 us  [body(): lax.ppermute(strips, ('date', 'strip'), [(2 * a + s, 2 * b + 1 - s) for a...]
    ppermute x2 -> x0, starting transfers between devices: 10.6 us -> none  [the longest x1 6.92 us: body(): payload = lax.ppermute(payload, 'date', swap)]
    unnamed x8 -> x34, local copies, waits for them, and re-layouts: 2.27 us -> 10.2 us
    ppermute x1, starting transfers between devices: 0.01 us -> 3.71 us  [body(): lax.ppermute(strips, ('date', 'strip'), [(2 * a + s, 2 * b + 1 - s) for a...]
    ppermute x1, starting transfers between devices: 2.31 us -> 4.83 us  [body(): inner = lax.ppermute(inner, 'date', down)]
    pallas_call x1, Pallas kernels: 1.24 us -> 3.33 us  [body(): pl.pallas_call(functools.partial(beside_kernel, plan), out_shape=(payload...]
    ppermute x1, waiting for transfers between devices: 1.6 us -> 0.17 us  [body(): inner = lax.ppermute(inner, 'date', down)]
  transfers between devices with their start and end apart: 7 -> 6, of which waited for: 2 -> 1; matrix products, arithmetic and copies ran while one was open for 2% -> 0% of each run, Pallas kernels for 37% -> 22%
where the time goes in v4:
time: 94.5 us; the launch traced here: 92.9 us
  Pallas kernels  29.7 us (31%)
  blocking collectives  27.9 us (30%)
  between operations  13.6 us (14%)
  starting transfers between devices  11.3 us (12%)
  local copies, waits for them, and re-layouts  10.2 us (11%)
    all_gather x1, blocking collectives, body(): payload = lax.all_gather(payload, 'date', axis_index_groups=mates)  27.9 us
    pallas_call x1, Pallas kernels, body(): pl.pallas_call(lambda *refs: own_kernel(plan, refs[:3], *refs[3:]), out_s...  11.2 us
    pallas_call x3, Pallas kernels, more_pairs(): pl.pallas_call(lambda *refs: kernel(plan, refs[:3], *refs[3:]), out_shape...  10.8 us
    unnamed x34, local copies, waits for them, and re-layouts  10.2 us
    ppermute x1, starting transfers between devices, body(): inner = lax.ppermute(inner, 'date', down)  4.83 us
    ppermute x1, starting transfers between devices, body(): lax.ppermute(strips, ('date', 'strip'), [(2 * a + s, 2 * b + 1 - s) for a...  3.71 us
    pallas_call x1, Pallas kernels, body(): pl.pallas_call(functools.partial(beside_kernel, plan), out_shape=(payload...  3.33 us
    pallas_call x1, Pallas kernels, body(): pl.pallas_call(functools.partial(early_kernel, plan), out_shape=(images(d...  2.83 us
  transfers between devices with their start and end apart: 6, of which 1 were waited for; matrix products, arithmetic and copies ran while one was open for 0% of the time, Pallas kernels for 22%

profile of v4, /device:TPU:0, one launch (start us, length us, event | category | flops | bytes accessed | tf_op | source)
XLA Modules:
  0.0 92.9 jit_solution(12417934160216389890)
XLA Ops:
  6.5 0.0 all-gather.4.cloned.1.call-start
  6.5 2.8 %early_images.1 = (bf16[2,4,64,512]{3,2,1,0:T(8,128)(2,1)}, bf16[64,128]{1,0:T(8,128)(2,1)}, bf16[2,6,64,128]{3,2,1,0:T(8,128)(2,1)}) custom-call(bf16[2,6,64,512]{3,2,1,0:T(8,128)(2,1)} %refs_3_.7, s32[2,192]{1,0:T(2,128)} %bitcast.5), custom_call_target="tpu_custom_call" | custom-call | tf_op jit(solution)/shard_map/early_images/pallas_call | solution.py:535
  9.4 0.5 collective-permute-start
  9.9 3.7 %collective-permute-start.3 = (bf16[64,128]{1,0:T(8,128)(2,1)}, bf16[64,128]{1,0:T(8,128)(2,1)S(1)}, u32[]{:S(2)}, u32[]{:S(2)}) collective-permute-start(bf16[64,128]{1,0:T(8,128)(2,1)} %get-tuple-element.16), channel_id=1, source_target_pairs={{0,9},{1,8},{2,11},{3,10},{4,13},{5,12},{6,15},{7,14},{8,1},{9,0},... | collective-permute-start | bytes 49160 | tf_op jit(solution)/shard_map/ppermute | solution.py:550
  13.6 0.0 all-gather.4.cloned.1.call-update
  13.6 0.5 range_bands.1.refs_5_
  14.2 0.0 copy-start
  14.2 0.0 collective-permute-done.refs_4_.rim_ref
  14.2 0.0 copy-start.4
  14.2 0.7 copy-done.4
  14.9 3.3 %beside_images.1 = (bf16[400,512]{1,0:T(8,128)(2,1)}, bf16[400,512]{1,0:T(8,128)(2,1)}) custom-call(bf16[2,6,64,512]{3,2,1,0:T(8,128)(2,1)} %refs_3_.7, bf16[2,6,64,128]{3,2,1,0:T(8,128)(2,1)} %copy-done.4), custom_call_target="tpu_custom_call" | custom-call | tf_op jit(solution)/shard_map/beside_images/pallas_call | solution.py:553
  18.3 1.5 %collective-permute-start.2 = (bf16[400,512]{1,0:T(8,128)(2,1)}, bf16[400,512]{1,0:T(8,128)(2,1)S(1)}, u32[]{:S(2)}, u32[]{:S(2)}) collective-permute-start(bf16[400,512]{1,0:T(8,128)(2,1)} %get-tuple-element.15), channel_id=1, source_target_pairs={{6,0},{0,2},{2,4},{4,6},{10,8},{12,10},{14,12},{8,14},{7,1},{1,3},... | collective-permute-start | bytes 1228808 | tf_op jit(solution)/shard_map/ppermute | solution.py:566
  19.8 0.7 collective-permute-start.4
  20.5 4.8 %collective-permute-start.1 = (bf16[400,512]{1,0:T(8,128)(2,1)}, bf16[400,512]{1,0:T(8,128)(2,1)S(1)}, u32[]{:S(2)}, u32[]{:S(2)}) collective-permute-start(bf16[400,512]{1,0:T(8,128)(2,1)} %get-tuple-element.14), channel_id=1, source_target_pairs={{0,6},{2,0},{4,2},{6,4},{8,10},{10,12},{12,14},{14,8},{1,7},{3,1},... | collective-permute-start | bytes 1228808 | tf_op jit(solution)/shard_map/ppermute | solution.py:565
  25.3 0.0 copy-start.2
  25.3 1.1 %copy-done.2 = bf16[2,6,64,512]{3,2,1,0:T(8,128)(2,1)S(1)} copy-done((bf16[2,6,64,512]{3,2,1,0:T(8,128)(2,1)S(1)}, bf16[2,6,64,512]{3,2,1,0:T(8,128)(2,1)}, u32[]{:S(2)}) %copy-start.2) | copy-done | bytes 786456
  26.4 0.0 copy-start.5
  26.4 0.9 copy-done.5
  27.4 0.0 copy-start.8
  27.4 0.7 copy-done.8
  28.1 0.0 copy-start.11
  28.1 0.7 copy-done.11
  28.7 0.0 copy-start.14
  28.7 0.7 copy-done.14
  29.4 0.0 copy-start.9
  29.4 0.0 copy-start.12
  29.4 0.0 copy-start.15
  29.4 11.2 %own_pairs.1 = (f32[2,24,64,512]{3,2,1,0:T(8,128)}, bf16[6,64,1536]{2,1,0:T(8,128)(2,1)S(1)}) custom-call(s32[2,192]{1,0:T(2,128)S(1)} %bitcast.6, s32[192]{0:T(256)S(1)} %copy-done.11, s32[192]{0:T(256)S(1)} %copy-done.14, bf16[2,6,64,512]{3,2,1,0:T(8,128)(2,1)S(1)} %copy-done.2, bf16[2,6,64,128]{3,2,1,0:T(8,128)(2,1)S(1)} %copy-done.5, ...), custom_call_target="tpu_custom_call" | custom-call | flops 20000000000 | bytes 1 | tf_op jit(solution)/shard_map/own_pairs/pallas_call | solution.py:593
  40.7 0.2 collective-permute-done.1.inner_ref.refs_7_
  40.8 0.0 collective-permute-done.2.refs_8_
  40.8 0.0 collective-permute-done.4.refs_9_
  40.8 0.0 copy-done
  40.8 0.0 copy-done.9
  40.9 0.0 copy-done.12
  40.9 0.0 copy-done.15
  40.9 0.0 copy-start.3
  40.9 0.0 copy-start.6
  40.9 3.9 %near_pairs.1.refs_11_ = f32[2,24,64,512]{3,2,1,0:T(8,128)} custom-call(s32[2,192]{1,0:T(2,128)S(1)} %bitcast.7, s32[192]{0:T(256)S(1)} %copy-done.12, s32[192]{0:T(256)S(1)} %copy-done.15, bf16[2,6,64,512]{3,2,1,0:T(8,128)(2,1)S(1)} %copy-done.2, bf16[2,6,64,128]{3,2,1,0:T(8,128)(2,1)S(1)} %copy-done.5, ...), custom_call_target="tpu_custom_call", output_to_operand_aliasing={{}: (10, {})} | custom-call | flops 1 | bytes 1 | tf_op jit(solution)/shard_map/near_pairs/pallas_call | solution.py:605
  44.8 0.0 collective-permute-done.3.refs_1_.refs_10_
  44.8 1.0 %late_images.1 = bf16[272,512]{1,0:T(8,128)(2,1)S(1)} custom-call(bf16[2,6,64,512]{3,2,1,0:T(8,128)(2,1)S(1)} %copy-done.2, bf16[2,6,64,128]{3,2,1,0:T(8,128)(2,1)S(1)} %copy-done.5, bf16[400,512]{1,0:T(8,128)(2,1)S(1)} %collective-permute-done.1.inner_ref.refs_7_, s32[2,192]{1,0:T(2,128)S(1)} %bitcast.8, ...), custom_call_target="tpu_custom_call" | custom-call | tf_op jit(solution)/shard_map/late_images/pallas_call | solution.py:618
  45.8 27.9 %all-gather = bf16[544,512]{1,0:T(8,128)(2,1)S(1)} all-gather(bf16[272,512]{1,0:T(8,128)(2,1)S(1)} %late_images.1), channel_id=2, replica_groups={{0,8},{2,10},{4,12},{6,14},{1,9},{3,11},{5,13},{7,15},{16,24},{18,26},{..., dimensions={0}, use_global_device_ids=true | all-gather | bytes 835584 | tf_op jit(solution)/shard_map/all_gather | solution.py:627
  73.7 0.0 all-gather.4.cloned.1.call-done
  73.7 0.0 copy-done.3
  73.7 0.0 copy-done.6
  73.7 0.0 copy-start.1
  73.8 2.1 %copy-done.1 = bf16[5,2,768,256]{3,2,1,0:T(8,128)(2,1)S(1)} copy-done((bf16[5,2,768,256]{3,2,1,0:T(8,128)(2,1)S(1)}, bf16[5,2,768,256]{3,2,1,0:T(8,128)(2,1)}, u32[]{:S(2)}) %copy-start.1) | copy-done | bytes 3932184
  75.9 0.0 copy-start.7
  75.9 1.2 %copy-done.7 = bf16[4,4,64,512]{3,2,1,0:T(8,128)(2,1)S(1)} copy-done((bf16[4,4,64,512]{3,2,1,0:T(8,128)(2,1)S(1)}, bf16[4,4,64,512]{3,2,1,0:T(8,128)(2,1)}, u32[]{:S(2)}) %copy-start.7) | copy-done | bytes 1048600
  77.1 0.0 copy-start.10
  77.1 0.7 copy-done.10
  77.8 0.0 copy-start.13
  77.8 0.7 copy-done.13
  78.5 0.0 copy-start.16
  78.5 0.7 copy-done.16
  79.1 4.2 %annual_pairs.1.refs_11_ = f32[2,24,64,512]{3,2,1,0:T(8,128)} custom-call(s32[2,192]{1,0:T(2,128)S(1)} %bitcast.9, s32[192]{0:T(256)S(1)} %copy-done.13, s32[192]{0:T(256)S(1)} %copy-done.16, bf16[2,6,64,512]{3,2,1,0:T(8,128)(2,1)S(1)} %copy-done.3, bf16[2,6,64,128]{3,2,1,0:T(8,128)(2,1)S(1)} %copy-done.6, ...), custom_call_target="tpu_custom_call", output_to_operand_aliasing={{}: (11, {})} | custom-call | flops 1 | bytes 1 | tf_op jit(solution)/shard_map/annual_pairs/pallas_call | solution.py:605
  83.3 2.8 %last_pairs.1 = f32[2,24,64,512]{3,2,1,0:T(8,128)} custom-call(s32[2,192]{1,0:T(2,128)S(1)} %bitcast.10, s32[192]{0:T(256)S(1)} %copy-done.13, s32[192]{0:T(256)S(1)} %copy-done.16, bf16[2,6,64,512]{3,2,1,0:T(8,128)(2,1)S(1)} %copy-done.3, bf16[2,6,64,128]{3,2,1,0:T(8,128)(2,1)S(1)} %copy-done.6, ...), custom_call_target="tpu_custom_call", output_to_operand_aliasing={{}: (11, {})} | custom-call | flops 1 | bytes 1 | tf_op jit(solution)/shard_map/last_pairs/pallas_call | solution.py:605
Async XLA Ops:
  6.5 67.2 %all-gather.4.cloned.1.call-start = ((), (), s32[]{:S(2)}) async-start(), calls=%async_computation | async-start | bytes 1572864 | tf_op jit(solution)/shard_map/all_gather | solution.py:548
  9.4 4.8 %collective-permute-start = (bf16[2,6,64,128]{3,2,1,0:T(8,128)(2,1)}, bf16[2,6,64,128]{3,2,1,0:T(8,128)(2,1)S(1)}, u32[]{:S(2)}, u32[]{:S(2)}) collective-permute-start(bf16[2,6,64,128]{3,2,1,0:T(8,128)(2,1)} %get-tuple-element.12), channel_id=1, source_target_pairs={{0,1},{1,0},{2,3},{3,2},{4,5},{5,4},{6,7},{7,6},{8,9},{9,8},{10,11... | collective-permute-start | bytes 589832 | tf_op jit(solution)/shard_map/ppermute | solution.py:549
  9.9 34.9 %collective-permute-start.3 = (bf16[64,128]{1,0:T(8,128)(2,1)}, bf16[64,128]{1,0:T(8,128)(2,1)S(1)}, u32[]{:S(2)}, u32[]{:S(2)}) collective-permute-start(bf16[64,128]{1,0:T(8,128)(2,1)} %get-tuple-element.16), channel_id=1, source_target_pairs={{0,9},{1,8},{2,11},{3,10},{4,13},{5,12},{6,15},{7,14},{8,1},{9,0},... | collective-permute-start | bytes 49160 | tf_op jit(solution)/shard_map/ppermute | solution.py:550
  14.2 26.7 %copy-start = (bf16[5,2,768,256]{3,2,1,0:T(8,128)(2,1)}, bf16[5,2,768,256]{3,2,1,0:T(8,128)(2,1)S(1)}, u32[]{:S(2)}) copy-start(bf16[5,2,768,256]{3,2,1,0:T(8,128)(2,1)S(1)} %range_bands.1.refs_5_) | copy-start | bytes 11796484
  14.2 0.7 copy-start.4
  18.3 22.6 %collective-permute-start.2 = (bf16[400,512]{1,0:T(8,128)(2,1)}, bf16[400,512]{1,0:T(8,128)(2,1)S(1)}, u32[]{:S(2)}, u32[]{:S(2)}) collective-permute-start(bf16[400,512]{1,0:T(8,128)(2,1)} %get-tuple-element.15), channel_id=1, source_target_pairs={{6,0},{0,2},{2,4},{4,6},{10,8},{12,10},{14,12},{8,14},{7,1},{1,3},... | collective-permute-start | bytes 1228808 | tf_op jit(solution)/shard_map/ppermute | solution.py:566
  19.8 21.0 %collective-permute-start.4 = (bf16[400,512]{1,0:T(8,128)(2,1)}, bf16[400,512]{1,0:T(8,128)(2,1)S(1)}, u32[]{:S(2)}, u32[]{:S(2)}) collective-permute-start(bf16[400,512]{1,0:T(8,128)(2,1)} %get-tuple-element.15), channel_id=1, source_target_pairs={{6,8},{8,6},{7,9},{9,7},{22,24},{24,22},{23,25},{25,23}} | collective-permute-start | bytes 1228808 | tf_op jit(solution)/shard_map/ppermute | solution.py:564
  20.5 20.3 %collective-permute-start.1 = (bf16[400,512]{1,0:T(8,128)(2,1)}, bf16[400,512]{1,0:T(8,128)(2,1)S(1)}, u32[]{:S(2)}, u32[]{:S(2)}) collective-permute-start(bf16[400,512]{1,0:T(8,128)(2,1)} %get-tuple-element.14), channel_id=1, source_target_pairs={{0,6},{2,0},{4,2},{6,4},{8,10},{10,12},{12,14},{14,8},{1,7},{3,1},... | collective-permute-start | bytes 1228808 | tf_op jit(solution)/shard_map/ppermute | solution.py:565
  25.3 1.1 %copy-start.2 = (bf16[2,6,64,512]{3,2,1,0:T(8,128)(2,1)S(1)}, bf16[2,6,64,512]{3,2,1,0:T(8,128)(2,1)}, u32[]{:S(2)}) copy-start(bf16[2,6,64,512]{3,2,1,0:T(8,128)(2,1)} %refs_3_.7) | copy-start | bytes 2359300
  26.4 0.9 copy-start.5
  27.4 0.7 copy-start.8
  28.1 0.7 copy-start.11
  28.7 0.7 copy-start.14
  29.4 11.4 %copy-start.9 = (s32[192,2]{0,1:T(2,128)S(1)}, s32[192,2]{0,1:T(2,128)}, u32[]{:S(2)}) copy-start(s32[192,2]{0,1:T(2,128)} %param.5) | copy-start | bytes 4612
  29.4 11.4 %copy-start.12 = (s32[192]{0:T(256)S(1)}, s32[192]{0:T(256)}, u32[]{:S(2)}) copy-start(s32[192]{0:T(256)} %refs_1_.7) | copy-start | bytes 2308
  29.4 11.4 %copy-start.15 = (s32[192]{0:T(256)S(1)}, s32[192]{0:T(256)}, u32[]{:S(2)}) copy-start(s32[192]{0:T(256)} %refs_2_.7) | copy-start | bytes 2308
  40.9 32.9 %copy-start.3 = (bf16[2,6,64,512]{3,2,1,0:T(8,128)(2,1)S(1)}, bf16[2,6,64,512]{3,2,1,0:T(8,128)(2,1)}, u32[]{:S(2)}) copy-start(bf16[2,6,64,512]{3,2,1,0:T(8,128)(2,1)} %refs_3_.7) | copy-start | bytes 2359300
  40.9 32.9 %copy-start.6 = (bf16[2,6,64,128]{3,2,1,0:T(8,128)(2,1)S(1)}, bf16[2,6,64,128]{3,2,1,0:T(8,128)(2,1)}, u32[]{:S(2)}) copy-start(bf16[2,6,64,128]{3,2,1,0:T(8,128)(2,1)} %copy-done.4) | copy-start | bytes 589828
  73.7 2.1 %copy-start.1 = (bf16[5,2,768,256]{3,2,1,0:T(8,128)(2,1)S(1)}, bf16[5,2,768,256]{3,2,1,0:T(8,128)(2,1)}, u32[]{:S(2)}) copy-start(bf16[5,2,768,256]{3,2,1,0:T(8,128)(2,1)} %copy-done) | copy-start | bytes 11796484
  75.9 1.2 %copy-start.7 = (bf16[4,4,64,512]{3,2,1,0:T(8,128)(2,1)S(1)}, bf16[4,4,64,512]{3,2,1,0:T(8,128)(2,1)}, u32[]{:S(2)}) copy-start(bf16[4,4,64,512]{3,2,1,0:T(8,128)(2,1)} %all-gather.4.cloned.1.call-done) | copy-start | bytes 3145732
  77.1 0.7 copy-start.10
  77.8 0.7 copy-start.13
  78.5 0.7 copy-start.16
Sparse Core Ops, SparseCore 0:
  13.8 41.4 all-gather.3

commit v5 on v4

--- a/solution.py
+++ b/solution.py
@@ -14,6 +14,8 @@
 EPSILON = 1e-06
 TILE = 128
 INNER = TILE // 2
+WORK_MIB = 16
+FIRST_MIB = 56
 ANY = pl.BlockSpec(memory_space=pl.ANY)
 SMEM = pl.BlockSpec(memory_space=pltpu.SMEM)
 VMEM = pl.BlockSpec(memory_space=pltpu.VMEM)
@@ -61,32 +63,56 @@
     )
 
 
-def early_kernel(plan, slc_ref, pairs_ref, early_ref, strips_ref, rim_ref, sems):
-    me, strip = lax.axis_index("date"), lax.axis_index("strip")
-    dates, late, cols = plan["dates"], plan["late"], plan["cols"]
-    half = plan["devices"] // 2
+def wanted_images(plan, pairs_ref):
+    me = lax.axis_index("date")
+    dates, half = plan["dates"], plan["devices"] // 2
     mate = lax.rem(me + half, 2 * half)
-    mate_slot = jnp.where(mate < half, late, 0)
+    wanted = []
+    for k in range(dates - plan["late"]):
+        date = mate * dates + jnp.where(mate < half, plan["late"], 0) + k
+        at = pairs_ref[1, date * plan["per_date"] + NEAR] - me * dates
+        wanted.append(jnp.clip(at, 0, dates - 1))
+    return wanted
+
+
+def image_copies(slc_ref, wanted, early_ref, sems):
+    return [
+        pltpu.make_async_copy(slc_ref.at[:, at], early_ref.at[:, k], sems.at[k])
+        for k, at in enumerate(wanted)
+    ]
+
+
+def early_kernel(plan, slc_ref, pairs_ref, early_ref, rim_ref, strips_ref, tiles_ref, sems,
+                 tile_sems, rim_sem):
+    strip, cols = lax.axis_index("strip"), plan["cols"]
     start = pl.multiple_of(jnp.where(strip == 0, cols - TILE, 0), TILE)
-    copies = [
+    wanted = wanted_images(plan, pairs_ref)
+    rim_copy = pltpu.make_async_copy(slc_ref.at[:, :, :, pl.ds(start, TILE)], rim_ref, rim_sem)
+    early_copies = image_copies(slc_ref, wanted, early_ref, sems)
+    tile_copies = [
         pltpu.make_async_copy(
-            slc_ref.at[:, :, :, pl.ds(start, TILE)], rim_ref, sems.at[dates - late]
+            slc_ref.at[:, at, :, pl.ds(start, TILE)], tiles_ref.at[k], tile_sems.at[k]
         )
+        for k, at in enumerate(wanted)
     ]
-    for k in range(dates - late):
-        date = mate * dates + mate_slot + k
-        wanted = pairs_ref[1, date * plan["per_date"] + NEAR] - me * dates
-        wanted = jnp.clip(wanted, 0, dates - 1)
-        copies.append(
-            pltpu.make_async_copy(slc_ref.at[:, wanted], early_ref.at[:, k], sems.at[k])
-        )
-    run_copies(copies)
-    tiles = []
-    for k in range(dates - late):
-        for c in range(2):
-            left, right = early_ref[c, k, :, :TILE], early_ref[c, k, :, cols - TILE :]
-            tiles.append(jnp.where(strip == 1, left, right))
+    for copy in tile_copies + [rim_copy]:
+        copy.start()
+
+    @pl.when(strip == 0)
+    def _():
+        for copy in early_copies:
+            copy.start()
+
+    for copy in tile_copies:
+        copy.wait()
+    tiles = [tiles_ref[k, c] for k in range(len(wanted)) for c in range(2)]
     strips_ref[...] = gather_strips(tiles, 1 - strip)
+    rim_copy.wait()
+
+    @pl.when(strip == 0)
+    def _():
+        for copy in early_copies:
+            copy.wait()
 
 
 def rim_kernel(slc_ref, rim_ref, sem):
@@ -95,7 +121,8 @@
     run_copies([pltpu.make_async_copy(slc_ref.at[:, :, :, pl.ds(start, TILE)], rim_ref, sem)])
 
 
-def beside_kernel(plan, slc_ref, rim_ref, inner_ref, outer_ref, sems):
+def beside_kernel(plan, slc_ref, pairs_ref, rim_ref, inner_ref, outer_ref, early_ref, sems,
+                  early_sems):
     me, strip = lax.axis_index("date"), lax.axis_index("strip")
     dates, rows = plan["dates"], plan["rows"]
     upper = me >= plan["devices"] // 2
@@ -111,11 +138,25 @@
                 )
     for copy in copies:
         copy.start()
+    early_copies = image_copies(
+        slc_ref, wanted_images(plan, pairs_ref), early_ref, early_sems
+    )
+
+    @pl.when(strip == 1)
+    def _():
+        for copy in early_copies:
+            copy.start()
+
     for out_ref, first in zip((inner_ref, outer_ref), firsts):
         tiles = [rim_ref[c, first + k] for k in range(NEAR) for c in range(2)]
         write_strips(out_ref, gather_strips(tiles, strip))
     for copy in copies:
         copy.wait()
+
+    @pl.when(strip == 1)
+    def _():
+        for copy in early_copies:
+            copy.wait()
 
 
 def late_kernel(plan, slc_ref, rim_ref, inner_ref, pairs_ref, *refs):
@@ -210,12 +251,26 @@
         self.slc_ref, self.rim_ref = slc_ref, rim_ref
         self.bands_ref, self.powers_ref, self.out_ref = bands_ref, powers_ref, out_ref
         (self.left_ref, self.stack_ref, self.other_ref, self.other_rim_ref, self.stage_ref,
-         self.count_ref, self.sems) = scratch
+         self.list_ref, self.sems) = scratch
         self.me, self.strip = lax.axis_index("date"), lax.axis_index("strip")
-        self.count_ref[0] = 0
 
     def partner(self, pair):
         return self.pairs_ref[1, pair]
+
+    def near_item(self, n):
+        slot, kind = n // NEAR, lax.rem(n, NEAR)
+        dates = self.plan["dates"]
+        pair = (self.me * dates + slot) * self.plan["per_date"] + kind
+        return slot, kind, self.partner(pair) - self.me * dates
+
+    def near_list(self, own):
+        count = 0
+        for n in range(self.plan["dates"] * NEAR):
+            local = self.near_item(n)[2]
+            inside = (local >= 0) & (local < self.plan["dates"])
+            self.list_ref[count] = n
+            count = count + jnp.where(inside == own, 1, 0)
+        return count
 
     def own_other(self, index):
         return (
@@ -223,86 +278,98 @@
             lambda c: self.rim_ref[c, index],
         )
 
-    def fetched_other(self):
+    def fetched_other(self, x):
         return (
-            lambda c, cols: self.other_ref[c, :, cols],
-            lambda c: self.other_rim_ref[c],
+            lambda c, cols: self.other_ref[x, c, :, cols],
+            lambda c: self.other_rim_ref[x, c],
         )
 
-    def fetch_payload(self, ref, index):
+    def fetch_payload(self, x, ref, index):
         rows = self.plan["rows"]
         packed = read_strips(ref, rows)
         for c in range(2):
             at = pl.multiple_of((2 * index + c) * rows, rows)
-            self.other_ref[c] = ref[pl.ds(at, rows)]
-            self.other_rim_ref[c] = place_strip(packed, 2 * index + c, self.strip)
-
-    def out_copy(self, slot, pair):
+            self.other_ref[x, c] = ref[pl.ds(at, rows)]
+            self.other_rim_ref[x, c] = place_strip(packed, 2 * index + c, self.strip)
+
+    def out_copy(self, stage, x, pair):
         return pltpu.make_async_copy(
-            self.stage_ref.at[slot], self.out_ref.at[:, pair], self.sems.at[slot]
+            self.stage_ref.at[stage, x], self.out_ref.at[:, pair], self.sems.at[stage, x]
         )
 
-    def finish(self):
-        count = self.count_ref[0]
-
-        @pl.when(count >= 1)
-        def _():
-            self.out_copy(lax.rem(count + 1, 2), 0).wait()
-
-        @pl.when(count >= 2)
-        def _():
-            self.out_copy(lax.rem(count, 2), 0).wait()
-
-    def run(self, slot, kind, other, other_power=None):
-        plan, left_ref, stack_ref = self.plan, self.left_ref, self.stack_ref
+    def run(self, count, work):
+        steps = (count + 1) // 2
+
+        def step(n, carry):
+            stage = lax.rem(n, 2)
+
+            @pl.when(n >= 2)
+            def _():
+                for x in range(2):
+                    self.out_copy(stage, x, 0).wait()
+
+            items = [work(x, jnp.minimum(2 * n + x, count - 1)) for x in range(2)]
+            self.compute(stage, items)
+            for x, (slot, kind, _, _) in enumerate(items):
+                copy = self.out_copy(stage, x, slot * self.plan["per_date"] + kind)
+                pl.when(2 * n + x < count)(copy.start)
+            return carry
+
+        lax.fori_loop(0, steps, step, 0)
+        for back in (2, 1):
+            for x in range(2):
+                used = (steps >= back) & (2 * (steps - back) + x < count)
+                pl.when(used)(self.out_copy(lax.rem(steps + back, 2), x, 0).wait)
+
+    def compute(self, stage, items):
+        plan = self.plan
         rows, dates, per_date = plan["rows"], plan["dates"], plan["per_date"]
-        count = self.count_ref[0]
-        stage = lax.rem(count, 2)
-
-        @pl.when(count >= 2)
-        def _():
-            self.out_copy(stage, 0).wait()
-
-        pair = (self.me * dates + slot) * per_date + kind
-        height = self.az_ref[pair]
-        width = jnp.clip(self.rng_ref[pair] - REACH_LO, 0, HALO - REACH_LO)
         part = [(pl.ds(f * rows, rows),) for f in range(4)]
-        left_ref[*part[2]] = self.powers_ref[slot]
-        if other_power is not None:
-            left_ref[*part[3]] = self.powers_ref[other_power]
-        first = self.own_other(slot)
-        for t in range(5):
-            a_real, a_imag = tile_of(*first, t)
-            b_real, b_imag = tile_of(*other, t)
-            put(left_ref, part[0], t, a_real * b_real + a_imag * b_imag)
-            put(left_ref, part[1], t, a_imag * b_real - a_real * b_imag)
-            if other_power is None:
-                put(left_ref, part[3], t, b_real * b_real + b_imag * b_imag)
         depth = self.bands_ref.shape[2]
         wide = self.bands_ref.shape[3]
+        heights, widths = [], []
+        for slot, kind, _, _ in items:
+            pair = (self.me * dates + slot) * per_date + kind
+            heights.append(self.az_ref[pair])
+            widths.append(jnp.clip(self.rng_ref[pair] - REACH_LO, 0, HALO - REACH_LO))
+        for x, (slot, kind, other, other_power) in enumerate(items):
+            left_ref = self.left_ref.at[x]
+            left_ref[*part[2]] = self.powers_ref[slot]
+            if other_power is not None:
+                left_ref[*part[3]] = self.powers_ref[other_power]
+            first = self.own_other(slot)
+            for t in range(5):
+                a_real, a_imag = tile_of(*first, t)
+                b_real, b_imag = tile_of(*other, t)
+                put(left_ref, part[0], t, a_real * b_real + a_imag * b_imag)
+                put(left_ref, part[1], t, a_imag * b_real - a_real * b_imag)
+                if other_power is None:
+                    put(left_ref, part[3], t, b_real * b_real + b_imag * b_imag)
         for n in range(2):
-            ranged = jnp.dot(
-                left_ref[:, n * depth : (n + 1) * depth],
-                self.bands_ref[width, n],
-                preferred_element_type=jnp.float32,
-            )
-            for low, values in enumerate(split(ranged)):
-                for f in range(4):
-                    stack_ref[f, low * rows : (low + 1) * rows, n * wide : (n + 1) * wide] = values[
-                        f * rows : (f + 1) * rows
-                    ]
+            for x in range(2):
+                ranged = jnp.dot(
+                    self.left_ref[x, :, n * depth : (n + 1) * depth],
+                    self.bands_ref[widths[x], n],
+                    preferred_element_type=jnp.float32,
+                )
+                there = slice(n * wide, (n + 1) * wide)
+                for low, values in enumerate(split(ranged)):
+                    for f in range(4):
+                        self.stack_ref[x, f, low * rows : (low + 1) * rows, there] = values[
+                            f * rows : (f + 1) * rows
+                        ]
         row = lax.broadcasted_iota(jnp.int32, (rows, 2 * rows), 0)
         col = lax.broadcasted_iota(jnp.int32, (rows, 2 * rows), 1)
         col = jnp.where(col < rows, col, col - rows)
-        band = (jnp.abs(row - col) <= height).astype(jnp.float32).astype(jnp.bfloat16)
-        looked = [
-            jnp.dot(band, stack_ref[f], preferred_element_type=jnp.float32) for f in range(4)
-        ]
-        inverse = lax.rsqrt(looked[2] * looked[3] + EPSILON)
-        for c in range(2):
-            self.stage_ref[stage, c] = looked[c] * inverse
-        self.out_copy(stage, slot * per_date + kind).start()
-        self.count_ref[0] = count + 1
+        for x in range(2):
+            band = (jnp.abs(row - col) <= heights[x]).astype(jnp.float32).astype(jnp.bfloat16)
+            looked = [
+                jnp.dot(band, self.stack_ref[x, f], preferred_element_type=jnp.float32)
+                for f in range(4)
+            ]
+            inverse = lax.rsqrt(looked[2] * looked[3] + EPSILON)
+            for c in range(2):
+                self.stage_ref[stage, x, c] = looked[c] * inverse
 
 
 def own_kernel(plan, lists, slc_ref, rim_ref, bands_ref, out_ref, powers_ref, *scratch):
@@ -317,75 +384,60 @@
 
     lax.fori_loop(0, dates, power, 0)
 
-    def step(n, carry):
-        slot, kind = n // NEAR, lax.rem(n, NEAR)
-        pair = (pairs.me * dates + slot) * plan["per_date"] + kind
-        local = pairs.partner(pair) - pairs.me * dates
-
-        @pl.when((local >= 0) & (local < dates))
-        def _():
-            pairs.run(slot, kind, pairs.own_other(local), local)
-
-        return carry
-
-    lax.fori_loop(0, dates * NEAR, step, 0)
-    pairs.finish()
+    def work(x, n):
+        slot, kind, local = pairs.near_item(pairs.list_ref[n])
+        return slot, kind, pairs.own_other(local), local
+
+    pairs.run(pairs.near_list(True), work)
 
 
 def rest_kernel(plan, lists, slc_ref, rim_ref, bands_ref, powers_ref, inner_ref, outer_ref,
                 middle_ref, _, out_ref, *scratch):
     pairs = Pairs(plan, lists, slc_ref, rim_ref, bands_ref, powers_ref, out_ref, scratch)
     dates, half = plan["dates"], plan["devices"] // 2
-    upper = pairs.me >= half
     if plan["halves"]:
+        upper = pairs.me >= half
         in_middle = jnp.where(upper, pairs.me == half, pairs.me == half - 1)
     else:
         upper, in_middle = True, False
 
-    def step(n, carry):
-        slot, kind = n // NEAR, lax.rem(n, NEAR)
-        pair = (pairs.me * dates + slot) * plan["per_date"] + kind
-        local = pairs.partner(pair) - pairs.me * dates
+    def work(x, n):
+        slot, kind, local = pairs.near_item(pairs.list_ref[n])
         below = local < 0
         index = jnp.clip(jnp.where(below, local + NEAR, local - dates), 0, NEAR - 1)
         inner = below == upper
-
-        @pl.when(below | (local >= dates))
-        def _():
-            middle = inner & in_middle
-            pl.when(middle)(lambda: pairs.fetch_payload(middle_ref, index))
-            pl.when(inner & jnp.logical_not(middle))(
-                lambda: pairs.fetch_payload(inner_ref, index)
-            )
-            pl.when(jnp.logical_not(inner))(lambda: pairs.fetch_payload(outer_ref, index))
-            pairs.run(slot, kind, pairs.fetched_other())
-
-        return carry
-
-    lax.fori_loop(0, dates * NEAR, step, 0)
-    pairs.finish()
+        middle = inner & in_middle
+        sources = (
+            (jnp.logical_not(inner), outer_ref),
+            (inner & jnp.logical_not(middle), inner_ref),
+            (middle, middle_ref),
+        )
+        for chosen, ref in sources:
+            pl.when(chosen)(functools.partial(pairs.fetch_payload, x, ref, index))
+        return slot, kind, pairs.fetched_other(x), None
+
+    pairs.run(pairs.near_list(False), work)
 
 
 def annual_kernel(plan, is_late, lists, slc_ref, rim_ref, bands_ref, powers_ref, inner_ref,
-                  outer_ref, images_ref, strips_ref, _, out_ref, *scratch):
+                  outer_ref, images_ref, more_ref, strips_ref, _, out_ref, *scratch):
     pairs = Pairs(plan, lists, slc_ref, rim_ref, bands_ref, powers_ref, out_ref, scratch)
-    dates, late, rows = plan["dates"], plan["late"], plan["rows"]
+    dates, late = plan["dates"], plan["late"]
     half = plan["devices"] // 2
     me, split_date = pairs.me, half * dates
     lower = me < half
-    mate = jnp.where(lower, 1, 0)
     if is_late:
         base, count = jnp.where(lower, 0, dates - late), late
     else:
         base, count = jnp.where(lower, late, 0), dates - late
 
-    def fetch_early(k):
+    def fetch_early(x, k, ref):
         packed = strips_ref[...]
         for c in range(2):
-            pairs.other_ref[c] = images_ref[mate, c, k]
-            pairs.other_rim_ref[c] = place_strip(packed, 2 * k + c, pairs.strip)
-
-    def step(k, carry):
+            pairs.other_ref[x, c] = ref[c, k]
+            pairs.other_rim_ref[x, c] = place_strip(packed, 2 * k + c, pairs.strip)
+
+    def work(x, k):
         slot = base + k
         date = me * dates + slot
         other = pairs.partner(date * plan["per_date"] + NEAR)
@@ -393,43 +445,34 @@
         from_inner = jnp.where(lower, me != 0, me == half)
         inner_at = jnp.where(lower, other, other - (2 * split_date - NEAR))
         outer_at = jnp.where(lower, other - (split_date - NEAR), other - split_date)
-
-        @pl.when(far & from_inner)
-        def _():
-            pairs.fetch_payload(inner_ref, jnp.clip(inner_at, 0, NEAR - 1))
-
-        @pl.when(far & jnp.logical_not(from_inner))
-        def _():
-            pairs.fetch_payload(outer_ref, jnp.clip(outer_at, 0, NEAR - 1))
-
-        @pl.when(jnp.logical_not(far))
-        def _():
-            if is_late:
-                pairs.fetch_payload(images_ref.at[mate], k)
-            else:
-                fetch_early(k)
-
-        pairs.run(slot, NEAR, pairs.fetched_other())
-        return carry
-
-    lax.fori_loop(0, count, step, 0)
-    pairs.finish()
+        inner_at, outer_at = jnp.clip(inner_at, 0, NEAR - 1), jnp.clip(outer_at, 0, NEAR - 1)
+        fetch = pairs.fetch_payload
+        pl.when(far & from_inner)(lambda: fetch(x, inner_ref, inner_at))
+        pl.when(far & jnp.logical_not(from_inner))(lambda: fetch(x, outer_ref, outer_at))
+        near_side = jnp.logical_not(far)
+        if is_late:
+            pl.when(near_side)(lambda: fetch(x, images_ref, k))
+        else:
+            first = pairs.strip == 0
+            pl.when(near_side & first)(lambda: fetch_early(x, k, images_ref))
+            pl.when(near_side & jnp.logical_not(first))(lambda: fetch_early(x, k, more_ref))
+        return slot, NEAR, pairs.fetched_other(x), None
+
+    pairs.run(count, work)
 
 
 def plain_kernel(plan, lists, slc_ref, rim_ref, bands_ref, powers_ref, images_ref,
                  image_rim_ref, _, out_ref, *scratch):
     pairs = Pairs(plan, lists, slc_ref, rim_ref, bands_ref, powers_ref, out_ref, scratch)
 
-    def step(slot, carry):
+    def work(x, slot):
         other = (
             lambda c, cols: images_ref[c, slot, :, cols],
             lambda c: image_rim_ref[c, slot],
         )
-        pairs.run(slot, NEAR, other)
-        return carry
-
-    lax.fori_loop(0, plan["dates"], step, 0)
-    pairs.finish()
+        return slot, NEAR, other, None
+
+    pairs.run(plan["dates"], work)
 
 
 def arrivals_by_distance(slc, pair_list, plan):
@@ -513,7 +556,7 @@
             in_specs=[ANY],
             out_specs=VMEM,
             scratch_shapes=[pltpu.SemaphoreType.DMA],
-            compiler_params=limit(4),
+            compiler_params=limit(WORK_MIB),
             name="rim_blocks",
         )(values)
         return lax.ppermute(out, "strip", swap_strips)
@@ -526,42 +569,59 @@
         grid=(widths,),
         out_shape=jax.ShapeDtypeStruct((widths, *band_shape), jnp.bfloat16),
         out_specs=pl.BlockSpec((1, *band_shape), lambda n: (n, 0, 0, 0)),
-        compiler_params=limit(4),
+        compiler_params=limit(WORK_MIB),
         name="range_bands",
     )()
     if halves:
         swap = [(i, (i + half) % devices) for i in range(devices)]
-        mates = [[i, i + half] for i in range(half)]
-        early, strips, rim = pl.pallas_call(
+
+        def on_strip(route, strip):
+            return [(2 * a + strip, 2 * b + strip) for a, b in route]
+
+        both = ("date", "strip")
+        early, rim, strips = pl.pallas_call(
             functools.partial(early_kernel, plan),
             out_shape=(
                 images(dates - late),
+                rim_shape(dates),
                 jax.ShapeDtypeStruct((rows, TILE), dtype),
-                rim_shape(dates),
             ),
             in_specs=[ANY, SMEM],
             out_specs=(VMEM, VMEM, VMEM),
-            scratch_shapes=[pltpu.SemaphoreType.DMA((dates - late + 1,))],
-            compiler_params=limit(56),
+            scratch_shapes=[
+                pltpu.VMEM((dates - late, planes, rows, TILE), dtype),
+                pltpu.SemaphoreType.DMA((dates - late,)),
+                pltpu.SemaphoreType.DMA((dates - late,)),
+                pltpu.SemaphoreType.DMA,
+            ],
+            compiler_params=limit(FIRST_MIB),
             name="early_images",
         )(slc, lists[0])
-        early = lax.all_gather(early, "date", axis_index_groups=mates)
+        early = lax.ppermute(early, both, on_strip(swap, 0))
         rim = lax.ppermute(rim, "strip", swap_strips)
-        strips = lax.ppermute(
-            strips, ("date", "strip"), [(2 * a + s, 2 * b + 1 - s) for a, b in swap for s in (0, 1)]
-        )
-        inner, outer = pl.pallas_call(
+        inner, outer, more = pl.pallas_call(
             functools.partial(beside_kernel, plan),
-            out_shape=(payload_shape(NEAR), payload_shape(NEAR)),
-            in_specs=[ANY, VMEM],
-            out_specs=(VMEM, VMEM),
-            scratch_shapes=[pltpu.SemaphoreType.DMA((2, NEAR, 2))],
-            compiler_params=limit(56),
+            out_shape=(
+                payload_shape(NEAR),
+                payload_shape(NEAR),
+                images(dates - late),
+            ),
+            in_specs=[ANY, SMEM, VMEM],
+            out_specs=(VMEM, VMEM, VMEM),
+            scratch_shapes=[
+                pltpu.SemaphoreType.DMA((2, NEAR, 2)),
+                pltpu.SemaphoreType.DMA((dates - late,)),
+            ],
+            compiler_params=limit(WORK_MIB),
             name="beside_images",
-        )(slc, rim)
+        )(slc, lists[0], rim)
         down = [(i, (i - 1) % half) for i in range(half)]
         down += [(half + i, half + (i + 1) % half) for i in range(half)]
         middle = lax.ppermute(outer, "date", [(half - 1, half), (half, half - 1)])
+        more = lax.ppermute(more, both, on_strip(swap, 1))
+        strips = lax.ppermute(
+            strips, both, [(2 * a + s, 2 * b + 1 - s) for a, b in swap for s in (0, 1)]
+        )
         inner = lax.ppermute(inner, "date", down)
         outer = lax.ppermute(outer, "date", [(b, a) for a, b in down])
     else:
@@ -578,13 +638,13 @@
     out_shape = jax.ShapeDtypeStruct((planes, dates * per_date, rows, cols), jnp.float32)
     depth = 2 * band_shape[1]
     scratch = [
-        pltpu.VMEM((4 * rows, depth), jnp.bfloat16),
-        pltpu.VMEM((4, 2 * rows, cols), jnp.bfloat16),
-        pltpu.VMEM((planes, rows, cols), dtype),
-        pltpu.VMEM((planes, rows, TILE), dtype),
-        pltpu.VMEM((2, planes, rows, cols), jnp.float32),
-        pltpu.SMEM((1,), jnp.int32),
-        pltpu.SemaphoreType.DMA((2,)),
+        pltpu.VMEM((2, 4 * rows, depth), jnp.bfloat16),
+        pltpu.VMEM((2, 4, 2 * rows, cols), jnp.bfloat16),
+        pltpu.VMEM((2, planes, rows, cols), dtype),
+        pltpu.VMEM((2, planes, rows, TILE), dtype),
+        pltpu.VMEM((2, 2, planes, rows, cols), jnp.float32),
+        pltpu.SMEM((dates * NEAR + 1,), jnp.int32),
+        pltpu.SemaphoreType.DMA((2, 2)),
     ]
 
     def cost(flops):
@@ -596,7 +656,7 @@
         in_specs=[SMEM] * 3 + [VMEM] * 3,
         out_specs=(ANY, VMEM),
         scratch_shapes=scratch,
-        compiler_params=limit(24),
+        compiler_params=limit(WORK_MIB),
         cost_estimate=cost(20_000_000_000),
         name="own_pairs",
     )(*lists, slc, rim, bands)
@@ -609,7 +669,7 @@
             out_specs=ANY,
             scratch_shapes=scratch,
             input_output_aliases={7 + len(others): 0},
-            compiler_params=limit(24),
+            compiler_params=limit(WORK_MIB),
             cost_estimate=cost(1),
             name=name,
         )(*lists, slc, rim, bands, powers, *others, out)
@@ -621,16 +681,16 @@
             in_specs=[VMEM, VMEM, VMEM, SMEM, ANY, ANY],
             out_specs=VMEM,
             scratch_shapes=[pltpu.VMEM((late, planes, rows, TILE), dtype)],
-            compiler_params=limit(4),
+            compiler_params=limit(WORK_MIB),
             name="late_images",
         )(slc, rim, inner, lists[0], powers, strips)
-        payload = lax.all_gather(payload, "date", axis_index_groups=mates)
+        payload = lax.ppermute(payload, "date", swap)
     out = more_pairs(rest_kernel, out, (inner, outer, middle), "near_pairs")
     if halves:
         kernel = lambda plan, *refs: annual_kernel(plan, False, *refs)
-        out = more_pairs(kernel, out, (inner, outer, early, strips), "annual_pairs")
+        out = more_pairs(kernel, out, (inner, outer, early, more, strips), "annual_pairs")
         kernel = lambda plan, *refs: annual_kernel(plan, True, *refs)
-        out = more_pairs(kernel, out, (inner, outer, payload, strips), "last_pairs")
+        out = more_pairs(kernel, out, (inner, outer, payload, payload, strips), "last_pairs")
     else:
         out = more_pairs(plain_kernel, out, (annual, swapped_rims(annual)), "annual_pairs")
     return out

time: 94.5 us -> 61.6 us (0.65)
  the two profiles are of different devices: /device:TPU:0 before, /device:TPU:16 now
where the time goes in v5:
time: 61.6 us; the launch traced here: 60.7 us
  Pallas kernels  25.5 us (41%)
  waiting for transfers between devices  20.8 us (34%)
  starting transfers between devices  11.1 us (18%)
  local copies, waits for them, and re-layouts  3.16 us (5%)
    ppermute x1, waiting for transfers between devices, body(): middle = lax.ppermute(outer, 'date', [(half - 1, half), (half, half - 1)])  14.8 us
    pallas_call x3, Pallas kernels, more_pairs(): pl.pallas_call(lambda *refs: kernel(plan, refs[:3], *refs[3:]), out_shape...  12.6 us
    pallas_call x1, Pallas kernels, body(): pl.pallas_call(lambda *refs: own_kernel(plan, refs[:3], *refs[3:]), out_s...  6.7 us
    ppermute x1, waiting for transfers between devices, body(): inner = lax.ppermute(inner, 'date', down)  5.95 us
    ppermute x1, starting transfers between devices, body(): early = lax.ppermute(early, both, on_strip(swap, 0))  4.86 us
    ppermute x1, starting transfers between devices, body(): middle = lax.ppermute(outer, 'date', [(half - 1, half), (half, half - 1)])  3.3 us
    unnamed x8, local copies, waits for them, and re-layouts  3.16 us
    pallas_call x1, Pallas kernels, body(): pl.pallas_call(functools.partial(early_kernel, plan), out_shape=(images(d...  2.89 us
  transfers between devices with their start and end apart: 8, of which 2 were waited for; matrix products, arithmetic and copies ran while one was open for 0% of the time, Pallas kernels for 33%

profile of v5, /device:TPU:16, one launch (start us, length us, event | category | flops | bytes accessed | tf_op | source)
XLA Modules:
  0.0 60.7 jit_solution(11652417269677141536)
XLA Ops:
  0.0 2.9 %early_images.1 = (bf16[2,4,64,512]{3,2,1,0:T(8,128)(2,1)}, bf16[2,6,64,128]{3,2,1,0:T(8,128)(2,1)}, bf16[64,128]{1,0:T(8,128)(2,1)}) custom-call(bf16[2,6,64,512]{3,2,1,0:T(8,128)(2,1)} %refs_3_.7, s32[2,192]{1,0:T(2,128)} %bitcast.1), custom_call_target="tpu_custom_call" | custom-call | tf_op jit(solution)/shard_map/early_images/pallas_call | solution.py:582
  2.9 0.1 collective-permute-start
  3.0 0.1 collective-permute-start.3
  3.1 4.9 %collective-permute-start.5 = (bf16[2,4,64,512]{3,2,1,0:T(8,128)(2,1)}, bf16[2,4,64,512]{3,2,1,0:T(8,128)(2,1)S(1)}, u32[]{:S(2)}, u32[]{:S(2)}) collective-permute-start(bf16[2,4,64,512]{3,2,1,0:T(8,128)(2,1)} %get-tuple-element.18), channel_id=1, source_target_pairs={{0,8},{2,10},{4,12},{6,14},{8,0},{10,2},{12,4},{14,6},{16,24},{18,... | collective-permute-start | bytes 1572872 | tf_op jit(solution)/shard_map/ppermute | solution.py:600
  7.9 0.5 range_bands.1.refs_5_
  8.5 0.0 collective-permute-done.refs_4_.rim_ref
  8.5 0.0 copy-start
  8.5 1.1 %copy-done = bf16[2,6,64,512]{3,2,1,0:T(8,128)(2,1)S(1)} copy-done((bf16[2,6,64,512]{3,2,1,0:T(8,128)(2,1)S(1)}, bf16[2,6,64,512]{3,2,1,0:T(8,128)(2,1)}, u32[]{:S(2)}) %copy-start) | copy-done | bytes 786456
  9.6 0.0 copy-start.1
  9.6 0.7 %copy-done.1 = s32[192,2]{0,1:T(2,128)S(1)} copy-done((s32[192,2]{0,1:T(2,128)S(1)}, s32[192,2]{0,1:T(2,128)}, u32[]{:S(2)}) %copy-start.1) | copy-done | bytes 1560
  10.3 1.9 %beside_images.1 = (bf16[400,512]{1,0:T(8,128)(2,1)S(1)}, bf16[400,512]{1,0:T(8,128)(2,1)S(1)}, bf16[2,4,64,512]{3,2,1,0:T(8,128)(2,1)S(1)}) custom-call(bf16[2,6,64,512]{3,2,1,0:T(8,128)(2,1)S(1)} %copy-done, s32[2,192]{1,0:T(2,128)S(1)} %bitcast.2, bf16[2,6,64,128]{3,2,1,0:T(8,128)(2,1)S(1)} %collective-permute-done.refs_4_.rim_ref), custom_call_target="tpu_custom_call" | custom-call | tf_op jit(solution)/shard_map/beside_images/pallas_call | solution.py:602
  12.2 3.3 %collective-permute-start.7 = (bf16[400,512]{1,0:T(8,128)(2,1)S(1)}, bf16[400,512]{1,0:T(8,128)(2,1)S(1)}, u32[]{:S(2)}, u32[]{:S(2)}) collective-permute-start(bf16[400,512]{1,0:T(8,128)(2,1)S(1)} %get-tuple-element.16), channel_id=1, source_target_pairs={{6,8},{8,6},{7,9},{9,7},{22,24},{24,22},{23,25},{25,23}} | collective-permute-start | bytes 1228808 | tf_op jit(solution)/shard_map/ppermute | solution.py:620
  15.5 0.2 collective-permute-start.2
  15.7 1.9 %collective-permute-start.1 = (bf16[400,512]{1,0:T(8,128)(2,1)S(1)}, bf16[400,512]{1,0:T(8,128)(2,1)S(1)}, u32[]{:S(2)}, u32[]{:S(2)}) collective-permute-start(bf16[400,512]{1,0:T(8,128)(2,1)S(1)} %get-tuple-element.15), channel_id=1, source_target_pairs={{0,6},{2,0},{4,2},{6,4},{8,10},{10,12},{12,14},{14,8},{1,7},{3,1},... | collective-permute-start | bytes 1228808 | tf_op jit(solution)/shard_map/ppermute | solution.py:625
  17.6 0.0 collective-permute-done.3.refs_1_.refs_11_
  17.6 0.7 %collective-permute-start.6 = (bf16[2,4,64,512]{3,2,1,0:T(8,128)(2,1)S(1)}, bf16[2,4,64,512]{3,2,1,0:T(8,128)(2,1)S(1)}, u32[]{:S(2)}, u32[]{:S(2)}) collective-permute-start(bf16[2,4,64,512]{3,2,1,0:T(8,128)(2,1)S(1)} %get-tuple-element.19), channel_id=1, source_target_pairs={{1,9},{3,11},{5,13},{7,15},{9,1},{11,3},{13,5},{15,7},{17,25},{19,... | collective-permute-start | bytes 1572872 | tf_op jit(solution)/shard_map/ppermute | solution.py:621
  18.3 0.0 copy-start.2
  18.3 0.7 %copy-done.2 = s32[192]{0:T(256)S(1)} copy-done((s32[192]{0:T(256)S(1)}, s32[192]{0:T(256)}, u32[]{:S(2)}) %copy-start.2) | copy-done | bytes 792
  19.0 0.0 copy-start.3
  19.0 0.7 %copy-done.3 = s32[192]{0:T(256)S(1)} copy-done((s32[192]{0:T(256)S(1)}, s32[192]{0:T(256)}, u32[]{:S(2)}) %copy-start.3) | copy-done | bytes 792
  19.6 6.7 %own_pairs.1 = (f32[2,24,64,512]{3,2,1,0:T(8,128)}, bf16[6,64,1536]{2,1,0:T(8,128)(2,1)S(1)}) custom-call(s32[2,192]{1,0:T(2,128)S(1)} %bitcast.3, s32[192]{0:T(256)S(1)} %copy-done.2, s32[192]{0:T(256)S(1)} %copy-done.3, bf16[2,6,64,512]{3,2,1,0:T(8,128)(2,1)S(1)} %copy-done, bf16[2,6,64,128]{3,2,1,0:T(8,128)(2,1)S(1)} %collective-permute-done.refs_4_.rim_ref, ...), custom_call_target="tpu_custom_call" | custom-call | flops 20000000000 | bytes 1 | tf_op jit(solution)/shard_map/own_pairs/pallas_call | solution.py:653
  26.3 6.0 %collective-permute-done.1.inner_ref.refs_7_ = bf16[400,512]{1,0:T(8,128)(2,1)S(1)} collective-permute-done((bf16[400,512]{1,0:T(8,128)(2,1)S(1)}, bf16[400,512]{1,0:T(8,128)(2,1)S(1)}, u32[]{:S(2)}, u32[]{:S(2)}) %collective-permute-start.1) | collective-permute-done | bytes 409632 | tf_op jit(solution)/shard_map/ppermute | solution.py:625
  32.3 0.8 %late_images.1 = bf16[272,512]{1,0:T(8,128)(2,1)S(1)} custom-call(bf16[2,6,64,512]{3,2,1,0:T(8,128)(2,1)S(1)} %copy-done, bf16[2,6,64,128]{3,2,1,0:T(8,128)(2,1)S(1)} %collective-permute-done.refs_4_.rim_ref, bf16[400,512]{1,0:T(8,128)(2,1)S(1)} %collective-permute-done.1.inner_ref.refs_7_, s32[2,192]{1,0:T(2,128)S(1)} %bitcast.4, ...), custom_call_target="tpu_custom_call" | custom-call | tf_op jit(solution)/shard_map/late_images/pallas_call | solution.py:678
  33.1 0.1 collective-permute-start.4
  33.2 14.8 %collective-permute-done.7.refs_9_ = bf16[400,512]{1,0:T(8,128)(2,1)S(1)} collective-permute-done((bf16[400,512]{1,0:T(8,128)(2,1)S(1)}, bf16[400,512]{1,0:T(8,128)(2,1)S(1)}, u32[]{:S(2)}, u32[]{:S(2)}) %collective-permute-start.7) | collective-permute-done | bytes 409632 | tf_op jit(solution)/shard_map/ppermute | solution.py:620
  48.0 0.0 collective-permute-done.2.refs_8_
  48.0 6.2 %near_pairs.1.refs_12_ = f32[2,24,64,512]{3,2,1,0:T(8,128)} custom-call(s32[2,192]{1,0:T(2,128)S(1)} %bitcast.5, s32[192]{0:T(256)S(1)} %copy-done.2, s32[192]{0:T(256)S(1)} %copy-done.3, bf16[2,6,64,512]{3,2,1,0:T(8,128)(2,1)S(1)} %copy-done, bf16[2,6,64,128]{3,2,1,0:T(8,128)(2,1)S(1)} %collective-permute-done.refs_4_.rim_ref, ...), custom_call_target="tpu_custom_call", output_to_operand_aliasing={{}: (10, {})} | custom-call | flops 1 | bytes 1 | tf_op jit(solution)/shard_map/near_pairs/pallas_call | solution.py:665
  54.3 0.0 collective-permute-done.5.refs_9_
  54.3 0.0 collective-permute-done.6.refs_10_
  54.3 3.8 %annual_pairs.1.refs_12_ = f32[2,24,64,512]{3,2,1,0:T(8,128)} custom-call(s32[2,192]{1,0:T(2,128)S(1)} %bitcast.6, s32[192]{0:T(256)S(1)} %copy-done.2, s32[192]{0:T(256)S(1)} %copy-done.3, bf16[2,6,64,512]{3,2,1,0:T(8,128)(2,1)S(1)} %copy-done, bf16[2,6,64,128]{3,2,1,0:T(8,128)(2,1)S(1)} %collective-permute-done.refs_4_.rim_ref, ...), custom_call_target="tpu_custom_call", output_to_operand_aliasing={{}: (12, {})} | custom-call | flops 1 | bytes 1 | tf_op jit(solution)/shard_map/annual_pairs/pallas_call | solution.py:665
  58.1 0.0 collective-permute-done.4.refs_9_.refs_10_
  58.1 2.6 %last_pairs.1 = f32[2,24,64,512]{3,2,1,0:T(8,128)} custom-call(s32[2,192]{1,0:T(2,128)S(1)} %bitcast.7, s32[192]{0:T(256)S(1)} %copy-done.2, s32[192]{0:T(256)S(1)} %copy-done.3, bf16[2,6,64,512]{3,2,1,0:T(8,128)(2,1)S(1)} %copy-done, bf16[2,6,64,128]{3,2,1,0:T(8,128)(2,1)S(1)} %collective-permute-done.refs_4_.rim_ref, ...), custom_call_target="tpu_custom_call", output_to_operand_aliasing={{}: (12, {})} | custom-call | flops 1 | bytes 1 | tf_op jit(solution)/shard_map/last_pairs/pallas_call | solution.py:665
Async XLA Ops:
  2.9 5.6 %collective-permute-start = (bf16[2,6,64,128]{3,2,1,0:T(8,128)(2,1)}, bf16[2,6,64,128]{3,2,1,0:T(8,128)(2,1)S(1)}, u32[]{:S(2)}, u32[]{:S(2)}) collective-permute-start(bf16[2,6,64,128]{3,2,1,0:T(8,128)(2,1)} %get-tuple-element.13), channel_id=1, source_target_pairs={{0,1},{1,0},{2,3},{3,2},{4,5},{5,4},{6,7},{7,6},{8,9},{9,8},{10,11... | collective-permute-start | bytes 589832 | tf_op jit(solution)/shard_map/ppermute | solution.py:601
  3.0 14.6 %collective-permute-start.3 = (bf16[64,128]{1,0:T(8,128)(2,1)}, bf16[64,128]{1,0:T(8,128)(2,1)S(1)}, u32[]{:S(2)}, u32[]{:S(2)}) collective-permute-start(bf16[64,128]{1,0:T(8,128)(2,1)} %get-tuple-element.17), channel_id=1, source_target_pairs={{0,9},{1,8},{2,11},{3,10},{4,13},{5,12},{6,15},{7,14},{8,1},{9,0},... | collective-permute-start | bytes 49160 | tf_op jit(solution)/shard_map/ppermute | solution.py:622
  3.1 51.2 %collective-permute-start.5 = (bf16[2,4,64,512]{3,2,1,0:T(8,128)(2,1)}, bf16[2,4,64,512]{3,2,1,0:T(8,128)(2,1)S(1)}, u32[]{:S(2)}, u32[]{:S(2)}) collective-permute-start(bf16[2,4,64,512]{3,2,1,0:T(8,128)(2,1)} %get-tuple-element.18), channel_id=1, source_target_pairs={{0,8},{2,10},{4,12},{6,14},{8,0},{10,2},{12,4},{14,6},{16,24},{18,... | collective-permute-start | bytes 1572872 | tf_op jit(solution)/shard_map/ppermute | solution.py:600
  8.5 1.1 %copy-start = (bf16[2,6,64,512]{3,2,1,0:T(8,128)(2,1)S(1)}, bf16[2,6,64,512]{3,2,1,0:T(8,128)(2,1)}, u32[]{:S(2)}) copy-start(bf16[2,6,64,512]{3,2,1,0:T(8,128)(2,1)} %refs_3_.7) | copy-start | bytes 2359300
  9.6 0.7 %copy-start.1 = (s32[192,2]{0,1:T(2,128)S(1)}, s32[192,2]{0,1:T(2,128)}, u32[]{:S(2)}) copy-start(s32[192,2]{0,1:T(2,128)} %param.5) | copy-start | bytes 4612
  12.2 35.8 %collective-permute-start.7 = (bf16[400,512]{1,0:T(8,128)(2,1)S(1)}, bf16[400,512]{1,0:T(8,128)(2,1)S(1)}, u32[]{:S(2)}, u32[]{:S(2)}) collective-permute-start(bf16[400,512]{1,0:T(8,128)(2,1)S(1)} %get-tuple-element.16), channel_id=1, source_target_pairs={{6,8},{8,6},{7,9},{9,7},{22,24},{24,22},{23,25},{25,23}} | collective-permute-start | bytes 1228808 | tf_op jit(solution)/shard_map/ppermute | solution.py:620
  15.5 32.5 %collective-permute-start.2 = (bf16[400,512]{1,0:T(8,128)(2,1)S(1)}, bf16[400,512]{1,0:T(8,128)(2,1)S(1)}, u32[]{:S(2)}, u32[]{:S(2)}) collective-permute-start(bf16[400,512]{1,0:T(8,128)(2,1)S(1)} %get-tuple-element.16), channel_id=1, source_target_pairs={{6,0},{0,2},{2,4},{4,6},{10,8},{12,10},{14,12},{8,14},{7,1},{1,3},... | collective-permute-start | bytes 1228808 | tf_op jit(solution)/shard_map/ppermute | solution.py:626
  15.7 16.6 %collective-permute-start.1 = (bf16[400,512]{1,0:T(8,128)(2,1)S(1)}, bf16[400,512]{1,0:T(8,128)(2,1)S(1)}, u32[]{:S(2)}, u32[]{:S(2)}) collective-permute-start(bf16[400,512]{1,0:T(8,128)(2,1)S(1)} %get-tuple-element.15), channel_id=1, source_target_pairs={{0,6},{2,0},{4,2},{6,4},{8,10},{10,12},{12,14},{14,8},{1,7},{3,1},... | collective-permute-start | bytes 1228808 | tf_op jit(solution)/shard_map/ppermute | solution.py:625
  17.6 36.7 %collective-permute-start.6 = (bf16[2,4,64,512]{3,2,1,0:T(8,128)(2,1)S(1)}, bf16[2,4,64,512]{3,2,1,0:T(8,128)(2,1)S(1)}, u32[]{:S(2)}, u32[]{:S(2)}) collective-permute-start(bf16[2,4,64,512]{3,2,1,0:T(8,128)(2,1)S(1)} %get-tuple-element.19), channel_id=1, source_target_pairs={{1,9},{3,11},{5,13},{7,15},{9,1},{11,3},{13,5},{15,7},{17,25},{19,... | collective-permute-start | bytes 1572872 | tf_op jit(solution)/shard_map/ppermute | solution.py:621
  18.3 0.7 %copy-start.2 = (s32[192]{0:T(256)S(1)}, s32[192]{0:T(256)}, u32[]{:S(2)}) copy-start(s32[192]{0:T(256)} %refs_1_.7) | copy-start | bytes 2308
  19.0 0.7 %copy-start.3 = (s32[192]{0:T(256)S(1)}, s32[192]{0:T(256)}, u32[]{:S(2)}) copy-start(s32[192]{0:T(256)} %refs_2_.7) | copy-start | bytes 2308
  33.1 25.0 %collective-permute-start.4 = (bf16[272,512]{1,0:T(8,128)(2,1)S(1)}, bf16[272,512]{1,0:T(8,128)(2,1)S(1)}, u32[]{:S(2)}, u32[]{:S(2)}) collective-permute-start(bf16[272,512]{1,0:T(8,128)(2,1)S(1)} %late_images.1), channel_id=1, source_target_pairs={{0,8},{2,10},{4,12},{6,14},{8,0},{10,2},{12,4},{14,6},{1,9},{3,11}... | collective-permute-start | bytes 835592 | tf_op jit(solution)/shard_map/ppermute | solution.py:687

commit v6 on v5

--- a/solution.py
+++ b/solution.py
@@ -14,6 +14,7 @@
 EPSILON = 1e-06
 TILE = 128
 INNER = TILE // 2
+PARTNER, HEIGHT, REACH = 1, 2, 3
 WORK_MIB = 16
 FIRST_MIB = 56
 ANY = pl.BlockSpec(memory_space=pl.ANY)
@@ -70,7 +71,7 @@
     wanted = []
     for k in range(dates - plan["late"]):
         date = mate * dates + jnp.where(mate < half, plan["late"], 0) + k
-        at = pairs_ref[1, date * plan["per_date"] + NEAR] - me * dates
+        at = pairs_ref[PARTNER, date * plan["per_date"] + NEAR] - me * dates
         wanted.append(jnp.clip(at, 0, dates - 1))
     return wanted
 
@@ -159,8 +160,10 @@
             copy.wait()
 
 
-def late_kernel(plan, slc_ref, rim_ref, inner_ref, pairs_ref, *refs):
-    late_ref, tiles_ref = refs[-2:]
+def late_kernel(plan, slc_ref, rim_ref, inner_ref, outgoing_ref, pairs_ref, *refs):
+    late_ref, middle_ref, tiles_ref, sem = refs[-4:]
+    copy = pltpu.make_async_copy(outgoing_ref, middle_ref, sem)
+    copy.start()
     me, strip = lax.axis_index("date"), lax.axis_index("strip")
     dates, late, rows = plan["dates"], plan["late"], plan["rows"]
     half = plan["devices"] // 2
@@ -169,7 +172,7 @@
     packed = read_strips(inner_ref, rows)
     for k in range(late):
         date = mate * dates + mate_slot + k
-        wanted = pairs_ref[1, date * plan["per_date"] + NEAR] - me * dates
+        wanted = pairs_ref[PARTNER, date * plan["per_date"] + NEAR] - me * dates
         own = (wanted >= 0) & (wanted < dates)
         own_at = jnp.clip(wanted, 0, dates - 1)
         other_at = jnp.clip(jnp.where(me < half, wanted - dates, wanted + NEAR), 0, NEAR - 1)
@@ -189,6 +192,7 @@
 
     tiles = [tiles_ref[k, c] for k in range(late) for c in range(2)]
     write_strips(late_ref, gather_strips(tiles, strip))
+    copy.wait()
 
 
 def bands_kernel(cols, out_ref):
@@ -247,7 +251,7 @@
 class Pairs:
     def __init__(self, plan, lists, slc_ref, rim_ref, bands_ref, powers_ref, out_ref, scratch):
         self.plan = plan
-        self.pairs_ref, self.az_ref, self.rng_ref = lists
+        self.lists = lists
         self.slc_ref, self.rim_ref = slc_ref, rim_ref
         self.bands_ref, self.powers_ref, self.out_ref = bands_ref, powers_ref, out_ref
         (self.left_ref, self.stack_ref, self.other_ref, self.other_rim_ref, self.stage_ref,
@@ -255,7 +259,7 @@
         self.me, self.strip = lax.axis_index("date"), lax.axis_index("strip")
 
     def partner(self, pair):
-        return self.pairs_ref[1, pair]
+        return self.lists[PARTNER, pair]
 
     def near_item(self, n):
         slot, kind = n // NEAR, lax.rem(n, NEAR)
@@ -263,14 +267,21 @@
         pair = (self.me * dates + slot) * self.plan["per_date"] + kind
         return slot, kind, self.partner(pair) - self.me * dates
 
-    def near_list(self, own):
+    def near_list(self, chosen):
         count = 0
         for n in range(self.plan["dates"] * NEAR):
-            local = self.near_item(n)[2]
-            inside = (local >= 0) & (local < self.plan["dates"])
             self.list_ref[count] = n
-            count = count + jnp.where(inside == own, 1, 0)
+            count = count + jnp.where(chosen(self.near_item(n)[2]), 1, 0)
         return count
+
+    def own(self, local):
+        return (local >= 0) & (local < self.plan["dates"])
+
+    def in_middle(self, local):
+        half, dates = self.plan["devices"] // 2, self.plan["dates"]
+        if not self.plan["halves"]:
+            return False
+        return ((self.me == half) & (local < 0)) | ((self.me == half - 1) & (local >= dates))
 
     def own_other(self, index):
         return (
@@ -330,8 +341,8 @@
         heights, widths = [], []
         for slot, kind, _, _ in items:
             pair = (self.me * dates + slot) * per_date + kind
-            heights.append(self.az_ref[pair])
-            widths.append(jnp.clip(self.rng_ref[pair] - REACH_LO, 0, HALO - REACH_LO))
+            heights.append(self.lists[HEIGHT, pair])
+            widths.append(jnp.clip(self.lists[REACH, pair] - REACH_LO, 0, HALO - REACH_LO))
         for x, (slot, kind, other, other_power) in enumerate(items):
             left_ref = self.left_ref.at[x]
             left_ref[*part[2]] = self.powers_ref[slot]
@@ -372,7 +383,8 @@
                 self.stage_ref[stage, x, c] = looked[c] * inverse
 
 
-def own_kernel(plan, lists, slc_ref, rim_ref, bands_ref, out_ref, powers_ref, *scratch):
+def own_kernel(plan, lists, slc_ref, rim_ref, bands_ref, *refs):
+    out_ref, powers_ref, *scratch = refs[1 if plan["halves"] else 0 :]
     pairs = Pairs(plan, lists, slc_ref, rim_ref, bands_ref, powers_ref, out_ref, scratch)
     dates = plan["dates"]
 
@@ -388,35 +400,42 @@
         slot, kind, local = pairs.near_item(pairs.list_ref[n])
         return slot, kind, pairs.own_other(local), local
 
-    pairs.run(pairs.near_list(True), work)
-
-
-def rest_kernel(plan, lists, slc_ref, rim_ref, bands_ref, powers_ref, inner_ref, outer_ref,
-                middle_ref, _, out_ref, *scratch):
+    pairs.run(pairs.near_list(pairs.own), work)
+
+
+def rest_kernel(plan, lists, slc_ref, rim_ref, bands_ref, powers_ref, inner_ref, outer_ref, _,
+                out_ref, *scratch):
     pairs = Pairs(plan, lists, slc_ref, rim_ref, bands_ref, powers_ref, out_ref, scratch)
-    dates, half = plan["dates"], plan["devices"] // 2
-    if plan["halves"]:
-        upper = pairs.me >= half
-        in_middle = jnp.where(upper, pairs.me == half, pairs.me == half - 1)
-    else:
-        upper, in_middle = True, False
+    dates = plan["dates"]
+    upper = pairs.me >= plan["devices"] // 2 if plan["halves"] else True
 
     def work(x, n):
         slot, kind, local = pairs.near_item(pairs.list_ref[n])
         below = local < 0
         index = jnp.clip(jnp.where(below, local + NEAR, local - dates), 0, NEAR - 1)
         inner = below == upper
-        middle = inner & in_middle
-        sources = (
-            (jnp.logical_not(inner), outer_ref),
-            (inner & jnp.logical_not(middle), inner_ref),
-            (middle, middle_ref),
-        )
-        for chosen, ref in sources:
-            pl.when(chosen)(functools.partial(pairs.fetch_payload, x, ref, index))
+        pl.when(inner)(lambda: pairs.fetch_payload(x, inner_ref, index))
+        pl.when(jnp.logical_not(inner))(lambda: pairs.fetch_payload(x, outer_ref, index))
         return slot, kind, pairs.fetched_other(x), None
 
-    pairs.run(pairs.near_list(False), work)
+    def chosen(local):
+        return jnp.logical_not(pairs.own(local) | pairs.in_middle(local))
+
+    pairs.run(pairs.near_list(chosen), work)
+
+
+def middle_kernel(plan, lists, slc_ref, rim_ref, bands_ref, powers_ref, middle_ref, _, out_ref,
+                  *scratch):
+    pairs = Pairs(plan, lists, slc_ref, rim_ref, bands_ref, powers_ref, out_ref, scratch)
+    dates = plan["dates"]
+
+    def work(x, n):
+        slot, kind, local = pairs.near_item(pairs.list_ref[n])
+        index = jnp.clip(jnp.where(local < 0, local + NEAR, local - dates), 0, NEAR - 1)
+        pairs.fetch_payload(x, middle_ref, index)
+        return slot, kind, pairs.fetched_other(x), None
+
+    pairs.run(pairs.near_list(pairs.in_middle), work)
 
 
 def annual_kernel(plan, is_late, lists, slc_ref, rim_ref, bands_ref, powers_ref, inner_ref,
@@ -537,7 +556,8 @@
     }
     dtype = slc.dtype
     rim_rows = rows * TILE // cols
-    lists = (pair_list.T, az_half, rng_half)
+    pairs = pair_list.T
+    lists = jnp.concatenate([pairs, az_half[None], rng_half[None]])
     swap_strips = [(0, 1), (1, 0)]
 
     def images(count):
@@ -561,6 +581,9 @@
         )(values)
         return lax.ppermute(out, "strip", swap_strips)
 
+    def cost(flops):
+        return pl.CostEstimate(flops=flops, bytes_accessed=1, transcendentals=0)
+
     wide = cols // 2
     widths = HALO - REACH_LO + 1
     band_shape = (2, 2 * wide + 2 * TILE, wide)
@@ -570,6 +593,7 @@
         out_shape=jax.ShapeDtypeStruct((widths, *band_shape), jnp.bfloat16),
         out_specs=pl.BlockSpec((1, *band_shape), lambda n: (n, 0, 0, 0)),
         compiler_params=limit(WORK_MIB),
+        cost_estimate=cost(20_000_000_000),
         name="range_bands",
     )()
     if halves:
@@ -596,7 +620,7 @@
             ],
             compiler_params=limit(FIRST_MIB),
             name="early_images",
-        )(slc, lists[0])
+        )(slc, pairs)
         early = lax.ppermute(early, both, on_strip(swap, 0))
         rim = lax.ppermute(rim, "strip", swap_strips)
         inner, outer, more = pl.pallas_call(
@@ -614,16 +638,16 @@
             ],
             compiler_params=limit(WORK_MIB),
             name="beside_images",
-        )(slc, lists[0], rim)
+        )(slc, lists, rim)
         down = [(i, (i - 1) % half) for i in range(half)]
         down += [(half + i, half + (i + 1) % half) for i in range(half)]
-        middle = lax.ppermute(outer, "date", [(half - 1, half), (half, half - 1)])
         more = lax.ppermute(more, both, on_strip(swap, 1))
         strips = lax.ppermute(
             strips, both, [(2 * a + s, 2 * b + 1 - s) for a, b in swap for s in (0, 1)]
         )
+        outgoing = outer
+        outer = lax.ppermute(outer, "date", [(b, a) for a, b in down])
         inner = lax.ppermute(inner, "date", down)
-        outer = lax.ppermute(outer, "date", [(b, a) for a, b in down])
     else:
         rim = swapped_rims(slc)
         annual = arrivals_by_distance(slc, pair_list, plan)
@@ -633,7 +657,6 @@
         outer = payload_of(slc[:, :NEAR], rim[:, :NEAR], strip)
         inner = lax.ppermute(inner, "date", ups)
         outer = lax.ppermute(outer, "date", [(b, a) for a, b in ups])
-        middle = inner
 
     out_shape = jax.ShapeDtypeStruct((planes, dates * per_date, rows, cols), jnp.float32)
     depth = 2 * band_shape[1]
@@ -647,48 +670,54 @@
         pltpu.SemaphoreType.DMA((2, 2)),
     ]
 
-    def cost(flops):
-        return pl.CostEstimate(flops=flops, bytes_accessed=1, transcendentals=0)
+    if halves:
+        payload, middle = pl.pallas_call(
+            functools.partial(late_kernel, plan),
+            out_shape=(payload_shape(late), payload_shape(NEAR)),
+            in_specs=[VMEM, VMEM, VMEM, ANY, SMEM, ANY, ANY],
+            out_specs=(VMEM, VMEM),
+            scratch_shapes=[
+                pltpu.VMEM((late, planes, rows, TILE), dtype),
+                pltpu.SemaphoreType.DMA,
+            ],
+            compiler_params=limit(WORK_MIB),
+            name="late_images",
+        )(slc, rim, inner, outgoing, lists, bands, strips)
+        after = (payload,)
+        middle = lax.ppermute(middle, "date", [(half - 1, half), (half, half - 1)])
+        payload = lax.ppermute(payload, "date", swap)
+    else:
+        after = ()
 
     out, powers = pl.pallas_call(
-        lambda *refs: own_kernel(plan, refs[:3], *refs[3:]),
+        functools.partial(own_kernel, plan),
         out_shape=(out_shape, jax.ShapeDtypeStruct((dates, rows, depth), jnp.bfloat16)),
-        in_specs=[SMEM] * 3 + [VMEM] * 3,
+        in_specs=[SMEM] + [VMEM] * 3 + [ANY] * len(after),
         out_specs=(ANY, VMEM),
         scratch_shapes=scratch,
         compiler_params=limit(WORK_MIB),
-        cost_estimate=cost(20_000_000_000),
+        cost_estimate=cost(1),
         name="own_pairs",
-    )(*lists, slc, rim, bands)
+    )(lists, slc, rim, bands, *after)
 
     def more_pairs(kernel, out, others, name):
         return pl.pallas_call(
-            lambda *refs: kernel(plan, refs[:3], *refs[3:]),
+            functools.partial(kernel, plan),
             out_shape=out_shape,
-            in_specs=[SMEM] * 3 + [VMEM] * (4 + len(others)) + [ANY],
+            in_specs=[SMEM] + [VMEM] * (4 + len(others)) + [ANY],
             out_specs=ANY,
             scratch_shapes=scratch,
-            input_output_aliases={7 + len(others): 0},
+            input_output_aliases={5 + len(others): 0},
             compiler_params=limit(WORK_MIB),
             cost_estimate=cost(1),
             name=name,
-        )(*lists, slc, rim, bands, powers, *others, out)
-
-    if halves:
-        payload = pl.pallas_call(
-            functools.partial(late_kernel, plan),
-            out_shape=payload_shape(late),
-            in_specs=[VMEM, VMEM, VMEM, SMEM, ANY, ANY],
-            out_specs=VMEM,
-            scratch_shapes=[pltpu.VMEM((late, planes, rows, TILE), dtype)],
-            compiler_params=limit(WORK_MIB),
-            name="late_images",
-        )(slc, rim, inner, lists[0], powers, strips)
-        payload = lax.ppermute(payload, "date", swap)
-    out = more_pairs(rest_kernel, out, (inner, outer, middle), "near_pairs")
+        )(lists, slc, rim, bands, powers, *others, out)
+
+    out = more_pairs(rest_kernel, out, (inner, outer), "near_pairs")
     if halves:
         kernel = lambda plan, *refs: annual_kernel(plan, False, *refs)
         out = more_pairs(kernel, out, (inner, outer, early, more, strips), "annual_pairs")
+        out = more_pairs(middle_kernel, out, (middle,), "middle_pairs")
         kernel = lambda plan, *refs: annual_kernel(plan, True, *refs)
         out = more_pairs(kernel, out, (inner, outer, payload, payload, strips), "last_pairs")
     else:

time: 61.6 us -> 59.8 us (0.971)
  the two profiles are of different devices: /device:TPU:16 before, /device:TPU:0 now
where the time goes in v6:
time: 59.8 us; the launch traced here: 59.6 us
  Pallas kernels  24.8 us (41%)
  waiting for transfers between devices  17.2 us (29%)
  starting transfers between devices  15.6 us (26%)
  local copies, waits for them, and re-layouts  1.13 us (2%)
  other arithmetic  0.73 us (1%)
    ppermute x1, waiting for transfers between devices, body(): inner = lax.ppermute(inner, 'date', down)  15.1 us
    pallas_call x1, Pallas kernels, body(): pl.pallas_call(functools.partial(own_kernel, plan), out_shape=(out_shape,...  10.3 us
    pallas_call x4, Pallas kernels, more_pairs(): pl.pallas_call(functools.partial(kernel, plan), out_shape=out_shape, in_s...  7.99 us
    ppermute x1, starting transfers between devices, body(): payload = lax.ppermute(payload, 'date', swap)  5.21 us
    ppermute x1, starting transfers between devices, body(): lax.ppermute(strips, both, [(2 * a + s, 2 * b + 1 - s) for a, b in swap f...  3.99 us
    pallas_call x1, Pallas kernels, body(): pl.pallas_call(functools.partial(early_kernel, plan), out_shape=(images(d...  2.9 us
    ppermute x1, starting transfers between devices, body(): inner = lax.ppermute(inner, 'date', down)  2.81 us
    ppermute x1, waiting for transfers between devices, body(): payload = lax.ppermute(payload, 'date', swap)  2.03 us
  transfers between devices with their start and end apart: 8, of which 2 were waited for; matrix products, arithmetic and copies ran while one was open for 1% of the time, Pallas kernels for 32%

profile of v6, /device:TPU:0, one launch (start us, length us, event | category | flops | bytes accessed | tf_op | source)
XLA Modules:
  0.0 59.6 jit_solution(4403202232472320923)
XLA Ops:
  0.0 2.9 %early_images.1 = (bf16[2,4,64,512]{3,2,1,0:T(8,128)(2,1)}, bf16[2,6,64,128]{3,2,1,0:T(8,128)(2,1)}, bf16[64,128]{1,0:T(8,128)(2,1)}) custom-call(bf16[2,6,64,512]{3,2,1,0:T(8,128)(2,1)} %refs_1_.3, s32[2,192]{1,0:T(2,128)} %bitcast.3), custom_call_target="tpu_custom_call" | custom-call | tf_op jit(solution)/shard_map/early_images/pallas_call | solution.py:606
  2.9 0.3 collective-permute-start
  3.2 4.0 %collective-permute-start.2 = (bf16[64,128]{1,0:T(8,128)(2,1)}, bf16[64,128]{1,0:T(8,128)(2,1)S(1)}, u32[]{:S(2)}, u32[]{:S(2)}) collective-permute-start(bf16[64,128]{1,0:T(8,128)(2,1)} %get-tuple-element.18), channel_id=1, source_target_pairs={{0,9},{1,8},{2,11},{3,10},{4,13},{5,12},{6,15},{7,14},{8,1},{9,0},... | collective-permute-start | bytes 49160 | tf_op jit(solution)/shard_map/ppermute | solution.py:645
  7.2 1.9 %collective-permute-start.6 = (bf16[2,4,64,512]{3,2,1,0:T(8,128)(2,1)}, bf16[2,4,64,512]{3,2,1,0:T(8,128)(2,1)S(1)}, u32[]{:S(2)}, u32[]{:S(2)}) collective-permute-start(bf16[2,4,64,512]{3,2,1,0:T(8,128)(2,1)} %get-tuple-element.22), channel_id=1, source_target_pairs={{0,8},{2,10},{4,12},{6,14},{8,0},{10,2},{12,4},{14,6},{16,24},{18,... | collective-permute-start | bytes 1572872 | tf_op jit(solution)/shard_map/ppermute | solution.py:624
  9.2 0.7 %pad_add_fusion.pairs_ref.lists.refs_0_ = s32[4,192]{1,0:T(4,128)S(1)} fusion(s32[1,192]{1,0:T(1,128)} %bitcast.5, s32[1,192]{1,0:T(1,128)} %bitcast.6, s32[2,192]{1,0:T(2,128)} %bitcast.4), kind=kLoop, calls=%fused_computation | loop fusion | flops 1536 | bytes 6144 | tf_op jit(solution)/shard_map/concatenate | solution.py:560
  9.9 0.0 collective-permute-done.rim_ref.refs_2_
  9.9 0.0 copy-start
  9.9 1.1 %copy-done = bf16[2,6,64,512]{3,2,1,0:T(8,128)(2,1)S(1)} copy-done((bf16[2,6,64,512]{3,2,1,0:T(8,128)(2,1)S(1)}, bf16[2,6,64,512]{3,2,1,0:T(8,128)(2,1)}, u32[]{:S(2)}) %copy-start) | copy-done | bytes 786456
  11.0 1.9 %beside_images.1 = (bf16[400,512]{1,0:T(8,128)(2,1)S(1)}, bf16[400,512]{1,0:T(8,128)(2,1)S(1)}, bf16[2,4,64,512]{3,2,1,0:T(8,128)(2,1)S(1)}) custom-call(bf16[2,6,64,512]{3,2,1,0:T(8,128)(2,1)S(1)} %copy-done, s32[4,192]{1,0:T(4,128)S(1)} %pad_add_fusion.pairs_ref.lists.refs_0_, bf16[2,6,64,128]{3,2,1,0:T(8,128)(2,1)S(1)} %collective-permute-done.rim_ref.refs_2_), custom_call_target="tpu_custom_call" | custom-call | tf_op jit(solution)/shard_map/beside_images/pallas_call | solution.py:626
  13.0 2.8 %collective-permute-start.1 = (bf16[400,512]{1,0:T(8,128)(2,1)S(1)}, bf16[400,512]{1,0:T(8,128)(2,1)S(1)}, u32[]{:S(2)}, u32[]{:S(2)}) collective-permute-start(bf16[400,512]{1,0:T(8,128)(2,1)S(1)} %get-tuple-element.16), channel_id=1, source_target_pairs={{0,6},{2,0},{4,2},{6,4},{8,10},{10,12},{12,14},{14,8},{1,7},{3,1},... | collective-permute-start | bytes 1228808 | tf_op jit(solution)/shard_map/ppermute | solution.py:650
  15.8 0.0 collective-permute-start.3
  15.8 0.7 %collective-permute-start.7 = (bf16[2,4,64,512]{3,2,1,0:T(8,128)(2,1)S(1)}, bf16[2,4,64,512]{3,2,1,0:T(8,128)(2,1)S(1)}, u32[]{:S(2)}, u32[]{:S(2)}) collective-permute-start(bf16[2,4,64,512]{3,2,1,0:T(8,128)(2,1)S(1)} %get-tuple-element.23), channel_id=1, source_target_pairs={{1,9},{3,11},{5,13},{7,15},{9,1},{11,3},{13,5},{15,7},{17,25},{19,... | collective-permute-start | bytes 1572872 | tf_op jit(solution)/shard_map/ppermute | solution.py:644
  16.5 0.5 range_bands.1.refs_0_.bands_ref.refs_3_
  17.0 0.0 collective-permute-done.2.refs_1_.refs_9_
  17.0 15.1 %collective-permute-done.1.inner_ref.refs_5_ = bf16[400,512]{1,0:T(8,128)(2,1)S(1)} collective-permute-done((bf16[400,512]{1,0:T(8,128)(2,1)S(1)}, bf16[400,512]{1,0:T(8,128)(2,1)S(1)}, u32[]{:S(2)}, u32[]{:S(2)}) %collective-permute-start.1) | collective-permute-done | bytes 409632 | tf_op jit(solution)/shard_map/ppermute | solution.py:650
  32.2 1.1 %late_images.1 = (bf16[272,512]{1,0:T(8,128)(2,1)S(1)}, bf16[400,512]{1,0:T(8,128)(2,1)S(1)}) custom-call(bf16[2,6,64,512]{3,2,1,0:T(8,128)(2,1)S(1)} %copy-done, bf16[2,6,64,128]{3,2,1,0:T(8,128)(2,1)S(1)} %collective-permute-done.rim_ref.refs_2_, bf16[400,512]{1,0:T(8,128)(2,1)S(1)} %collective-permute-done.1.inner_ref.refs_5_, ...), custom_call_target="tpu_custom_call" | custom-call | tf_op jit(solution)/shard_map/late_images/pallas_call | solution.py:674
  33.3 0.7 %collective-permute-start.5 = (bf16[400,512]{1,0:T(8,128)(2,1)S(1)}, bf16[400,512]{1,0:T(8,128)(2,1)S(1)}, u32[]{:S(2)}, u32[]{:S(2)}) collective-permute-start(bf16[400,512]{1,0:T(8,128)(2,1)S(1)} %get-tuple-element.21), channel_id=1, source_target_pairs={{6,8},{8,6},{7,9},{9,7},{22,24},{24,22},{23,25},{25,23}} | collective-permute-start | bytes 1228808 | tf_op jit(solution)/shard_map/ppermute | solution.py:687
  34.0 5.2 %collective-permute-start.4 = (bf16[272,512]{1,0:T(8,128)(2,1)S(1)}, bf16[272,512]{1,0:T(8,128)(2,1)S(1)}, u32[]{:S(2)}, u32[]{:S(2)}) collective-permute-start(bf16[272,512]{1,0:T(8,128)(2,1)S(1)} %get-tuple-element.19.refs_0_), channel_id=1, source_target_pairs={{0,8},{2,10},{4,12},{6,14},{8,0},{10,2},{12,4},{14,6},{1,9},{3,11}... | collective-permute-start | bytes 835592 | tf_op jit(solution)/shard_map/ppermute | solution.py:688
  39.2 10.3 %own_pairs.1 = (f32[2,24,64,512]{3,2,1,0:T(8,128)}, bf16[6,64,1536]{2,1,0:T(8,128)(2,1)S(1)}) custom-call(s32[4,192]{1,0:T(4,128)S(1)} %pad_add_fusion.pairs_ref.lists.refs_0_, bf16[2,6,64,512]{3,2,1,0:T(8,128)(2,1)S(1)} %copy-done, bf16[2,6,64,128]{3,2,1,0:T(8,128)(2,1)S(1)} %collective-permute-done.rim_ref.refs_2_, ...), custom_call_target="tpu_custom_call" | custom-call | flops 1 | bytes 1 | tf_op jit(solution)/shard_map/own_pairs/pallas_call | solution.py:692
  49.5 0.0 collective-permute-done.3.outer_ref.refs_6_
  49.6 0.8 %near_pairs.1.refs_10_ = f32[2,24,64,512]{3,2,1,0:T(8,128)} custom-call(s32[4,192]{1,0:T(4,128)S(1)} %pad_add_fusion.pairs_ref.lists.refs_0_, bf16[2,6,64,512]{3,2,1,0:T(8,128)(2,1)S(1)} %copy-done, bf16[2,6,64,128]{3,2,1,0:T(8,128)(2,1)S(1)} %collective-permute-done.rim_ref.refs_2_, ...), custom_call_target="tpu_custom_call", output_to_operand_aliasing={{}: (7, {})} | custom-call | flops 1 | bytes 1 | tf_op jit(solution)/shard_map/near_pairs/pallas_call | solution.py:704
  50.4 0.0 collective-permute-done.6.refs_7_
  50.4 0.0 collective-permute-done.7.refs_8_
  50.4 3.8 %annual_pairs.1._ = f32[2,24,64,512]{3,2,1,0:T(8,128)} custom-call(s32[4,192]{1,0:T(4,128)S(1)} %pad_add_fusion.pairs_ref.lists.refs_0_, bf16[2,6,64,512]{3,2,1,0:T(8,128)(2,1)S(1)} %copy-done, bf16[2,6,64,128]{3,2,1,0:T(8,128)(2,1)S(1)} %collective-permute-done.rim_ref.refs_2_, ...), custom_call_target="tpu_custom_call", output_to_operand_aliasing={{}: (10, {})} | custom-call | flops 1 | bytes 1 | tf_op jit(solution)/shard_map/annual_pairs/pallas_call | solution.py:704
  54.2 0.0 collective-permute-done.5.middle_ref
  54.2 0.8 %middle_pairs.1.refs_10_ = f32[2,24,64,512]{3,2,1,0:T(8,128)} custom-call(s32[4,192]{1,0:T(4,128)S(1)} %pad_add_fusion.pairs_ref.lists.refs_0_, bf16[2,6,64,512]{3,2,1,0:T(8,128)(2,1)S(1)} %copy-done, bf16[2,6,64,128]{3,2,1,0:T(8,128)(2,1)S(1)} %collective-permute-done.rim_ref.refs_2_, ...), custom_call_target="tpu_custom_call", output_to_operand_aliasing={{}: (6, {})} | custom-call | flops 1 | bytes 1 | tf_op jit(solution)/shard_map/middle_pairs/pallas_call | solution.py:704
  55.0 2.0 %collective-permute-done.4.refs_7_.refs_8_ = bf16[272,512]{1,0:T(8,128)(2,1)S(1)} collective-permute-done((bf16[272,512]{1,0:T(8,128)(2,1)S(1)}, bf16[272,512]{1,0:T(8,128)(2,1)S(1)}, u32[]{:S(2)}, u32[]{:S(2)}) %collective-permute-start.4) | collective-permute-done | bytes 278560 | tf_op jit(solution)/shard_map/ppermute | solution.py:688
  57.0 2.6 %last_pairs.1 = f32[2,24,64,512]{3,2,1,0:T(8,128)} custom-call(s32[4,192]{1,0:T(4,128)S(1)} %pad_add_fusion.pairs_ref.lists.refs_0_, bf16[2,6,64,512]{3,2,1,0:T(8,128)(2,1)S(1)} %copy-done, bf16[2,6,64,128]{3,2,1,0:T(8,128)(2,1)S(1)} %collective-permute-done.rim_ref.refs_2_, ...), custom_call_target="tpu_custom_call", output_to_operand_aliasing={{}: (10, {})} | custom-call | flops 1 | bytes 1 | tf_op jit(solution)/shard_map/last_pairs/pallas_call | solution.py:704
Async XLA Ops:
  2.9 7.0 %collective-permute-start = (bf16[2,6,64,128]{3,2,1,0:T(8,128)(2,1)}, bf16[2,6,64,128]{3,2,1,0:T(8,128)(2,1)S(1)}, u32[]{:S(2)}, u32[]{:S(2)}) collective-permute-start(bf16[2,6,64,128]{3,2,1,0:T(8,128)(2,1)} %get-tuple-element.15), channel_id=1, source_target_pairs={{0,1},{1,0},{2,3},{3,2},{4,5},{5,4},{6,7},{7,6},{8,9},{9,8},{10,11... | collective-permute-start | bytes 589832 | tf_op jit(solution)/shard_map/ppermute | solution.py:625
  3.2 13.8 %collective-permute-start.2 = (bf16[64,128]{1,0:T(8,128)(2,1)}, bf16[64,128]{1,0:T(8,128)(2,1)S(1)}, u32[]{:S(2)}, u32[]{:S(2)}) collective-permute-start(bf16[64,128]{1,0:T(8,128)(2,1)} %get-tuple-element.18), channel_id=1, source_target_pairs={{0,9},{1,8},{2,11},{3,10},{4,13},{5,12},{6,15},{7,14},{8,1},{9,0},... | collective-permute-start | bytes 49160 | tf_op jit(solution)/shard_map/ppermute | solution.py:645
  7.2 43.1 %collective-permute-start.6 = (bf16[2,4,64,512]{3,2,1,0:T(8,128)(2,1)}, bf16[2,4,64,512]{3,2,1,0:T(8,128)(2,1)S(1)}, u32[]{:S(2)}, u32[]{:S(2)}) collective-permute-start(bf16[2,4,64,512]{3,2,1,0:T(8,128)(2,1)} %get-tuple-element.22), channel_id=1, source_target_pairs={{0,8},{2,10},{4,12},{6,14},{8,0},{10,2},{12,4},{14,6},{16,24},{18,... | collective-permute-start | bytes 1572872 | tf_op jit(solution)/shard_map/ppermute | solution.py:624
  9.9 1.1 %copy-start = (bf16[2,6,64,512]{3,2,1,0:T(8,128)(2,1)S(1)}, bf16[2,6,64,512]{3,2,1,0:T(8,128)(2,1)}, u32[]{:S(2)}) copy-start(bf16[2,6,64,512]{3,2,1,0:T(8,128)(2,1)} %refs_1_.3) | copy-start | bytes 2359300
  13.0 19.2 %collective-permute-start.1 = (bf16[400,512]{1,0:T(8,128)(2,1)S(1)}, bf16[400,512]{1,0:T(8,128)(2,1)S(1)}, u32[]{:S(2)}, u32[]{:S(2)}) collective-permute-start(bf16[400,512]{1,0:T(8,128)(2,1)S(1)} %get-tuple-element.16), channel_id=1, source_target_pairs={{0,6},{2,0},{4,2},{6,4},{8,10},{10,12},{12,14},{14,8},{1,7},{3,1},... | collective-permute-start | bytes 1228808 | tf_op jit(solution)/shard_map/ppermute | solution.py:650
  15.8 33.8 %collective-permute-start.3 = (bf16[400,512]{1,0:T(8,128)(2,1)S(1)}, bf16[400,512]{1,0:T(8,128)(2,1)S(1)}, u32[]{:S(2)}, u32[]{:S(2)}) collective-permute-start(bf16[400,512]{1,0:T(8,128)(2,1)S(1)} %get-tuple-element.17.outgoing_ref), channel_id=1, source_target_pairs={{6,0},{0,2},{2,4},{4,6},{10,8},{12,10},{14,12},{8,14},{7,1},{1,3},... | collective-permute-start | bytes 1228808 | tf_op jit(solution)/shard_map/ppermute | solution.py:649
  15.8 34.6 %collective-permute-start.7 = (bf16[2,4,64,512]{3,2,1,0:T(8,128)(2,1)S(1)}, bf16[2,4,64,512]{3,2,1,0:T(8,128)(2,1)S(1)}, u32[]{:S(2)}, u32[]{:S(2)}) collective-permute-start(bf16[2,4,64,512]{3,2,1,0:T(8,128)(2,1)S(1)} %get-tuple-element.23), channel_id=1, source_target_pairs={{1,9},{3,11},{5,13},{7,15},{9,1},{11,3},{13,5},{15,7},{17,25},{19,... | collective-permute-start | bytes 1572872 | tf_op jit(solution)/shard_map/ppermute | solution.py:644
  33.3 20.9 %collective-permute-start.5 = (bf16[400,512]{1,0:T(8,128)(2,1)S(1)}, bf16[400,512]{1,0:T(8,128)(2,1)S(1)}, u32[]{:S(2)}, u32[]{:S(2)}) collective-permute-start(bf16[400,512]{1,0:T(8,128)(2,1)S(1)} %get-tuple-element.21), channel_id=1, source_target_pairs={{6,8},{8,6},{7,9},{9,7},{22,24},{24,22},{23,25},{25,23}} | collective-permute-start | bytes 1228808 | tf_op jit(solution)/shard_map/ppermute | solution.py:687
  34.0 23.0 %collective-permute-start.4 = (bf16[272,512]{1,0:T(8,128)(2,1)S(1)}, bf16[272,512]{1,0:T(8,128)(2,1)S(1)}, u32[]{:S(2)}, u32[]{:S(2)}) collective-permute-start(bf16[272,512]{1,0:T(8,128)(2,1)S(1)} %get-tuple-element.19.refs_0_), channel_id=1, source_target_pairs={{0,8},{2,10},{4,12},{6,14},{8,0},{10,2},{12,4},{14,6},{1,9},{3,11}... | collective-permute-start | bytes 835592 | tf_op jit(solution)/shard_map/ppermute | solution.py:688

commit v7 on v6

--- a/solution.py
+++ b/solution.py
@@ -96,24 +96,14 @@
         )
         for k, at in enumerate(wanted)
     ]
-    for copy in tile_copies + [rim_copy]:
+    for copy in tile_copies + [rim_copy] + early_copies:
         copy.start()
-
-    @pl.when(strip == 0)
-    def _():
-        for copy in early_copies:
-            copy.start()
-
     for copy in tile_copies:
         copy.wait()
     tiles = [tiles_ref[k, c] for k in range(len(wanted)) for c in range(2)]
     strips_ref[...] = gather_strips(tiles, 1 - strip)
-    rim_copy.wait()
-
-    @pl.when(strip == 0)
-    def _():
-        for copy in early_copies:
-            copy.wait()
+    for copy in [rim_copy] + early_copies:
+        copy.wait()
 
 
 def rim_kernel(slc_ref, rim_ref, sem):
@@ -122,8 +112,7 @@
     run_copies([pltpu.make_async_copy(slc_ref.at[:, :, :, pl.ds(start, TILE)], rim_ref, sem)])
 
 
-def beside_kernel(plan, slc_ref, pairs_ref, rim_ref, inner_ref, outer_ref, early_ref, sems,
-                  early_sems):
+def beside_kernel(plan, slc_ref, rim_ref, inner_ref, outer_ref, sems):
     me, strip = lax.axis_index("date"), lax.axis_index("strip")
     dates, rows = plan["dates"], plan["rows"]
     upper = me >= plan["devices"] // 2
@@ -139,31 +128,15 @@
                 )
     for copy in copies:
         copy.start()
-    early_copies = image_copies(
-        slc_ref, wanted_images(plan, pairs_ref), early_ref, early_sems
-    )
-
-    @pl.when(strip == 1)
-    def _():
-        for copy in early_copies:
-            copy.start()
-
     for out_ref, first in zip((inner_ref, outer_ref), firsts):
         tiles = [rim_ref[c, first + k] for k in range(NEAR) for c in range(2)]
         write_strips(out_ref, gather_strips(tiles, strip))
     for copy in copies:
         copy.wait()
 
-    @pl.when(strip == 1)
-    def _():
-        for copy in early_copies:
-            copy.wait()
-
-
-def late_kernel(plan, slc_ref, rim_ref, inner_ref, outgoing_ref, pairs_ref, *refs):
-    late_ref, middle_ref, tiles_ref, sem = refs[-4:]
-    copy = pltpu.make_async_copy(outgoing_ref, middle_ref, sem)
-    copy.start()
+
+def late_kernel(plan, slc_ref, rim_ref, inner_ref, pairs_ref, *refs):
+    late_ref, tiles_ref = refs[-2:]
     me, strip = lax.axis_index("date"), lax.axis_index("strip")
     dates, late, rows = plan["dates"], plan["late"], plan["rows"]
     half = plan["devices"] // 2
@@ -192,7 +165,6 @@
 
     tiles = [tiles_ref[k, c] for k in range(late) for c in range(2)]
     write_strips(late_ref, gather_strips(tiles, strip))
-    copy.wait()
 
 
 def bands_kernel(cols, out_ref):
@@ -383,8 +355,7 @@
                 self.stage_ref[stage, x, c] = looked[c] * inverse
 
 
-def own_kernel(plan, lists, slc_ref, rim_ref, bands_ref, *refs):
-    out_ref, powers_ref, *scratch = refs[1 if plan["halves"] else 0 :]
+def own_kernel(plan, lists, slc_ref, rim_ref, bands_ref, out_ref, powers_ref, *scratch):
     pairs = Pairs(plan, lists, slc_ref, rim_ref, bands_ref, powers_ref, out_ref, scratch)
     dates = plan["dates"]
 
@@ -403,8 +374,8 @@
     pairs.run(pairs.near_list(pairs.own), work)
 
 
-def rest_kernel(plan, lists, slc_ref, rim_ref, bands_ref, powers_ref, inner_ref, outer_ref, _,
-                out_ref, *scratch):
+def rest_kernel(plan, lists, slc_ref, rim_ref, bands_ref, powers_ref, inner_ref, outer_ref, _sent,
+                _, out_ref, *scratch):
     pairs = Pairs(plan, lists, slc_ref, rim_ref, bands_ref, powers_ref, out_ref, scratch)
     dates = plan["dates"]
     upper = pairs.me >= plan["devices"] // 2 if plan["halves"] else True
@@ -439,7 +410,7 @@
 
 
 def annual_kernel(plan, is_late, lists, slc_ref, rim_ref, bands_ref, powers_ref, inner_ref,
-                  outer_ref, images_ref, more_ref, strips_ref, _, out_ref, *scratch):
+                  outer_ref, images_ref, strips_ref, _, out_ref, *scratch):
     pairs = Pairs(plan, lists, slc_ref, rim_ref, bands_ref, powers_ref, out_ref, scratch)
     dates, late = plan["dates"], plan["late"]
     half = plan["devices"] // 2
@@ -472,9 +443,7 @@
         if is_late:
             pl.when(near_side)(lambda: fetch(x, images_ref, k))
         else:
-            first = pairs.strip == 0
-            pl.when(near_side & first)(lambda: fetch_early(x, k, images_ref))
-            pl.when(near_side & jnp.logical_not(first))(lambda: fetch_early(x, k, more_ref))
+            pl.when(near_side)(lambda: fetch_early(x, k, images_ref))
         return slot, NEAR, pairs.fetched_other(x), None
 
     pairs.run(count, work)
@@ -593,15 +562,11 @@
         out_shape=jax.ShapeDtypeStruct((widths, *band_shape), jnp.bfloat16),
         out_specs=pl.BlockSpec((1, *band_shape), lambda n: (n, 0, 0, 0)),
         compiler_params=limit(WORK_MIB),
-        cost_estimate=cost(20_000_000_000),
+        cost_estimate=cost(1),
         name="range_bands",
     )()
     if halves:
         swap = [(i, (i + half) % devices) for i in range(devices)]
-
-        def on_strip(route, strip):
-            return [(2 * a + strip, 2 * b + strip) for a, b in route]
-
         both = ("date", "strip")
         early, rim, strips = pl.pallas_call(
             functools.partial(early_kernel, plan),
@@ -621,31 +586,23 @@
             compiler_params=limit(FIRST_MIB),
             name="early_images",
         )(slc, pairs)
-        early = lax.ppermute(early, both, on_strip(swap, 0))
+        early = lax.ppermute(early, "date", swap)
         rim = lax.ppermute(rim, "strip", swap_strips)
-        inner, outer, more = pl.pallas_call(
+        inner, outer = pl.pallas_call(
             functools.partial(beside_kernel, plan),
-            out_shape=(
-                payload_shape(NEAR),
-                payload_shape(NEAR),
-                images(dates - late),
-            ),
-            in_specs=[ANY, SMEM, VMEM],
-            out_specs=(VMEM, VMEM, VMEM),
-            scratch_shapes=[
-                pltpu.SemaphoreType.DMA((2, NEAR, 2)),
-                pltpu.SemaphoreType.DMA((dates - late,)),
-            ],
+            out_shape=(payload_shape(NEAR), payload_shape(NEAR)),
+            in_specs=[ANY, VMEM],
+            out_specs=(VMEM, VMEM),
+            scratch_shapes=[pltpu.SemaphoreType.DMA((2, NEAR, 2))],
             compiler_params=limit(WORK_MIB),
             name="beside_images",
-        )(slc, lists, rim)
+        )(slc, rim)
         down = [(i, (i - 1) % half) for i in range(half)]
         down += [(half + i, half + (i + 1) % half) for i in range(half)]
-        more = lax.ppermute(more, both, on_strip(swap, 1))
         strips = lax.ppermute(
             strips, both, [(2 * a + s, 2 * b + 1 - s) for a, b in swap for s in (0, 1)]
         )
-        outgoing = outer
+        middle = lax.ppermute(outer, "date", [(half - 1, half), (half, half - 1)])
         outer = lax.ppermute(outer, "date", [(b, a) for a, b in down])
         inner = lax.ppermute(inner, "date", down)
     else:
@@ -670,35 +627,16 @@
         pltpu.SemaphoreType.DMA((2, 2)),
     ]
 
-    if halves:
-        payload, middle = pl.pallas_call(
-            functools.partial(late_kernel, plan),
-            out_shape=(payload_shape(late), payload_shape(NEAR)),
-            in_specs=[VMEM, VMEM, VMEM, ANY, SMEM, ANY, ANY],
-            out_specs=(VMEM, VMEM),
-            scratch_shapes=[
-                pltpu.VMEM((late, planes, rows, TILE), dtype),
-                pltpu.SemaphoreType.DMA,
-            ],
-            compiler_params=limit(WORK_MIB),
-            name="late_images",
-        )(slc, rim, inner, outgoing, lists, bands, strips)
-        after = (payload,)
-        middle = lax.ppermute(middle, "date", [(half - 1, half), (half, half - 1)])
-        payload = lax.ppermute(payload, "date", swap)
-    else:
-        after = ()
-
     out, powers = pl.pallas_call(
         functools.partial(own_kernel, plan),
         out_shape=(out_shape, jax.ShapeDtypeStruct((dates, rows, depth), jnp.bfloat16)),
-        in_specs=[SMEM] + [VMEM] * 3 + [ANY] * len(after),
+        in_specs=[SMEM] + [VMEM] * 3,
         out_specs=(ANY, VMEM),
         scratch_shapes=scratch,
         compiler_params=limit(WORK_MIB),
-        cost_estimate=cost(1),
+        cost_estimate=cost(20_000_000_000),
         name="own_pairs",
-    )(lists, slc, rim, bands, *after)
+    )(lists, slc, rim, bands)
 
     def more_pairs(kernel, out, others, name):
         return pl.pallas_call(
@@ -713,13 +651,26 @@
             name=name,
         )(lists, slc, rim, bands, powers, *others, out)
 
-    out = more_pairs(rest_kernel, out, (inner, outer), "near_pairs")
+    if halves:
+        payload = sent = pl.pallas_call(
+            functools.partial(late_kernel, plan),
+            out_shape=payload_shape(late),
+            in_specs=[VMEM, VMEM, VMEM, SMEM, ANY, ANY],
+            out_specs=VMEM,
+            scratch_shapes=[pltpu.VMEM((late, planes, rows, TILE), dtype)],
+            compiler_params=limit(WORK_MIB),
+            name="late_images",
+        )(slc, rim, inner, lists, powers, strips)
+        payload = lax.ppermute(payload, "date", swap)
+    else:
+        sent = inner
+    out = more_pairs(rest_kernel, out, (inner, outer, sent), "near_pairs")
     if halves:
         kernel = lambda plan, *refs: annual_kernel(plan, False, *refs)
-        out = more_pairs(kernel, out, (inner, outer, early, more, strips), "annual_pairs")
+        out = more_pairs(kernel, out, (inner, outer, early, strips), "annual_pairs")
         out = more_pairs(middle_kernel, out, (middle,), "middle_pairs")
         kernel = lambda plan, *refs: annual_kernel(plan, True, *refs)
-        out = more_pairs(kernel, out, (inner, outer, payload, payload, strips), "last_pairs")
+        out = more_pairs(kernel, out, (inner, outer, payload, strips), "last_pairs")
     else:
         out = more_pairs(plain_kernel, out, (annual, swapped_rims(annual)), "annual_pairs")
     return out

time: 59.8 us -> 57 us (0.953)
  waiting for transfers between devices: 17.2 us -> 13.2 us
  Pallas kernels: 24.8 us -> 26.1 us
    ppermute x1, waiting for transfers between devices: 15.1 us -> 4.51 us  [body(): inner = lax.ppermute(inner, 'date', down)]
    ppermute x1, waiting for transfers between devices: 2.03 us -> 8.7 us  [body(): payload = lax.ppermute(payload, 'date', swap)]
    pallas_call x4, Pallas kernels: 7.99 us -> 11 us  [more_pairs(): pl.pallas_call(functools.partial(kernel, plan), out_shape=out_shape, in_s...]
    ppermute x3 -> x2, starting transfers between devices: 3.28 us -> 0.73 us  [the longest x1 0.69 us: body(): middle = lax.ppermute(outer, 'date', [(half - 1, half), (half, half - 1)])]
    ppermute x1, starting transfers between devices: 0.01 us -> 1.82 us  [body(): outer = lax.ppermute(outer, 'date', [(b, a) for a, b in down])]
    ppermute x1, starting transfers between devices: 2.81 us -> 3.86 us  [body(): inner = lax.ppermute(inner, 'date', down)]
    pallas_call x1, Pallas kernels: 10.3 us -> 9.33 us  [body(): pl.pallas_call(functools.partial(own_kernel, plan), out_shape=(out_shape,...]
    pallas_call x1, Pallas kernels: 1.93 us -> 1.24 us  [body(): pl.pallas_call(functools.partial(beside_kernel, plan), out_shape=(payload...]
  transfers between devices with their start and end apart: 8 -> 7, of which waited for: 2 -> 2; matrix products, arithmetic and copies ran while one was open for 1% -> 1% of each run, Pallas kernels for 32% -> 36%
where the time goes in v7:
time: 57 us; the launch traced here: 56.8 us
  Pallas kernels  26.1 us (46%)
  starting transfers between devices  15.5 us (27%)
  waiting for transfers between devices  13.2 us (23%)
  local copies, waits for them, and re-layouts  1.13 us (2%)
  other arithmetic  0.73 us (1%)
    pallas_call x4, Pallas kernels, more_pairs(): pl.pallas_call(functools.partial(kernel, plan), out_shape=out_shape, in_s...  11 us
    pallas_call x1, Pallas kernels, body(): pl.pallas_call(functools.partial(own_kernel, plan), out_shape=(out_shape,...  9.33 us
    ppermute x1, waiting for transfers between devices, body(): payload = lax.ppermute(payload, 'date', swap)  8.7 us
    ppermute x1, starting transfers between devices, body(): payload = lax.ppermute(payload, 'date', swap)  4.91 us
    ppermute x1, waiting for transfers between devices, body(): inner = lax.ppermute(inner, 'date', down)  4.51 us
    ppermute x1, starting transfers between devices, body(): inner = lax.ppermute(inner, 'date', down)  3.86 us
    ppermute x1, starting transfers between devices, body(): lax.ppermute(strips, both, [(2 * a + s, 2 * b + 1 - s) for a, b in swap f...  3.73 us
    pallas_call x1, Pallas kernels, body(): pl.pallas_call(functools.partial(early_kernel, plan), out_shape=(images(d...  2.93 us
  transfers between devices with their start and end apart: 7, of which 2 were waited for; matrix products, arithmetic and copies ran while one was open for 1% of the time, Pallas kernels for 36%

profile of v7, /device:TPU:0, one launch (start us, length us, event | category | flops | bytes accessed | tf_op | source)
XLA Modules:
  0.0 56.8 jit_solution(3569927104713354046)
XLA Ops:
  0.0 2.9 %early_images.1 = (bf16[2,4,64,512]{3,2,1,0:T(8,128)(2,1)}, bf16[2,6,64,128]{3,2,1,0:T(8,128)(2,1)}, bf16[64,128]{1,0:T(8,128)(2,1)}) custom-call(bf16[2,6,64,512]{3,2,1,0:T(8,128)(2,1)} %refs_1_.3, s32[2,192]{1,0:T(2,128)} %bitcast.3), custom_call_target="tpu_custom_call" | custom-call | tf_op jit(solution)/shard_map/early_images/pallas_call | solution.py:571
  2.9 0.5 collective-permute-start
  3.4 3.7 %collective-permute-start.3 = (bf16[64,128]{1,0:T(8,128)(2,1)}, bf16[64,128]{1,0:T(8,128)(2,1)S(1)}, u32[]{:S(2)}, u32[]{:S(2)}) collective-permute-start(bf16[64,128]{1,0:T(8,128)(2,1)} %get-tuple-element.16), channel_id=1, source_target_pairs={{0,9},{1,8},{2,11},{3,10},{4,13},{5,12},{6,15},{7,14},{8,1},{9,0},... | collective-permute-start | bytes 49160 | tf_op jit(solution)/shard_map/ppermute | solution.py:602
  7.1 0.0 collective-permute-start.6
  7.2 0.5 range_bands.1.bands_ref.refs_3_
  7.7 0.7 %pad_add_fusion.lists.pairs_ref.refs_0_ = s32[4,192]{1,0:T(4,128)S(1)} fusion(s32[1,192]{1,0:T(1,128)} %bitcast.5, s32[1,192]{1,0:T(1,128)} %bitcast.6, s32[2,192]{1,0:T(2,128)} %bitcast.4), kind=kLoop, calls=%fused_computation | loop fusion | flops 1536 | bytes 6144 | tf_op jit(solution)/shard_map/concatenate | solution.py:529
  8.5 0.0 collective-permute-done.rim_ref.refs_2_
  8.5 0.0 copy-start
  8.5 1.1 %copy-done = bf16[2,6,64,512]{3,2,1,0:T(8,128)(2,1)S(1)} copy-done((bf16[2,6,64,512]{3,2,1,0:T(8,128)(2,1)S(1)}, bf16[2,6,64,512]{3,2,1,0:T(8,128)(2,1)}, u32[]{:S(2)}) %copy-start) | copy-done | bytes 786456
  9.6 1.2 %beside_images.1 = (bf16[400,512]{1,0:T(8,128)(2,1)S(1)}, bf16[400,512]{1,0:T(8,128)(2,1)S(1)}) custom-call(bf16[2,6,64,512]{3,2,1,0:T(8,128)(2,1)S(1)} %copy-done, bf16[2,6,64,128]{3,2,1,0:T(8,128)(2,1)S(1)} %collective-permute-done.rim_ref.refs_2_), custom_call_target="tpu_custom_call" | custom-call | tf_op jit(solution)/shard_map/beside_images/pallas_call | solution.py:591
  10.8 0.7 %collective-permute-start.5 = (bf16[400,512]{1,0:T(8,128)(2,1)S(1)}, bf16[400,512]{1,0:T(8,128)(2,1)S(1)}, u32[]{:S(2)}, u32[]{:S(2)}) collective-permute-start(bf16[400,512]{1,0:T(8,128)(2,1)S(1)} %get-tuple-element.15), channel_id=1, source_target_pairs={{6,8},{8,6},{7,9},{9,7},{22,24},{24,22},{23,25},{25,23}} | collective-permute-start | bytes 1228808 | tf_op jit(solution)/shard_map/ppermute | solution.py:605
  11.5 1.8 %collective-permute-start.2 = (bf16[400,512]{1,0:T(8,128)(2,1)S(1)}, bf16[400,512]{1,0:T(8,128)(2,1)S(1)}, u32[]{:S(2)}, u32[]{:S(2)}) collective-permute-start(bf16[400,512]{1,0:T(8,128)(2,1)S(1)} %get-tuple-element.15), channel_id=1, source_target_pairs={{6,0},{0,2},{2,4},{4,6},{10,8},{12,10},{14,12},{8,14},{7,1},{1,3},... | collective-permute-start | bytes 1228808 | tf_op jit(solution)/shard_map/ppermute | solution.py:606
  13.4 3.9 %collective-permute-start.1 = (bf16[400,512]{1,0:T(8,128)(2,1)S(1)}, bf16[400,512]{1,0:T(8,128)(2,1)S(1)}, u32[]{:S(2)}, u32[]{:S(2)}) collective-permute-start(bf16[400,512]{1,0:T(8,128)(2,1)S(1)} %get-tuple-element.14), channel_id=1, source_target_pairs={{0,6},{2,0},{4,2},{6,4},{8,10},{10,12},{12,14},{14,8},{1,7},{3,1},... | collective-permute-start | bytes 1228808 | tf_op jit(solution)/shard_map/ppermute | solution.py:607
  17.2 9.3 %own_pairs.1 = (f32[2,24,64,512]{3,2,1,0:T(8,128)}, bf16[6,64,1536]{2,1,0:T(8,128)(2,1)S(1)}) custom-call(s32[4,192]{1,0:T(4,128)S(1)} %pad_add_fusion.lists.pairs_ref.refs_0_, bf16[2,6,64,512]{3,2,1,0:T(8,128)(2,1)S(1)} %copy-done, bf16[2,6,64,128]{3,2,1,0:T(8,128)(2,1)S(1)} %collective-permute-done.rim_ref.refs_2_, ...), custom_call_target="tpu_custom_call" | custom-call | flops 20000000000 | bytes 1 | tf_op jit(solution)/shard_map/own_pairs/pallas_call | solution.py:630
  26.6 0.0 collective-permute-done.3.refs_1_.refs_8_
  26.6 4.5 %collective-permute-done.1.inner_ref.refs_5_ = bf16[400,512]{1,0:T(8,128)(2,1)S(1)} collective-permute-done((bf16[400,512]{1,0:T(8,128)(2,1)S(1)}, bf16[400,512]{1,0:T(8,128)(2,1)S(1)}, u32[]{:S(2)}, u32[]{:S(2)}) %collective-permute-start.1) | collective-permute-done | bytes 409632 | tf_op jit(solution)/shard_map/ppermute | solution.py:607
  31.1 1.0 %late_images.1._sent = bf16[272,512]{1,0:T(8,128)(2,1)S(1)} custom-call(bf16[2,6,64,512]{3,2,1,0:T(8,128)(2,1)S(1)} %copy-done, bf16[2,6,64,128]{3,2,1,0:T(8,128)(2,1)S(1)} %collective-permute-done.rim_ref.refs_2_, bf16[400,512]{1,0:T(8,128)(2,1)S(1)} %collective-permute-done.1.inner_ref.refs_5_, s32[4,192]{1,0:T(4,128)S(1)} %pad_add_fusion.lists.pairs_ref.refs_0_, ...), custom_call_target="tpu_custom_call" | custom-call | tf_op jit(solution)/shard_map/late_images/pallas_call | solution.py:655
  32.1 4.9 %collective-permute-start.4 = (bf16[272,512]{1,0:T(8,128)(2,1)S(1)}, bf16[272,512]{1,0:T(8,128)(2,1)S(1)}, u32[]{:S(2)}, u32[]{:S(2)}) collective-permute-start(bf16[272,512]{1,0:T(8,128)(2,1)S(1)} %late_images.1._sent), channel_id=1, source_target_pairs={{0,8},{2,10},{4,12},{6,14},{8,0},{10,2},{12,4},{14,6},{1,9},{3,11}... | collective-permute-start | bytes 835592 | tf_op jit(solution)/shard_map/ppermute | solution.py:664
  37.0 0.0 collective-permute-done.2.outer_ref.refs_6_
  37.0 3.9 %near_pairs.1.refs_9_ = f32[2,24,64,512]{3,2,1,0:T(8,128)} custom-call(s32[4,192]{1,0:T(4,128)S(1)} %pad_add_fusion.lists.pairs_ref.refs_0_, bf16[2,6,64,512]{3,2,1,0:T(8,128)(2,1)S(1)} %copy-done, bf16[2,6,64,128]{3,2,1,0:T(8,128)(2,1)S(1)} %collective-permute-done.rim_ref.refs_2_, ...), custom_call_target="tpu_custom_call", output_to_operand_aliasing={{}: (8, {})} | custom-call | flops 1 | bytes 1 | tf_op jit(solution)/shard_map/near_pairs/pallas_call | solution.py:642
  40.9 0.0 collective-permute-done.6.refs_7_
  40.9 3.8 %annual_pairs.1._ = f32[2,24,64,512]{3,2,1,0:T(8,128)} custom-call(s32[4,192]{1,0:T(4,128)S(1)} %pad_add_fusion.lists.pairs_ref.refs_0_, bf16[2,6,64,512]{3,2,1,0:T(8,128)(2,1)S(1)} %copy-done, bf16[2,6,64,128]{3,2,1,0:T(8,128)(2,1)S(1)} %collective-permute-done.rim_ref.refs_2_, ...), custom_call_target="tpu_custom_call", output_to_operand_aliasing={{}: (9, {})} | custom-call | flops 1 | bytes 1 | tf_op jit(solution)/shard_map/annual_pairs/pallas_call | solution.py:642
  44.7 0.0 collective-permute-done.5.middle_ref
  44.7 0.8 %middle_pairs.1.refs_9_ = f32[2,24,64,512]{3,2,1,0:T(8,128)} custom-call(s32[4,192]{1,0:T(4,128)S(1)} %pad_add_fusion.lists.pairs_ref.refs_0_, bf16[2,6,64,512]{3,2,1,0:T(8,128)(2,1)S(1)} %copy-done, bf16[2,6,64,128]{3,2,1,0:T(8,128)(2,1)S(1)} %collective-permute-done.rim_ref.refs_2_, ...), custom_call_target="tpu_custom_call", output_to_operand_aliasing={{}: (6, {})} | custom-call | flops 1 | bytes 1 | tf_op jit(solution)/shard_map/middle_pairs/pallas_call | solution.py:642
  45.5 8.7 %collective-permute-done.4.refs_7_ = bf16[272,512]{1,0:T(8,128)(2,1)S(1)} collective-permute-done((bf16[272,512]{1,0:T(8,128)(2,1)S(1)}, bf16[272,512]{1,0:T(8,128)(2,1)S(1)}, u32[]{:S(2)}, u32[]{:S(2)}) %collective-permute-start.4) | collective-permute-done | bytes 278560 | tf_op jit(solution)/shard_map/ppermute | solution.py:664
  54.2 2.6 %last_pairs.1 = f32[2,24,64,512]{3,2,1,0:T(8,128)} custom-call(s32[4,192]{1,0:T(4,128)S(1)} %pad_add_fusion.lists.pairs_ref.refs_0_, bf16[2,6,64,512]{3,2,1,0:T(8,128)(2,1)S(1)} %copy-done, bf16[2,6,64,128]{3,2,1,0:T(8,128)(2,1)S(1)} %collective-permute-done.rim_ref.refs_2_, ...), custom_call_target="tpu_custom_call", output_to_operand_aliasing={{}: (9, {})} | custom-call | flops 1 | bytes 1 | tf_op jit(solution)/shard_map/last_pairs/pallas_call | solution.py:642
Async XLA Ops:
  2.9 5.5 %collective-permute-start = (bf16[2,6,64,128]{3,2,1,0:T(8,128)(2,1)}, bf16[2,6,64,128]{3,2,1,0:T(8,128)(2,1)S(1)}, u32[]{:S(2)}, u32[]{:S(2)}) collective-permute-start(bf16[2,6,64,128]{3,2,1,0:T(8,128)(2,1)} %get-tuple-element.12), channel_id=1, source_target_pairs={{0,1},{1,0},{2,3},{3,2},{4,5},{5,4},{6,7},{7,6},{8,9},{9,8},{10,11... | collective-permute-start | bytes 589832 | tf_op jit(solution)/shard_map/ppermute | solution.py:590
  3.4 23.1 %collective-permute-start.3 = (bf16[64,128]{1,0:T(8,128)(2,1)}, bf16[64,128]{1,0:T(8,128)(2,1)S(1)}, u32[]{:S(2)}, u32[]{:S(2)}) collective-permute-start(bf16[64,128]{1,0:T(8,128)(2,1)} %get-tuple-element.16), channel_id=1, source_target_pairs={{0,9},{1,8},{2,11},{3,10},{4,13},{5,12},{6,15},{7,14},{8,1},{9,0},... | collective-permute-start | bytes 49160 | tf_op jit(solution)/shard_map/ppermute | solution.py:602
  7.1 33.7 %collective-permute-start.6 = (bf16[2,4,64,512]{3,2,1,0:T(8,128)(2,1)}, bf16[2,4,64,512]{3,2,1,0:T(8,128)(2,1)S(1)}, u32[]{:S(2)}, u32[]{:S(2)}) collective-permute-start(bf16[2,4,64,512]{3,2,1,0:T(8,128)(2,1)} %get-tuple-element.17), channel_id=1, source_target_pairs={{0,8},{2,10},{4,12},{6,14},{8,0},{10,2},{12,4},{14,6},{1,9},{3,11}... | collective-permute-start | bytes 1572872 | tf_op jit(solution)/shard_map/ppermute | solution.py:589
  8.5 1.1 %copy-start = (bf16[2,6,64,512]{3,2,1,0:T(8,128)(2,1)S(1)}, bf16[2,6,64,512]{3,2,1,0:T(8,128)(2,1)}, u32[]{:S(2)}) copy-start(bf16[2,6,64,512]{3,2,1,0:T(8,128)(2,1)} %refs_1_.3) | copy-start | bytes 2359300
  10.8 33.9 %collective-permute-start.5 = (bf16[400,512]{1,0:T(8,128)(2,1)S(1)}, bf16[400,512]{1,0:T(8,128)(2,1)S(1)}, u32[]{:S(2)}, u32[]{:S(2)}) collective-permute-start(bf16[400,512]{1,0:T(8,128)(2,1)S(1)} %get-tuple-element.15), channel_id=1, source_target_pairs={{6,8},{8,6},{7,9},{9,7},{22,24},{24,22},{23,25},{25,23}} | collective-permute-start | bytes 1228808 | tf_op jit(solution)/shard_map/ppermute | solution.py:605
  11.5 25.5 %collective-permute-start.2 = (bf16[400,512]{1,0:T(8,128)(2,1)S(1)}, bf16[400,512]{1,0:T(8,128)(2,1)S(1)}, u32[]{:S(2)}, u32[]{:S(2)}) collective-permute-start(bf16[400,512]{1,0:T(8,128)(2,1)S(1)} %get-tuple-element.15), channel_id=1, source_target_pairs={{6,0},{0,2},{2,4},{4,6},{10,8},{12,10},{14,12},{8,14},{7,1},{1,3},... | collective-permute-start | bytes 1228808 | tf_op jit(solution)/shard_map/ppermute | solution.py:606
  13.4 17.7 %collective-permute-start.1 = (bf16[400,512]{1,0:T(8,128)(2,1)S(1)}, bf16[400,512]{1,0:T(8,128)(2,1)S(1)}, u32[]{:S(2)}, u32[]{:S(2)}) collective-permute-start(bf16[400,512]{1,0:T(8,128)(2,1)S(1)} %get-tuple-element.14), channel_id=1, source_target_pairs={{0,6},{2,0},{4,2},{6,4},{8,10},{10,12},{12,14},{14,8},{1,7},{3,1},... | collective-permute-start | bytes 1228808 | tf_op jit(solution)/shard_map/ppermute | solution.py:607
  32.1 22.1 %collective-permute-start.4 = (bf16[272,512]{1,0:T(8,128)(2,1)S(1)}, bf16[272,512]{1,0:T(8,128)(2,1)S(1)}, u32[]{:S(2)}, u32[]{:S(2)}) collective-permute-start(bf16[272,512]{1,0:T(8,128)(2,1)S(1)} %late_images.1._sent), channel_id=1, source_target_pairs={{0,8},{2,10},{4,12},{6,14},{8,0},{10,2},{12,4},{14,6},{1,9},{3,11}... | collective-permute-start | bytes 835592 | tf_op jit(solution)/shard_map/ppermute | solution.py:664

commit v8 on v7

--- a/solution.py
+++ b/solution.py
@@ -135,8 +135,10 @@
         copy.wait()
 
 
-def late_kernel(plan, slc_ref, rim_ref, inner_ref, pairs_ref, *refs):
-    late_ref, tiles_ref = refs[-2:]
+def late_kernel(plan, slc_ref, rim_ref, inner_ref, held_ref, pairs_ref, *refs):
+    late_ref, outer_ref, tiles_ref, sem = refs[-4:]
+    copy = pltpu.make_async_copy(held_ref, outer_ref, sem)
+    copy.start()
     me, strip = lax.axis_index("date"), lax.axis_index("strip")
     dates, late, rows = plan["dates"], plan["late"], plan["rows"]
     half = plan["devices"] // 2
@@ -165,6 +167,7 @@
 
     tiles = [tiles_ref[k, c] for k in range(late) for c in range(2)]
     write_strips(late_ref, gather_strips(tiles, strip))
+    copy.wait()
 
 
 def bands_kernel(cols, out_ref):
@@ -374,8 +377,8 @@
     pairs.run(pairs.near_list(pairs.own), work)
 
 
-def rest_kernel(plan, lists, slc_ref, rim_ref, bands_ref, powers_ref, inner_ref, outer_ref, _sent,
-                _, out_ref, *scratch):
+def rest_kernel(plan, lists, slc_ref, rim_ref, bands_ref, powers_ref, inner_ref, outer_ref,
+                middle_ref, _, out_ref, *scratch):
     pairs = Pairs(plan, lists, slc_ref, rim_ref, bands_ref, powers_ref, out_ref, scratch)
     dates = plan["dates"]
     upper = pairs.me >= plan["devices"] // 2 if plan["halves"] else True
@@ -384,33 +387,21 @@
         slot, kind, local = pairs.near_item(pairs.list_ref[n])
         below = local < 0
         index = jnp.clip(jnp.where(below, local + NEAR, local - dates), 0, NEAR - 1)
-        inner = below == upper
-        pl.when(inner)(lambda: pairs.fetch_payload(x, inner_ref, index))
-        pl.when(jnp.logical_not(inner))(lambda: pairs.fetch_payload(x, outer_ref, index))
+        inner, middle = below == upper, pairs.in_middle(local)
+        sources = (
+            (jnp.logical_not(inner), outer_ref),
+            (inner & jnp.logical_not(middle), inner_ref),
+            (inner & middle, middle_ref),
+        )
+        for chosen, ref in sources:
+            pl.when(chosen)(functools.partial(pairs.fetch_payload, x, ref, index))
         return slot, kind, pairs.fetched_other(x), None
 
-    def chosen(local):
-        return jnp.logical_not(pairs.own(local) | pairs.in_middle(local))
-
-    pairs.run(pairs.near_list(chosen), work)
-
-
-def middle_kernel(plan, lists, slc_ref, rim_ref, bands_ref, powers_ref, middle_ref, _, out_ref,
-                  *scratch):
-    pairs = Pairs(plan, lists, slc_ref, rim_ref, bands_ref, powers_ref, out_ref, scratch)
-    dates = plan["dates"]
-
-    def work(x, n):
-        slot, kind, local = pairs.near_item(pairs.list_ref[n])
-        index = jnp.clip(jnp.where(local < 0, local + NEAR, local - dates), 0, NEAR - 1)
-        pairs.fetch_payload(x, middle_ref, index)
-        return slot, kind, pairs.fetched_other(x), None
-
-    pairs.run(pairs.near_list(pairs.in_middle), work)
-
-
-def annual_kernel(plan, is_late, lists, slc_ref, rim_ref, bands_ref, powers_ref, inner_ref,
-                  outer_ref, images_ref, strips_ref, _, out_ref, *scratch):
+    pairs.run(pairs.near_list(lambda local: jnp.logical_not(pairs.own(local))), work)
+
+
+def annual_kernel(plan, lists, slc_ref, rim_ref, bands_ref, powers_ref, ring_ref,
+                  images_ref, strips_ref, _, out_ref, *scratch, is_late):
     pairs = Pairs(plan, lists, slc_ref, rim_ref, bands_ref, powers_ref, out_ref, scratch)
     dates, late = plan["dates"], plan["late"]
     half = plan["devices"] // 2
@@ -432,13 +423,14 @@
         date = me * dates + slot
         other = pairs.partner(date * plan["per_date"] + NEAR)
         far = (other < split_date) == lower
-        from_inner = jnp.where(lower, me != 0, me == half)
-        inner_at = jnp.where(lower, other, other - (2 * split_date - NEAR))
-        outer_at = jnp.where(lower, other - (split_date - NEAR), other - split_date)
-        inner_at, outer_at = jnp.clip(inner_at, 0, NEAR - 1), jnp.clip(outer_at, 0, NEAR - 1)
+        end = 2 * split_date
+        if is_late:
+            ring_at = jnp.where(lower, other - (split_date - NEAR), other - split_date)
+        else:
+            ring_at = jnp.where(lower, other, other - (end - NEAR))
+        ring_at = jnp.clip(ring_at, 0, NEAR - 1)
         fetch = pairs.fetch_payload
-        pl.when(far & from_inner)(lambda: fetch(x, inner_ref, inner_at))
-        pl.when(far & jnp.logical_not(from_inner))(lambda: fetch(x, outer_ref, outer_at))
+        pl.when(far)(lambda: fetch(x, ring_ref, ring_at))
         near_side = jnp.logical_not(far)
         if is_late:
             pl.when(near_side)(lambda: fetch(x, images_ref, k))
@@ -603,7 +595,6 @@
             strips, both, [(2 * a + s, 2 * b + 1 - s) for a, b in swap for s in (0, 1)]
         )
         middle = lax.ppermute(outer, "date", [(half - 1, half), (half, half - 1)])
-        outer = lax.ppermute(outer, "date", [(b, a) for a, b in down])
         inner = lax.ppermute(inner, "date", down)
     else:
         rim = swapped_rims(slc)
@@ -652,26 +643,28 @@
         )(lists, slc, rim, bands, powers, *others, out)
 
     if halves:
-        payload = sent = pl.pallas_call(
+        payload, outer = pl.pallas_call(
             functools.partial(late_kernel, plan),
-            out_shape=payload_shape(late),
-            in_specs=[VMEM, VMEM, VMEM, SMEM, ANY, ANY],
-            out_specs=VMEM,
-            scratch_shapes=[pltpu.VMEM((late, planes, rows, TILE), dtype)],
+            out_shape=(payload_shape(late), payload_shape(NEAR)),
+            in_specs=[VMEM, VMEM, VMEM, ANY, SMEM, ANY, ANY],
+            out_specs=(VMEM, VMEM),
+            scratch_shapes=[
+                pltpu.VMEM((late, planes, rows, TILE), dtype),
+                pltpu.SemaphoreType.DMA,
+            ],
             compiler_params=limit(WORK_MIB),
             name="late_images",
-        )(slc, rim, inner, lists, powers, strips)
+        )(slc, rim, inner, outer, lists, powers, strips)
         payload = lax.ppermute(payload, "date", swap)
+        outer = lax.ppermute(outer, "date", [(b, a) for a, b in down])
+    if halves:
+        early_pairs = functools.partial(annual_kernel, is_late=False)
+        out = more_pairs(early_pairs, out, (inner, early, strips), "annual_pairs")
+        out = more_pairs(rest_kernel, out, (inner, outer, middle), "near_pairs")
+        late_pairs = functools.partial(annual_kernel, is_late=True)
+        out = more_pairs(late_pairs, out, (outer, payload, strips), "last_pairs")
     else:
-        sent = inner
-    out = more_pairs(rest_kernel, out, (inner, outer, sent), "near_pairs")
-    if halves:
-        kernel = lambda plan, *refs: annual_kernel(plan, False, *refs)
-        out = more_pairs(kernel, out, (inner, outer, early, strips), "annual_pairs")
-        out = more_pairs(middle_kernel, out, (middle,), "middle_pairs")
-        kernel = lambda plan, *refs: annual_kernel(plan, True, *refs)
-        out = more_pairs(kernel, out, (inner, outer, payload, strips), "last_pairs")
-    else:
+        out = more_pairs(rest_kernel, out, (inner, outer, inner), "near_pairs")
         out = more_pairs(plain_kernel, out, (annual, swapped_rims(annual)), "annual_pairs")
     return out
 

time: 57 us -> 57.9 us (1.016)
  the two profiles are of different devices: /device:TPU:0 before, /device:TPU:8 now
where the time goes in v8:
time: 57.9 us; the launch traced here: 57.1 us
  Pallas kernels  26 us (45%)
  starting transfers between devices  20.2 us (35%)
  waiting for transfers between devices  8.96 us (15%)
  local copies, waits for them, and re-layouts  1.13 us (2%)
  other arithmetic  0.73 us (1%)
    pallas_call x3, Pallas kernels, more_pairs(): pl.pallas_call(functools.partial(kernel, plan), out_shape=out_shape, in_s...  13.7 us
    ppermute x1, starting transfers between devices, body(): outer = lax.ppermute(outer, 'date', [(b, a) for a, b in down])  8.43 us
    ppermute x1, starting transfers between devices, body(): payload = lax.ppermute(payload, 'date', swap)  6.53 us
    pallas_call x1, Pallas kernels, body(): pl.pallas_call(functools.partial(own_kernel, plan), out_shape=(out_shape,...  6.5 us
    ppermute x1, waiting for transfers between devices, body(): outer = lax.ppermute(outer, 'date', [(b, a) for a, b in down])  6.36 us
    pallas_call x1, Pallas kernels, body(): pl.pallas_call(functools.partial(early_kernel, plan), out_shape=(images(d...  2.89 us
    ppermute x1, starting transfers between devices, body(): lax.ppermute(strips, both, [(2 * a + s, 2 * b + 1 - s) for a, b in swap f...  2.71 us
    ppermute x1, waiting for transfers between devices, body(): inner = lax.ppermute(inner, 'date', down)  2.6 us
  transfers between devices with their start and end apart: 7, of which 2 were waited for; matrix products, arithmetic and copies ran while one was open for 1% of the time, Pallas kernels for 36%

profile of v8, /device:TPU:8, one launch (start us, length us, event | category | flops | bytes accessed | tf_op | source)
XLA Modules:
  0.0 57.1 jit_solution(16066415043650334621)
XLA Ops:
  0.0 2.9 %early_images.1 = (bf16[2,4,64,512]{3,2,1,0:T(8,128)(2,1)}, bf16[2,6,64,128]{3,2,1,0:T(8,128)(2,1)}, bf16[64,128]{1,0:T(8,128)(2,1)}) custom-call(bf16[2,6,64,512]{3,2,1,0:T(8,128)(2,1)} %slc_ref.13, s32[2,192]{1,0:T(2,128)} %bitcast.3), custom_call_target="tpu_custom_call" | custom-call | tf_op jit(solution)/shard_map/early_images/pallas_call | solution.py:563
  2.9 0.1 collective-permute-start
  3.0 2.7 %collective-permute-start.2 = (bf16[64,128]{1,0:T(8,128)(2,1)}, bf16[64,128]{1,0:T(8,128)(2,1)S(1)}, u32[]{:S(2)}, u32[]{:S(2)}) collective-permute-start(bf16[64,128]{1,0:T(8,128)(2,1)} %get-tuple-element.18), channel_id=1, source_target_pairs={{0,9},{1,8},{2,11},{3,10},{4,13},{5,12},{6,15},{7,14},{8,1},{9,0},... | collective-permute-start | bytes 49160 | tf_op jit(solution)/shard_map/ppermute | solution.py:594
  5.7 0.3 collective-permute-start.6
  6.0 0.5 range_bands.1.bands_ref
  6.6 0.7 %pad_add_fusion.lists.pairs_ref = s32[4,192]{1,0:T(4,128)S(1)} fusion(s32[1,192]{1,0:T(1,128)} %bitcast.5, s32[1,192]{1,0:T(1,128)} %bitcast.6, s32[2,192]{1,0:T(2,128)} %bitcast.4), kind=kLoop, calls=%fused_computation | loop fusion | flops 1536 | bytes 6144 | tf_op jit(solution)/shard_map/concatenate | solution.py:521
  7.3 0.0 collective-permute-done.rim_ref
  7.3 0.0 copy-start
  7.3 1.1 %copy-done = bf16[2,6,64,512]{3,2,1,0:T(8,128)(2,1)S(1)} copy-done((bf16[2,6,64,512]{3,2,1,0:T(8,128)(2,1)S(1)}, bf16[2,6,64,512]{3,2,1,0:T(8,128)(2,1)}, u32[]{:S(2)}) %copy-start) | copy-done | bytes 786456
  8.4 1.2 %beside_images.1 = (bf16[400,512]{1,0:T(8,128)(2,1)S(1)}, bf16[400,512]{1,0:T(8,128)(2,1)S(1)}) custom-call(bf16[2,6,64,512]{3,2,1,0:T(8,128)(2,1)S(1)} %copy-done, bf16[2,6,64,128]{3,2,1,0:T(8,128)(2,1)S(1)} %collective-permute-done.rim_ref), custom_call_target="tpu_custom_call" | custom-call | tf_op jit(solution)/shard_map/beside_images/pallas_call | solution.py:583
  9.7 1.4 %collective-permute-start.1 = (bf16[400,512]{1,0:T(8,128)(2,1)S(1)}, bf16[400,512]{1,0:T(8,128)(2,1)S(1)}, u32[]{:S(2)}, u32[]{:S(2)}) collective-permute-start(bf16[400,512]{1,0:T(8,128)(2,1)S(1)} %get-tuple-element.16), channel_id=1, source_target_pairs={{0,6},{2,0},{4,2},{6,4},{8,10},{10,12},{12,14},{14,8},{1,7},{3,1},... | collective-permute-start | bytes 1228808 | tf_op jit(solution)/shard_map/ppermute | solution.py:598
  11.1 0.7 %collective-permute-start.5 = (bf16[400,512]{1,0:T(8,128)(2,1)S(1)}, bf16[400,512]{1,0:T(8,128)(2,1)S(1)}, u32[]{:S(2)}, u32[]{:S(2)}) collective-permute-start(bf16[400,512]{1,0:T(8,128)(2,1)S(1)} %get-tuple-element.17.held_ref), channel_id=1, source_target_pairs={{6,8},{8,6},{7,9},{9,7},{22,24},{24,22},{23,25},{25,23}} | collective-permute-start | bytes 1228808 | tf_op jit(solution)/shard_map/ppermute | solution.py:597
  11.8 6.5 %own_pairs.1 = (f32[2,24,64,512]{3,2,1,0:T(8,128)}, bf16[6,64,1536]{2,1,0:T(8,128)(2,1)S(1)}) custom-call(s32[4,192]{1,0:T(4,128)S(1)} %pad_add_fusion.lists.pairs_ref, bf16[2,6,64,512]{3,2,1,0:T(8,128)(2,1)S(1)} %copy-done, bf16[2,6,64,128]{3,2,1,0:T(8,128)(2,1)S(1)} %collective-permute-done.rim_ref, bf16[5,2,768,256]{3,2,1,0:T(8,128)(2,1)S(1)} %range_bands.1.bands_ref), custom_call_target="tpu_custom_call" | custom-call | flops 20000000000 | bytes 1 | tf_op jit(solution)/shard_map/own_pairs/pallas_call | solution.py:621
  18.3 0.0 collective-permute-done.2.refs_1_.strips_ref
  18.3 2.6 %collective-permute-done.1.inner_ref.ring_ref = bf16[400,512]{1,0:T(8,128)(2,1)S(1)} collective-permute-done((bf16[400,512]{1,0:T(8,128)(2,1)S(1)}, bf16[400,512]{1,0:T(8,128)(2,1)S(1)}, u32[]{:S(2)}, u32[]{:S(2)}) %collective-permute-start.1) | collective-permute-done | bytes 409632 | tf_op jit(solution)/shard_map/ppermute | solution.py:598
  20.9 1.1 %late_images.1 = (bf16[272,512]{1,0:T(8,128)(2,1)S(1)}, bf16[400,512]{1,0:T(8,128)(2,1)S(1)}) custom-call(bf16[2,6,64,512]{3,2,1,0:T(8,128)(2,1)S(1)} %copy-done, bf16[2,6,64,128]{3,2,1,0:T(8,128)(2,1)S(1)} %collective-permute-done.rim_ref, bf16[400,512]{1,0:T(8,128)(2,1)S(1)} %collective-permute-done.1.inner_ref.ring_ref, ...), custom_call_target="tpu_custom_call" | custom-call | tf_op jit(solution)/shard_map/late_images/pallas_call | solution.py:646
  22.0 8.4 %collective-permute-start.3 = (bf16[400,512]{1,0:T(8,128)(2,1)S(1)}, bf16[400,512]{1,0:T(8,128)(2,1)S(1)}, u32[]{:S(2)}, u32[]{:S(2)}) collective-permute-start(bf16[400,512]{1,0:T(8,128)(2,1)S(1)} %get-tuple-element.19), channel_id=1, source_target_pairs={{6,0},{0,2},{2,4},{4,6},{10,8},{12,10},{14,12},{8,14},{7,1},{1,3},... | collective-permute-start | bytes 1228808 | tf_op jit(solution)/shard_map/ppermute | solution.py:659
  30.4 6.5 %collective-permute-start.4 = (bf16[272,512]{1,0:T(8,128)(2,1)S(1)}, bf16[272,512]{1,0:T(8,128)(2,1)S(1)}, u32[]{:S(2)}, u32[]{:S(2)}) collective-permute-start(bf16[272,512]{1,0:T(8,128)(2,1)S(1)} %get-tuple-element.20), channel_id=1, source_target_pairs={{0,8},{2,10},{4,12},{6,14},{8,0},{10,2},{12,4},{14,6},{1,9},{3,11}... | collective-permute-start | bytes 835592 | tf_op jit(solution)/shard_map/ppermute | solution.py:658
  37.0 0.0 collective-permute-done.6.images_ref
  37.0 3.8 %annual_pairs.1._ = f32[2,24,64,512]{3,2,1,0:T(8,128)} custom-call(s32[4,192]{1,0:T(4,128)S(1)} %pad_add_fusion.lists.pairs_ref, bf16[2,6,64,512]{3,2,1,0:T(8,128)(2,1)S(1)} %copy-done, bf16[2,6,64,128]{3,2,1,0:T(8,128)(2,1)S(1)} %collective-permute-done.rim_ref, bf16[5,2,768,256]{3,2,1,0:T(8,128)(2,1)S(1)} %range_bands.1.bands_ref, ...), custom_call_target="tpu_custom_call", output_to_operand_aliasing={{}: (8, {})} | custom-call | flops 1 | bytes 1 | tf_op jit(solution)/shard_map/annual_pairs/pallas_call | solution.py:633
  40.7 0.0 collective-permute-done.5.middle_ref
  40.8 6.4 %collective-permute-done.3.outer_ref.ring_ref = bf16[400,512]{1,0:T(8,128)(2,1)S(1)} collective-permute-done((bf16[400,512]{1,0:T(8,128)(2,1)S(1)}, bf16[400,512]{1,0:T(8,128)(2,1)S(1)}, u32[]{:S(2)}, u32[]{:S(2)}) %collective-permute-start.3) | collective-permute-done | bytes 409632 | tf_op jit(solution)/shard_map/ppermute | solution.py:659
  47.1 7.3 %near_pairs.1._ = f32[2,24,64,512]{3,2,1,0:T(8,128)} custom-call(s32[4,192]{1,0:T(4,128)S(1)} %pad_add_fusion.lists.pairs_ref, bf16[2,6,64,512]{3,2,1,0:T(8,128)(2,1)S(1)} %copy-done, bf16[2,6,64,128]{3,2,1,0:T(8,128)(2,1)S(1)} %collective-permute-done.rim_ref, bf16[5,2,768,256]{3,2,1,0:T(8,128)(2,1)S(1)} %range_bands.1.bands_ref, ...), custom_call_target="tpu_custom_call", output_to_operand_aliasing={{}: (8, {})} | custom-call | flops 1 | bytes 1 | tf_op jit(solution)/shard_map/near_pairs/pallas_call | solution.py:633
  54.5 0.0 collective-permute-done.4.images_ref
  54.5 2.6 %last_pairs.1 = f32[2,24,64,512]{3,2,1,0:T(8,128)} custom-call(s32[4,192]{1,0:T(4,128)S(1)} %pad_add_fusion.lists.pairs_ref, bf16[2,6,64,512]{3,2,1,0:T(8,128)(2,1)S(1)} %copy-done, bf16[2,6,64,128]{3,2,1,0:T(8,128)(2,1)S(1)} %collective-permute-done.rim_ref, bf16[5,2,768,256]{3,2,1,0:T(8,128)(2,1)S(1)} %range_bands.1.bands_ref, ...), custom_call_target="tpu_custom_call", output_to_operand_aliasing={{}: (8, {})} | custom-call | flops 1 | bytes 1 | tf_op jit(solution)/shard_map/last_pairs/pallas_call | solution.py:633
Async XLA Ops:
  2.9 4.4 %collective-permute-start = (bf16[2,6,64,128]{3,2,1,0:T(8,128)(2,1)}, bf16[2,6,64,128]{3,2,1,0:T(8,128)(2,1)S(1)}, u32[]{:S(2)}, u32[]{:S(2)}) collective-permute-start(bf16[2,6,64,128]{3,2,1,0:T(8,128)(2,1)} %get-tuple-element.14), channel_id=1, source_target_pairs={{0,1},{1,0},{2,3},{3,2},{4,5},{5,4},{6,7},{7,6},{8,9},{9,8},{10,11... | collective-permute-start | bytes 589832 | tf_op jit(solution)/shard_map/ppermute | solution.py:582
  3.0 15.3 %collective-permute-start.2 = (bf16[64,128]{1,0:T(8,128)(2,1)}, bf16[64,128]{1,0:T(8,128)(2,1)S(1)}, u32[]{:S(2)}, u32[]{:S(2)}) collective-permute-start(bf16[64,128]{1,0:T(8,128)(2,1)} %get-tuple-element.18), channel_id=1, source_target_pairs={{0,9},{1,8},{2,11},{3,10},{4,13},{5,12},{6,15},{7,14},{8,1},{9,0},... | collective-permute-start | bytes 49160 | tf_op jit(solution)/shard_map/ppermute | solution.py:594
  5.7 31.3 %collective-permute-start.6 = (bf16[2,4,64,512]{3,2,1,0:T(8,128)(2,1)}, bf16[2,4,64,512]{3,2,1,0:T(8,128)(2,1)S(1)}, u32[]{:S(2)}, u32[]{:S(2)}) collective-permute-start(bf16[2,4,64,512]{3,2,1,0:T(8,128)(2,1)} %get-tuple-element.21), channel_id=1, source_target_pairs={{0,8},{2,10},{4,12},{6,14},{8,0},{10,2},{12,4},{14,6},{1,9},{3,11}... | collective-permute-start | bytes 1572872 | tf_op jit(solution)/shard_map/ppermute | solution.py:581
  7.3 1.1 %copy-start = (bf16[2,6,64,512]{3,2,1,0:T(8,128)(2,1)S(1)}, bf16[2,6,64,512]{3,2,1,0:T(8,128)(2,1)}, u32[]{:S(2)}) copy-start(bf16[2,6,64,512]{3,2,1,0:T(8,128)(2,1)} %slc_ref.13) | copy-start | bytes 2359300
  9.7 11.2 %collective-permute-start.1 = (bf16[400,512]{1,0:T(8,128)(2,1)S(1)}, bf16[400,512]{1,0:T(8,128)(2,1)S(1)}, u32[]{:S(2)}, u32[]{:S(2)}) collective-permute-start(bf16[400,512]{1,0:T(8,128)(2,1)S(1)} %get-tuple-element.16), channel_id=1, source_target_pairs={{0,6},{2,0},{4,2},{6,4},{8,10},{10,12},{12,14},{14,8},{1,7},{3,1},... | collective-permute-start | bytes 1228808 | tf_op jit(solution)/shard_map/ppermute | solution.py:598
  11.1 29.6 %collective-permute-start.5 = (bf16[400,512]{1,0:T(8,128)(2,1)S(1)}, bf16[400,512]{1,0:T(8,128)(2,1)S(1)}, u32[]{:S(2)}, u32[]{:S(2)}) collective-permute-start(bf16[400,512]{1,0:T(8,128)(2,1)S(1)} %get-tuple-element.17.held_ref), channel_id=1, source_target_pairs={{6,8},{8,6},{7,9},{9,7},{22,24},{24,22},{23,25},{25,23}} | collective-permute-start | bytes 1228808 | tf_op jit(solution)/shard_map/ppermute | solution.py:597
  22.0 25.1 %collective-permute-start.3 = (bf16[400,512]{1,0:T(8,128)(2,1)S(1)}, bf16[400,512]{1,0:T(8,128)(2,1)S(1)}, u32[]{:S(2)}, u32[]{:S(2)}) collective-permute-start(bf16[400,512]{1,0:T(8,128)(2,1)S(1)} %get-tuple-element.19), channel_id=1, source_target_pairs={{6,0},{0,2},{2,4},{4,6},{10,8},{12,10},{14,12},{8,14},{7,1},{1,3},... | collective-permute-start | bytes 1228808 | tf_op jit(solution)/shard_map/ppermute | solution.py:659
  30.4 24.0 %collective-permute-start.4 = (bf16[272,512]{1,0:T(8,128)(2,1)S(1)}, bf16[272,512]{1,0:T(8,128)(2,1)S(1)}, u32[]{:S(2)}, u32[]{:S(2)}) collective-permute-start(bf16[272,512]{1,0:T(8,128)(2,1)S(1)} %get-tuple-element.20), channel_id=1, source_target_pairs={{0,8},{2,10},{4,12},{6,14},{8,0},{10,2},{12,4},{14,6},{1,9},{3,11}... | collective-permute-start | bytes 835592 | tf_op jit(solution)/shard_map/ppermute | solution.py:658

commit v9 on v8

--- a/solution.py
+++ b/solution.py
@@ -14,6 +14,7 @@
 EPSILON = 1e-06
 TILE = 128
 INNER = TILE // 2
+PER_TILE = TILE // HALO
 PARTNER, HEIGHT, REACH = 1, 2, 3
 WORK_MIB = 16
 FIRST_MIB = 56
@@ -83,26 +84,28 @@
     ]
 
 
-def early_kernel(plan, slc_ref, pairs_ref, early_ref, rim_ref, strips_ref, tiles_ref, sems,
-                 tile_sems, rim_sem):
+def gather_all(tiles, side):
+    return [gather_strips(tiles[n * PER_TILE : (n + 1) * PER_TILE], side) for n in range(2)]
+
+
+def early_kernel(plan, slc_ref, pairs_ref, early_ref, packed_ref, strips_ref, tiles_ref, sems,
+                 tile_sem):
     strip, cols = lax.axis_index("strip"), plan["cols"]
     start = pl.multiple_of(jnp.where(strip == 0, cols - TILE, 0), TILE)
     wanted = wanted_images(plan, pairs_ref)
-    rim_copy = pltpu.make_async_copy(slc_ref.at[:, :, :, pl.ds(start, TILE)], rim_ref, rim_sem)
+    tile_copy = pltpu.make_async_copy(
+        slc_ref.at[:, :, :, pl.ds(start, TILE)], tiles_ref, tile_sem
+    )
     early_copies = image_copies(slc_ref, wanted, early_ref, sems)
-    tile_copies = [
-        pltpu.make_async_copy(
-            slc_ref.at[:, at, :, pl.ds(start, TILE)], tiles_ref.at[k], tile_sems.at[k]
-        )
-        for k, at in enumerate(wanted)
-    ]
-    for copy in tile_copies + [rim_copy] + early_copies:
+    for copy in [tile_copy] + early_copies:
         copy.start()
-    for copy in tile_copies:
-        copy.wait()
-    tiles = [tiles_ref[k, c] for k in range(len(wanted)) for c in range(2)]
+    tile_copy.wait()
+    tiles = [tiles_ref[c, k] for k in range(plan["dates"]) for c in range(2)]
+    for n, packed in enumerate(gather_all(tiles, 1 - strip)):
+        packed_ref[n] = packed
+    tiles = [tiles_ref[c, at] for at in wanted for c in range(2)]
     strips_ref[...] = gather_strips(tiles, 1 - strip)
-    for copy in [rim_copy] + early_copies:
+    for copy in early_copies:
         copy.wait()
 
 
@@ -112,7 +115,7 @@
     run_copies([pltpu.make_async_copy(slc_ref.at[:, :, :, pl.ds(start, TILE)], rim_ref, sem)])
 
 
-def beside_kernel(plan, slc_ref, rim_ref, inner_ref, outer_ref, sems):
+def beside_kernel(plan, slc_ref, packed_ref, inner_ref, outer_ref, rim_ref, sems):
     me, strip = lax.axis_index("date"), lax.axis_index("strip")
     dates, rows = plan["dates"], plan["rows"]
     upper = me >= plan["devices"] // 2
@@ -128,6 +131,10 @@
                 )
     for copy in copies:
         copy.start()
+    for k in range(dates):
+        for c in range(2):
+            tile, n = divmod(2 * k + c, PER_TILE)
+            rim_ref[c, k] = place_strip(packed_ref[tile], n, strip)
     for out_ref, first in zip((inner_ref, outer_ref), firsts):
         tiles = [rim_ref[c, first + k] for k in range(NEAR) for c in range(2)]
         write_strips(out_ref, gather_strips(tiles, strip))
@@ -135,7 +142,7 @@
         copy.wait()
 
 
-def late_kernel(plan, slc_ref, rim_ref, inner_ref, held_ref, pairs_ref, *refs):
+def late_kernel(plan, slc_ref, rim_ref, inner_ref, middle_ref, held_ref, pairs_ref, *refs):
     late_ref, outer_ref, tiles_ref, sem = refs[-4:]
     copy = pltpu.make_async_copy(held_ref, outer_ref, sem)
     copy.start()
@@ -144,7 +151,7 @@
     half = plan["devices"] // 2
     mate = lax.rem(me + half, 2 * half)
     mate_slot = jnp.where(mate < half, 0, dates - late)
-    packed = read_strips(inner_ref, rows)
+    in_middle = (me == half) | (me == half - 1)
     for k in range(late):
         date = mate * dates + mate_slot + k
         wanted = pairs_ref[PARTNER, date * plan["per_date"] + NEAR] - me * dates
@@ -159,11 +166,14 @@
                 late_ref[here] = slc_ref[c, own_at]
                 tiles_ref[k, c] = rim_ref[c, own_at]
 
-            @pl.when(jnp.logical_not(own))
-            def _():
-                there = pl.multiple_of((2 * other_at + c) * rows, rows)
-                late_ref[here] = inner_ref[pl.ds(there, rows)]
-                tiles_ref[k, c] = place_strip(packed, 2 * other_at + c, strip)
+            for chosen, ref in ((in_middle, middle_ref), (jnp.logical_not(in_middle), inner_ref)):
+
+                @pl.when(chosen & jnp.logical_not(own))
+                def _():
+                    there = pl.multiple_of((2 * other_at + c) * rows, rows)
+                    late_ref[here] = ref[pl.ds(there, rows)]
+                    packed = read_strips(ref, rows)
+                    tiles_ref[k, c] = place_strip(packed, 2 * other_at + c, strip)
 
     tiles = [tiles_ref[k, c] for k in range(late) for c in range(2)]
     write_strips(late_ref, gather_strips(tiles, strip))
@@ -422,20 +432,14 @@
         slot = base + k
         date = me * dates + slot
         other = pairs.partner(date * plan["per_date"] + NEAR)
-        far = (other < split_date) == lower
-        end = 2 * split_date
         if is_late:
-            ring_at = jnp.where(lower, other - (split_date - NEAR), other - split_date)
+            pairs.fetch_payload(x, images_ref, k)
         else:
-            ring_at = jnp.where(lower, other, other - (end - NEAR))
-        ring_at = jnp.clip(ring_at, 0, NEAR - 1)
-        fetch = pairs.fetch_payload
-        pl.when(far)(lambda: fetch(x, ring_ref, ring_at))
-        near_side = jnp.logical_not(far)
-        if is_late:
-            pl.when(near_side)(lambda: fetch(x, images_ref, k))
-        else:
-            pl.when(near_side)(lambda: fetch_early(x, k, images_ref))
+            far = (other < split_date) == lower
+            ring_at = jnp.where(lower, other, other - (2 * split_date - NEAR))
+            ring_at = jnp.clip(ring_at, 0, NEAR - 1)
+            pl.when(far)(lambda: pairs.fetch_payload(x, ring_ref, ring_at))
+            pl.when(jnp.logical_not(far))(lambda: fetch_early(x, k, images_ref))
         return slot, NEAR, pairs.fetched_other(x), None
 
     pairs.run(count, work)
@@ -503,7 +507,7 @@
     half = devices // 2
     late = half * dates - year
     halves = devices % 2 == 0 and 0 < late <= NEAR and 2 * late <= dates
-    halves = halves and 2 * (dates - late) * HALO <= TILE
+    halves = halves and dates - late <= PER_TILE // 2 and dates <= PER_TILE
     plan = {
         "dates": dates,
         "devices": devices,
@@ -560,18 +564,17 @@
     if halves:
         swap = [(i, (i + half) % devices) for i in range(devices)]
         both = ("date", "strip")
-        early, rim, strips = pl.pallas_call(
+        early, packed, strips = pl.pallas_call(
             functools.partial(early_kernel, plan),
             out_shape=(
                 images(dates - late),
-                rim_shape(dates),
+                jax.ShapeDtypeStruct((2, rows, TILE), dtype),
                 jax.ShapeDtypeStruct((rows, TILE), dtype),
             ),
             in_specs=[ANY, SMEM],
             out_specs=(VMEM, VMEM, VMEM),
             scratch_shapes=[
-                pltpu.VMEM((dates - late, planes, rows, TILE), dtype),
-                pltpu.SemaphoreType.DMA((dates - late,)),
+                pltpu.VMEM((planes, dates, rows, TILE), dtype),
                 pltpu.SemaphoreType.DMA((dates - late,)),
                 pltpu.SemaphoreType.DMA,
             ],
@@ -579,16 +582,16 @@
             name="early_images",
         )(slc, pairs)
         early = lax.ppermute(early, "date", swap)
-        rim = lax.ppermute(rim, "strip", swap_strips)
-        inner, outer = pl.pallas_call(
+        packed = lax.ppermute(packed, "strip", swap_strips)
+        inner, outer, rim = pl.pallas_call(
             functools.partial(beside_kernel, plan),
-            out_shape=(payload_shape(NEAR), payload_shape(NEAR)),
+            out_shape=(payload_shape(NEAR), payload_shape(NEAR), rim_shape(dates)),
             in_specs=[ANY, VMEM],
-            out_specs=(VMEM, VMEM),
+            out_specs=(VMEM, VMEM, VMEM),
             scratch_shapes=[pltpu.SemaphoreType.DMA((2, NEAR, 2))],
             compiler_params=limit(WORK_MIB),
             name="beside_images",
-        )(slc, rim)
+        )(slc, packed)
         down = [(i, (i - 1) % half) for i in range(half)]
         down += [(half + i, half + (i + 1) % half) for i in range(half)]
         strips = lax.ppermute(
@@ -646,7 +649,7 @@
         payload, outer = pl.pallas_call(
             functools.partial(late_kernel, plan),
             out_shape=(payload_shape(late), payload_shape(NEAR)),
-            in_specs=[VMEM, VMEM, VMEM, ANY, SMEM, ANY, ANY],
+            in_specs=[VMEM, VMEM, VMEM, VMEM, ANY, SMEM, ANY, ANY],
             out_specs=(VMEM, VMEM),
             scratch_shapes=[
                 pltpu.VMEM((late, planes, rows, TILE), dtype),
@@ -654,15 +657,16 @@
             ],
             compiler_params=limit(WORK_MIB),
             name="late_images",
-        )(slc, rim, inner, outer, lists, powers, strips)
+        )(slc, rim, inner, middle, outer, lists, powers, strips)
+        up = [(b, a) for a, b in down if b not in (half - 1, half)]
+        outer = lax.ppermute(outer, "date", up)
         payload = lax.ppermute(payload, "date", swap)
-        outer = lax.ppermute(outer, "date", [(b, a) for a, b in down])
     if halves:
         early_pairs = functools.partial(annual_kernel, is_late=False)
         out = more_pairs(early_pairs, out, (inner, early, strips), "annual_pairs")
         out = more_pairs(rest_kernel, out, (inner, outer, middle), "near_pairs")
         late_pairs = functools.partial(annual_kernel, is_late=True)
-        out = more_pairs(late_pairs, out, (outer, payload, strips), "last_pairs")
+        out = more_pairs(late_pairs, out, (inner, payload, strips), "last_pairs")
     else:
         out = more_pairs(rest_kernel, out, (inner, outer, inner), "near_pairs")
         out = more_pairs(plain_kernel, out, (annual, swapped_rims(annual)), "annual_pairs")

time: 57.9 us -> 62.2 us (1.074)
  the two profiles are of different devices: /device:TPU:8 before, /device:TPU:0 now
where the time goes in v9:
time: 62.2 us; the launch traced here: 61.8 us
  starting transfers between devices  25.2 us (41%)
  Pallas kernels  24.6 us (40%)
  waiting for transfers between devices  10.2 us (16%)
  local copies, waits for them, and re-layouts  1.13 us (2%)
  other arithmetic  0.72 us (1%)
    pallas_call x3, Pallas kernels, more_pairs(): pl.pallas_call(functools.partial(kernel, plan), out_shape=out_shape, in_s...  11.3 us
    ppermute x1, starting transfers between devices, body(): payload = lax.ppermute(payload, 'date', swap)  9.45 us
    ppermute x1, starting transfers between devices, body(): outer = lax.ppermute(outer, 'date', up)  7.91 us
    pallas_call x1, Pallas kernels, body(): pl.pallas_call(functools.partial(own_kernel, plan), out_shape=(out_shape,...  7.52 us
    ppermute x1, waiting for transfers between devices, body(): inner = lax.ppermute(inner, 'date', down)  6.18 us
    ppermute x1, waiting for transfers between devices, body(): payload = lax.ppermute(payload, 'date', swap)  3.97 us
    ppermute x1, starting transfers between devices, body(): lax.ppermute(strips, both, [(2 * a + s, 2 * b + 1 - s) for a, b in swap f...  3.71 us
    ppermute x1, starting transfers between devices, body(): inner = lax.ppermute(inner, 'date', down)  2.85 us
  transfers between devices with their start and end apart: 7, of which 2 were waited for; matrix products, arithmetic and copies ran while one was open for 1% of the time, Pallas kernels for 31%

profile of v9, /device:TPU:0, one launch (start us, length us, event | category | flops | bytes accessed | tf_op | source)
XLA Modules:
  0.0 61.8 jit_solution(5210985071667517705)
XLA Ops:
  0.0 2.8 %early_images.1 = (bf16[2,4,64,512]{3,2,1,0:T(8,128)(2,1)}, bf16[2,64,128]{2,1,0:T(8,128)(2,1)}, bf16[64,128]{1,0:T(8,128)(2,1)}) custom-call(bf16[2,6,64,512]{3,2,1,0:T(8,128)(2,1)} %slc_ref.13, s32[2,192]{1,0:T(2,128)} %bitcast.3), custom_call_target="tpu_custom_call" | custom-call | tf_op jit(solution)/shard_map/early_images/pallas_call | solution.py:567
  2.8 0.5 collective-permute-start
  3.3 3.7 %collective-permute-start.3 = (bf16[64,128]{1,0:T(8,128)(2,1)}, bf16[64,128]{1,0:T(8,128)(2,1)S(1)}, u32[]{:S(2)}, u32[]{:S(2)}) collective-permute-start(bf16[64,128]{1,0:T(8,128)(2,1)} %get-tuple-element.20), channel_id=1, source_target_pairs={{0,9},{1,8},{2,11},{3,10},{4,13},{5,12},{6,15},{7,14},{8,1},{9,0},... | collective-permute-start | bytes 49160 | tf_op jit(solution)/shard_map/ppermute | solution.py:597
  7.0 0.0 collective-permute-start.6
  7.0 0.7 %pad_add_fusion.lists.pairs_ref = s32[4,192]{1,0:T(4,128)S(1)} fusion(s32[1,192]{1,0:T(1,128)} %bitcast.5, s32[1,192]{1,0:T(1,128)} %bitcast.6, s32[2,192]{1,0:T(2,128)} %bitcast.4), kind=kLoop, calls=%fused_computation | loop fusion | flops 1536 | bytes 6144 | tf_op jit(solution)/shard_map/concatenate | solution.py:525
  7.8 0.5 range_bands.1.bands_ref
  8.3 0.0 collective-permute-done.packed_ref
  8.3 0.0 copy-start
  8.3 1.1 %copy-done = bf16[2,6,64,512]{3,2,1,0:T(8,128)(2,1)S(1)} copy-done((bf16[2,6,64,512]{3,2,1,0:T(8,128)(2,1)S(1)}, bf16[2,6,64,512]{3,2,1,0:T(8,128)(2,1)}, u32[]{:S(2)}) %copy-start) | copy-done | bytes 786456
  9.4 1.4 %beside_images.1 = (bf16[400,512]{1,0:T(8,128)(2,1)S(1)}, bf16[400,512]{1,0:T(8,128)(2,1)S(1)}, bf16[2,6,64,128]{3,2,1,0:T(8,128)(2,1)S(1)}) custom-call(bf16[2,6,64,512]{3,2,1,0:T(8,128)(2,1)S(1)} %copy-done, bf16[2,64,128]{2,1,0:T(8,128)(2,1)S(1)} %collective-permute-done.packed_ref), custom_call_target="tpu_custom_call" | custom-call | tf_op jit(solution)/shard_map/beside_images/pallas_call | solution.py:586
  10.8 2.9 %collective-permute-start.1 = (bf16[400,512]{1,0:T(8,128)(2,1)S(1)}, bf16[400,512]{1,0:T(8,128)(2,1)S(1)}, u32[]{:S(2)}, u32[]{:S(2)}) collective-permute-start(bf16[400,512]{1,0:T(8,128)(2,1)S(1)} %get-tuple-element.18), channel_id=1, source_target_pairs={{0,6},{2,0},{4,2},{6,4},{8,10},{10,12},{12,14},{14,8},{1,7},{3,1},... | collective-permute-start | bytes 1228808 | tf_op jit(solution)/shard_map/ppermute | solution.py:601
  13.7 0.7 %collective-permute-start.2 = (bf16[400,512]{1,0:T(8,128)(2,1)S(1)}, bf16[400,512]{1,0:T(8,128)(2,1)S(1)}, u32[]{:S(2)}, u32[]{:S(2)}) collective-permute-start(bf16[400,512]{1,0:T(8,128)(2,1)S(1)} %get-tuple-element.19.held_ref), channel_id=1, source_target_pairs={{6,8},{8,6},{7,9},{9,7},{22,24},{24,22},{23,25},{25,23}} | collective-permute-start | bytes 1228808 | tf_op jit(solution)/shard_map/ppermute | solution.py:600
  14.3 7.5 %own_pairs.1 = (f32[2,24,64,512]{3,2,1,0:T(8,128)}, bf16[6,64,1536]{2,1,0:T(8,128)(2,1)S(1)}) custom-call(s32[4,192]{1,0:T(4,128)S(1)} %pad_add_fusion.lists.pairs_ref, bf16[2,6,64,512]{3,2,1,0:T(8,128)(2,1)S(1)} %copy-done, bf16[2,6,64,128]{3,2,1,0:T(8,128)(2,1)S(1)} %get-tuple-element.16.rim_ref, bf16[5,2,768,256]{3,2,1,0:T(8,128)(2,1)S(1)} %range_bands.1.bands_ref), custom_call_target="tpu_custom_call" | custom-call | flops 20000000000 | bytes 1 | tf_op jit(solution)/shard_map/own_pairs/pallas_call | solution.py:624
  21.9 0.0 collective-permute-done.3.refs_1_.strips_ref
  21.9 6.2 %collective-permute-done.1.inner_ref.ring_ref = bf16[400,512]{1,0:T(8,128)(2,1)S(1)} collective-permute-done((bf16[400,512]{1,0:T(8,128)(2,1)S(1)}, bf16[400,512]{1,0:T(8,128)(2,1)S(1)}, u32[]{:S(2)}, u32[]{:S(2)}) %collective-permute-start.1) | collective-permute-done | bytes 409632 | tf_op jit(solution)/shard_map/ppermute | solution.py:601
  28.1 0.0 collective-permute-done.2.middle_ref
  28.1 1.1 %late_images.1 = (bf16[272,512]{1,0:T(8,128)(2,1)S(1)}, bf16[400,512]{1,0:T(8,128)(2,1)S(1)}) custom-call(bf16[2,6,64,512]{3,2,1,0:T(8,128)(2,1)S(1)} %copy-done, bf16[2,6,64,128]{3,2,1,0:T(8,128)(2,1)S(1)} %get-tuple-element.16.rim_ref, bf16[400,512]{1,0:T(8,128)(2,1)S(1)} %collective-permute-done.1.inner_ref.ring_ref, ...), custom_call_target="tpu_custom_call" | custom-call | tf_op jit(solution)/shard_map/late_images/pallas_call | solution.py:649
  29.2 7.9 %collective-permute-start.5 = (bf16[400,512]{1,0:T(8,128)(2,1)S(1)}, bf16[400,512]{1,0:T(8,128)(2,1)S(1)}, u32[]{:S(2)}, u32[]{:S(2)}) collective-permute-start(bf16[400,512]{1,0:T(8,128)(2,1)S(1)} %get-tuple-element.22), channel_id=1, source_target_pairs={{0,2},{2,4},{4,6},{10,8},{12,10},{14,12},{1,3},{3,5},{5,7},{11,9},... | collective-permute-start | bytes 1228808 | tf_op jit(solution)/shard_map/ppermute | solution.py:662
  37.1 9.4 %collective-permute-start.4 = (bf16[272,512]{1,0:T(8,128)(2,1)S(1)}, bf16[272,512]{1,0:T(8,128)(2,1)S(1)}, u32[]{:S(2)}, u32[]{:S(2)}) collective-permute-start(bf16[272,512]{1,0:T(8,128)(2,1)S(1)} %get-tuple-element.21), channel_id=1, source_target_pairs={{0,8},{2,10},{4,12},{6,14},{8,0},{10,2},{12,4},{14,6},{1,9},{3,11}... | collective-permute-start | bytes 835592 | tf_op jit(solution)/shard_map/ppermute | solution.py:663
  46.6 0.0 collective-permute-done.6.images_ref
  46.6 3.8 %annual_pairs.1._ = f32[2,24,64,512]{3,2,1,0:T(8,128)} custom-call(s32[4,192]{1,0:T(4,128)S(1)} %pad_add_fusion.lists.pairs_ref, bf16[2,6,64,512]{3,2,1,0:T(8,128)(2,1)S(1)} %copy-done, bf16[2,6,64,128]{3,2,1,0:T(8,128)(2,1)S(1)} %get-tuple-element.16.rim_ref, bf16[5,2,768,256]{3,2,1,0:T(8,128)(2,1)S(1)} %range_bands.1.bands_ref, ...), custom_call_target="tpu_custom_call", output_to_operand_aliasing={{}: (8, {})} | custom-call | flops 1 | bytes 1 | tf_op jit(solution)/shard_map/annual_pairs/pallas_call | solution.py:636
  50.4 0.0 collective-permute-done.5.outer_ref
  50.4 5.1 %near_pairs.1._ = f32[2,24,64,512]{3,2,1,0:T(8,128)} custom-call(s32[4,192]{1,0:T(4,128)S(1)} %pad_add_fusion.lists.pairs_ref, bf16[2,6,64,512]{3,2,1,0:T(8,128)(2,1)S(1)} %copy-done, bf16[2,6,64,128]{3,2,1,0:T(8,128)(2,1)S(1)} %get-tuple-element.16.rim_ref, bf16[5,2,768,256]{3,2,1,0:T(8,128)(2,1)S(1)} %range_bands.1.bands_ref, ...), custom_call_target="tpu_custom_call", output_to_operand_aliasing={{}: (8, {})} | custom-call | flops 1 | bytes 1 | tf_op jit(solution)/shard_map/near_pairs/pallas_call | solution.py:636
  55.5 4.0 %collective-permute-done.4.images_ref = bf16[272,512]{1,0:T(8,128)(2,1)S(1)} collective-permute-done((bf16[272,512]{1,0:T(8,128)(2,1)S(1)}, bf16[272,512]{1,0:T(8,128)(2,1)S(1)}, u32[]{:S(2)}, u32[]{:S(2)}) %collective-permute-start.4) | collective-permute-done | bytes 278560 | tf_op jit(solution)/shard_map/ppermute | solution.py:663
  59.4 2.4 %last_pairs.1 = f32[2,24,64,512]{3,2,1,0:T(8,128)} custom-call(s32[4,192]{1,0:T(4,128)S(1)} %pad_add_fusion.lists.pairs_ref, bf16[2,6,64,512]{3,2,1,0:T(8,128)(2,1)S(1)} %copy-done, bf16[2,6,64,128]{3,2,1,0:T(8,128)(2,1)S(1)} %get-tuple-element.16.rim_ref, bf16[5,2,768,256]{3,2,1,0:T(8,128)(2,1)S(1)} %range_bands.1.bands_ref, ...), custom_call_target="tpu_custom_call", output_to_operand_aliasing={{}: (8, {})} | custom-call | flops 1 | bytes 1 | tf_op jit(solution)/shard_map/last_pairs/pallas_call | solution.py:636
Async XLA Ops:
  2.8 5.5 %collective-permute-start = (bf16[2,64,128]{2,1,0:T(8,128)(2,1)}, bf16[2,64,128]{2,1,0:T(8,128)(2,1)S(1)}, u32[]{:S(2)}, u32[]{:S(2)}) collective-permute-start(bf16[2,64,128]{2,1,0:T(8,128)(2,1)} %get-tuple-element.15), channel_id=1, source_target_pairs={{0,1},{1,0},{2,3},{3,2},{4,5},{5,4},{6,7},{7,6},{8,9},{9,8},{10,11... | collective-permute-start | bytes 98312 | tf_op jit(solution)/shard_map/ppermute | solution.py:585
  3.3 18.6 %collective-permute-start.3 = (bf16[64,128]{1,0:T(8,128)(2,1)}, bf16[64,128]{1,0:T(8,128)(2,1)S(1)}, u32[]{:S(2)}, u32[]{:S(2)}) collective-permute-start(bf16[64,128]{1,0:T(8,128)(2,1)} %get-tuple-element.20), channel_id=1, source_target_pairs={{0,9},{1,8},{2,11},{3,10},{4,13},{5,12},{6,15},{7,14},{8,1},{9,0},... | collective-permute-start | bytes 49160 | tf_op jit(solution)/shard_map/ppermute | solution.py:597
  7.0 39.6 %collective-permute-start.6 = (bf16[2,4,64,512]{3,2,1,0:T(8,128)(2,1)}, bf16[2,4,64,512]{3,2,1,0:T(8,128)(2,1)S(1)}, u32[]{:S(2)}, u32[]{:S(2)}) collective-permute-start(bf16[2,4,64,512]{3,2,1,0:T(8,128)(2,1)} %get-tuple-element.23), channel_id=1, source_target_pairs={{0,8},{2,10},{4,12},{6,14},{8,0},{10,2},{12,4},{14,6},{1,9},{3,11}... | collective-permute-start | bytes 1572872 | tf_op jit(solution)/shard_map/ppermute | solution.py:584
  8.3 1.1 %copy-start = (bf16[2,6,64,512]{3,2,1,0:T(8,128)(2,1)S(1)}, bf16[2,6,64,512]{3,2,1,0:T(8,128)(2,1)}, u32[]{:S(2)}) copy-start(bf16[2,6,64,512]{3,2,1,0:T(8,128)(2,1)} %slc_ref.13) | copy-start | bytes 2359300
  10.8 17.3 %collective-permute-start.1 = (bf16[400,512]{1,0:T(8,128)(2,1)S(1)}, bf16[400,512]{1,0:T(8,128)(2,1)S(1)}, u32[]{:S(2)}, u32[]{:S(2)}) collective-permute-start(bf16[400,512]{1,0:T(8,128)(2,1)S(1)} %get-tuple-element.18), channel_id=1, source_target_pairs={{0,6},{2,0},{4,2},{6,4},{8,10},{10,12},{12,14},{14,8},{1,7},{3,1},... | collective-permute-start | bytes 1228808 | tf_op jit(solution)/shard_map/ppermute | solution.py:601
  13.7 14.4 %collective-permute-start.2 = (bf16[400,512]{1,0:T(8,128)(2,1)S(1)}, bf16[400,512]{1,0:T(8,128)(2,1)S(1)}, u32[]{:S(2)}, u32[]{:S(2)}) collective-permute-start(bf16[400,512]{1,0:T(8,128)(2,1)S(1)} %get-tuple-element.19.held_ref), channel_id=1, source_target_pairs={{6,8},{8,6},{7,9},{9,7},{22,24},{24,22},{23,25},{25,23}} | collective-permute-start | bytes 1228808 | tf_op jit(solution)/shard_map/ppermute | solution.py:600
  29.2 21.1 %collective-permute-start.5 = (bf16[400,512]{1,0:T(8,128)(2,1)S(1)}, bf16[400,512]{1,0:T(8,128)(2,1)S(1)}, u32[]{:S(2)}, u32[]{:S(2)}) collective-permute-start(bf16[400,512]{1,0:T(8,128)(2,1)S(1)} %get-tuple-element.22), channel_id=1, source_target_pairs={{0,2},{2,4},{4,6},{10,8},{12,10},{14,12},{1,3},{3,5},{5,7},{11,9},... | collective-permute-start | bytes 1228808 | tf_op jit(solution)/shard_map/ppermute | solution.py:662
  37.1 22.3 %collective-permute-start.4 = (bf16[272,512]{1,0:T(8,128)(2,1)S(1)}, bf16[272,512]{1,0:T(8,128)(2,1)S(1)}, u32[]{:S(2)}, u32[]{:S(2)}) collective-permute-start(bf16[272,512]{1,0:T(8,128)(2,1)S(1)} %get-tuple-element.21), channel_id=1, source_target_pairs={{0,8},{2,10},{4,12},{6,14},{8,0},{10,2},{12,4},{14,6},{1,9},{3,11}... | collective-permute-start | bytes 835592 | tf_op jit(solution)/shard_map/ppermute | solution.py:663

commit v10 on v9

--- a/solution.py
+++ b/solution.py
@@ -142,14 +142,13 @@
         copy.wait()
 
 
-def late_kernel(plan, slc_ref, rim_ref, inner_ref, middle_ref, held_ref, pairs_ref, *refs):
-    late_ref, outer_ref, tiles_ref, sem = refs[-4:]
-    copy = pltpu.make_async_copy(held_ref, outer_ref, sem)
-    copy.start()
+def late_kernel(plan, slc_ref, rim_ref, inner_ref, middle_ref, pairs_ref, *refs):
+    late_ref, tiles_ref = refs[-2:]
     me, strip = lax.axis_index("date"), lax.axis_index("strip")
     dates, late, rows = plan["dates"], plan["late"], plan["rows"]
     half = plan["devices"] // 2
     mate = lax.rem(me + half, 2 * half)
+    mate = jnp.where(me == half - 1, 0, jnp.where(me == half, 2 * half - 1, mate))
     mate_slot = jnp.where(mate < half, 0, dates - late)
     in_middle = (me == half) | (me == half - 1)
     for k in range(late):
@@ -177,7 +176,6 @@
 
     tiles = [tiles_ref[k, c] for k in range(late) for c in range(2)]
     write_strips(late_ref, gather_strips(tiles, strip))
-    copy.wait()
 
 
 def bands_kernel(cols, out_ref):
@@ -411,7 +409,7 @@
 
 
 def annual_kernel(plan, lists, slc_ref, rim_ref, bands_ref, powers_ref, ring_ref,
-                  images_ref, strips_ref, _, out_ref, *scratch, is_late):
+                  images_ref, strips_ref, _sent, _, out_ref, *scratch, is_late):
     pairs = Pairs(plan, lists, slc_ref, rim_ref, bands_ref, powers_ref, out_ref, scratch)
     dates, late = plan["dates"], plan["late"]
     half = plan["devices"] // 2
@@ -597,7 +595,9 @@
         strips = lax.ppermute(
             strips, both, [(2 * a + s, 2 * b + 1 - s) for a, b in swap for s in (0, 1)]
         )
+        up = [(b, a) for a, b in down if b not in (half - 1, half)]
         middle = lax.ppermute(outer, "date", [(half - 1, half), (half, half - 1)])
+        outer = lax.ppermute(outer, "date", up)
         inner = lax.ppermute(inner, "date", down)
     else:
         rim = swapped_rims(slc)
@@ -646,27 +646,24 @@
         )(lists, slc, rim, bands, powers, *others, out)
 
     if halves:
-        payload, outer = pl.pallas_call(
+        payload = sent = pl.pallas_call(
             functools.partial(late_kernel, plan),
-            out_shape=(payload_shape(late), payload_shape(NEAR)),
-            in_specs=[VMEM, VMEM, VMEM, VMEM, ANY, SMEM, ANY, ANY],
-            out_specs=(VMEM, VMEM),
-            scratch_shapes=[
-                pltpu.VMEM((late, planes, rows, TILE), dtype),
-                pltpu.SemaphoreType.DMA,
-            ],
+            out_shape=payload_shape(late),
+            in_specs=[VMEM, VMEM, VMEM, VMEM, SMEM, ANY, ANY],
+            out_specs=VMEM,
+            scratch_shapes=[pltpu.VMEM((late, planes, rows, TILE), dtype)],
             compiler_params=limit(WORK_MIB),
             name="late_images",
-        )(slc, rim, inner, middle, outer, lists, powers, strips)
-        up = [(b, a) for a, b in down if b not in (half - 1, half)]
-        outer = lax.ppermute(outer, "date", up)
-        payload = lax.ppermute(payload, "date", swap)
+        )(slc, rim, inner, middle, lists, powers, strips)
+        late_swap = [(a, b) for a, b in swap if a not in (half - 1, half)]
+        late_swap += [(half - 1, 0), (half, devices - 1)]
+        payload = lax.ppermute(payload, "date", late_swap)
     if halves:
         early_pairs = functools.partial(annual_kernel, is_late=False)
-        out = more_pairs(early_pairs, out, (inner, early, strips), "annual_pairs")
+        out = more_pairs(early_pairs, out, (inner, early, strips, sent), "annual_pairs")
         out = more_pairs(rest_kernel, out, (inner, outer, middle), "near_pairs")
         late_pairs = functools.partial(annual_kernel, is_late=True)
-        out = more_pairs(late_pairs, out, (inner, payload, strips), "last_pairs")
+        out = more_pairs(late_pairs, out, (inner, payload, strips, sent), "last_pairs")
     else:
         out = more_pairs(rest_kernel, out, (inner, outer, inner), "near_pairs")
         out = more_pairs(plain_kernel, out, (annual, swapped_rims(annual)), "annual_pairs")

time: 62.2 us -> 61.8 us (level)
  waiting for transfers between devices: 10.2 us -> 0.3 us
  starting transfers between devices: 25.2 us -> 33.7 us
    ppermute x1, starting transfers between devices: 9.45 us -> 21.9 us  [body(): payload = lax.ppermute(payload, 'date', late_swap)]
    ppermute x1, waiting for transfers between devices: 6.18 us -> 0.28 us  [body(): inner = lax.ppermute(inner, 'date', down)]
    ppermute x1, starting transfers between devices: 7.91 us -> 3.72 us  [body(): outer = lax.ppermute(outer, 'date', up)]
    ppermute x1, waiting for transfers between devices: 3.97 us -> 0.01 us  [body(): payload = lax.ppermute(payload, 'date', late_swap)]
    pallas_call x1, Pallas kernels: 7.52 us -> 9.33 us  [body(): pl.pallas_call(functools.partial(own_kernel, plan), out_shape=(out_shape,...]
    pallas_call x3, Pallas kernels: 11.3 us -> 9.99 us  [more_pairs(): pl.pallas_call(functools.partial(kernel, plan), out_shape=out_shape, in_s...]
  transfers between devices with their start and end apart: 7 -> 7, of which waited for: 2 -> 1; matrix products, arithmetic and copies ran while one was open for 1% -> 1% of each run, Pallas kernels for 31% -> 32%
where the time goes in v10:
time: 61.8 us; the launch traced here: 60.9 us
  starting transfers between devices  33.7 us (55%)
  Pallas kernels  24.9 us (40%)
  local copies, waits for them, and re-layouts  1.13 us (2%)
  other arithmetic  0.72 us (1%)
    ppermute x1, starting transfers between devices, body(): payload = lax.ppermute(payload, 'date', late_swap)  21.9 us
    pallas_call x3, Pallas kernels, more_pairs(): pl.pallas_call(functools.partial(kernel, plan), out_shape=out_shape, in_s...  9.99 us
    pallas_call x1, Pallas kernels, body(): pl.pallas_call(functools.partial(own_kernel, plan), out_shape=(out_shape,...  9.33 us
    ppermute x1, starting transfers between devices, body(): outer = lax.ppermute(outer, 'date', up)  3.72 us
    ppermute x1, starting transfers between devices, body(): lax.ppermute(strips, both, [(2 * a + s, 2 * b + 1 - s) for a, b in swap f...  3.54 us
    ppermute x1, starting transfers between devices, body(): inner = lax.ppermute(inner, 'date', down)  3.2 us
    pallas_call x1, Pallas kernels, body(): pl.pallas_call(functools.partial(early_kernel, plan), out_shape=(images(d...  2.76 us
    pallas_call x1, Pallas kernels, body(): pl.pallas_call(functools.partial(beside_kernel, plan), out_shape=(payload...  1.36 us
  transfers between devices with their start and end apart: 7, of which 1 were waited for; matrix products, arithmetic and copies ran while one was open for 1% of the time, Pallas kernels for 32%

profile of v10, /device:TPU:0, one launch (start us, length us, event | category | flops | bytes accessed | tf_op | source)
XLA Modules:
  0.0 60.9 jit_solution(14085020587556124511)
XLA Ops:
  0.0 2.8 %early_images.1 = (bf16[2,4,64,512]{3,2,1,0:T(8,128)(2,1)}, bf16[2,64,128]{2,1,0:T(8,128)(2,1)}, bf16[64,128]{1,0:T(8,128)(2,1)}) custom-call(bf16[2,6,64,512]{3,2,1,0:T(8,128)(2,1)} %slc_ref.13, s32[2,192]{1,0:T(2,128)} %bitcast.3), custom_call_target="tpu_custom_call" | custom-call | tf_op jit(solution)/shard_map/early_images/pallas_call | solution.py:565
  2.8 3.5 %collective-permute-start.3 = (bf16[64,128]{1,0:T(8,128)(2,1)}, bf16[64,128]{1,0:T(8,128)(2,1)S(1)}, u32[]{:S(2)}, u32[]{:S(2)}) collective-permute-start(bf16[64,128]{1,0:T(8,128)(2,1)} %get-tuple-element.18), channel_id=1, source_target_pairs={{0,9},{1,8},{2,11},{3,10},{4,13},{5,12},{6,15},{7,14},{8,1},{9,0},... | collective-permute-start | bytes 49160 | tf_op jit(solution)/shard_map/ppermute | solution.py:595
  6.3 0.7 %collective-permute-start = (bf16[2,64,128]{2,1,0:T(8,128)(2,1)}, bf16[2,64,128]{2,1,0:T(8,128)(2,1)S(1)}, u32[]{:S(2)}, u32[]{:S(2)}) collective-permute-start(bf16[2,64,128]{2,1,0:T(8,128)(2,1)} %get-tuple-element.13), channel_id=1, source_target_pairs={{0,1},{1,0},{2,3},{3,2},{4,5},{5,4},{6,7},{7,6},{8,9},{9,8},{10,11... | collective-permute-start | bytes 98312 | tf_op jit(solution)/shard_map/ppermute | solution.py:583
  7.0 0.0 collective-permute-start.6
  7.0 0.7 %pad_add_fusion.lists.pairs_ref = s32[4,192]{1,0:T(4,128)S(1)} fusion(s32[1,192]{1,0:T(1,128)} %bitcast.5, s32[1,192]{1,0:T(1,128)} %bitcast.6, s32[2,192]{1,0:T(2,128)} %bitcast.4), kind=kLoop, calls=%fused_computation | loop fusion | flops 1536 | bytes 6144 | tf_op jit(solution)/shard_map/concatenate | solution.py:523
  7.7 0.5 range_bands.1.bands_ref
  8.3 0.0 collective-permute-done.packed_ref
  8.3 0.0 copy-start
  8.3 1.1 %copy-done = bf16[2,6,64,512]{3,2,1,0:T(8,128)(2,1)S(1)} copy-done((bf16[2,6,64,512]{3,2,1,0:T(8,128)(2,1)S(1)}, bf16[2,6,64,512]{3,2,1,0:T(8,128)(2,1)}, u32[]{:S(2)}) %copy-start) | copy-done | bytes 786456
  9.4 1.4 %beside_images.1 = (bf16[400,512]{1,0:T(8,128)(2,1)S(1)}, bf16[400,512]{1,0:T(8,128)(2,1)S(1)}, bf16[2,6,64,128]{3,2,1,0:T(8,128)(2,1)S(1)}) custom-call(bf16[2,6,64,512]{3,2,1,0:T(8,128)(2,1)S(1)} %copy-done, bf16[2,64,128]{2,1,0:T(8,128)(2,1)S(1)} %collective-permute-done.packed_ref), custom_call_target="tpu_custom_call" | custom-call | tf_op jit(solution)/shard_map/beside_images/pallas_call | solution.py:584
  10.8 3.7 %collective-permute-start.5 = (bf16[400,512]{1,0:T(8,128)(2,1)S(1)}, bf16[400,512]{1,0:T(8,128)(2,1)S(1)}, u32[]{:S(2)}, u32[]{:S(2)}) collective-permute-start(bf16[400,512]{1,0:T(8,128)(2,1)S(1)} %get-tuple-element.17), channel_id=1, source_target_pairs={{0,2},{2,4},{4,6},{10,8},{12,10},{14,12},{1,3},{3,5},{5,7},{11,9},... | collective-permute-start | bytes 1228808 | tf_op jit(solution)/shard_map/ppermute | solution.py:600
  14.5 0.7 %collective-permute-start.2 = (bf16[400,512]{1,0:T(8,128)(2,1)S(1)}, bf16[400,512]{1,0:T(8,128)(2,1)S(1)}, u32[]{:S(2)}, u32[]{:S(2)}) collective-permute-start(bf16[400,512]{1,0:T(8,128)(2,1)S(1)} %get-tuple-element.17), channel_id=1, source_target_pairs={{6,8},{8,6},{7,9},{9,7},{22,24},{24,22},{23,25},{25,23}} | collective-permute-start | bytes 1228808 | tf_op jit(solution)/shard_map/ppermute | solution.py:599
  15.2 3.2 %collective-permute-start.1 = (bf16[400,512]{1,0:T(8,128)(2,1)S(1)}, bf16[400,512]{1,0:T(8,128)(2,1)S(1)}, u32[]{:S(2)}, u32[]{:S(2)}) collective-permute-start(bf16[400,512]{1,0:T(8,128)(2,1)S(1)} %get-tuple-element.16), channel_id=1, source_target_pairs={{0,6},{2,0},{4,2},{6,4},{8,10},{10,12},{12,14},{14,8},{1,7},{3,1},... | collective-permute-start | bytes 1228808 | tf_op jit(solution)/shard_map/ppermute | solution.py:601
  18.4 9.3 %own_pairs.1 = (f32[2,24,64,512]{3,2,1,0:T(8,128)}, bf16[6,64,1536]{2,1,0:T(8,128)(2,1)S(1)}) custom-call(s32[4,192]{1,0:T(4,128)S(1)} %pad_add_fusion.lists.pairs_ref, bf16[2,6,64,512]{3,2,1,0:T(8,128)(2,1)S(1)} %copy-done, bf16[2,6,64,128]{3,2,1,0:T(8,128)(2,1)S(1)} %get-tuple-element.14.rim_ref, bf16[5,2,768,256]{3,2,1,0:T(8,128)(2,1)S(1)} %range_bands.1.bands_ref), custom_call_target="tpu_custom_call" | custom-call | flops 20000000000 | bytes 1 | tf_op jit(solution)/shard_map/own_pairs/pallas_call | solution.py:624
  27.7 0.0 collective-permute-done.3.refs_1_.strips_ref
  27.8 0.3 collective-permute-done.1.inner_ref.ring_ref
  28.0 0.0 collective-permute-done.2.middle_ref
  28.0 0.9 %late_images.1._sent = bf16[272,512]{1,0:T(8,128)(2,1)S(1)} custom-call(bf16[2,6,64,512]{3,2,1,0:T(8,128)(2,1)S(1)} %copy-done, bf16[2,6,64,128]{3,2,1,0:T(8,128)(2,1)S(1)} %get-tuple-element.14.rim_ref, bf16[400,512]{1,0:T(8,128)(2,1)S(1)} %collective-permute-done.1.inner_ref.ring_ref, bf16[400,512]{1,0:T(8,128)(2,1)S(1)} %collective-permute-done.2.middle_ref, ...), custom_call_target="tpu_custom_call" | custom-call | tf_op jit(solution)/shard_map/late_images/pallas_call | solution.py:649
  29.0 21.9 %collective-permute-start.4 = (bf16[272,512]{1,0:T(8,128)(2,1)S(1)}, bf16[272,512]{1,0:T(8,128)(2,1)S(1)}, u32[]{:S(2)}, u32[]{:S(2)}) collective-permute-start(bf16[272,512]{1,0:T(8,128)(2,1)S(1)} %late_images.1._sent), channel_id=1, source_target_pairs={{0,8},{2,10},{4,12},{10,2},{12,4},{14,6},{6,0},{8,14},{1,9},{3,11}... | collective-permute-start | bytes 835592 | tf_op jit(solution)/shard_map/ppermute | solution.py:660
  50.8 0.0 collective-permute-done.6.images_ref
  50.8 3.8 %annual_pairs.1._ = f32[2,24,64,512]{3,2,1,0:T(8,128)} custom-call(s32[4,192]{1,0:T(4,128)S(1)} %pad_add_fusion.lists.pairs_ref, bf16[2,6,64,512]{3,2,1,0:T(8,128)(2,1)S(1)} %copy-done, bf16[2,6,64,128]{3,2,1,0:T(8,128)(2,1)S(1)} %get-tuple-element.14.rim_ref, bf16[5,2,768,256]{3,2,1,0:T(8,128)(2,1)S(1)} %range_bands.1.bands_ref, ...), custom_call_target="tpu_custom_call", output_to_operand_aliasing={{}: (9, {})} | custom-call | flops 1 | bytes 1 | tf_op jit(solution)/shard_map/annual_pairs/pallas_call | solution.py:636
  54.6 0.0 collective-permute-done.5.outer_ref
  54.6 3.8 %near_pairs.1._ = f32[2,24,64,512]{3,2,1,0:T(8,128)} custom-call(s32[4,192]{1,0:T(4,128)S(1)} %pad_add_fusion.lists.pairs_ref, bf16[2,6,64,512]{3,2,1,0:T(8,128)(2,1)S(1)} %copy-done, bf16[2,6,64,128]{3,2,1,0:T(8,128)(2,1)S(1)} %get-tuple-element.14.rim_ref, bf16[5,2,768,256]{3,2,1,0:T(8,128)(2,1)S(1)} %range_bands.1.bands_ref, ...), custom_call_target="tpu_custom_call", output_to_operand_aliasing={{}: (8, {})} | custom-call | flops 1 | bytes 1 | tf_op jit(solution)/shard_map/near_pairs/pallas_call | solution.py:636
  58.4 0.0 collective-permute-done.4.images_ref
  58.5 2.4 %last_pairs.1 = f32[2,24,64,512]{3,2,1,0:T(8,128)} custom-call(s32[4,192]{1,0:T(4,128)S(1)} %pad_add_fusion.lists.pairs_ref, bf16[2,6,64,512]{3,2,1,0:T(8,128)(2,1)S(1)} %copy-done, bf16[2,6,64,128]{3,2,1,0:T(8,128)(2,1)S(1)} %get-tuple-element.14.rim_ref, bf16[5,2,768,256]{3,2,1,0:T(8,128)(2,1)S(1)} %range_bands.1.bands_ref, ...), custom_call_target="tpu_custom_call", output_to_operand_aliasing={{}: (9, {})} | custom-call | flops 1 | bytes 1 | tf_op jit(solution)/shard_map/last_pairs/pallas_call | solution.py:636
Async XLA Ops:
  2.8 25.0 %collective-permute-start.3 = (bf16[64,128]{1,0:T(8,128)(2,1)}, bf16[64,128]{1,0:T(8,128)(2,1)S(1)}, u32[]{:S(2)}, u32[]{:S(2)}) collective-permute-start(bf16[64,128]{1,0:T(8,128)(2,1)} %get-tuple-element.18), channel_id=1, source_target_pairs={{0,9},{1,8},{2,11},{3,10},{4,13},{5,12},{6,15},{7,14},{8,1},{9,0},... | collective-permute-start | bytes 49160 | tf_op jit(solution)/shard_map/ppermute | solution.py:595
  6.3 2.0 %collective-permute-start = (bf16[2,64,128]{2,1,0:T(8,128)(2,1)}, bf16[2,64,128]{2,1,0:T(8,128)(2,1)S(1)}, u32[]{:S(2)}, u32[]{:S(2)}) collective-permute-start(bf16[2,64,128]{2,1,0:T(8,128)(2,1)} %get-tuple-element.13), channel_id=1, source_target_pairs={{0,1},{1,0},{2,3},{3,2},{4,5},{5,4},{6,7},{7,6},{8,9},{9,8},{10,11... | collective-permute-start | bytes 98312 | tf_op jit(solution)/shard_map/ppermute | solution.py:583
  7.0 43.9 %collective-permute-start.6 = (bf16[2,4,64,512]{3,2,1,0:T(8,128)(2,1)}, bf16[2,4,64,512]{3,2,1,0:T(8,128)(2,1)S(1)}, u32[]{:S(2)}, u32[]{:S(2)}) collective-permute-start(bf16[2,4,64,512]{3,2,1,0:T(8,128)(2,1)} %get-tuple-element.19), channel_id=1, source_target_pairs={{0,8},{2,10},{4,12},{6,14},{8,0},{10,2},{12,4},{14,6},{1,9},{3,11}... | collective-permute-start | bytes 1572872 | tf_op jit(solution)/shard_map/ppermute | solution.py:582
  8.3 1.1 %copy-start = (bf16[2,6,64,512]{3,2,1,0:T(8,128)(2,1)S(1)}, bf16[2,6,64,512]{3,2,1,0:T(8,128)(2,1)}, u32[]{:S(2)}) copy-start(bf16[2,6,64,512]{3,2,1,0:T(8,128)(2,1)} %slc_ref.13) | copy-start | bytes 2359300
  10.8 43.8 %collective-permute-start.5 = (bf16[400,512]{1,0:T(8,128)(2,1)S(1)}, bf16[400,512]{1,0:T(8,128)(2,1)S(1)}, u32[]{:S(2)}, u32[]{:S(2)}) collective-permute-start(bf16[400,512]{1,0:T(8,128)(2,1)S(1)} %get-tuple-element.17), channel_id=1, source_target_pairs={{0,2},{2,4},{4,6},{10,8},{12,10},{14,12},{1,3},{3,5},{5,7},{11,9},... | collective-permute-start | bytes 1228808 | tf_op jit(solution)/shard_map/ppermute | solution.py:600
  14.5 13.5 %collective-permute-start.2 = (bf16[400,512]{1,0:T(8,128)(2,1)S(1)}, bf16[400,512]{1,0:T(8,128)(2,1)S(1)}, u32[]{:S(2)}, u32[]{:S(2)}) collective-permute-start(bf16[400,512]{1,0:T(8,128)(2,1)S(1)} %get-tuple-element.17), channel_id=1, source_target_pairs={{6,8},{8,6},{7,9},{9,7},{22,24},{24,22},{23,25},{25,23}} | collective-permute-start | bytes 1228808 | tf_op jit(solution)/shard_map/ppermute | solution.py:599
  15.2 12.8 %collective-permute-start.1 = (bf16[400,512]{1,0:T(8,128)(2,1)S(1)}, bf16[400,512]{1,0:T(8,128)(2,1)S(1)}, u32[]{:S(2)}, u32[]{:S(2)}) collective-permute-start(bf16[400,512]{1,0:T(8,128)(2,1)S(1)} %get-tuple-element.16), channel_id=1, source_target_pairs={{0,6},{2,0},{4,2},{6,4},{8,10},{10,12},{12,14},{14,8},{1,7},{3,1},... | collective-permute-start | bytes 1228808 | tf_op jit(solution)/shard_map/ppermute | solution.py:601
  29.0 29.5 %collective-permute-start.4 = (bf16[272,512]{1,0:T(8,128)(2,1)S(1)}, bf16[272,512]{1,0:T(8,128)(2,1)S(1)}, u32[]{:S(2)}, u32[]{:S(2)}) collective-permute-start(bf16[272,512]{1,0:T(8,128)(2,1)S(1)} %late_images.1._sent), channel_id=1, source_target_pairs={{0,8},{2,10},{4,12},{10,2},{12,4},{14,6},{6,0},{8,14},{1,9},{3,11}... | collective-permute-start | bytes 835592 | tf_op jit(solution)/shard_map/ppermute | solution.py:660

commit v11 on v10

--- a/solution.py
+++ b/solution.py
@@ -88,8 +88,8 @@
     return [gather_strips(tiles[n * PER_TILE : (n + 1) * PER_TILE], side) for n in range(2)]
 
 
-def early_kernel(plan, slc_ref, pairs_ref, early_ref, packed_ref, strips_ref, tiles_ref, sems,
-                 tile_sem):
+def early_kernel(plan, slc_ref, pairs_ref, early_ref, middle_ref, packed_ref, strips_ref,
+                 tiles_ref, sems, middle_sem, tile_sem):
     strip, cols = lax.axis_index("strip"), plan["cols"]
     start = pl.multiple_of(jnp.where(strip == 0, cols - TILE, 0), TILE)
     wanted = wanted_images(plan, pairs_ref)
@@ -99,6 +99,13 @@
     early_copies = image_copies(slc_ref, wanted, early_ref, sems)
     for copy in [tile_copy] + early_copies:
         copy.start()
+    me, half = lax.axis_index("date"), plan["devices"] // 2
+    first = jnp.where(me < half, plan["dates"] - NEAR, 0)
+    middle_copy = pltpu.make_async_copy(
+        slc_ref.at[:, pl.ds(first, NEAR)], middle_ref, middle_sem
+    )
+    in_middle = (me == half) | (me == half - 1)
+    pl.when(in_middle)(lambda: middle_copy.start())
     tile_copy.wait()
     tiles = [tiles_ref[c, k] for k in range(plan["dates"]) for c in range(2)]
     for n, packed in enumerate(gather_all(tiles, 1 - strip)):
@@ -107,6 +114,7 @@
     strips_ref[...] = gather_strips(tiles, 1 - strip)
     for copy in early_copies:
         copy.wait()
+    pl.when(in_middle)(lambda: middle_copy.wait())
 
 
 def rim_kernel(slc_ref, rim_ref, sem):
@@ -115,7 +123,7 @@
     run_copies([pltpu.make_async_copy(slc_ref.at[:, :, :, pl.ds(start, TILE)], rim_ref, sem)])
 
 
-def beside_kernel(plan, slc_ref, packed_ref, inner_ref, outer_ref, rim_ref, sems):
+def beside_kernel(plan, slc_ref, packed_ref, inner_ref, outer_ref, rim_ref, edges_ref, sems):
     me, strip = lax.axis_index("date"), lax.axis_index("strip")
     dates, rows = plan["dates"], plan["rows"]
     upper = me >= plan["devices"] // 2
@@ -137,12 +145,13 @@
             rim_ref[c, k] = place_strip(packed_ref[tile], n, strip)
     for out_ref, first in zip((inner_ref, outer_ref), firsts):
         tiles = [rim_ref[c, first + k] for k in range(NEAR) for c in range(2)]
-        write_strips(out_ref, gather_strips(tiles, strip))
+        edges_ref[...] = gather_strips(tiles, strip)
+        write_strips(out_ref, edges_ref[...])
     for copy in copies:
         copy.wait()
 
 
-def late_kernel(plan, slc_ref, rim_ref, inner_ref, middle_ref, pairs_ref, *refs):
+def late_kernel(plan, slc_ref, rim_ref, inner_ref, middle_ref, edges_ref, pairs_ref, *refs):
     late_ref, tiles_ref = refs[-2:]
     me, strip = lax.axis_index("date"), lax.axis_index("strip")
     dates, late, rows = plan["dates"], plan["late"], plan["rows"]
@@ -165,14 +174,17 @@
                 late_ref[here] = slc_ref[c, own_at]
                 tiles_ref[k, c] = rim_ref[c, own_at]
 
-            for chosen, ref in ((in_middle, middle_ref), (jnp.logical_not(in_middle), inner_ref)):
-
-                @pl.when(chosen & jnp.logical_not(own))
-                def _():
-                    there = pl.multiple_of((2 * other_at + c) * rows, rows)
-                    late_ref[here] = ref[pl.ds(there, rows)]
-                    packed = read_strips(ref, rows)
-                    tiles_ref[k, c] = place_strip(packed, 2 * other_at + c, strip)
+            @pl.when(jnp.logical_not(own | in_middle))
+            def _():
+                there = pl.multiple_of((2 * other_at + c) * rows, rows)
+                late_ref[here] = inner_ref[pl.ds(there, rows)]
+                packed = read_strips(inner_ref, rows)
+                tiles_ref[k, c] = place_strip(packed, 2 * other_at + c, strip)
+
+            @pl.when(jnp.logical_not(own) & in_middle)
+            def _():
+                late_ref[here] = middle_ref[c, other_at]
+                tiles_ref[k, c] = place_strip(edges_ref[...], 2 * other_at + c, strip)
 
     tiles = [tiles_ref[k, c] for k in range(late) for c in range(2)]
     write_strips(late_ref, gather_strips(tiles, strip))
@@ -284,6 +296,12 @@
         for c in range(2):
             at = pl.multiple_of((2 * index + c) * rows, rows)
             self.other_ref[x, c] = ref[pl.ds(at, rows)]
+            self.other_rim_ref[x, c] = place_strip(packed, 2 * index + c, self.strip)
+
+    def fetch_images(self, x, ref, packed_ref, index):
+        packed = packed_ref[...]
+        for c in range(2):
+            self.other_ref[x, c] = ref[c, index]
             self.other_rim_ref[x, c] = place_strip(packed, 2 * index + c, self.strip)
 
     def out_copy(self, stage, x, pair):
@@ -386,7 +404,7 @@
 
 
 def rest_kernel(plan, lists, slc_ref, rim_ref, bands_ref, powers_ref, inner_ref, outer_ref,
-                middle_ref, _, out_ref, *scratch):
+                middle_ref, edges_ref, _, out_ref, *scratch):
     pairs = Pairs(plan, lists, slc_ref, rim_ref, bands_ref, powers_ref, out_ref, scratch)
     dates = plan["dates"]
     upper = pairs.me >= plan["devices"] // 2 if plan["halves"] else True
@@ -396,13 +414,10 @@
         below = local < 0
         index = jnp.clip(jnp.where(below, local + NEAR, local - dates), 0, NEAR - 1)
         inner, middle = below == upper, pairs.in_middle(local)
-        sources = (
-            (jnp.logical_not(inner), outer_ref),
-            (inner & jnp.logical_not(middle), inner_ref),
-            (inner & middle, middle_ref),
-        )
-        for chosen, ref in sources:
-            pl.when(chosen)(functools.partial(pairs.fetch_payload, x, ref, index))
+        fetch = pairs.fetch_payload
+        pl.when(jnp.logical_not(inner))(lambda: fetch(x, outer_ref, index))
+        pl.when(inner & jnp.logical_not(middle))(lambda: fetch(x, inner_ref, index))
+        pl.when(inner & middle)(lambda: pairs.fetch_images(x, middle_ref, edges_ref, index))
         return slot, kind, pairs.fetched_other(x), None
 
     pairs.run(pairs.near_list(lambda local: jnp.logical_not(pairs.own(local))), work)
@@ -420,12 +435,6 @@
     else:
         base, count = jnp.where(lower, late, 0), dates - late
 
-    def fetch_early(x, k, ref):
-        packed = strips_ref[...]
-        for c in range(2):
-            pairs.other_ref[x, c] = ref[c, k]
-            pairs.other_rim_ref[x, c] = place_strip(packed, 2 * k + c, pairs.strip)
-
     def work(x, k):
         slot = base + k
         date = me * dates + slot
@@ -437,7 +446,7 @@
             ring_at = jnp.where(lower, other, other - (2 * split_date - NEAR))
             ring_at = jnp.clip(ring_at, 0, NEAR - 1)
             pl.when(far)(lambda: pairs.fetch_payload(x, ring_ref, ring_at))
-            pl.when(jnp.logical_not(far))(lambda: fetch_early(x, k, images_ref))
+            pl.when(jnp.logical_not(far))(lambda: pairs.fetch_images(x, images_ref, strips_ref, k))
         return slot, NEAR, pairs.fetched_other(x), None
 
     pairs.run(count, work)
@@ -562,18 +571,20 @@
     if halves:
         swap = [(i, (i + half) % devices) for i in range(devices)]
         both = ("date", "strip")
-        early, packed, strips = pl.pallas_call(
+        early, middle, packed, strips = pl.pallas_call(
             functools.partial(early_kernel, plan),
             out_shape=(
                 images(dates - late),
+                images(NEAR),
                 jax.ShapeDtypeStruct((2, rows, TILE), dtype),
                 jax.ShapeDtypeStruct((rows, TILE), dtype),
             ),
             in_specs=[ANY, SMEM],
-            out_specs=(VMEM, VMEM, VMEM),
+            out_specs=(VMEM, VMEM, VMEM, VMEM),
             scratch_shapes=[
                 pltpu.VMEM((planes, dates, rows, TILE), dtype),
                 pltpu.SemaphoreType.DMA((dates - late,)),
+                pltpu.SemaphoreType.DMA,
                 pltpu.SemaphoreType.DMA,
             ],
             compiler_params=limit(FIRST_MIB),
@@ -581,11 +592,16 @@
         )(slc, pairs)
         early = lax.ppermute(early, "date", swap)
         packed = lax.ppermute(packed, "strip", swap_strips)
-        inner, outer, rim = pl.pallas_call(
+        inner, outer, rim, edges = pl.pallas_call(
             functools.partial(beside_kernel, plan),
-            out_shape=(payload_shape(NEAR), payload_shape(NEAR), rim_shape(dates)),
+            out_shape=(
+                payload_shape(NEAR),
+                payload_shape(NEAR),
+                rim_shape(dates),
+                jax.ShapeDtypeStruct((rows, TILE), dtype),
+            ),
             in_specs=[ANY, VMEM],
-            out_specs=(VMEM, VMEM, VMEM),
+            out_specs=(VMEM, VMEM, VMEM, VMEM),
             scratch_shapes=[pltpu.SemaphoreType.DMA((2, NEAR, 2))],
             compiler_params=limit(WORK_MIB),
             name="beside_images",
@@ -596,7 +612,9 @@
             strips, both, [(2 * a + s, 2 * b + 1 - s) for a, b in swap for s in (0, 1)]
         )
         up = [(b, a) for a, b in down if b not in (half - 1, half)]
-        middle = lax.ppermute(outer, "date", [(half - 1, half), (half, half - 1)])
+        across = [(half - 1, half), (half, half - 1)]
+        middle = lax.ppermute(middle, "date", across)
+        edges = lax.ppermute(edges, "date", across)
         outer = lax.ppermute(outer, "date", up)
         inner = lax.ppermute(inner, "date", down)
     else:
@@ -649,23 +667,23 @@
         payload = sent = pl.pallas_call(
             functools.partial(late_kernel, plan),
             out_shape=payload_shape(late),
-            in_specs=[VMEM, VMEM, VMEM, VMEM, SMEM, ANY, ANY],
+            in_specs=[VMEM] * 5 + [SMEM, ANY, ANY],
             out_specs=VMEM,
             scratch_shapes=[pltpu.VMEM((late, planes, rows, TILE), dtype)],
             compiler_params=limit(WORK_MIB),
             name="late_images",
-        )(slc, rim, inner, middle, lists, powers, strips)
+        )(slc, rim, inner, middle, edges, lists, powers, strips)
         late_swap = [(a, b) for a, b in swap if a not in (half - 1, half)]
         late_swap += [(half - 1, 0), (half, devices - 1)]
         payload = lax.ppermute(payload, "date", late_swap)
     if halves:
         early_pairs = functools.partial(annual_kernel, is_late=False)
         out = more_pairs(early_pairs, out, (inner, early, strips, sent), "annual_pairs")
-        out = more_pairs(rest_kernel, out, (inner, outer, middle), "near_pairs")
+        out = more_pairs(rest_kernel, out, (inner, outer, middle, edges), "near_pairs")
         late_pairs = functools.partial(annual_kernel, is_late=True)
         out = more_pairs(late_pairs, out, (inner, payload, strips, sent), "last_pairs")
     else:
-        out = more_pairs(rest_kernel, out, (inner, outer, inner), "near_pairs")
+        out = more_pairs(rest_kernel, out, (inner, outer, annual, rim[0, 0]), "near_pairs")
         out = more_pairs(plain_kernel, out, (annual, swapped_rims(annual)), "annual_pairs")
     return out
 

time: 61.8 us -> 67.8 us (1.097)
  waiting for transfers between devices: 0.3 us -> 10.7 us
  starting transfers between devices: 33.7 us -> 31.5 us
  Pallas kernels: 24.9 us -> 23 us
    ppermute x1, waiting for transfers between devices: 0.28 us -> 7.16 us  [body(): inner = lax.ppermute(inner, 'date', down)]
    ppermute x1, starting transfers between devices: 21.9 us -> 16.6 us  [body(): payload = lax.ppermute(payload, 'date', late_swap)]
    ppermute x1, starting transfers between devices: 0.04 us -> 5.13 us  [body(): early = lax.ppermute(early, 'date', swap)]
    ppermute x1, waiting for transfers between devices: 0.01 us -> 3.5 us  [body(): payload = lax.ppermute(payload, 'date', late_swap)]
    pallas_call x3, Pallas kernels: 9.99 us -> 6.93 us  [more_pairs(): pl.pallas_call(functools.partial(kernel, plan), out_shape=out_shape, in_s...]
    ppermute x1, starting transfers between devices: 3.72 us -> 1.3 us  [body(): outer = lax.ppermute(outer, 'date', up)]
    pallas_call x1, Pallas kernels: 9.33 us -> 10.4 us  [body(): pl.pallas_call(functools.partial(own_kernel, plan), out_shape=(out_shape,...]
  transfers between devices with their start and end apart: 7 -> 8, of which waited for: 1 -> 2; matrix products, arithmetic and copies ran while one was open for 1% -> 1% of each run, Pallas kernels for 32% -> 26%
where the time goes in v11:
time: 67.8 us; the launch traced here: 67.1 us
  starting transfers between devices  31.5 us (46%)
  Pallas kernels  23 us (34%)
  waiting for transfers between devices  10.7 us (16%)
  local copies, waits for them, and re-layouts  1.13 us (2%)
  other arithmetic  0.72 us (1%)
    ppermute x1, starting transfers between devices, body(): payload = lax.ppermute(payload, 'date', late_swap)  16.6 us
    pallas_call x1, Pallas kernels, body(): pl.pallas_call(functools.partial(own_kernel, plan), out_shape=(out_shape,...  10.4 us
    ppermute x1, waiting for transfers between devices, body(): inner = lax.ppermute(inner, 'date', down)  7.16 us
    pallas_call x3, Pallas kernels, more_pairs(): pl.pallas_call(functools.partial(kernel, plan), out_shape=out_shape, in_s...  6.93 us
    ppermute x1, starting transfers between devices, body(): early = lax.ppermute(early, 'date', swap)  5.13 us
    ppermute x1, starting transfers between devices, body(): lax.ppermute(strips, both, [(2 * a + s, 2 * b + 1 - s) for a, b in swap f...  3.61 us
    ppermute x1, waiting for transfers between devices, body(): payload = lax.ppermute(payload, 'date', late_swap)  3.5 us
    pallas_call x1, Pallas kernels, body(): pl.pallas_call(functools.partial(early_kernel, plan), out_shape=(images(d...  2.97 us
  transfers between devices with their start and end apart: 8, of which 2 were waited for; matrix products, arithmetic and copies ran while one was open for 1% of the time, Pallas kernels for 26%

profile of v11, /device:TPU:0, one launch (start us, length us, event | category | flops | bytes accessed | tf_op | source)
XLA Modules:
  0.0 67.1 jit_solution(8073869975339967028)
XLA Ops:
  0.0 3.0 %early_images.1 = (bf16[2,4,64,512]{3,2,1,0:T(8,128)(2,1)}, bf16[2,3,64,512]{3,2,1,0:T(8,128)(2,1)}, bf16[2,64,128]{2,1,0:T(8,128)(2,1)}, bf16[64,128]{1,0:T(8,128)(2,1)}) custom-call(bf16[2,6,64,512]{3,2,1,0:T(8,128)(2,1)} %slc_ref.13, s32[2,192]{1,0:T(2,128)} %bitcast.3), custom_call_target="tpu_custom_call" | custom-call | tf_op jit(solution)/shard_map/early_images/pallas_call | solution.py:574
  3.0 3.6 %collective-permute-start.4 = (bf16[64,128]{1,0:T(8,128)(2,1)}, bf16[64,128]{1,0:T(8,128)(2,1)S(1)}, u32[]{:S(2)}, u32[]{:S(2)}) collective-permute-start(bf16[64,128]{1,0:T(8,128)(2,1)} %get-tuple-element.21), channel_id=1, source_target_pairs={{0,9},{1,8},{2,11},{3,10},{4,13},{5,12},{6,15},{7,14},{8,1},{9,0},... | collective-permute-start | bytes 49160 | tf_op jit(solution)/shard_map/ppermute | solution.py:611
  6.6 0.7 collective-permute-start
  7.3 0.7 %collective-permute-start.2 = (bf16[2,3,64,512]{3,2,1,0:T(8,128)(2,1)}, bf16[2,3,64,512]{3,2,1,0:T(8,128)(2,1)S(1)}, u32[]{:S(2)}, u32[]{:S(2)}) collective-permute-start(bf16[2,3,64,512]{3,2,1,0:T(8,128)(2,1)} %get-tuple-element.19), channel_id=1, source_target_pairs={{6,8},{8,6},{7,9},{9,7},{22,24},{24,22},{23,25},{25,23}} | collective-permute-start | bytes 1179656 | tf_op jit(solution)/shard_map/ppermute | solution.py:616
  7.9 5.1 %collective-permute-start.7 = (bf16[2,4,64,512]{3,2,1,0:T(8,128)(2,1)}, bf16[2,4,64,512]{3,2,1,0:T(8,128)(2,1)S(1)}, u32[]{:S(2)}, u32[]{:S(2)}) collective-permute-start(bf16[2,4,64,512]{3,2,1,0:T(8,128)(2,1)} %get-tuple-element.23), channel_id=1, source_target_pairs={{0,8},{2,10},{4,12},{6,14},{8,0},{10,2},{12,4},{14,6},{1,9},{3,11}... | collective-permute-start | bytes 1572872 | tf_op jit(solution)/shard_map/ppermute | solution.py:593
  13.1 0.7 %pad_add_fusion.lists.pairs_ref = s32[4,192]{1,0:T(4,128)S(1)} fusion(s32[1,192]{1,0:T(1,128)} %bitcast.5, s32[1,192]{1,0:T(1,128)} %bitcast.6, s32[2,192]{1,0:T(2,128)} %bitcast.4), kind=kLoop, calls=%fused_computation | loop fusion | flops 1536 | bytes 6144 | tf_op jit(solution)/shard_map/concatenate | solution.py:532
  13.8 0.5 range_bands.1.bands_ref
  14.3 0.0 collective-permute-done.packed_ref
  14.3 0.0 copy-start
  14.4 1.1 %copy-done = bf16[2,6,64,512]{3,2,1,0:T(8,128)(2,1)S(1)} copy-done((bf16[2,6,64,512]{3,2,1,0:T(8,128)(2,1)S(1)}, bf16[2,6,64,512]{3,2,1,0:T(8,128)(2,1)}, u32[]{:S(2)}) %copy-start) | copy-done | bytes 786456
  15.5 1.4 %beside_images.1 = (bf16[400,512]{1,0:T(8,128)(2,1)S(1)}, bf16[400,512]{1,0:T(8,128)(2,1)S(1)}, bf16[2,6,64,128]{3,2,1,0:T(8,128)(2,1)S(1)}, bf16[64,128]{1,0:T(8,128)(2,1)S(1)}) custom-call(bf16[2,6,64,512]{3,2,1,0:T(8,128)(2,1)S(1)} %copy-done, bf16[2,64,128]{2,1,0:T(8,128)(2,1)S(1)} %collective-permute-done.packed_ref), custom_call_target="tpu_custom_call" | custom-call | tf_op jit(solution)/shard_map/beside_images/pallas_call | solution.py:595
  16.9 0.7 collective-permute-start.3
  17.5 2.8 %collective-permute-start.1 = (bf16[400,512]{1,0:T(8,128)(2,1)S(1)}, bf16[400,512]{1,0:T(8,128)(2,1)S(1)}, u32[]{:S(2)}, u32[]{:S(2)}) collective-permute-start(bf16[400,512]{1,0:T(8,128)(2,1)S(1)} %get-tuple-element.18), channel_id=1, source_target_pairs={{0,6},{2,0},{4,2},{6,4},{8,10},{10,12},{12,14},{14,8},{1,7},{3,1},... | collective-permute-start | bytes 1228808 | tf_op jit(solution)/shard_map/ppermute | solution.py:619
  20.3 0.0 collective-permute-done.4.refs_1_.strips_ref
  20.3 1.3 %collective-permute-start.6 = (bf16[400,512]{1,0:T(8,128)(2,1)S(1)}, bf16[400,512]{1,0:T(8,128)(2,1)S(1)}, u32[]{:S(2)}, u32[]{:S(2)}) collective-permute-start(bf16[400,512]{1,0:T(8,128)(2,1)S(1)} %get-tuple-element.22), channel_id=1, source_target_pairs={{0,2},{2,4},{4,6},{10,8},{12,10},{14,12},{1,3},{3,5},{5,7},{11,9},... | collective-permute-start | bytes 1228808 | tf_op jit(solution)/shard_map/ppermute | solution.py:618
  21.6 10.4 %own_pairs.1 = (f32[2,24,64,512]{3,2,1,0:T(8,128)}, bf16[6,64,1536]{2,1,0:T(8,128)(2,1)S(1)}) custom-call(s32[4,192]{1,0:T(4,128)S(1)} %pad_add_fusion.lists.pairs_ref, bf16[2,6,64,512]{3,2,1,0:T(8,128)(2,1)S(1)} %copy-done, bf16[2,6,64,128]{3,2,1,0:T(8,128)(2,1)S(1)} %get-tuple-element.16.rim_ref, bf16[5,2,768,256]{3,2,1,0:T(8,128)(2,1)S(1)} %range_bands.1.bands_ref), custom_call_target="tpu_custom_call" | custom-call | flops 20000000000 | bytes 1 | tf_op jit(solution)/shard_map/own_pairs/pallas_call | solution.py:642
  32.0 0.0 collective-permute-done.3.edges_ref
  32.0 0.0 collective-permute-done.2.middle_ref
  32.0 7.2 %collective-permute-done.1.inner_ref.ring_ref = bf16[400,512]{1,0:T(8,128)(2,1)S(1)} collective-permute-done((bf16[400,512]{1,0:T(8,128)(2,1)S(1)}, bf16[400,512]{1,0:T(8,128)(2,1)S(1)}, u32[]{:S(2)}, u32[]{:S(2)}) %collective-permute-start.1) | collective-permute-done | bytes 409632 | tf_op jit(solution)/shard_map/ppermute | solution.py:619
  39.2 0.9 %late_images.1._sent = bf16[272,512]{1,0:T(8,128)(2,1)S(1)} custom-call(bf16[2,6,64,512]{3,2,1,0:T(8,128)(2,1)S(1)} %copy-done, bf16[2,6,64,128]{3,2,1,0:T(8,128)(2,1)S(1)} %get-tuple-element.16.rim_ref, bf16[400,512]{1,0:T(8,128)(2,1)S(1)} %collective-permute-done.1.inner_ref.ring_ref, bf16[2,3,64,512]{3,2,1,0:T(8,128)(2,1)S(1)} %collective-permute-done.2.middle_ref, ...), custom_call_target="tpu_custom_call" | custom-call | tf_op jit(solution)/shard_map/late_images/pallas_call | solution.py:667
  40.1 16.6 %collective-permute-start.5 = (bf16[272,512]{1,0:T(8,128)(2,1)S(1)}, bf16[272,512]{1,0:T(8,128)(2,1)S(1)}, u32[]{:S(2)}, u32[]{:S(2)}) collective-permute-start(bf16[272,512]{1,0:T(8,128)(2,1)S(1)} %late_images.1._sent), channel_id=1, source_target_pairs={{0,8},{2,10},{4,12},{10,2},{12,4},{14,6},{6,0},{8,14},{1,9},{3,11}... | collective-permute-start | bytes 835592 | tf_op jit(solution)/shard_map/ppermute | solution.py:678
  56.7 0.0 collective-permute-done.7.images_ref
  56.7 3.8 %annual_pairs.1._ = f32[2,24,64,512]{3,2,1,0:T(8,128)} custom-call(s32[4,192]{1,0:T(4,128)S(1)} %pad_add_fusion.lists.pairs_ref, bf16[2,6,64,512]{3,2,1,0:T(8,128)(2,1)S(1)} %copy-done, bf16[2,6,64,128]{3,2,1,0:T(8,128)(2,1)S(1)} %get-tuple-element.16.rim_ref, bf16[5,2,768,256]{3,2,1,0:T(8,128)(2,1)S(1)} %range_bands.1.bands_ref, ...), custom_call_target="tpu_custom_call", output_to_operand_aliasing={{}: (9, {})} | custom-call | flops 1 | bytes 1 | tf_op jit(solution)/shard_map/annual_pairs/pallas_call | solution.py:654
  60.4 0.0 collective-permute-done.6.outer_ref
  60.5 0.8 %near_pairs.1._ = f32[2,24,64,512]{3,2,1,0:T(8,128)} custom-call(s32[4,192]{1,0:T(4,128)S(1)} %pad_add_fusion.lists.pairs_ref, bf16[2,6,64,512]{3,2,1,0:T(8,128)(2,1)S(1)} %copy-done, bf16[2,6,64,128]{3,2,1,0:T(8,128)(2,1)S(1)} %get-tuple-element.16.rim_ref, bf16[5,2,768,256]{3,2,1,0:T(8,128)(2,1)S(1)} %range_bands.1.bands_ref, ...), custom_call_target="tpu_custom_call", output_to_operand_aliasing={{}: (9, {})} | custom-call | flops 1 | bytes 1 | tf_op jit(solution)/shard_map/near_pairs/pallas_call | solution.py:654
  61.2 3.5 %collective-permute-done.5.images_ref = bf16[272,512]{1,0:T(8,128)(2,1)S(1)} collective-permute-done((bf16[272,512]{1,0:T(8,128)(2,1)S(1)}, bf16[272,512]{1,0:T(8,128)(2,1)S(1)}, u32[]{:S(2)}, u32[]{:S(2)}) %collective-permute-start.5) | collective-permute-done | bytes 278560 | tf_op jit(solution)/shard_map/ppermute | solution.py:678
  64.7 2.4 %last_pairs.1 = f32[2,24,64,512]{3,2,1,0:T(8,128)} custom-call(s32[4,192]{1,0:T(4,128)S(1)} %pad_add_fusion.lists.pairs_ref, bf16[2,6,64,512]{3,2,1,0:T(8,128)(2,1)S(1)} %copy-done, bf16[2,6,64,128]{3,2,1,0:T(8,128)(2,1)S(1)} %get-tuple-element.16.rim_ref, bf16[5,2,768,256]{3,2,1,0:T(8,128)(2,1)S(1)} %range_bands.1.bands_ref, ...), custom_call_target="tpu_custom_call", output_to_operand_aliasing={{}: (9, {})} | custom-call | flops 1 | bytes 1 | tf_op jit(solution)/shard_map/last_pairs/pallas_call | solution.py:654
Async XLA Ops:
  3.0 17.3 %collective-permute-start.4 = (bf16[64,128]{1,0:T(8,128)(2,1)}, bf16[64,128]{1,0:T(8,128)(2,1)S(1)}, u32[]{:S(2)}, u32[]{:S(2)}) collective-permute-start(bf16[64,128]{1,0:T(8,128)(2,1)} %get-tuple-element.21), channel_id=1, source_target_pairs={{0,9},{1,8},{2,11},{3,10},{4,13},{5,12},{6,15},{7,14},{8,1},{9,0},... | collective-permute-start | bytes 49160 | tf_op jit(solution)/shard_map/ppermute | solution.py:611
  6.6 7.7 %collective-permute-start = (bf16[2,64,128]{2,1,0:T(8,128)(2,1)}, bf16[2,64,128]{2,1,0:T(8,128)(2,1)S(1)}, u32[]{:S(2)}, u32[]{:S(2)}) collective-permute-start(bf16[2,64,128]{2,1,0:T(8,128)(2,1)} %get-tuple-element.15), channel_id=1, source_target_pairs={{0,1},{1,0},{2,3},{3,2},{4,5},{5,4},{6,7},{7,6},{8,9},{9,8},{10,11... | collective-permute-start | bytes 98312 | tf_op jit(solution)/shard_map/ppermute | solution.py:594
  7.3 24.7 %collective-permute-start.2 = (bf16[2,3,64,512]{3,2,1,0:T(8,128)(2,1)}, bf16[2,3,64,512]{3,2,1,0:T(8,128)(2,1)S(1)}, u32[]{:S(2)}, u32[]{:S(2)}) collective-permute-start(bf16[2,3,64,512]{3,2,1,0:T(8,128)(2,1)} %get-tuple-element.19), channel_id=1, source_target_pairs={{6,8},{8,6},{7,9},{9,7},{22,24},{24,22},{23,25},{25,23}} | collective-permute-start | bytes 1179656 | tf_op jit(solution)/shard_map/ppermute | solution.py:616
  7.9 48.7 %collective-permute-start.7 = (bf16[2,4,64,512]{3,2,1,0:T(8,128)(2,1)}, bf16[2,4,64,512]{3,2,1,0:T(8,128)(2,1)S(1)}, u32[]{:S(2)}, u32[]{:S(2)}) collective-permute-start(bf16[2,4,64,512]{3,2,1,0:T(8,128)(2,1)} %get-tuple-element.23), channel_id=1, source_target_pairs={{0,8},{2,10},{4,12},{6,14},{8,0},{10,2},{12,4},{14,6},{1,9},{3,11}... | collective-permute-start | bytes 1572872 | tf_op jit(solution)/shard_map/ppermute | solution.py:593
  14.3 1.1 %copy-start = (bf16[2,6,64,512]{3,2,1,0:T(8,128)(2,1)S(1)}, bf16[2,6,64,512]{3,2,1,0:T(8,128)(2,1)}, u32[]{:S(2)}) copy-start(bf16[2,6,64,512]{3,2,1,0:T(8,128)(2,1)} %slc_ref.13) | copy-start | bytes 2359300
  16.9 15.1 %collective-permute-start.3 = (bf16[64,128]{1,0:T(8,128)(2,1)S(1)}, bf16[64,128]{1,0:T(8,128)(2,1)S(1)}, u32[]{:S(2)}, u32[]{:S(2)}) collective-permute-start(bf16[64,128]{1,0:T(8,128)(2,1)S(1)} %get-tuple-element.20), channel_id=1, source_target_pairs={{6,8},{8,6},{7,9},{9,7},{22,24},{24,22},{23,25},{25,23}} | collective-permute-start | bytes 49160 | tf_op jit(solution)/shard_map/ppermute | solution.py:617
  17.5 21.6 %collective-permute-start.1 = (bf16[400,512]{1,0:T(8,128)(2,1)S(1)}, bf16[400,512]{1,0:T(8,128)(2,1)S(1)}, u32[]{:S(2)}, u32[]{:S(2)}) collective-permute-start(bf16[400,512]{1,0:T(8,128)(2,1)S(1)} %get-tuple-element.18), channel_id=1, source_target_pairs={{0,6},{2,0},{4,2},{6,4},{8,10},{10,12},{12,14},{14,8},{1,7},{3,1},... | collective-permute-start | bytes 1228808 | tf_op jit(solution)/shard_map/ppermute | solution.py:619
  20.3 40.2 %collective-permute-start.6 = (bf16[400,512]{1,0:T(8,128)(2,1)S(1)}, bf16[400,512]{1,0:T(8,128)(2,1)S(1)}, u32[]{:S(2)}, u32[]{:S(2)}) collective-permute-start(bf16[400,512]{1,0:T(8,128)(2,1)S(1)} %get-tuple-element.22), channel_id=1, source_target_pairs={{0,2},{2,4},{4,6},{10,8},{12,10},{14,12},{1,3},{3,5},{5,7},{11,9},... | collective-permute-start | bytes 1228808 | tf_op jit(solution)/shard_map/ppermute | solution.py:618
  40.1 24.7 %collective-permute-start.5 = (bf16[272,512]{1,0:T(8,128)(2,1)S(1)}, bf16[272,512]{1,0:T(8,128)(2,1)S(1)}, u32[]{:S(2)}, u32[]{:S(2)}) collective-permute-start(bf16[272,512]{1,0:T(8,128)(2,1)S(1)} %late_images.1._sent), channel_id=1, source_target_pairs={{0,8},{2,10},{4,12},{10,2},{12,4},{14,6},{6,0},{8,14},{1,9},{3,11}... | collective-permute-start | bytes 835592 | tf_op jit(solution)/shard_map/ppermute | solution.py:678

commit v12 on v8

--- a/solution.py
+++ b/solution.py
@@ -14,6 +14,8 @@
 EPSILON = 1e-06
 TILE = 128
 INNER = TILE // 2
+OWN_FLOPS = 4_000_000_000
+ANNUAL_FLOPS = 8_000_000_000
 PARTNER, HEIGHT, REACH = 1, 2, 3
 WORK_MIB = 16
 FIRST_MIB = 56
@@ -135,10 +137,8 @@
         copy.wait()
 
 
-def late_kernel(plan, slc_ref, rim_ref, inner_ref, held_ref, pairs_ref, *refs):
-    late_ref, outer_ref, tiles_ref, sem = refs[-4:]
-    copy = pltpu.make_async_copy(held_ref, outer_ref, sem)
-    copy.start()
+def late_kernel(plan, slc_ref, rim_ref, inner_ref, pairs_ref, *refs):
+    late_ref, tiles_ref = refs[-2:]
     me, strip = lax.axis_index("date"), lax.axis_index("strip")
     dates, late, rows = plan["dates"], plan["late"], plan["rows"]
     half = plan["devices"] // 2
@@ -167,7 +167,6 @@
 
     tiles = [tiles_ref[k, c] for k in range(late) for c in range(2)]
     write_strips(late_ref, gather_strips(tiles, strip))
-    copy.wait()
 
 
 def bands_kernel(cols, out_ref):
@@ -401,7 +400,7 @@
 
 
 def annual_kernel(plan, lists, slc_ref, rim_ref, bands_ref, powers_ref, ring_ref,
-                  images_ref, strips_ref, _, out_ref, *scratch, is_late):
+                  images_ref, strips_ref, _sent, _, out_ref, *scratch, is_late):
     pairs = Pairs(plan, lists, slc_ref, rim_ref, bands_ref, powers_ref, out_ref, scratch)
     dates, late = plan["dates"], plan["late"]
     half = plan["devices"] // 2
@@ -595,6 +594,7 @@
             strips, both, [(2 * a + s, 2 * b + 1 - s) for a, b in swap for s in (0, 1)]
         )
         middle = lax.ppermute(outer, "date", [(half - 1, half), (half, half - 1)])
+        outer = lax.ppermute(outer, "date", [(b, a) for a, b in down])
         inner = lax.ppermute(inner, "date", down)
     else:
         rim = swapped_rims(slc)
@@ -625,11 +625,11 @@
         out_specs=(ANY, VMEM),
         scratch_shapes=scratch,
         compiler_params=limit(WORK_MIB),
-        cost_estimate=cost(20_000_000_000),
+        cost_estimate=cost(OWN_FLOPS),
         name="own_pairs",
     )(lists, slc, rim, bands)
 
-    def more_pairs(kernel, out, others, name):
+    def more_pairs(kernel, out, others, name, flops=1):
         return pl.pallas_call(
             functools.partial(kernel, plan),
             out_shape=out_shape,
@@ -638,31 +638,27 @@
             scratch_shapes=scratch,
             input_output_aliases={5 + len(others): 0},
             compiler_params=limit(WORK_MIB),
-            cost_estimate=cost(1),
+            cost_estimate=cost(flops),
             name=name,
         )(lists, slc, rim, bands, powers, *others, out)
 
     if halves:
-        payload, outer = pl.pallas_call(
+        payload = sent = pl.pallas_call(
             functools.partial(late_kernel, plan),
-            out_shape=(payload_shape(late), payload_shape(NEAR)),
-            in_specs=[VMEM, VMEM, VMEM, ANY, SMEM, ANY, ANY],
-            out_specs=(VMEM, VMEM),
-            scratch_shapes=[
-                pltpu.VMEM((late, planes, rows, TILE), dtype),
-                pltpu.SemaphoreType.DMA,
-            ],
+            out_shape=payload_shape(late),
+            in_specs=[VMEM, VMEM, VMEM, SMEM, ANY, ANY],
+            out_specs=VMEM,
+            scratch_shapes=[pltpu.VMEM((late, planes, rows, TILE), dtype)],
             compiler_params=limit(WORK_MIB),
             name="late_images",
-        )(slc, rim, inner, outer, lists, powers, strips)
+        )(slc, rim, inner, lists, powers, strips)
         payload = lax.ppermute(payload, "date", swap)
-        outer = lax.ppermute(outer, "date", [(b, a) for a, b in down])
     if halves:
         early_pairs = functools.partial(annual_kernel, is_late=False)
-        out = more_pairs(early_pairs, out, (inner, early, strips), "annual_pairs")
+        out = more_pairs(early_pairs, out, (inner, early, strips, sent), "annual_pairs", ANNUAL_FLOPS)
         out = more_pairs(rest_kernel, out, (inner, outer, middle), "near_pairs")
         late_pairs = functools.partial(annual_kernel, is_late=True)
-        out = more_pairs(late_pairs, out, (outer, payload, strips), "last_pairs")
+        out = more_pairs(late_pairs, out, (outer, payload, strips, sent), "last_pairs")
     else:
         out = more_pairs(rest_kernel, out, (inner, outer, inner), "near_pairs")
         out = more_pairs(plain_kernel, out, (annual, swapped_rims(annual)), "annual_pairs")

time: 57.9 us -> 55.4 us (0.957)
  the two profiles are of different devices: /device:TPU:8 before, /device:TPU:0 now
where the time goes in v12:
time: 55.4 us; the launch traced here: 55.2 us
  Pallas kernels  25.3 us (46%)
  waiting for transfers between devices  20.2 us (36%)
  starting transfers between devices  7.76 us (14%)
  local copies, waits for them, and re-layouts  1.13 us (2%)
  other arithmetic  0.72 us (1%)
    pallas_call x3, Pallas kernels, more_pairs(): pl.pallas_call(functools.partial(kernel, plan), out_shape=out_shape, in_s...  11.4 us
    ppermute x1, waiting for transfers between devices, body(): payload = lax.ppermute(payload, 'date', swap)  11.1 us
    ppermute x1, waiting for transfers between devices, body(): lax.ppermute(strips, both, [(2 * a + s, 2 * b + 1 - s) for a, b in swap f...  9.06 us
    pallas_call x1, Pallas kernels, body(): pl.pallas_call(functools.partial(own_kernel, plan), out_shape=(out_shape,...  8.39 us
    ppermute x1, starting transfers between devices, body(): early = lax.ppermute(early, 'date', swap)  3.68 us
    pallas_call x1, Pallas kernels, body(): pl.pallas_call(functools.partial(early_kernel, plan), out_shape=(images(d...  2.89 us
    ppermute x1, starting transfers between devices, body(): inner = lax.ppermute(inner, 'date', down)  2.57 us
    pallas_call x1, Pallas kernels, body(): pl.pallas_call(functools.partial(beside_kernel, plan), out_shape=(payload...  1.24 us
  transfers between devices with their start and end apart: 7, of which 2 were waited for; matrix products, arithmetic and copies ran while one was open for 1% of the time, Pallas kernels for 36%

profile of v12, /device:TPU:0, one launch (start us, length us, event | category | flops | bytes accessed | tf_op | source)
XLA Modules:
  0.0 55.2 jit_solution(17233390694685941927)
XLA Ops:
  0.0 2.9 %early_images.1 = (bf16[2,4,64,512]{3,2,1,0:T(8,128)(2,1)}, bf16[2,6,64,128]{3,2,1,0:T(8,128)(2,1)}, bf16[64,128]{1,0:T(8,128)(2,1)}) custom-call(bf16[2,6,64,512]{3,2,1,0:T(8,128)(2,1)} %slc_ref.13, s32[2,192]{1,0:T(2,128)} %bitcast.3), custom_call_target="tpu_custom_call" | custom-call | tf_op jit(solution)/shard_map/early_images/pallas_call | solution.py:562
  2.9 0.5 collective-permute-start
  3.4 3.7 %collective-permute-start.6 = (bf16[2,4,64,512]{3,2,1,0:T(8,128)(2,1)}, bf16[2,4,64,512]{3,2,1,0:T(8,128)(2,1)S(1)}, u32[]{:S(2)}, u32[]{:S(2)}) collective-permute-start(bf16[2,4,64,512]{3,2,1,0:T(8,128)(2,1)} %get-tuple-element.17), channel_id=1, source_target_pairs={{0,8},{2,10},{4,12},{6,14},{8,0},{10,2},{12,4},{14,6},{1,9},{3,11}... | collective-permute-start | bytes 1572872 | tf_op jit(solution)/shard_map/ppermute | solution.py:580
  7.1 0.1 collective-permute-start.3
  7.2 0.0 collective-permute-done.rim_ref
  7.2 0.0 copy-start
  7.2 1.1 %copy-done = bf16[2,6,64,512]{3,2,1,0:T(8,128)(2,1)S(1)} copy-done((bf16[2,6,64,512]{3,2,1,0:T(8,128)(2,1)S(1)}, bf16[2,6,64,512]{3,2,1,0:T(8,128)(2,1)}, u32[]{:S(2)}) %copy-start) | copy-done | bytes 786456
  8.3 1.2 %beside_images.1 = (bf16[400,512]{1,0:T(8,128)(2,1)S(1)}, bf16[400,512]{1,0:T(8,128)(2,1)S(1)}) custom-call(bf16[2,6,64,512]{3,2,1,0:T(8,128)(2,1)S(1)} %copy-done, bf16[2,6,64,128]{3,2,1,0:T(8,128)(2,1)S(1)} %collective-permute-done.rim_ref), custom_call_target="tpu_custom_call" | custom-call | tf_op jit(solution)/shard_map/beside_images/pallas_call | solution.py:582
  9.6 2.6 %collective-permute-start.2 = (bf16[400,512]{1,0:T(8,128)(2,1)S(1)}, bf16[400,512]{1,0:T(8,128)(2,1)S(1)}, u32[]{:S(2)}, u32[]{:S(2)}) collective-permute-start(bf16[400,512]{1,0:T(8,128)(2,1)S(1)} %get-tuple-element.15), channel_id=1, source_target_pairs={{0,6},{2,0},{4,2},{6,4},{8,10},{10,12},{12,14},{14,8},{1,7},{3,1},... | collective-permute-start | bytes 1228808 | tf_op jit(solution)/shard_map/ppermute | solution.py:598
  12.1 0.7 %pad_add_fusion.lists.pairs_ref = s32[4,192]{1,0:T(4,128)S(1)} fusion(s32[1,192]{1,0:T(1,128)} %bitcast.5, s32[1,192]{1,0:T(1,128)} %bitcast.6, s32[2,192]{1,0:T(2,128)} %bitcast.4), kind=kLoop, calls=%fused_computation | loop fusion | flops 1536 | bytes 6144 | tf_op jit(solution)/shard_map/concatenate | solution.py:520
  12.9 0.5 range_bands.1.bands_ref
  13.4 0.1 collective-permute-start.1
  13.5 0.7 %collective-permute-start.5 = (bf16[400,512]{1,0:T(8,128)(2,1)S(1)}, bf16[400,512]{1,0:T(8,128)(2,1)S(1)}, u32[]{:S(2)}, u32[]{:S(2)}) collective-permute-start(bf16[400,512]{1,0:T(8,128)(2,1)S(1)} %get-tuple-element.14), channel_id=1, source_target_pairs={{6,8},{8,6},{7,9},{9,7},{22,24},{24,22},{23,25},{25,23}} | collective-permute-start | bytes 1228808 | tf_op jit(solution)/shard_map/ppermute | solution.py:596
  14.1 8.4 %own_pairs.1 = (f32[2,24,64,512]{3,2,1,0:T(8,128)}, bf16[6,64,1536]{2,1,0:T(8,128)(2,1)S(1)}) custom-call(s32[4,192]{1,0:T(4,128)S(1)} %pad_add_fusion.lists.pairs_ref, bf16[2,6,64,512]{3,2,1,0:T(8,128)(2,1)S(1)} %copy-done, bf16[2,6,64,128]{3,2,1,0:T(8,128)(2,1)S(1)} %collective-permute-done.rim_ref, bf16[5,2,768,256]{3,2,1,0:T(8,128)(2,1)S(1)} %range_bands.1.bands_ref), custom_call_target="tpu_custom_call" | custom-call | flops 4000000000 | bytes 1 | tf_op jit(solution)/shard_map/own_pairs/pallas_call | solution.py:621
  22.5 9.1 %collective-permute-done.3.refs_1_.strips_ref = bf16[64,128]{1,0:T(8,128)(2,1)S(1)} collective-permute-done((bf16[64,128]{1,0:T(8,128)(2,1)}, bf16[64,128]{1,0:T(8,128)(2,1)S(1)}, u32[]{:S(2)}, u32[]{:S(2)}) %collective-permute-start.3) | collective-permute-done | bytes 16416 | tf_op jit(solution)/shard_map/ppermute | solution.py:593
  31.6 0.0 collective-permute-done.2.inner_ref.ring_ref
  31.6 0.9 %late_images.1._sent = bf16[272,512]{1,0:T(8,128)(2,1)S(1)} custom-call(bf16[2,6,64,512]{3,2,1,0:T(8,128)(2,1)S(1)} %copy-done, bf16[2,6,64,128]{3,2,1,0:T(8,128)(2,1)S(1)} %collective-permute-done.rim_ref, bf16[400,512]{1,0:T(8,128)(2,1)S(1)} %collective-permute-done.2.inner_ref.ring_ref, s32[4,192]{1,0:T(4,128)S(1)} %pad_add_fusion.lists.pairs_ref, ...), custom_call_target="tpu_custom_call" | custom-call | tf_op jit(solution)/shard_map/late_images/pallas_call | solution.py:646
  32.5 0.2 collective-permute-start.4
  32.7 0.0 collective-permute-done.6.images_ref
  32.7 3.8 %annual_pairs.1._ = f32[2,24,64,512]{3,2,1,0:T(8,128)} custom-call(s32[4,192]{1,0:T(4,128)S(1)} %pad_add_fusion.lists.pairs_ref, bf16[2,6,64,512]{3,2,1,0:T(8,128)(2,1)S(1)} %copy-done, bf16[2,6,64,128]{3,2,1,0:T(8,128)(2,1)S(1)} %collective-permute-done.rim_ref, bf16[5,2,768,256]{3,2,1,0:T(8,128)(2,1)S(1)} %range_bands.1.bands_ref, ...), custom_call_target="tpu_custom_call", output_to_operand_aliasing={{}: (9, {})} | custom-call | flops 8000000000 | bytes 1 | tf_op jit(solution)/shard_map/annual_pairs/pallas_call | solution.py:633
  36.5 0.0 collective-permute-done.1.outer_ref.ring_ref
  36.5 0.0 collective-permute-done.5.middle_ref
  36.5 5.0 %near_pairs.1._ = f32[2,24,64,512]{3,2,1,0:T(8,128)} custom-call(s32[4,192]{1,0:T(4,128)S(1)} %pad_add_fusion.lists.pairs_ref, bf16[2,6,64,512]{3,2,1,0:T(8,128)(2,1)S(1)} %copy-done, bf16[2,6,64,128]{3,2,1,0:T(8,128)(2,1)S(1)} %collective-permute-done.rim_ref, bf16[5,2,768,256]{3,2,1,0:T(8,128)(2,1)S(1)} %range_bands.1.bands_ref, ...), custom_call_target="tpu_custom_call", output_to_operand_aliasing={{}: (8, {})} | custom-call | flops 1 | bytes 1 | tf_op jit(solution)/shard_map/near_pairs/pallas_call | solution.py:633
  41.5 11.1 %collective-permute-done.4.images_ref = bf16[272,512]{1,0:T(8,128)(2,1)S(1)} collective-permute-done((bf16[272,512]{1,0:T(8,128)(2,1)S(1)}, bf16[272,512]{1,0:T(8,128)(2,1)S(1)}, u32[]{:S(2)}, u32[]{:S(2)}) %collective-permute-start.4) | collective-permute-done | bytes 278560 | tf_op jit(solution)/shard_map/ppermute | solution.py:655
  52.6 2.6 %last_pairs.1 = f32[2,24,64,512]{3,2,1,0:T(8,128)} custom-call(s32[4,192]{1,0:T(4,128)S(1)} %pad_add_fusion.lists.pairs_ref, bf16[2,6,64,512]{3,2,1,0:T(8,128)(2,1)S(1)} %copy-done, bf16[2,6,64,128]{3,2,1,0:T(8,128)(2,1)S(1)} %collective-permute-done.rim_ref, bf16[5,2,768,256]{3,2,1,0:T(8,128)(2,1)S(1)} %range_bands.1.bands_ref, ...), custom_call_target="tpu_custom_call", output_to_operand_aliasing={{}: (9, {})} | custom-call | flops 1 | bytes 1 | tf_op jit(solution)/shard_map/last_pairs/pallas_call | solution.py:633
Async XLA Ops:
  2.9 4.3 %collective-permute-start = (bf16[2,6,64,128]{3,2,1,0:T(8,128)(2,1)}, bf16[2,6,64,128]{3,2,1,0:T(8,128)(2,1)S(1)}, u32[]{:S(2)}, u32[]{:S(2)}) collective-permute-start(bf16[2,6,64,128]{3,2,1,0:T(8,128)(2,1)} %get-tuple-element.12), channel_id=1, source_target_pairs={{0,1},{1,0},{2,3},{3,2},{4,5},{5,4},{6,7},{7,6},{8,9},{9,8},{10,11... | collective-permute-start | bytes 589832 | tf_op jit(solution)/shard_map/ppermute | solution.py:581
  3.4 29.3 %collective-permute-start.6 = (bf16[2,4,64,512]{3,2,1,0:T(8,128)(2,1)}, bf16[2,4,64,512]{3,2,1,0:T(8,128)(2,1)S(1)}, u32[]{:S(2)}, u32[]{:S(2)}) collective-permute-start(bf16[2,4,64,512]{3,2,1,0:T(8,128)(2,1)} %get-tuple-element.17), channel_id=1, source_target_pairs={{0,8},{2,10},{4,12},{6,14},{8,0},{10,2},{12,4},{14,6},{1,9},{3,11}... | collective-permute-start | bytes 1572872 | tf_op jit(solution)/shard_map/ppermute | solution.py:580
  7.1 24.5 %collective-permute-start.3 = (bf16[64,128]{1,0:T(8,128)(2,1)}, bf16[64,128]{1,0:T(8,128)(2,1)S(1)}, u32[]{:S(2)}, u32[]{:S(2)}) collective-permute-start(bf16[64,128]{1,0:T(8,128)(2,1)} %get-tuple-element.16), channel_id=1, source_target_pairs={{0,9},{1,8},{2,11},{3,10},{4,13},{5,12},{6,15},{7,14},{8,1},{9,0},... | collective-permute-start | bytes 49160 | tf_op jit(solution)/shard_map/ppermute | solution.py:593
  7.2 1.1 %copy-start = (bf16[2,6,64,512]{3,2,1,0:T(8,128)(2,1)S(1)}, bf16[2,6,64,512]{3,2,1,0:T(8,128)(2,1)}, u32[]{:S(2)}) copy-start(bf16[2,6,64,512]{3,2,1,0:T(8,128)(2,1)} %slc_ref.13) | copy-start | bytes 2359300
  9.6 22.1 %collective-permute-start.2 = (bf16[400,512]{1,0:T(8,128)(2,1)S(1)}, bf16[400,512]{1,0:T(8,128)(2,1)S(1)}, u32[]{:S(2)}, u32[]{:S(2)}) collective-permute-start(bf16[400,512]{1,0:T(8,128)(2,1)S(1)} %get-tuple-element.15), channel_id=1, source_target_pairs={{0,6},{2,0},{4,2},{6,4},{8,10},{10,12},{12,14},{14,8},{1,7},{3,1},... | collective-permute-start | bytes 1228808 | tf_op jit(solution)/shard_map/ppermute | solution.py:598
  13.4 23.1 %collective-permute-start.1 = (bf16[400,512]{1,0:T(8,128)(2,1)S(1)}, bf16[400,512]{1,0:T(8,128)(2,1)S(1)}, u32[]{:S(2)}, u32[]{:S(2)}) collective-permute-start(bf16[400,512]{1,0:T(8,128)(2,1)S(1)} %get-tuple-element.14), channel_id=1, source_target_pairs={{6,0},{0,2},{2,4},{4,6},{10,8},{12,10},{14,12},{8,14},{7,1},{1,3},... | collective-permute-start | bytes 1228808 | tf_op jit(solution)/shard_map/ppermute | solution.py:597
  13.5 23.0 %collective-permute-start.5 = (bf16[400,512]{1,0:T(8,128)(2,1)S(1)}, bf16[400,512]{1,0:T(8,128)(2,1)S(1)}, u32[]{:S(2)}, u32[]{:S(2)}) collective-permute-start(bf16[400,512]{1,0:T(8,128)(2,1)S(1)} %get-tuple-element.14), channel_id=1, source_target_pairs={{6,8},{8,6},{7,9},{9,7},{22,24},{24,22},{23,25},{25,23}} | collective-permute-start | bytes 1228808 | tf_op jit(solution)/shard_map/ppermute | solution.py:596
  32.5 20.1 %collective-permute-start.4 = (bf16[272,512]{1,0:T(8,128)(2,1)S(1)}, bf16[272,512]{1,0:T(8,128)(2,1)S(1)}, u32[]{:S(2)}, u32[]{:S(2)}) collective-permute-start(bf16[272,512]{1,0:T(8,128)(2,1)S(1)} %late_images.1._sent), channel_id=1, source_target_pairs={{0,8},{2,10},{4,12},{6,14},{8,0},{10,2},{12,4},{14,6},{1,9},{3,11}... | collective-permute-start | bytes 835592 | tf_op jit(solution)/shard_map/ppermute | solution.py:655

commit v13 on v12

--- a/solution.py
+++ b/solution.py
@@ -138,7 +138,7 @@
 
 
 def late_kernel(plan, slc_ref, rim_ref, inner_ref, pairs_ref, *refs):
-    late_ref, tiles_ref = refs[-2:]
+    late_ref, end_ref, tiles_ref = refs[-3:]
     me, strip = lax.axis_index("date"), lax.axis_index("strip")
     dates, late, rows = plan["dates"], plan["late"], plan["rows"]
     half = plan["devices"] // 2
@@ -167,6 +167,20 @@
 
     tiles = [tiles_ref[k, c] for k in range(late) for c in range(2)]
     write_strips(late_ref, gather_strips(tiles, strip))
+
+    @pl.when((me == half) | (me == half - 1))
+    def _():
+        end = jnp.where(me < half, 0, 2 * half - 1)
+        end_slot = jnp.where(me < half, 0, dates - late)
+        tiles = []
+        for k in range(late):
+            date = end * dates + end_slot + k
+            at = pairs_ref[PARTNER, date * plan["per_date"] + NEAR] - me * dates
+            at = jnp.clip(at, 0, dates - 1)
+            for c in range(2):
+                end_ref[pl.ds((2 * k + c) * rows, rows)] = slc_ref[c, at]
+                tiles.append(rim_ref[c, at])
+        write_strips(end_ref, gather_strips(tiles, strip))
 
 
 def bands_kernel(cols, out_ref):
@@ -424,7 +438,7 @@
         far = (other < split_date) == lower
         end = 2 * split_date
         if is_late:
-            ring_at = jnp.where(lower, other - (split_date - NEAR), other - split_date)
+            ring_at = k
         else:
             ring_at = jnp.where(lower, other, other - (end - NEAR))
         ring_at = jnp.clip(ring_at, 0, NEAR - 1)
@@ -593,8 +607,11 @@
         strips = lax.ppermute(
             strips, both, [(2 * a + s, 2 * b + 1 - s) for a, b in swap for s in (0, 1)]
         )
-        middle = lax.ppermute(outer, "date", [(half - 1, half), (half, half - 1)])
-        outer = lax.ppermute(outer, "date", [(b, a) for a, b in down])
+        up = [(b, a) for a, b in down if b not in (half - 1, half)]
+        across = [(half - 1, half), (half, half - 1)]
+        second = outer
+        outer = lax.ppermute(second, "date", up)
+        middle = lax.ppermute(second, "date", across)
         inner = lax.ppermute(inner, "date", down)
     else:
         rim = swapped_rims(slc)
@@ -643,22 +660,24 @@
         )(lists, slc, rim, bands, powers, *others, out)
 
     if halves:
-        payload = sent = pl.pallas_call(
+        payload, ending = pl.pallas_call(
             functools.partial(late_kernel, plan),
-            out_shape=payload_shape(late),
+            out_shape=(payload_shape(late), payload_shape(late)),
             in_specs=[VMEM, VMEM, VMEM, SMEM, ANY, ANY],
-            out_specs=VMEM,
+            out_specs=(VMEM, VMEM),
             scratch_shapes=[pltpu.VMEM((late, planes, rows, TILE), dtype)],
             compiler_params=limit(WORK_MIB),
             name="late_images",
         )(slc, rim, inner, lists, powers, strips)
+        sent = payload
         payload = lax.ppermute(payload, "date", swap)
+        ending = lax.ppermute(ending, "date", [(half - 1, 0), (half, devices - 1)])
     if halves:
         early_pairs = functools.partial(annual_kernel, is_late=False)
         out = more_pairs(early_pairs, out, (inner, early, strips, sent), "annual_pairs", ANNUAL_FLOPS)
         out = more_pairs(rest_kernel, out, (inner, outer, middle), "near_pairs")
         late_pairs = functools.partial(annual_kernel, is_late=True)
-        out = more_pairs(late_pairs, out, (outer, payload, strips, sent), "last_pairs")
+        out = more_pairs(late_pairs, out, (ending, payload, strips, sent), "last_pairs")
     else:
         out = more_pairs(rest_kernel, out, (inner, outer, inner), "near_pairs")
         out = more_pairs(plain_kernel, out, (annual, swapped_rims(annual)), "annual_pairs")

time: 55.4 us -> 56.1 us (1.013); the launches traced: 55.2 us -> 55.2 us
  starting transfers between devices: 7.76 us -> 16.3 us
  waiting for transfers between devices: 20.2 us -> 12.8 us
  Pallas kernels: 25.3 us -> 24.1 us
    ppermute x1, waiting for transfers between devices: 11.1 us -> 5.16 us  [body(): payload = lax.ppermute(payload, 'date', swap)]
    ppermute x1, starting transfers between devices: 0.17 us -> 6.03 us  [body(): payload = lax.ppermute(payload, 'date', swap)]
    ppermute x2 -> x3, starting transfers between devices: 0.74 us -> 3.41 us  [the longest x1 1.43 us: body(): outer = lax.ppermute(second, 'date', up)]
    ppermute x1, waiting for transfers between devices: 9.06 us -> 7.6 us  [body(): lax.ppermute(strips, both, [(2 * a + s, 2 * b + 1 - s) for a, b in swap f...]
    pallas_call x3, Pallas kernels: 11.4 us -> 10.3 us  [more_pairs(): pl.pallas_call(functools.partial(kernel, plan), out_shape=out_shape, in_s...]
  transfers between devices with their start and end apart: 7 -> 8, of which waited for: 2 -> 2; matrix products, arithmetic and copies ran while one was open for 1% -> 1% of each run, Pallas kernels for 36% -> 34%
where the time goes in v13:
time: 56.1 us; the launch traced here: 55.2 us
  Pallas kernels  24.1 us (43%)
  starting transfers between devices  16.3 us (29%)
  waiting for transfers between devices  12.8 us (23%)
  local copies, waits for them, and re-layouts  1.13 us (2%)
  other arithmetic  0.72 us (1%)
    pallas_call x3, Pallas kernels, more_pairs(): pl.pallas_call(functools.partial(kernel, plan), out_shape=out_shape, in_s...  10.3 us
    pallas_call x1, Pallas kernels, body(): pl.pallas_call(functools.partial(own_kernel, plan), out_shape=(out_shape,...  8.47 us
    ppermute x1, waiting for transfers between devices, body(): lax.ppermute(strips, both, [(2 * a + s, 2 * b + 1 - s) for a, b in swap f...  7.6 us
    ppermute x1, starting transfers between devices, body(): payload = lax.ppermute(payload, 'date', swap)  6.03 us
    ppermute x1, waiting for transfers between devices, body(): payload = lax.ppermute(payload, 'date', swap)  5.16 us
    ppermute x1, starting transfers between devices, body(): early = lax.ppermute(early, 'date', swap)  3.71 us
    pallas_call x1, Pallas kernels, body(): pl.pallas_call(functools.partial(early_kernel, plan), out_shape=(images(d...  2.9 us
    ppermute x1, starting transfers between devices, body(): inner = lax.ppermute(inner, 'date', down)  2.58 us
  transfers between devices with their start and end apart: 8, of which 2 were waited for; matrix products, arithmetic and copies ran while one was open for 1% of the time, Pallas kernels for 34%

profile of v13, /device:TPU:0, one launch (start us, length us, event | category | flops | bytes accessed | tf_op | source)
XLA Modules:
  0.0 55.2 jit_solution(13906863197090460322)
XLA Ops:
  0.0 2.9 %early_images.1 = (bf16[2,4,64,512]{3,2,1,0:T(8,128)(2,1)}, bf16[2,6,64,128]{3,2,1,0:T(8,128)(2,1)}, bf16[64,128]{1,0:T(8,128)(2,1)}) custom-call(bf16[2,6,64,512]{3,2,1,0:T(8,128)(2,1)} %slc_ref.13, s32[2,192]{1,0:T(2,128)} %bitcast.3), custom_call_target="tpu_custom_call" | custom-call | tf_op jit(solution)/shard_map/early_images/pallas_call | solution.py:576
  2.9 0.5 collective-permute-start
  3.4 3.7 %collective-permute-start.7 = (bf16[2,4,64,512]{3,2,1,0:T(8,128)(2,1)}, bf16[2,4,64,512]{3,2,1,0:T(8,128)(2,1)S(1)}, u32[]{:S(2)}, u32[]{:S(2)}) collective-permute-start(bf16[2,4,64,512]{3,2,1,0:T(8,128)(2,1)} %get-tuple-element.21), channel_id=1, source_target_pairs={{0,8},{2,10},{4,12},{6,14},{8,0},{10,2},{12,4},{14,6},{1,9},{3,11}... | collective-permute-start | bytes 1572872 | tf_op jit(solution)/shard_map/ppermute | solution.py:594
  7.1 0.1 collective-permute-start.2
  7.2 0.0 collective-permute-done.rim_ref
  7.2 0.0 copy-start
  7.2 1.1 %copy-done = bf16[2,6,64,512]{3,2,1,0:T(8,128)(2,1)S(1)} copy-done((bf16[2,6,64,512]{3,2,1,0:T(8,128)(2,1)S(1)}, bf16[2,6,64,512]{3,2,1,0:T(8,128)(2,1)}, u32[]{:S(2)}) %copy-start) | copy-done | bytes 786456
  8.3 1.2 %beside_images.1 = (bf16[400,512]{1,0:T(8,128)(2,1)S(1)}, bf16[400,512]{1,0:T(8,128)(2,1)S(1)}) custom-call(bf16[2,6,64,512]{3,2,1,0:T(8,128)(2,1)S(1)} %copy-done, bf16[2,6,64,128]{3,2,1,0:T(8,128)(2,1)S(1)} %collective-permute-done.rim_ref), custom_call_target="tpu_custom_call" | custom-call | tf_op jit(solution)/shard_map/beside_images/pallas_call | solution.py:596
  9.6 2.6 %collective-permute-start.1 = (bf16[400,512]{1,0:T(8,128)(2,1)S(1)}, bf16[400,512]{1,0:T(8,128)(2,1)S(1)}, u32[]{:S(2)}, u32[]{:S(2)}) collective-permute-start(bf16[400,512]{1,0:T(8,128)(2,1)S(1)} %get-tuple-element.16), channel_id=1, source_target_pairs={{0,6},{2,0},{4,2},{6,4},{8,10},{10,12},{12,14},{14,8},{1,7},{3,1},... | collective-permute-start | bytes 1228808 | tf_op jit(solution)/shard_map/ppermute | solution.py:615
  12.2 0.7 %pad_add_fusion.lists.pairs_ref = s32[4,192]{1,0:T(4,128)S(1)} fusion(s32[1,192]{1,0:T(1,128)} %bitcast.5, s32[1,192]{1,0:T(1,128)} %bitcast.6, s32[2,192]{1,0:T(2,128)} %bitcast.4), kind=kLoop, calls=%fused_computation | loop fusion | flops 1536 | bytes 6144 | tf_op jit(solution)/shard_map/concatenate | solution.py:534
  12.9 0.5 range_bands.1.bands_ref
  13.4 1.4 %collective-permute-start.5 = (bf16[400,512]{1,0:T(8,128)(2,1)S(1)}, bf16[400,512]{1,0:T(8,128)(2,1)S(1)}, u32[]{:S(2)}, u32[]{:S(2)}) collective-permute-start(bf16[400,512]{1,0:T(8,128)(2,1)S(1)} %get-tuple-element.20), channel_id=1, source_target_pairs={{0,2},{2,4},{4,6},{10,8},{12,10},{14,12},{1,3},{3,5},{5,7},{11,9},... | collective-permute-start | bytes 1228808 | tf_op jit(solution)/shard_map/ppermute | solution.py:613
  14.9 0.7 %collective-permute-start.6 = (bf16[400,512]{1,0:T(8,128)(2,1)S(1)}, bf16[400,512]{1,0:T(8,128)(2,1)S(1)}, u32[]{:S(2)}, u32[]{:S(2)}) collective-permute-start(bf16[400,512]{1,0:T(8,128)(2,1)S(1)} %get-tuple-element.20), channel_id=1, source_target_pairs={{6,8},{8,6},{7,9},{9,7},{22,24},{24,22},{23,25},{25,23}} | collective-permute-start | bytes 1228808 | tf_op jit(solution)/shard_map/ppermute | solution.py:614
  15.6 8.5 %own_pairs.1 = (f32[2,24,64,512]{3,2,1,0:T(8,128)}, bf16[6,64,1536]{2,1,0:T(8,128)(2,1)S(1)}) custom-call(s32[4,192]{1,0:T(4,128)S(1)} %pad_add_fusion.lists.pairs_ref, bf16[2,6,64,512]{3,2,1,0:T(8,128)(2,1)S(1)} %copy-done, bf16[2,6,64,128]{3,2,1,0:T(8,128)(2,1)S(1)} %collective-permute-done.rim_ref, bf16[5,2,768,256]{3,2,1,0:T(8,128)(2,1)S(1)} %range_bands.1.bands_ref), custom_call_target="tpu_custom_call" | custom-call | flops 4000000000 | bytes 1 | tf_op jit(solution)/shard_map/own_pairs/pallas_call | solution.py:638
  24.0 7.6 %collective-permute-done.2.refs_1_.strips_ref = bf16[64,128]{1,0:T(8,128)(2,1)S(1)} collective-permute-done((bf16[64,128]{1,0:T(8,128)(2,1)}, bf16[64,128]{1,0:T(8,128)(2,1)S(1)}, u32[]{:S(2)}, u32[]{:S(2)}) %collective-permute-start.2) | collective-permute-done | bytes 16416 | tf_op jit(solution)/shard_map/ppermute | solution.py:607
  31.6 0.0 collective-permute-done.1.inner_ref.ring_ref
  31.6 0.8 %late_images.1 = (bf16[272,512]{1,0:T(8,128)(2,1)S(1)}, bf16[272,512]{1,0:T(8,128)(2,1)S(1)}) custom-call(bf16[2,6,64,512]{3,2,1,0:T(8,128)(2,1)S(1)} %copy-done, bf16[2,6,64,128]{3,2,1,0:T(8,128)(2,1)S(1)} %collective-permute-done.rim_ref, bf16[400,512]{1,0:T(8,128)(2,1)S(1)} %collective-permute-done.1.inner_ref.ring_ref, ...), custom_call_target="tpu_custom_call" | custom-call | tf_op jit(solution)/shard_map/late_images/pallas_call | solution.py:663
  32.4 1.3 %collective-permute-start.3 = (bf16[272,512]{1,0:T(8,128)(2,1)S(1)}, bf16[272,512]{1,0:T(8,128)(2,1)S(1)}, u32[]{:S(2)}, u32[]{:S(2)}) collective-permute-start(bf16[272,512]{1,0:T(8,128)(2,1)S(1)} %get-tuple-element.18), channel_id=1, source_target_pairs={{6,0},{8,14},{7,1},{9,15},{22,16},{24,30},{23,17},{25,31}} | collective-permute-start | bytes 835592 | tf_op jit(solution)/shard_map/ppermute | solution.py:674
  33.7 6.0 %collective-permute-start.4 = (bf16[272,512]{1,0:T(8,128)(2,1)S(1)}, bf16[272,512]{1,0:T(8,128)(2,1)S(1)}, u32[]{:S(2)}, u32[]{:S(2)}) collective-permute-start(bf16[272,512]{1,0:T(8,128)(2,1)S(1)} %get-tuple-element.19._sent), channel_id=1, source_target_pairs={{0,8},{2,10},{4,12},{6,14},{8,0},{10,2},{12,4},{14,6},{1,9},{3,11}... | collective-permute-start | bytes 835592 | tf_op jit(solution)/shard_map/ppermute | solution.py:673
  39.7 0.0 collective-permute-done.7.images_ref
  39.7 3.8 %annual_pairs.1._ = f32[2,24,64,512]{3,2,1,0:T(8,128)} custom-call(s32[4,192]{1,0:T(4,128)S(1)} %pad_add_fusion.lists.pairs_ref, bf16[2,6,64,512]{3,2,1,0:T(8,128)(2,1)S(1)} %copy-done, bf16[2,6,64,128]{3,2,1,0:T(8,128)(2,1)S(1)} %collective-permute-done.rim_ref, bf16[5,2,768,256]{3,2,1,0:T(8,128)(2,1)S(1)} %range_bands.1.bands_ref, ...), custom_call_target="tpu_custom_call", output_to_operand_aliasing={{}: (9, {})} | custom-call | flops 8000000000 | bytes 1 | tf_op jit(solution)/shard_map/annual_pairs/pallas_call | solution.py:650
  43.5 0.0 collective-permute-done.5.outer_ref
  43.5 0.0 collective-permute-done.6.middle_ref
  43.5 3.9 %near_pairs.1._ = f32[2,24,64,512]{3,2,1,0:T(8,128)} custom-call(s32[4,192]{1,0:T(4,128)S(1)} %pad_add_fusion.lists.pairs_ref, bf16[2,6,64,512]{3,2,1,0:T(8,128)(2,1)S(1)} %copy-done, bf16[2,6,64,128]{3,2,1,0:T(8,128)(2,1)S(1)} %collective-permute-done.rim_ref, bf16[5,2,768,256]{3,2,1,0:T(8,128)(2,1)S(1)} %range_bands.1.bands_ref, ...), custom_call_target="tpu_custom_call", output_to_operand_aliasing={{}: (8, {})} | custom-call | flops 1 | bytes 1 | tf_op jit(solution)/shard_map/near_pairs/pallas_call | solution.py:650
  47.4 0.0 collective-permute-done.3.ring_ref
  47.5 5.2 %collective-permute-done.4.images_ref = bf16[272,512]{1,0:T(8,128)(2,1)S(1)} collective-permute-done((bf16[272,512]{1,0:T(8,128)(2,1)S(1)}, bf16[272,512]{1,0:T(8,128)(2,1)S(1)}, u32[]{:S(2)}, u32[]{:S(2)}) %collective-permute-start.4) | collective-permute-done | bytes 278560 | tf_op jit(solution)/shard_map/ppermute | solution.py:673
  52.6 2.6 %last_pairs.1 = f32[2,24,64,512]{3,2,1,0:T(8,128)} custom-call(s32[4,192]{1,0:T(4,128)S(1)} %pad_add_fusion.lists.pairs_ref, bf16[2,6,64,512]{3,2,1,0:T(8,128)(2,1)S(1)} %copy-done, bf16[2,6,64,128]{3,2,1,0:T(8,128)(2,1)S(1)} %collective-permute-done.rim_ref, bf16[5,2,768,256]{3,2,1,0:T(8,128)(2,1)S(1)} %range_bands.1.bands_ref, ...), custom_call_target="tpu_custom_call", output_to_operand_aliasing={{}: (9, {})} | custom-call | flops 1 | bytes 1 | tf_op jit(solution)/shard_map/last_pairs/pallas_call | solution.py:650
Async XLA Ops:
  2.9 4.3 %collective-permute-start = (bf16[2,6,64,128]{3,2,1,0:T(8,128)(2,1)}, bf16[2,6,64,128]{3,2,1,0:T(8,128)(2,1)S(1)}, u32[]{:S(2)}, u32[]{:S(2)}) collective-permute-start(bf16[2,6,64,128]{3,2,1,0:T(8,128)(2,1)} %get-tuple-element.14), channel_id=1, source_target_pairs={{0,1},{1,0},{2,3},{3,2},{4,5},{5,4},{6,7},{7,6},{8,9},{9,8},{10,11... | collective-permute-start | bytes 589832 | tf_op jit(solution)/shard_map/ppermute | solution.py:595
  3.4 36.3 %collective-permute-start.7 = (bf16[2,4,64,512]{3,2,1,0:T(8,128)(2,1)}, bf16[2,4,64,512]{3,2,1,0:T(8,128)(2,1)S(1)}, u32[]{:S(2)}, u32[]{:S(2)}) collective-permute-start(bf16[2,4,64,512]{3,2,1,0:T(8,128)(2,1)} %get-tuple-element.21), channel_id=1, source_target_pairs={{0,8},{2,10},{4,12},{6,14},{8,0},{10,2},{12,4},{14,6},{1,9},{3,11}... | collective-permute-start | bytes 1572872 | tf_op jit(solution)/shard_map/ppermute | solution.py:594
  7.1 24.5 %collective-permute-start.2 = (bf16[64,128]{1,0:T(8,128)(2,1)}, bf16[64,128]{1,0:T(8,128)(2,1)S(1)}, u32[]{:S(2)}, u32[]{:S(2)}) collective-permute-start(bf16[64,128]{1,0:T(8,128)(2,1)} %get-tuple-element.17), channel_id=1, source_target_pairs={{0,9},{1,8},{2,11},{3,10},{4,13},{5,12},{6,15},{7,14},{8,1},{9,0},... | collective-permute-start | bytes 49160 | tf_op jit(solution)/shard_map/ppermute | solution.py:607
  7.2 1.1 %copy-start = (bf16[2,6,64,512]{3,2,1,0:T(8,128)(2,1)S(1)}, bf16[2,6,64,512]{3,2,1,0:T(8,128)(2,1)}, u32[]{:S(2)}) copy-start(bf16[2,6,64,512]{3,2,1,0:T(8,128)(2,1)} %slc_ref.13) | copy-start | bytes 2359300
  9.6 22.1 %collective-permute-start.1 = (bf16[400,512]{1,0:T(8,128)(2,1)S(1)}, bf16[400,512]{1,0:T(8,128)(2,1)S(1)}, u32[]{:S(2)}, u32[]{:S(2)}) collective-permute-start(bf16[400,512]{1,0:T(8,128)(2,1)S(1)} %get-tuple-element.16), channel_id=1, source_target_pairs={{0,6},{2,0},{4,2},{6,4},{8,10},{10,12},{12,14},{14,8},{1,7},{3,1},... | collective-permute-start | bytes 1228808 | tf_op jit(solution)/shard_map/ppermute | solution.py:615
  13.4 30.1 %collective-permute-start.5 = (bf16[400,512]{1,0:T(8,128)(2,1)S(1)}, bf16[400,512]{1,0:T(8,128)(2,1)S(1)}, u32[]{:S(2)}, u32[]{:S(2)}) collective-permute-start(bf16[400,512]{1,0:T(8,128)(2,1)S(1)} %get-tuple-element.20), channel_id=1, source_target_pairs={{0,2},{2,4},{4,6},{10,8},{12,10},{14,12},{1,3},{3,5},{5,7},{11,9},... | collective-permute-start | bytes 1228808 | tf_op jit(solution)/shard_map/ppermute | solution.py:613
  14.9 28.7 %collective-permute-start.6 = (bf16[400,512]{1,0:T(8,128)(2,1)S(1)}, bf16[400,512]{1,0:T(8,128)(2,1)S(1)}, u32[]{:S(2)}, u32[]{:S(2)}) collective-permute-start(bf16[400,512]{1,0:T(8,128)(2,1)S(1)} %get-tuple-element.20), channel_id=1, source_target_pairs={{6,8},{8,6},{7,9},{9,7},{22,24},{24,22},{23,25},{25,23}} | collective-permute-start | bytes 1228808 | tf_op jit(solution)/shard_map/ppermute | solution.py:614
  32.4 15.0 %collective-permute-start.3 = (bf16[272,512]{1,0:T(8,128)(2,1)S(1)}, bf16[272,512]{1,0:T(8,128)(2,1)S(1)}, u32[]{:S(2)}, u32[]{:S(2)}) collective-permute-start(bf16[272,512]{1,0:T(8,128)(2,1)S(1)} %get-tuple-element.18), channel_id=1, source_target_pairs={{6,0},{8,14},{7,1},{9,15},{22,16},{24,30},{23,17},{25,31}} | collective-permute-start | bytes 835592 | tf_op jit(solution)/shard_map/ppermute | solution.py:674
  33.7 18.9 %collective-permute-start.4 = (bf16[272,512]{1,0:T(8,128)(2,1)S(1)}, bf16[272,512]{1,0:T(8,128)(2,1)S(1)}, u32[]{:S(2)}, u32[]{:S(2)}) collective-permute-start(bf16[272,512]{1,0:T(8,128)(2,1)S(1)} %get-tuple-element.19._sent), channel_id=1, source_target_pairs={{0,8},{2,10},{4,12},{6,14},{8,0},{10,2},{12,4},{14,6},{1,9},{3,11}... | collective-permute-start | bytes 835592 | tf_op jit(solution)/shard_map/ppermute | solution.py:673

commit v14 on v13

--- a/solution.py
+++ b/solution.py
@@ -138,7 +138,7 @@
 
 
 def late_kernel(plan, slc_ref, rim_ref, inner_ref, pairs_ref, *refs):
-    late_ref, end_ref, tiles_ref = refs[-3:]
+    late_ref, tiles_ref = refs[-2:]
     me, strip = lax.axis_index("date"), lax.axis_index("strip")
     dates, late, rows = plan["dates"], plan["late"], plan["rows"]
     half = plan["devices"] // 2
@@ -168,18 +168,39 @@
     tiles = [tiles_ref[k, c] for k in range(late) for c in range(2)]
     write_strips(late_ref, gather_strips(tiles, strip))
 
+
+def ending_kernel(plan, slc_ref, rim_ref, middle_ref, pairs_ref, _, end_ref, tiles_ref):
+    me, strip = lax.axis_index("date"), lax.axis_index("strip")
+    dates, late, rows = plan["dates"], plan["late"], plan["rows"]
+    half = plan["devices"] // 2
+
     @pl.when((me == half) | (me == half - 1))
     def _():
         end = jnp.where(me < half, 0, 2 * half - 1)
         end_slot = jnp.where(me < half, 0, dates - late)
-        tiles = []
+        packed = read_strips(middle_ref, rows)
         for k in range(late):
             date = end * dates + end_slot + k
-            at = pairs_ref[PARTNER, date * plan["per_date"] + NEAR] - me * dates
-            at = jnp.clip(at, 0, dates - 1)
+            wanted = pairs_ref[PARTNER, date * plan["per_date"] + NEAR] - me * dates
+            own = (wanted >= 0) & (wanted < dates)
+            own_at = jnp.clip(wanted, 0, dates - 1)
+            other_at = jnp.where(me < half, wanted - dates, wanted + NEAR)
+            other_at = jnp.clip(other_at, 0, NEAR - 1)
             for c in range(2):
-                end_ref[pl.ds((2 * k + c) * rows, rows)] = slc_ref[c, at]
-                tiles.append(rim_ref[c, at])
+                here = pl.ds((2 * k + c) * rows, rows)
+
+                @pl.when(own)
+                def _():
+                    end_ref[here] = slc_ref[c, own_at]
+                    tiles_ref[k, c] = rim_ref[c, own_at]
+
+                @pl.when(jnp.logical_not(own))
+                def _():
+                    there = pl.multiple_of((2 * other_at + c) * rows, rows)
+                    end_ref[here] = middle_ref[pl.ds(there, rows)]
+                    tiles_ref[k, c] = place_strip(packed, 2 * other_at + c, strip)
+
+        tiles = [tiles_ref[k, c] for k in range(late) for c in range(2)]
         write_strips(end_ref, gather_strips(tiles, strip))
 
 
@@ -391,7 +412,7 @@
 
 
 def rest_kernel(plan, lists, slc_ref, rim_ref, bands_ref, powers_ref, inner_ref, outer_ref,
-                middle_ref, _, out_ref, *scratch):
+                middle_ref, _sent, _late, _, out_ref, *scratch):
     pairs = Pairs(plan, lists, slc_ref, rim_ref, bands_ref, powers_ref, out_ref, scratch)
     dates = plan["dates"]
     upper = pairs.me >= plan["devices"] // 2 if plan["halves"] else True
@@ -415,6 +436,8 @@
 
 def annual_kernel(plan, lists, slc_ref, rim_ref, bands_ref, powers_ref, ring_ref,
                   images_ref, strips_ref, _sent, _, out_ref, *scratch, is_late):
+    mark_ref, *scratch = scratch
+    mark_ref[...] = jnp.zeros_like(mark_ref)
     pairs = Pairs(plan, lists, slc_ref, rim_ref, bands_ref, powers_ref, out_ref, scratch)
     dates, late = plan["dates"], plan["late"]
     half = plan["devices"] // 2
@@ -435,13 +458,13 @@
         slot = base + k
         date = me * dates + slot
         other = pairs.partner(date * plan["per_date"] + NEAR)
-        far = (other < split_date) == lower
-        end = 2 * split_date
         if is_late:
+            far = (me == 0) | (me == 2 * half - 1)
             ring_at = k
         else:
-            ring_at = jnp.where(lower, other, other - (end - NEAR))
-        ring_at = jnp.clip(ring_at, 0, NEAR - 1)
+            far = (other < split_date) == lower
+            ring_at = jnp.where(lower, other, other - (2 * split_date - NEAR))
+            ring_at = jnp.clip(ring_at, 0, NEAR - 1)
         fetch = pairs.fetch_payload
         pl.when(far)(lambda: fetch(x, ring_ref, ring_at))
         near_side = jnp.logical_not(far)
@@ -646,12 +669,12 @@
         name="own_pairs",
     )(lists, slc, rim, bands)
 
-    def more_pairs(kernel, out, others, name, flops=1):
+    def more_pairs(kernel, out, others, name, flops=1, marks=()):
         return pl.pallas_call(
             functools.partial(kernel, plan),
-            out_shape=out_shape,
+            out_shape=(out_shape, *marks),
             in_specs=[SMEM] + [VMEM] * (4 + len(others)) + [ANY],
-            out_specs=ANY,
+            out_specs=(ANY, *[VMEM for mark in marks]),
             scratch_shapes=scratch,
             input_output_aliases={5 + len(others): 0},
             compiler_params=limit(WORK_MIB),
@@ -660,27 +683,40 @@
         )(lists, slc, rim, bands, powers, *others, out)
 
     if halves:
-        payload, ending = pl.pallas_call(
+        payload = sent = pl.pallas_call(
             functools.partial(late_kernel, plan),
-            out_shape=(payload_shape(late), payload_shape(late)),
+            out_shape=payload_shape(late),
             in_specs=[VMEM, VMEM, VMEM, SMEM, ANY, ANY],
-            out_specs=(VMEM, VMEM),
+            out_specs=VMEM,
             scratch_shapes=[pltpu.VMEM((late, planes, rows, TILE), dtype)],
             compiler_params=limit(WORK_MIB),
             name="late_images",
         )(slc, rim, inner, lists, powers, strips)
-        sent = payload
-        payload = lax.ppermute(payload, "date", swap)
-        ending = lax.ppermute(ending, "date", [(half - 1, 0), (half, devices - 1)])
+        late_swap = [(a, b) for a, b in swap if a not in (half - 1, half)]
+        payload = lax.ppermute(payload, "date", late_swap)
     if halves:
         early_pairs = functools.partial(annual_kernel, is_late=False)
-        out = more_pairs(early_pairs, out, (inner, early, strips, sent), "annual_pairs", ANNUAL_FLOPS)
-        out = more_pairs(rest_kernel, out, (inner, outer, middle), "near_pairs")
+        marks = (jax.ShapeDtypeStruct((8, TILE), jnp.float32),)
+        others = (inner, early, strips, sent)
+        out, mark = more_pairs(early_pairs, out, others, "annual_pairs", ANNUAL_FLOPS, marks)
+        ending = ended = pl.pallas_call(
+            functools.partial(ending_kernel, plan),
+            out_shape=payload_shape(late),
+            in_specs=[VMEM, VMEM, VMEM, SMEM, ANY],
+            out_specs=VMEM,
+            scratch_shapes=[pltpu.VMEM((late, planes, rows, TILE), dtype)],
+            compiler_params=limit(WORK_MIB),
+            name="ending_images",
+        )(slc, rim, middle, lists, mark)
+        ending = lax.ppermute(ending, "date", [(half - 1, 0), (half, devices - 1)])
+        (out,) = more_pairs(rest_kernel, out, (inner, outer, middle, ended, payload), "near_pairs")
         late_pairs = functools.partial(annual_kernel, is_late=True)
-        out = more_pairs(late_pairs, out, (ending, payload, strips, sent), "last_pairs")
+        out, _ = more_pairs(
+            late_pairs, out, (ending, payload, strips, sent), "last_pairs", 1, marks
+        )
     else:
-        out = more_pairs(rest_kernel, out, (inner, outer, inner), "near_pairs")
-        out = more_pairs(plain_kernel, out, (annual, swapped_rims(annual)), "annual_pairs")
+        (out,) = more_pairs(rest_kernel, out, (inner, outer, inner, inner, inner), "near_pairs")
+        (out,) = more_pairs(plain_kernel, out, (annual, swapped_rims(annual)), "annual_pairs")
     return out
 
 

time: 56.1 us -> 60.9 us (1.086)
  waiting for transfers between devices: 12.8 us -> 20.9 us
  starting transfers between devices: 16.3 us -> 12.3 us
  Pallas kernels: 24.1 us -> 25.3 us
    ppermute x1, waiting for transfers between devices: 0.01 us -> 14.1 us  [body(): ending = lax.ppermute(ending, 'date', [(half - 1, 0), (half, devices - 1)])]
    ppermute x1, waiting for transfers between devices: 5.16 us -> 0.16 us  [body(): payload = lax.ppermute(payload, 'date', late_swap)]
    ppermute x1, starting transfers between devices: 6.03 us -> 2.06 us  [body(): payload = lax.ppermute(payload, 'date', late_swap)]
    ppermute x1, waiting for transfers between devices: 7.6 us -> 6.67 us  [body(): lax.ppermute(strips, both, [(2 * a + s, 2 * b + 1 - s) for a, b in swap f...]
    pallas_call x1, Pallas kernels: 8.47 us -> 9.4 us  [body(): pl.pallas_call(functools.partial(own_kernel, plan), out_shape=(out_shape,...]
    pallas_call x4 -> x5, Pallas kernels: 11 us -> 11.3 us  [the longest x3 9.63 us: more_pairs(): pl.pallas_call(functools.partial(kernel, plan), out_shape=(out_shape, *ma...]
  transfers between devices with their start and end apart: 8 -> 8, of which waited for: 2 -> 3; matrix products, arithmetic and copies ran while one was open for 1% -> 1% of each run, Pallas kernels for 34% -> 32%
where the time goes in v14:
time: 60.9 us; the launch traced here: 60.6 us
  Pallas kernels  25.3 us (42%)
  waiting for transfers between devices  20.9 us (34%)
  starting transfers between devices  12.3 us (20%)
  local copies, waits for them, and re-layouts  1.13 us (2%)
  other arithmetic  0.72 us (1%)
    ppermute x1, waiting for transfers between devices, body(): ending = lax.ppermute(ending, 'date', [(half - 1, 0), (half, devices - 1)])  14.1 us
    pallas_call x3, Pallas kernels, more_pairs(): pl.pallas_call(functools.partial(kernel, plan), out_shape=(out_shape, *ma...  9.63 us
    pallas_call x1, Pallas kernels, body(): pl.pallas_call(functools.partial(own_kernel, plan), out_shape=(out_shape,...  9.4 us
    ppermute x1, waiting for transfers between devices, body(): lax.ppermute(strips, both, [(2 * a + s, 2 * b + 1 - s) for a, b in swap f...  6.67 us
    ppermute x1, starting transfers between devices, body(): early = lax.ppermute(early, 'date', swap)  3.71 us
    pallas_call x1, Pallas kernels, body(): pl.pallas_call(functools.partial(early_kernel, plan), out_shape=(images(d...  2.89 us
    ppermute x1, starting transfers between devices, body(): inner = lax.ppermute(inner, 'date', down)  2.56 us
    ppermute x1, starting transfers between devices, body(): payload = lax.ppermute(payload, 'date', late_swap)  2.06 us
  transfers between devices with their start and end apart: 8, of which 3 were waited for; matrix products, arithmetic and copies ran while one was open for 1% of the time, Pallas kernels for 32%

profile of v14, /device:TPU:0, one launch (start us, length us, event | category | flops | bytes accessed | tf_op | source)
XLA Modules:
  0.0 60.6 jit_solution(6076900054899192994)
XLA Ops:
  0.0 2.9 %early_images.1 = (bf16[2,4,64,512]{3,2,1,0:T(8,128)(2,1)}, bf16[2,6,64,128]{3,2,1,0:T(8,128)(2,1)}, bf16[64,128]{1,0:T(8,128)(2,1)}) custom-call(bf16[2,6,64,512]{3,2,1,0:T(8,128)(2,1)} %slc_ref.15, s32[2,192]{1,0:T(2,128)} %bitcast.3), custom_call_target="tpu_custom_call" | custom-call | tf_op jit(solution)/shard_map/early_images/pallas_call | solution.py:599
  2.9 0.5 collective-permute-start
  3.4 3.7 %collective-permute-start.3 = (bf16[2,4,64,512]{3,2,1,0:T(8,128)(2,1)}, bf16[2,4,64,512]{3,2,1,0:T(8,128)(2,1)S(1)}, u32[]{:S(2)}, u32[]{:S(2)}) collective-permute-start(bf16[2,4,64,512]{3,2,1,0:T(8,128)(2,1)} %get-tuple-element.19), channel_id=1, source_target_pairs={{0,8},{2,10},{4,12},{6,14},{8,0},{10,2},{12,4},{14,6},{1,9},{3,11}... | collective-permute-start | bytes 1572872 | tf_op jit(solution)/shard_map/ppermute | solution.py:617
  7.1 0.1 collective-permute-start.4
  7.2 0.0 collective-permute-done.rim_ref
  7.2 0.0 copy-start
  7.2 1.1 %copy-done = bf16[2,6,64,512]{3,2,1,0:T(8,128)(2,1)S(1)} copy-done((bf16[2,6,64,512]{3,2,1,0:T(8,128)(2,1)S(1)}, bf16[2,6,64,512]{3,2,1,0:T(8,128)(2,1)}, u32[]{:S(2)}) %copy-start) | copy-done | bytes 786456
  8.3 1.2 %beside_images.1 = (bf16[400,512]{1,0:T(8,128)(2,1)S(1)}, bf16[400,512]{1,0:T(8,128)(2,1)S(1)}) custom-call(bf16[2,6,64,512]{3,2,1,0:T(8,128)(2,1)S(1)} %copy-done, bf16[2,6,64,128]{3,2,1,0:T(8,128)(2,1)S(1)} %collective-permute-done.rim_ref), custom_call_target="tpu_custom_call" | custom-call | tf_op jit(solution)/shard_map/beside_images/pallas_call | solution.py:619
  9.6 2.6 %collective-permute-start.2 = (bf16[400,512]{1,0:T(8,128)(2,1)S(1)}, bf16[400,512]{1,0:T(8,128)(2,1)S(1)}, u32[]{:S(2)}, u32[]{:S(2)}) collective-permute-start(bf16[400,512]{1,0:T(8,128)(2,1)S(1)} %get-tuple-element.18), channel_id=1, source_target_pairs={{0,6},{2,0},{4,2},{6,4},{8,10},{10,12},{12,14},{14,8},{1,7},{3,1},... | collective-permute-start | bytes 1228808 | tf_op jit(solution)/shard_map/ppermute | solution.py:638
  12.1 0.7 %pad_add_fusion.lists.pairs_ref = s32[4,192]{1,0:T(4,128)S(1)} fusion(s32[1,192]{1,0:T(1,128)} %bitcast.5, s32[1,192]{1,0:T(1,128)} %bitcast.6, s32[2,192]{1,0:T(2,128)} %bitcast.4), kind=kLoop, calls=%fused_computation | loop fusion | flops 1536 | bytes 6144 | tf_op jit(solution)/shard_map/concatenate | solution.py:557
  12.9 0.5 range_bands.1.bands_ref
  13.4 0.7 %collective-permute-start.1 = (bf16[400,512]{1,0:T(8,128)(2,1)S(1)}, bf16[400,512]{1,0:T(8,128)(2,1)S(1)}, u32[]{:S(2)}, u32[]{:S(2)}) collective-permute-start(bf16[400,512]{1,0:T(8,128)(2,1)S(1)} %get-tuple-element.17), channel_id=1, source_target_pairs={{6,8},{8,6},{7,9},{9,7},{22,24},{24,22},{23,25},{25,23}} | collective-permute-start | bytes 1228808 | tf_op jit(solution)/shard_map/ppermute | solution.py:637
  14.1 1.4 %collective-permute-start.7 = (bf16[400,512]{1,0:T(8,128)(2,1)S(1)}, bf16[400,512]{1,0:T(8,128)(2,1)S(1)}, u32[]{:S(2)}, u32[]{:S(2)}) collective-permute-start(bf16[400,512]{1,0:T(8,128)(2,1)S(1)} %get-tuple-element.17), channel_id=1, source_target_pairs={{0,2},{2,4},{4,6},{10,8},{12,10},{14,12},{1,3},{3,5},{5,7},{11,9},... | collective-permute-start | bytes 1228808 | tf_op jit(solution)/shard_map/ppermute | solution.py:636
  15.6 9.4 %own_pairs.1 = (f32[2,24,64,512]{3,2,1,0:T(8,128)}, bf16[6,64,1536]{2,1,0:T(8,128)(2,1)S(1)}) custom-call(s32[4,192]{1,0:T(4,128)S(1)} %pad_add_fusion.lists.pairs_ref, bf16[2,6,64,512]{3,2,1,0:T(8,128)(2,1)S(1)} %copy-done, bf16[2,6,64,128]{3,2,1,0:T(8,128)(2,1)S(1)} %collective-permute-done.rim_ref, bf16[5,2,768,256]{3,2,1,0:T(8,128)(2,1)S(1)} %range_bands.1.bands_ref), custom_call_target="tpu_custom_call" | custom-call | flops 4000000000 | bytes 1 | tf_op jit(solution)/shard_map/own_pairs/pallas_call | solution.py:661
  25.0 6.7 %collective-permute-done.4.refs_1_.strips_ref = bf16[64,128]{1,0:T(8,128)(2,1)S(1)} collective-permute-done((bf16[64,128]{1,0:T(8,128)(2,1)}, bf16[64,128]{1,0:T(8,128)(2,1)S(1)}, u32[]{:S(2)}, u32[]{:S(2)}) %collective-permute-start.4) | collective-permute-done | bytes 16416 | tf_op jit(solution)/shard_map/ppermute | solution.py:630
  31.6 0.0 collective-permute-done.2.inner_ref.ring_ref
  31.6 1.0 %late_images.1._sent = bf16[272,512]{1,0:T(8,128)(2,1)S(1)} custom-call(bf16[2,6,64,512]{3,2,1,0:T(8,128)(2,1)S(1)} %copy-done, bf16[2,6,64,128]{3,2,1,0:T(8,128)(2,1)S(1)} %collective-permute-done.rim_ref, bf16[400,512]{1,0:T(8,128)(2,1)S(1)} %collective-permute-done.2.inner_ref.ring_ref, s32[4,192]{1,0:T(4,128)S(1)} %pad_add_fusion.lists.pairs_ref, ...), custom_call_target="tpu_custom_call" | custom-call | tf_op jit(solution)/shard_map/late_images/pallas_call | solution.py:686
  32.7 2.1 %collective-permute-start.6 = (bf16[272,512]{1,0:T(8,128)(2,1)S(1)}, bf16[272,512]{1,0:T(8,128)(2,1)S(1)}, u32[]{:S(2)}, u32[]{:S(2)}) collective-permute-start(bf16[272,512]{1,0:T(8,128)(2,1)S(1)} %late_images.1._sent), channel_id=1, source_target_pairs={{0,8},{2,10},{4,12},{10,2},{12,4},{14,6},{1,9},{3,11},{5,13},{11,3... | collective-permute-start | bytes 835592 | tf_op jit(solution)/shard_map/ppermute | solution.py:696
  34.7 0.0 collective-permute-done.3.images_ref
  34.7 3.8 %annual_pairs.1 = (f32[2,24,64,512]{3,2,1,0:T(8,128)}, f32[8,128]{1,0:T(8,128)S(1)}) custom-call(s32[4,192]{1,0:T(4,128)S(1)} %pad_add_fusion.lists.pairs_ref, bf16[2,6,64,512]{3,2,1,0:T(8,128)(2,1)S(1)} %copy-done, bf16[2,6,64,128]{3,2,1,0:T(8,128)(2,1)S(1)} %collective-permute-done.rim_ref, ...), custom_call_target="tpu_custom_call", output_to_operand_aliasing={{0}: (9, {})} | custom-call | flops 8000000000 | bytes 1 | tf_op jit(solution)/shard_map/annual_pairs/pallas_call | solution.py:673
  38.5 0.0 collective-permute-done.1.middle_ref
  38.5 0.6 %ending_images.1._sent = bf16[272,512]{1,0:T(8,128)(2,1)S(1)} custom-call(bf16[2,6,64,512]{3,2,1,0:T(8,128)(2,1)S(1)} %copy-done, bf16[2,6,64,128]{3,2,1,0:T(8,128)(2,1)S(1)} %collective-permute-done.rim_ref, bf16[400,512]{1,0:T(8,128)(2,1)S(1)} %collective-permute-done.1.middle_ref, s32[4,192]{1,0:T(4,128)S(1)} %pad_add_fusion.lists.pairs_ref, ...), custom_call_target="tpu_custom_call" | custom-call | tf_op jit(solution)/shard_map/ending_images/pallas_call | solution.py:702
  39.1 1.3 %collective-permute-start.5 = (bf16[272,512]{1,0:T(8,128)(2,1)S(1)}, bf16[272,512]{1,0:T(8,128)(2,1)S(1)}, u32[]{:S(2)}, u32[]{:S(2)}) collective-permute-start(bf16[272,512]{1,0:T(8,128)(2,1)S(1)} %ending_images.1._sent), channel_id=1, source_target_pairs={{6,0},{8,14},{7,1},{9,15},{22,16},{24,30},{23,17},{25,31}} | collective-permute-start | bytes 835592 | tf_op jit(solution)/shard_map/ppermute | solution.py:711
  40.4 0.0 collective-permute-done.7.outer_ref
  40.5 0.2 collective-permute-done.6._late.images_ref
  40.6 2.7 %near_pairs.1._ = f32[2,24,64,512]{3,2,1,0:T(8,128)} custom-call(s32[4,192]{1,0:T(4,128)S(1)} %pad_add_fusion.lists.pairs_ref, bf16[2,6,64,512]{3,2,1,0:T(8,128)(2,1)S(1)} %copy-done, bf16[2,6,64,128]{3,2,1,0:T(8,128)(2,1)S(1)} %collective-permute-done.rim_ref, bf16[5,2,768,256]{3,2,1,0:T(8,128)(2,1)S(1)} %range_bands.1.bands_ref, ...), custom_call_target="tpu_custom_call", output_to_operand_aliasing={{}: (10, {})} | custom-call | flops 1 | bytes 1 | tf_op jit(solution)/shard_map/near_pairs/pallas_call | solution.py:673
  43.3 14.1 %collective-permute-done.5.ring_ref = bf16[272,512]{1,0:T(8,128)(2,1)S(1)} collective-permute-done((bf16[272,512]{1,0:T(8,128)(2,1)S(1)}, bf16[272,512]{1,0:T(8,128)(2,1)S(1)}, u32[]{:S(2)}, u32[]{:S(2)}) %collective-permute-start.5) | collective-permute-done | bytes 278560 | tf_op jit(solution)/shard_map/ppermute | solution.py:711
  57.4 3.2 %last_pairs.1 = (f32[2,24,64,512]{3,2,1,0:T(8,128)}, f32[8,128]{1,0:T(8,128)}) custom-call(s32[4,192]{1,0:T(4,128)S(1)} %pad_add_fusion.lists.pairs_ref, bf16[2,6,64,512]{3,2,1,0:T(8,128)(2,1)S(1)} %copy-done, bf16[2,6,64,128]{3,2,1,0:T(8,128)(2,1)S(1)} %collective-permute-done.rim_ref, ...), custom_call_target="tpu_custom_call", output_to_operand_aliasing={{0}: (9, {})} | custom-call | flops 1 | bytes 1 | tf_op jit(solution)/shard_map/last_pairs/pallas_call | solution.py:673
Async XLA Ops:
  2.9 4.3 %collective-permute-start = (bf16[2,6,64,128]{3,2,1,0:T(8,128)(2,1)}, bf16[2,6,64,128]{3,2,1,0:T(8,128)(2,1)S(1)}, u32[]{:S(2)}, u32[]{:S(2)}) collective-permute-start(bf16[2,6,64,128]{3,2,1,0:T(8,128)(2,1)} %get-tuple-element.15), channel_id=1, source_target_pairs={{0,1},{1,0},{2,3},{3,2},{4,5},{5,4},{6,7},{7,6},{8,9},{9,8},{10,11... | collective-permute-start | bytes 589832 | tf_op jit(solution)/shard_map/ppermute | solution.py:618
  3.4 31.3 %collective-permute-start.3 = (bf16[2,4,64,512]{3,2,1,0:T(8,128)(2,1)}, bf16[2,4,64,512]{3,2,1,0:T(8,128)(2,1)S(1)}, u32[]{:S(2)}, u32[]{:S(2)}) collective-permute-start(bf16[2,4,64,512]{3,2,1,0:T(8,128)(2,1)} %get-tuple-element.19), channel_id=1, source_target_pairs={{0,8},{2,10},{4,12},{6,14},{8,0},{10,2},{12,4},{14,6},{1,9},{3,11}... | collective-permute-start | bytes 1572872 | tf_op jit(solution)/shard_map/ppermute | solution.py:617
  7.1 24.5 %collective-permute-start.4 = (bf16[64,128]{1,0:T(8,128)(2,1)}, bf16[64,128]{1,0:T(8,128)(2,1)S(1)}, u32[]{:S(2)}, u32[]{:S(2)}) collective-permute-start(bf16[64,128]{1,0:T(8,128)(2,1)} %get-tuple-element.20), channel_id=1, source_target_pairs={{0,9},{1,8},{2,11},{3,10},{4,13},{5,12},{6,15},{7,14},{8,1},{9,0},... | collective-permute-start | bytes 49160 | tf_op jit(solution)/shard_map/ppermute | solution.py:630
  7.2 1.1 %copy-start = (bf16[2,6,64,512]{3,2,1,0:T(8,128)(2,1)S(1)}, bf16[2,6,64,512]{3,2,1,0:T(8,128)(2,1)}, u32[]{:S(2)}) copy-start(bf16[2,6,64,512]{3,2,1,0:T(8,128)(2,1)} %slc_ref.15) | copy-start | bytes 2359300
  9.6 22.1 %collective-permute-start.2 = (bf16[400,512]{1,0:T(8,128)(2,1)S(1)}, bf16[400,512]{1,0:T(8,128)(2,1)S(1)}, u32[]{:S(2)}, u32[]{:S(2)}) collective-permute-start(bf16[400,512]{1,0:T(8,128)(2,1)S(1)} %get-tuple-element.18), channel_id=1, source_target_pairs={{0,6},{2,0},{4,2},{6,4},{8,10},{10,12},{12,14},{14,8},{1,7},{3,1},... | collective-permute-start | bytes 1228808 | tf_op jit(solution)/shard_map/ppermute | solution.py:638
  13.4 25.1 %collective-permute-start.1 = (bf16[400,512]{1,0:T(8,128)(2,1)S(1)}, bf16[400,512]{1,0:T(8,128)(2,1)S(1)}, u32[]{:S(2)}, u32[]{:S(2)}) collective-permute-start(bf16[400,512]{1,0:T(8,128)(2,1)S(1)} %get-tuple-element.17), channel_id=1, source_target_pairs={{6,8},{8,6},{7,9},{9,7},{22,24},{24,22},{23,25},{25,23}} | collective-permute-start | bytes 1228808 | tf_op jit(solution)/shard_map/ppermute | solution.py:637
  14.1 26.4 %collective-permute-start.7 = (bf16[400,512]{1,0:T(8,128)(2,1)S(1)}, bf16[400,512]{1,0:T(8,128)(2,1)S(1)}, u32[]{:S(2)}, u32[]{:S(2)}) collective-permute-start(bf16[400,512]{1,0:T(8,128)(2,1)S(1)} %get-tuple-element.17), channel_id=1, source_target_pairs={{0,2},{2,4},{4,6},{10,8},{12,10},{14,12},{1,3},{3,5},{5,7},{11,9},... | collective-permute-start | bytes 1228808 | tf_op jit(solution)/shard_map/ppermute | solution.py:636
  32.7 8.0 %collective-permute-start.6 = (bf16[272,512]{1,0:T(8,128)(2,1)S(1)}, bf16[272,512]{1,0:T(8,128)(2,1)S(1)}, u32[]{:S(2)}, u32[]{:S(2)}) collective-permute-start(bf16[272,512]{1,0:T(8,128)(2,1)S(1)} %late_images.1._sent), channel_id=1, source_target_pairs={{0,8},{2,10},{4,12},{10,2},{12,4},{14,6},{1,9},{3,11},{5,13},{11,3... | collective-permute-start | bytes 835592 | tf_op jit(solution)/shard_map/ppermute | solution.py:696
  39.1 18.2 %collective-permute-start.5 = (bf16[272,512]{1,0:T(8,128)(2,1)S(1)}, bf16[272,512]{1,0:T(8,128)(2,1)S(1)}, u32[]{:S(2)}, u32[]{:S(2)}) collective-permute-start(bf16[272,512]{1,0:T(8,128)(2,1)S(1)} %ending_images.1._sent), channel_id=1, source_target_pairs={{6,0},{8,14},{7,1},{9,15},{22,16},{24,30},{23,17},{25,31}} | collective-permute-start | bytes 835592 | tf_op jit(solution)/shard_map/ppermute | solution.py:711

commit v15 on v12

--- a/solution.py
+++ b/solution.py
@@ -85,27 +85,28 @@
     ]
 
 
-def early_kernel(plan, slc_ref, pairs_ref, early_ref, rim_ref, strips_ref, tiles_ref, sems,
-                 tile_sems, rim_sem):
+def early_kernel(plan, slc_ref, pairs_ref, early_ref, rim_ref, sems, rim_sem):
+    strip, cols = lax.axis_index("strip"), plan["cols"]
+    start = pl.multiple_of(jnp.where(strip == 0, cols - TILE, 0), TILE)
+    rim_copy = pltpu.make_async_copy(slc_ref.at[:, :, :, pl.ds(start, TILE)], rim_ref, rim_sem)
+    early_copies = image_copies(slc_ref, wanted_images(plan, pairs_ref), early_ref, sems)
+    run_copies([rim_copy] + early_copies)
+
+
+def edges_kernel(plan, slc_ref, pairs_ref, _, strips_ref, tiles_ref, tile_sems):
     strip, cols = lax.axis_index("strip"), plan["cols"]
     start = pl.multiple_of(jnp.where(strip == 0, cols - TILE, 0), TILE)
     wanted = wanted_images(plan, pairs_ref)
-    rim_copy = pltpu.make_async_copy(slc_ref.at[:, :, :, pl.ds(start, TILE)], rim_ref, rim_sem)
-    early_copies = image_copies(slc_ref, wanted, early_ref, sems)
-    tile_copies = [
-        pltpu.make_async_copy(
-            slc_ref.at[:, at, :, pl.ds(start, TILE)], tiles_ref.at[k], tile_sems.at[k]
-        )
-        for k, at in enumerate(wanted)
-    ]
-    for copy in tile_copies + [rim_copy] + early_copies:
-        copy.start()
-    for copy in tile_copies:
-        copy.wait()
+    run_copies(
+        [
+            pltpu.make_async_copy(
+                slc_ref.at[:, at, :, pl.ds(start, TILE)], tiles_ref.at[k], tile_sems.at[k]
+            )
+            for k, at in enumerate(wanted)
+        ]
+    )
     tiles = [tiles_ref[k, c] for k in range(len(wanted)) for c in range(2)]
     strips_ref[...] = gather_strips(tiles, 1 - strip)
-    for copy in [rim_copy] + early_copies:
-        copy.wait()
 
 
 def rim_kernel(slc_ref, rim_ref, sem):
@@ -559,24 +560,27 @@
     if halves:
         swap = [(i, (i + half) % devices) for i in range(devices)]
         both = ("date", "strip")
-        early, rim, strips = pl.pallas_call(
+        early, rim = pl.pallas_call(
             functools.partial(early_kernel, plan),
-            out_shape=(
-                images(dates - late),
-                rim_shape(dates),
-                jax.ShapeDtypeStruct((rows, TILE), dtype),
-            ),
+            out_shape=(images(dates - late), rim_shape(dates)),
             in_specs=[ANY, SMEM],
-            out_specs=(VMEM, VMEM, VMEM),
+            out_specs=(VMEM, VMEM),
+            scratch_shapes=[pltpu.SemaphoreType.DMA((dates - late,)), pltpu.SemaphoreType.DMA],
+            compiler_params=limit(FIRST_MIB),
+            name="early_images",
+        )(slc, pairs)
+        strips = pl.pallas_call(
+            functools.partial(edges_kernel, plan),
+            out_shape=jax.ShapeDtypeStruct((rows, TILE), dtype),
+            in_specs=[ANY, SMEM, ANY],
+            out_specs=VMEM,
             scratch_shapes=[
                 pltpu.VMEM((dates - late, planes, rows, TILE), dtype),
                 pltpu.SemaphoreType.DMA((dates - late,)),
-                pltpu.SemaphoreType.DMA((dates - late,)),
-                pltpu.SemaphoreType.DMA,
             ],
             compiler_params=limit(FIRST_MIB),
-            name="early_images",
-        )(slc, pairs)
+            name="early_edges",
+        )(slc, pairs, rim)
         early = lax.ppermute(early, "date", swap)
         rim = lax.ppermute(rim, "strip", swap_strips)
         inner, outer = pl.pallas_call(

time: 55.4 us -> 56 us (1.011); the launches traced: 55.2 us -> 55 us
  waiting for transfers between devices: 20.2 us -> 15.9 us
  starting transfers between devices: 7.76 us -> 10.1 us
  Pallas kernels: 25.3 us -> 27.1 us
    ppermute x1, waiting for transfers between devices: 9.06 us -> 4.83 us  [body(): lax.ppermute(strips, both, [(2 * a + s, 2 * b + 1 - s) for a, b in swap f...]
    pallas_call x3, Pallas kernels: 11.4 us -> 8.97 us  [more_pairs(): pl.pallas_call(functools.partial(kernel, plan), out_shape=out_shape, in_s...]
    pallas_call x0 -> x1, Pallas kernels: none -> 2.27 us  [body(): pl.pallas_call(functools.partial(edges_kernel, plan), out_shape=jax.Shape...]
    ppermute x1, starting transfers between devices: 0.17 us -> 2.42 us  [body(): payload = lax.ppermute(payload, 'date', swap)]
    pallas_call x1, Pallas kernels: 8.39 us -> 10.3 us  [body(): pl.pallas_call(functools.partial(own_kernel, plan), out_shape=(out_shape,...]
  transfers between devices with their start and end apart: 7 -> 7, of which waited for: 2 -> 2; matrix products, arithmetic and copies ran while one was open for 1% -> 1% of each run, Pallas kernels for 36% -> 39%
where the time goes in v15:
time: 56 us; the launch traced here: 55 us
  Pallas kernels  27.1 us (48%)
  waiting for transfers between devices  15.9 us (28%)
  starting transfers between devices  10.1 us (18%)
  local copies, waits for them, and re-layouts  1.13 us (2%)
  other arithmetic  0.72 us (1%)
    ppermute x1, waiting for transfers between devices, body(): payload = lax.ppermute(payload, 'date', swap)  11.1 us
    pallas_call x1, Pallas kernels, body(): pl.pallas_call(functools.partial(own_kernel, plan), out_shape=(out_shape,...  10.3 us
    pallas_call x3, Pallas kernels, more_pairs(): pl.pallas_call(functools.partial(kernel, plan), out_shape=out_shape, in_s...  8.97 us
    ppermute x1, waiting for transfers between devices, body(): lax.ppermute(strips, both, [(2 * a + s, 2 * b + 1 - s) for a, b in swap f...  4.83 us
    ppermute x1, starting transfers between devices, body(): early = lax.ppermute(early, 'date', swap)  3.66 us
    pallas_call x1, Pallas kernels, body(): pl.pallas_call(functools.partial(early_kernel, plan), out_shape=(images(d...  2.8 us
    ppermute x1, starting transfers between devices, body(): inner = lax.ppermute(inner, 'date', down)  2.56 us
    ppermute x1, starting transfers between devices, body(): payload = lax.ppermute(payload, 'date', swap)  2.42 us
  transfers between devices with their start and end apart: 7, of which 2 were waited for; matrix products, arithmetic and copies ran while one was open for 1% of the time, Pallas kernels for 39%

profile of v15, /device:TPU:0, one launch (start us, length us, event | category | flops | bytes accessed | tf_op | source)
XLA Modules:
  0.0 55.0 jit_solution(5191769895614150892)
XLA Ops:
  0.0 2.8 %early_images.1 = (bf16[2,4,64,512]{3,2,1,0:T(8,128)(2,1)}, bf16[2,6,64,128]{3,2,1,0:T(8,128)(2,1)}) custom-call(bf16[2,6,64,512]{3,2,1,0:T(8,128)(2,1)} %slc_ref.15, s32[2,192]{1,0:T(2,128)} %bitcast.3), custom_call_target="tpu_custom_call" | custom-call | tf_op jit(solution)/shard_map/early_images/pallas_call | solution.py:563
  2.8 0.5 collective-permute-start
  3.3 3.7 %collective-permute-start.6 = (bf16[2,4,64,512]{3,2,1,0:T(8,128)(2,1)}, bf16[2,4,64,512]{3,2,1,0:T(8,128)(2,1)S(1)}, u32[]{:S(2)}, u32[]{:S(2)}) collective-permute-start(bf16[2,4,64,512]{3,2,1,0:T(8,128)(2,1)} %get-tuple-element.15), channel_id=1, source_target_pairs={{0,8},{2,10},{4,12},{6,14},{8,0},{10,2},{12,4},{14,6},{1,9},{3,11}... | collective-permute-start | bytes 1572872 | tf_op jit(solution)/shard_map/ppermute | solution.py:584
  7.0 2.3 %early_edges.1 = bf16[64,128]{1,0:T(8,128)(2,1)} custom-call(bf16[2,6,64,512]{3,2,1,0:T(8,128)(2,1)} %slc_ref.15, s32[2,192]{1,0:T(2,128)} %bitcast.4, bf16[2,6,64,128]{3,2,1,0:T(8,128)(2,1)} %get-tuple-element.11._), custom_call_target="tpu_custom_call" | custom-call | tf_op jit(solution)/shard_map/early_edges/pallas_call | solution.py:572
  9.3 0.2 collective-permute-start.3
  9.4 0.0 collective-permute-done.rim_ref
  9.4 0.0 copy-start
  9.4 1.1 %copy-done = bf16[2,6,64,512]{3,2,1,0:T(8,128)(2,1)S(1)} copy-done((bf16[2,6,64,512]{3,2,1,0:T(8,128)(2,1)S(1)}, bf16[2,6,64,512]{3,2,1,0:T(8,128)(2,1)}, u32[]{:S(2)}) %copy-start) | copy-done | bytes 786456
  10.6 1.2 %beside_images.1 = (bf16[400,512]{1,0:T(8,128)(2,1)S(1)}, bf16[400,512]{1,0:T(8,128)(2,1)S(1)}) custom-call(bf16[2,6,64,512]{3,2,1,0:T(8,128)(2,1)S(1)} %copy-done, bf16[2,6,64,128]{3,2,1,0:T(8,128)(2,1)S(1)} %collective-permute-done.rim_ref), custom_call_target="tpu_custom_call" | custom-call | tf_op jit(solution)/shard_map/beside_images/pallas_call | solution.py:586
  11.8 2.6 %collective-permute-start.2 = (bf16[400,512]{1,0:T(8,128)(2,1)S(1)}, bf16[400,512]{1,0:T(8,128)(2,1)S(1)}, u32[]{:S(2)}, u32[]{:S(2)}) collective-permute-start(bf16[400,512]{1,0:T(8,128)(2,1)S(1)} %get-tuple-element.14), channel_id=1, source_target_pairs={{0,6},{2,0},{4,2},{6,4},{8,10},{10,12},{12,14},{14,8},{1,7},{3,1},... | collective-permute-start | bytes 1228808 | tf_op jit(solution)/shard_map/ppermute | solution.py:602
  14.4 0.7 %pad_add_fusion.lists.pairs_ref = s32[4,192]{1,0:T(4,128)S(1)} fusion(s32[1,192]{1,0:T(1,128)} %bitcast.6, s32[1,192]{1,0:T(1,128)} %bitcast.7, s32[2,192]{1,0:T(2,128)} %bitcast.5), kind=kLoop, calls=%fused_computation | loop fusion | flops 1536 | bytes 6144 | tf_op jit(solution)/shard_map/concatenate | solution.py:521
  15.1 0.5 range_bands.1.bands_ref
  15.6 0.1 collective-permute-start.1
  15.7 0.7 %collective-permute-start.5 = (bf16[400,512]{1,0:T(8,128)(2,1)S(1)}, bf16[400,512]{1,0:T(8,128)(2,1)S(1)}, u32[]{:S(2)}, u32[]{:S(2)}) collective-permute-start(bf16[400,512]{1,0:T(8,128)(2,1)S(1)} %get-tuple-element.13), channel_id=1, source_target_pairs={{6,8},{8,6},{7,9},{9,7},{22,24},{24,22},{23,25},{25,23}} | collective-permute-start | bytes 1228808 | tf_op jit(solution)/shard_map/ppermute | solution.py:600
  16.4 10.3 %own_pairs.1 = (f32[2,24,64,512]{3,2,1,0:T(8,128)}, bf16[6,64,1536]{2,1,0:T(8,128)(2,1)S(1)}) custom-call(s32[4,192]{1,0:T(4,128)S(1)} %pad_add_fusion.lists.pairs_ref, bf16[2,6,64,512]{3,2,1,0:T(8,128)(2,1)S(1)} %copy-done, bf16[2,6,64,128]{3,2,1,0:T(8,128)(2,1)S(1)} %collective-permute-done.rim_ref, bf16[5,2,768,256]{3,2,1,0:T(8,128)(2,1)S(1)} %range_bands.1.bands_ref), custom_call_target="tpu_custom_call" | custom-call | flops 4000000000 | bytes 1 | tf_op jit(solution)/shard_map/own_pairs/pallas_call | solution.py:625
  26.7 4.8 %collective-permute-done.3.refs_1_.strips_ref = bf16[64,128]{1,0:T(8,128)(2,1)S(1)} collective-permute-done((bf16[64,128]{1,0:T(8,128)(2,1)}, bf16[64,128]{1,0:T(8,128)(2,1)S(1)}, u32[]{:S(2)}, u32[]{:S(2)}) %collective-permute-start.3) | collective-permute-done | bytes 16416 | tf_op jit(solution)/shard_map/ppermute | solution.py:597
  31.5 0.0 collective-permute-done.2.inner_ref.ring_ref
  31.5 1.0 %late_images.1._sent = bf16[272,512]{1,0:T(8,128)(2,1)S(1)} custom-call(bf16[2,6,64,512]{3,2,1,0:T(8,128)(2,1)S(1)} %copy-done, bf16[2,6,64,128]{3,2,1,0:T(8,128)(2,1)S(1)} %collective-permute-done.rim_ref, bf16[400,512]{1,0:T(8,128)(2,1)S(1)} %collective-permute-done.2.inner_ref.ring_ref, s32[4,192]{1,0:T(4,128)S(1)} %pad_add_fusion.lists.pairs_ref, ...), custom_call_target="tpu_custom_call" | custom-call | tf_op jit(solution)/shard_map/late_images/pallas_call | solution.py:650
  32.5 2.4 %collective-permute-start.4 = (bf16[272,512]{1,0:T(8,128)(2,1)S(1)}, bf16[272,512]{1,0:T(8,128)(2,1)S(1)}, u32[]{:S(2)}, u32[]{:S(2)}) collective-permute-start(bf16[272,512]{1,0:T(8,128)(2,1)S(1)} %late_images.1._sent), channel_id=1, source_target_pairs={{0,8},{2,10},{4,12},{6,14},{8,0},{10,2},{12,4},{14,6},{1,9},{3,11}... | collective-permute-start | bytes 835592 | tf_op jit(solution)/shard_map/ppermute | solution.py:659
  34.9 0.0 collective-permute-done.6.images_ref
  34.9 3.8 %annual_pairs.1._ = f32[2,24,64,512]{3,2,1,0:T(8,128)} custom-call(s32[4,192]{1,0:T(4,128)S(1)} %pad_add_fusion.lists.pairs_ref, bf16[2,6,64,512]{3,2,1,0:T(8,128)(2,1)S(1)} %copy-done, bf16[2,6,64,128]{3,2,1,0:T(8,128)(2,1)S(1)} %collective-permute-done.rim_ref, bf16[5,2,768,256]{3,2,1,0:T(8,128)(2,1)S(1)} %range_bands.1.bands_ref, ...), custom_call_target="tpu_custom_call", output_to_operand_aliasing={{}: (9, {})} | custom-call | flops 8000000000 | bytes 1 | tf_op jit(solution)/shard_map/annual_pairs/pallas_call | solution.py:637
  38.7 0.0 collective-permute-done.1.outer_ref.ring_ref
  38.7 0.0 collective-permute-done.5.middle_ref
  38.7 2.6 %near_pairs.1._ = f32[2,24,64,512]{3,2,1,0:T(8,128)} custom-call(s32[4,192]{1,0:T(4,128)S(1)} %pad_add_fusion.lists.pairs_ref, bf16[2,6,64,512]{3,2,1,0:T(8,128)(2,1)S(1)} %copy-done, bf16[2,6,64,128]{3,2,1,0:T(8,128)(2,1)S(1)} %collective-permute-done.rim_ref, bf16[5,2,768,256]{3,2,1,0:T(8,128)(2,1)S(1)} %range_bands.1.bands_ref, ...), custom_call_target="tpu_custom_call", output_to_operand_aliasing={{}: (8, {})} | custom-call | flops 1 | bytes 1 | tf_op jit(solution)/shard_map/near_pairs/pallas_call | solution.py:637
  41.4 11.1 %collective-permute-done.4.images_ref = bf16[272,512]{1,0:T(8,128)(2,1)S(1)} collective-permute-done((bf16[272,512]{1,0:T(8,128)(2,1)S(1)}, bf16[272,512]{1,0:T(8,128)(2,1)S(1)}, u32[]{:S(2)}, u32[]{:S(2)}) %collective-permute-start.4) | collective-permute-done | bytes 278560 | tf_op jit(solution)/shard_map/ppermute | solution.py:659
  52.5 2.6 %last_pairs.1 = f32[2,24,64,512]{3,2,1,0:T(8,128)} custom-call(s32[4,192]{1,0:T(4,128)S(1)} %pad_add_fusion.lists.pairs_ref, bf16[2,6,64,512]{3,2,1,0:T(8,128)(2,1)S(1)} %copy-done, bf16[2,6,64,128]{3,2,1,0:T(8,128)(2,1)S(1)} %collective-permute-done.rim_ref, bf16[5,2,768,256]{3,2,1,0:T(8,128)(2,1)S(1)} %range_bands.1.bands_ref, ...), custom_call_target="tpu_custom_call", output_to_operand_aliasing={{}: (9, {})} | custom-call | flops 1 | bytes 1 | tf_op jit(solution)/shard_map/last_pairs/pallas_call | solution.py:637
Async XLA Ops:
  2.8 6.6 %collective-permute-start = (bf16[2,6,64,128]{3,2,1,0:T(8,128)(2,1)}, bf16[2,6,64,128]{3,2,1,0:T(8,128)(2,1)S(1)}, u32[]{:S(2)}, u32[]{:S(2)}) collective-permute-start(bf16[2,6,64,128]{3,2,1,0:T(8,128)(2,1)} %get-tuple-element.11._), channel_id=1, source_target_pairs={{0,1},{1,0},{2,3},{3,2},{4,5},{5,4},{6,7},{7,6},{8,9},{9,8},{10,11... | collective-permute-start | bytes 589832 | tf_op jit(solution)/shard_map/ppermute | solution.py:585
  3.3 31.6 %collective-permute-start.6 = (bf16[2,4,64,512]{3,2,1,0:T(8,128)(2,1)}, bf16[2,4,64,512]{3,2,1,0:T(8,128)(2,1)S(1)}, u32[]{:S(2)}, u32[]{:S(2)}) collective-permute-start(bf16[2,4,64,512]{3,2,1,0:T(8,128)(2,1)} %get-tuple-element.15), channel_id=1, source_target_pairs={{0,8},{2,10},{4,12},{6,14},{8,0},{10,2},{12,4},{14,6},{1,9},{3,11}... | collective-permute-start | bytes 1572872 | tf_op jit(solution)/shard_map/ppermute | solution.py:584
  9.3 22.2 %collective-permute-start.3 = (bf16[64,128]{1,0:T(8,128)(2,1)}, bf16[64,128]{1,0:T(8,128)(2,1)S(1)}, u32[]{:S(2)}, u32[]{:S(2)}) collective-permute-start(bf16[64,128]{1,0:T(8,128)(2,1)} %early_edges.1), channel_id=1, source_target_pairs={{0,9},{1,8},{2,11},{3,10},{4,13},{5,12},{6,15},{7,14},{8,1},{9,0},... | collective-permute-start | bytes 49160 | tf_op jit(solution)/shard_map/ppermute | solution.py:597
  9.4 1.1 %copy-start = (bf16[2,6,64,512]{3,2,1,0:T(8,128)(2,1)S(1)}, bf16[2,6,64,512]{3,2,1,0:T(8,128)(2,1)}, u32[]{:S(2)}) copy-start(bf16[2,6,64,512]{3,2,1,0:T(8,128)(2,1)} %slc_ref.15) | copy-start | bytes 2359300
  11.8 19.7 %collective-permute-start.2 = (bf16[400,512]{1,0:T(8,128)(2,1)S(1)}, bf16[400,512]{1,0:T(8,128)(2,1)S(1)}, u32[]{:S(2)}, u32[]{:S(2)}) collective-permute-start(bf16[400,512]{1,0:T(8,128)(2,1)S(1)} %get-tuple-element.14), channel_id=1, source_target_pairs={{0,6},{2,0},{4,2},{6,4},{8,10},{10,12},{12,14},{14,8},{1,7},{3,1},... | collective-permute-start | bytes 1228808 | tf_op jit(solution)/shard_map/ppermute | solution.py:602
  15.6 23.1 %collective-permute-start.1 = (bf16[400,512]{1,0:T(8,128)(2,1)S(1)}, bf16[400,512]{1,0:T(8,128)(2,1)S(1)}, u32[]{:S(2)}, u32[]{:S(2)}) collective-permute-start(bf16[400,512]{1,0:T(8,128)(2,1)S(1)} %get-tuple-element.13), channel_id=1, source_target_pairs={{6,0},{0,2},{2,4},{4,6},{10,8},{12,10},{14,12},{8,14},{7,1},{1,3},... | collective-permute-start | bytes 1228808 | tf_op jit(solution)/shard_map/ppermute | solution.py:601
  15.7 23.0 %collective-permute-start.5 = (bf16[400,512]{1,0:T(8,128)(2,1)S(1)}, bf16[400,512]{1,0:T(8,128)(2,1)S(1)}, u32[]{:S(2)}, u32[]{:S(2)}) collective-permute-start(bf16[400,512]{1,0:T(8,128)(2,1)S(1)} %get-tuple-element.13), channel_id=1, source_target_pairs={{6,8},{8,6},{7,9},{9,7},{22,24},{24,22},{23,25},{25,23}} | collective-permute-start | bytes 1228808 | tf_op jit(solution)/shard_map/ppermute | solution.py:600
  32.5 19.9 %collective-permute-start.4 = (bf16[272,512]{1,0:T(8,128)(2,1)S(1)}, bf16[272,512]{1,0:T(8,128)(2,1)S(1)}, u32[]{:S(2)}, u32[]{:S(2)}) collective-permute-start(bf16[272,512]{1,0:T(8,128)(2,1)S(1)} %late_images.1._sent), channel_id=1, source_target_pairs={{0,8},{2,10},{4,12},{6,14},{8,0},{10,2},{12,4},{14,6},{1,9},{3,11}... | collective-permute-start | bytes 835592 | tf_op jit(solution)/shard_map/ppermute | solution.py:659
